TPU v7x, 32 devices: a whole 2x2x4 slice. The times are simulated.
32 devices in a mesh: gx: 4 (over z), gy: 4 (over x, core), layer: 2 (over y).
Axes of the slice: x: 2, y: 2, z: 4, core: 2. Of those that a mesh axis runs over, the one named last changes fastest.
Arguments:
- atom_feats: bfloat16 [2048, 128], P(('gx', 'gy', 'layer')), may hold values from -6 to 6
- bond_embed: bfloat16 [73728, 128], P(('gx', 'gy', 'layer')), may hold values from -6 to 6
- pair_dist: float32 [147456], P(('gx', 'gy', 'layer')), may hold values from 1.4 to 6.9
- neighbours: int32 [147456], P(('gx', 'gy', 'layer')), may hold values from 0 to 1151, as said below
- slot_kind: int32 [147456], P(('gx', 'gy', 'layer')), may hold values from 0 to 2
- own_rows: int32 [73728], P(('gx', 'gy', 'layer')), may hold values from 0 to 4607, as said below
- send_pos: int32 [73728], P(('gx', 'gy', 'layer')), may hold values from 0 to 2303, as said below
- recv_pos: int32 [147456], P(('gx', 'gy', 'layer')), may hold values from 0 to 2303, as said below
- w_left: bfloat16 [3, 128, 128], replicated, may hold values from -0.5 to 0.5
- w_right: bfloat16 [3, 128, 128], replicated, may hold values from -0.5 to 0.5
- w_edge_in: bfloat16 [3, 128, 128], replicated, may hold values from -0.5 to 0.5
- w_edge_out: bfloat16 [3, 128, 128], replicated, may hold values from -0.5 to 0.5
- w_msg: bfloat16 [2, 128, 128], replicated, may hold values from -0.5 to 0.5
- w_upd: bfloat16 [2, 128, 128], replicated, may hold values from -0.5 to 0.5
- node_gain: float32 [2, 128], replicated, may hold values from 0.1 to 1.9
- w_block: bfloat16 [128, 169], replicated, may hold values from -0.5 to 0.5
Outputs:
- blocks: bfloat16 [169, 147456], P(None, ('gx', 'gy', 'layer'))
Inputs may be any that keep to these rules, and one draw needn't show every extreme that they name: `neighbours`: slots pair up: a slot of kind 1 or 2 and the slot of its partner atom that points back form one pair, one of kind 1 and the other of kind 2, with equal distance; empty slots pair with empty slots. Each atom has 4 slots towards each of the 18 offsets, half of them owned. `own_rows`: each domain's rows list its 2304 owned slots once each; the valid ones (kind 1) come first, at most 2112 of them, and some domain has exactly 2112. `send_pos`: within a domain every value occurs once; value // 128 is the offset of the partner's domain. `recv_pos`: for slots of kind 2: value // 128 is the reverse of the offset of the partner's domain.
All inputs are finite; a program needn't handle non-finite values.
Results may differ from a plain program's by a relative error of at most 0.019.
Values may be sent and summed in bfloat16 or wider, within the bound.
No kernel may reach another device: no remote copies, remote signals or barrier semaphores. Data moves between devices by JAX's collectives and lax.ppermute only.
A program may use at most 64 MiB of HBM per device.

v0:
```python
import jax
import jax.numpy as jnp
from jax import lax
from jax.sharding import PartitionSpec as P

ORB = 13
GROUPS = 4
LAYERS = 3


def swapped(value, axis, bit):
    mask = 2**bit
    pairs = [(source, source ^ mask) for source in range(lax.axis_size(axis))]
    return lax.ppermute(value, axis, pairs)


def with_halo(block, sides, width):
    for axis, dim in sides:
        count = lax.axis_size(axis)
        forward = [(i, i + 1) for i in range(count - 1)]
        forward.append((count - 1, 0))
        backward = [(target, source) for source, target in forward]
        low = lax.ppermute(
            lax.slice_in_dim(block, block.shape[dim] - width, None, axis=dim), axis, forward
        )
        high = lax.ppermute(lax.slice_in_dim(block, 0, width, axis=dim), axis, backward)
        block = jnp.concatenate([low, block, high], axis=dim)
    return block


def from_behind(value, axis, steps):
    count = lax.axis_size(axis)
    pairs = [(source, (source + steps) % count) for source in range(count)]
    return lax.ppermute(value, axis, pairs)


def rms_norm(values):
    return values * lax.rsqrt(jnp.mean(values * values, axis=-1, keepdims=True) + 1e-06)


def cutoff(distance):
    scaled = distance / 7.0
    return (1.0 - scaled * scaled) ** 2


def padded_index(index, span):
    count = index.shape[0]
    tiles = -(-count // span)
    filler = jnp.full((tiles * span - count,), -1, jnp.int32)
    return (jnp.concatenate([index, filler]).reshape(tiles, span), tiles)


def select_rows(table, index):
    span = 512
    count = index.shape[0]
    blocked, tiles = padded_index(index, span)
    columns = lax.broadcasted_iota(jnp.int32, (span, table.shape[0]), 1)

    def select_one_tile(wanted):
        picker = (wanted[:, None] == columns).astype(table.dtype)
        return jnp.dot(picker, table, preferred_element_type=jnp.float32).astype(table.dtype)

    return lax.map(select_one_tile, blocked).reshape(tiles * span, table.shape[1])[:count]


def pick_columns(values, index):
    span = 512
    blocked, tiles = padded_index(index, span)
    sources = lax.broadcasted_iota(jnp.int32, (values.shape[1], span), 0)

    def pick_one_tile(wanted):
        picker = (sources == wanted[None, :]).astype(values.dtype)
        return jnp.dot(values, picker, preferred_element_type=jnp.float32).astype(values.dtype)

    gathered = lax.map(pick_one_tile, blocked)
    return jnp.moveaxis(gathered, 0, 1).reshape(values.shape[0], tiles * span)


def place_columns(values, index, width):
    span = 512
    tiles = -(-width // span)
    targets = lax.broadcasted_iota(jnp.int32, (index.shape[0], span), 1)

    def place_one_tile(tile_start):
        picker = (index[:, None] == targets + tile_start).astype(values.dtype)
        return jnp.dot(values, picker, preferred_element_type=jnp.float32).astype(values.dtype)

    placed = lax.map(place_one_tile, jnp.arange(tiles, dtype=jnp.int32) * span)
    return jnp.moveaxis(placed, 0, 1).reshape(values.shape[0], tiles * span)[:, :width]


def ghost_table(local_part):
    opposite = swapped(local_part, "layer", 0)
    sheets = jnp.stack([local_part, opposite])[:, None, None]
    framed = with_halo(sheets, (("gx", 1), ("gy", 2)), 1)
    return framed.reshape(-1, local_part.shape[1])


def deliver(outgoing):
    crossed = swapped(outgoing[:, 1], "layer", 0)
    sheets = jnp.stack([outgoing[:, 0], crossed], axis=1)
    along_rows = [sheets[:, :, 0], sheets[:, :, 1], sheets[:, :, 2]]
    for offset in (1, -1):
        along_rows[offset + 1] = from_behind(sheets[:, :, offset + 1], "gx", offset)
    shifted = jnp.stack(along_rows, axis=2)
    along_cols = [shifted[:, :, :, 0], shifted[:, :, :, 1], shifted[:, :, :, 2]]
    for offset in (1, -1):
        along_cols[offset + 1] = from_behind(shifted[:, :, :, offset + 1], "gy", offset)
    return jnp.stack(along_cols, axis=3).reshape(outgoing.shape[0], -1)


def shards(
    atom_feats,
    bond_embed,
    pair_dist,
    neighbours,
    slot_kind,
    own_rows,
    send_pos,
    recv_pos,
    w_left,
    w_right,
    w_edge_in,
    w_edge_out,
    w_msg,
    w_upd,
    node_gain,
    w_block,
):
    atom_count, channels = atom_feats.shape
    slot_count = neighbours.shape[0]
    fanout = slot_count // atom_count
    owned_total = own_rows.shape[0]
    edge_state = bond_embed
    row_atom = own_rows // fanout
    row_peer = jnp.take(neighbours, own_rows)
    envelope = cutoff(pair_dist) * (slot_kind > 0).astype(jnp.float32)
    hidden = atom_feats
    for layer_index in range(LAYERS):
        wants_message = layer_index + 1 < LAYERS
        near_proj = jnp.dot(hidden, w_left[layer_index], preferred_element_type=jnp.float32).astype(
            jnp.bfloat16
        )
        ghost_rows = ghost_table(hidden)
        far_table = jnp.dot(
            ghost_rows, w_right[layer_index], preferred_element_type=jnp.float32
        ).astype(jnp.bfloat16)
        message_table = far_table
        if wants_message:
            message_table = jnp.dot(
                ghost_rows, w_msg[layer_index], preferred_element_type=jnp.float32
            ).astype(jnp.bfloat16)
        inner_proj = jnp.dot(edge_state, w_edge_in[layer_index], preferred_element_type=jnp.float32)
        near_rows = select_rows(near_proj, row_atom).astype(jnp.float32)
        far_rows = select_rows(far_table, row_peer).astype(jnp.float32)
        mixed_gate = jax.nn.silu(inner_proj * near_rows * far_rows).astype(jnp.bfloat16)
        renewed = edge_state.astype(jnp.float32) + jnp.dot(
            mixed_gate, w_edge_out[layer_index], preferred_element_type=jnp.float32
        )
        if wants_message:
            gathered = (
                select_rows(message_table, neighbours).astype(jnp.float32) * envelope[:, None]
            )
            summed = (
                jnp.sum(gathered.reshape(atom_count, fanout, channels), axis=1) * 0.125
            ).astype(jnp.bfloat16)
            updated = hidden.astype(jnp.float32) + jax.nn.silu(
                jnp.dot(summed, w_upd[layer_index], preferred_element_type=jnp.float32)
            )
            hidden = (rms_norm(updated) * node_gain[layer_index]).astype(jnp.bfloat16)
        edge_state = rms_norm(renewed).astype(jnp.bfloat16)
    block_size = ORB * ORB
    capacity = GROUPS // 2 * atom_count
    direct = lax.dot_general(
        w_block, edge_state, (((0,), (1,)), ((), ())), preferred_element_type=jnp.float32
    ).astype(jnp.bfloat16)
    own_part = place_columns(direct, own_rows, slot_count)
    flipped = (
        direct.reshape(ORB, ORB, owned_total).transpose(1, 0, 2).reshape(block_size, owned_total)
    )
    outgoing = place_columns(flipped, send_pos, 18 * capacity)
    arrived = deliver(outgoing.reshape(block_size, 2, 3, 3, capacity))
    mirror = pick_columns(arrived, recv_pos)
    return jnp.where(
        slot_kind == 1, own_part, jnp.where(slot_kind == 2, mirror, jnp.zeros_like(mirror))
    )


def solution(mesh):
    placed = (
        P(("gx", "gy", "layer"), None),
        P(("gx", "gy", "layer"), None),
        P(("gx", "gy", "layer")),
        P(("gx", "gy", "layer")),
        P(("gx", "gy", "layer")),
        P(("gx", "gy", "layer")),
        P(("gx", "gy", "layer")),
        P(("gx", "gy", "layer")),
        P(),
        P(),
        P(),
        P(),
        P(),
        P(),
        P(),
        P(),
    )
    return jax.shard_map(
        shards,
        mesh=mesh,
        in_specs=placed,
        out_specs=P(None, ("gx", "gy", "layer")),
        check_vma=False,
    )
```

profile of v0, /device:TPU:0, one launch (start us, length us, event | category | flops | bytes accessed | tf_op | source)
XLA Modules:
  0.0 204.1 jit_solution(14073620949122184984)
XLA Ops:
  0.0 3.0 %collective-permute-start = (bf16[64,128]{1,0:T(8,128)(2,1)}, bf16[64,128]{1,0:T(8,128)(2,1)S(1)}, u32[]{:S(2)}, u32[]{:S(2)}) collective-permute-start(bf16[64,128]{1,0:T(8,128)(2,1)} %param.38), channel_id=1, source_target_pairs={{0,1},{1,0},{2,3},{3,2},{4,5},{5,4},{6,7},{7,6},{8,9},{9,8},{10,11... | collective-permute-start | bytes 49160 | tf_op jit(solution)/shard_map/ppermute | solution.py:14
  3.7 12.3 %gather_fusion = s32[2304]{0:T(1024)S(1)} fusion(s32[4608]{0:T(1024)S(1)} %copy-done.1, s32[3072]{0:T(1024)S(1)} %pad_clamp_fusion), kind=kCustom, calls=%fused_computation | custom fusion | bytes 27648 | tf_op jit(solution)/shard_map/jit(_take)/gather | solution.py:136
  16.4 1.6 while.121
  18.1 1.6 collective-permute-start.1
  19.7 2.2 %collective-permute-start.2 = (bf16[2,1,1,64,128]{4,3,2,1,0:T(8,128)(2,1)S(1)}, bf16[2,1,1,64,128]{4,3,2,1,0:T(8,128)(2,1)S(1)}, u32[]{:S(2)}, u32[]{:S(2)}) collective-permute-start(bf16[2,1,1,64,128]{4,3,2,1,0:T(8,128)(2,1)S(1)} %maximum_bitcast_fusion), channel_id=1, source_target_pairs={{8,0},{16,8},{24,16},{0,24},{9,1},{17,9},{25,17},{1,25},{10,2},{18... | collective-permute-start | bytes 98312 | tf_op jit(solution)/shard_map/ppermute | solution.py:26
  24.2 1.7 collective-permute-start.4
  26.5 1.7 collective-permute-done.3
  28.7 5.7 %while.123 = (s32[]{:T(128)}, bf16[9,512,128]{2,1,0:T(8,128)(2,1)S(1)}, s32[9,512]{1,0:T(8,128)S(1)}, bf16[1152,128]{1,0:T(8,128)(2,1)S(1)}, s32[]{:T(128)}) while((s32[]{:T(128)}, bf16[9,512,128]{2,1,0:T(8,128)(2,1)S(1)}, s32[9,512]{1,0:T(8,128)S(1)}, bf16[1152,128]{1,0:T(8,128)(2,1)S(1)}, s32[]{:T(128)}) %tuple.200), condition=%wide.region_6.7_spmd.clone, body=%wide.region_5.6_spmd.clone.sunk | while | flops 151650304 | bytes 432197 | solution.py:63
  37.7 1.6 while.124
  39.3 1.7 convolution_convert_fusion.8
  41.1 8.0 %while.122 = (s32[]{:T(128)}, bf16[5,512,128]{2,1,0:T(8,128)(2,1)S(1)}, s32[5,512]{1,0:T(8,128)S(1)}, bf16[1152,128]{1,0:T(8,128)(2,1)}, s32[]{:T(128)}) while((s32[]{:T(128)}, bf16[5,512,128]{2,1,0:T(8,128)(2,1)S(1)}, s32[5,512]{1,0:T(8,128)S(1)}, bf16[1152,128]{1,0:T(8,128)(2,1)}, s32[]{:T(128)}) %tuple.194), condition=%wide.region_3.4_spmd.clone, body=%wide.region_2.3_spmd.clone.sunk | while | flops 151650304 | bytes 432197 | solution.py:63
  41.1 1.6 fusion.229
  42.8 1.6 fusion.229
  44.4 1.6 fusion.229
  46.0 1.6 fusion.229
  47.6 1.6 fusion.229
  51.1 2.7 %collective-permute-start.7 = (bf16[2,1,1,64,128]{4,3,0,2,1:T(8,128)(2,1)S(1)}, bf16[2,1,1,64,128]{4,3,0,2,1:T(8,128)(2,1)S(1)}, u32[]{:S(2)}, u32[]{:S(2)}) collective-permute-start(bf16[2,1,1,64,128]{4,3,0,2,1:T(8,128)(2,1)S(1)} %maximum_bitcast_fusion.1), channel_id=1, source_target_pairs={{8,0},{16,8},{24,16},{0,24},{9,1},{17,9},{25,17},{1,25},{10,2},{18... | collective-permute-start | bytes 98312 | tf_op jit(solution)/shard_map/ppermute | solution.py:26
  53.8 2.5 %multiply_reduce_fusion.2 = (f32[2304]{0:T(1024)S(1)}, f32[2304,128]{0,1:T(8,128)}) fusion(bf16[3,128,128]{2,1,0:T(8,128)(2,1)} %param.49, bf16[2304,128]{1,0:T(8,128)(2,1)S(1)} %copy-done.3, bf16[2560,128]{1,0:T(8,128)(2,1)S(1)} %bitcast.307, bf16[2560,128]{1,0:T(8,128)(2,1)S(1)} %bitcast.305, bf16[3,128,128]{2,1,0:T(8,128)(2,1)} %param.48, ...), kind=kOutput, calls=%fused_computation.120 | convolution fusion | flops 154826496 | bytes 3613696 | tf_op jit(solution)/shard_map/dot_general | solution.py:157
  58.1 2.3 %collective-permute-done.8 = bf16[2,3,1,64,128]{4,3,0,2,1:T(8,128)(2,1)S(1)} collective-permute-done((bf16[2,3,1,64,128]{4,3,0,2,1:T(8,128)(2,1)S(1)}, bf16[2,3,1,64,128]{4,3,0,2,1:T(8,128)(2,1)S(1)}, u32[]{:S(2)}, u32[]{:S(2)}) %collective-permute-start.8) | collective-permute-done | bytes 98336 | tf_op jit(solution)/shard_map/ppermute | solution.py:23
  61.3 5.7 %while.126 = (s32[]{:T(128)}, bf16[9,512,128]{2,1,0:T(8,128)(2,1)S(1)}, s32[9,512]{1,0:T(8,128)S(1)}, bf16[1152,128]{1,0:T(8,128)(2,1)S(1)}, s32[]{:T(128)}) while((s32[]{:T(128)}, bf16[9,512,128]{2,1,0:T(8,128)(2,1)S(1)}, s32[9,512]{1,0:T(8,128)S(1)}, bf16[1152,128]{1,0:T(8,128)(2,1)S(1)}, s32[]{:T(128)}) %tuple.232), condition=%wide.region_15.16_spmd.clone, body=%wide.region_14.15_spmd.clone.sunk | while | flops 151650304 | bytes 432197 | solution.py:63
  68.9 1.4 collective-permute-start.10
  71.5 1.6 while.127
  73.2 3.1 %while.125 = (s32[]{:T(128)}, bf16[5,512,128]{2,1,0:T(8,128)(2,1)S(1)}, s32[5,512]{1,0:T(8,128)S(1)}, bf16[1152,128]{1,0:T(8,128)(2,1)S(1)}, s32[]{:T(128)}) while((s32[]{:T(128)}, bf16[5,512,128]{2,1,0:T(8,128)(2,1)S(1)}, s32[5,512]{1,0:T(8,128)S(1)}, bf16[1152,128]{1,0:T(8,128)(2,1)S(1)}, s32[]{:T(128)}) %tuple.228), condition=%wide.region_12.13_spmd.clone, body=%wide.region_11.12_spmd.clone.sunk | while | flops 151650304 | bytes 432197 | solution.py:63
  77.2 3.1 %collective-permute-start.12 = (bf16[2,1,1,64,128]{4,3,0,2,1:T(8,128)(2,1)S(1)}, bf16[2,1,1,64,128]{4,3,0,2,1:T(8,128)(2,1)S(1)}, u32[]{:S(2)}, u32[]{:S(2)}) collective-permute-start(bf16[2,1,1,64,128]{4,3,0,2,1:T(8,128)(2,1)S(1)} %maximum_bitcast_fusion.2), channel_id=1, source_target_pairs={{8,0},{16,8},{24,16},{0,24},{9,1},{17,9},{25,17},{1,25},{10,2},{18... | collective-permute-start | bytes 98312 | tf_op jit(solution)/shard_map/ppermute | solution.py:26
  80.3 3.6 %multiply_reduce_fusion.1 = (f32[2304]{0:T(1024)S(1)}, f32[2304,128]{0,1:T(8,128)}) fusion(bf16[3,128,128]{2,1,0:T(8,128)(2,1)S(1)} %copy-done.21, f32[2304,128]{0,1:T(8,128)} %get-tuple-element.546, bf16[2560,128]{1,0:T(8,128)(2,1)S(1)} %bitcast.309, bf16[2560,128]{1,0:T(8,128)(2,1)S(1)} %bitcast.306, f32[2304]{0:T(1024)S(1)} %add_rsqrt_fusion.2, ...), kind=kOutput, calls=%fused_computation.115 | convolution fusion | flops 156006144 | bytes 4817920 | tf_op jit(solution)/shard_map/dot_general | solution.py:157
  85.7 2.3 %collective-permute-done.13 = bf16[2,3,1,64,128]{4,3,0,2,1:T(8,128)(2,1)S(1)} collective-permute-done((bf16[2,3,1,64,128]{4,3,0,2,1:T(8,128)(2,1)S(1)}, bf16[2,3,1,64,128]{4,3,0,2,1:T(8,128)(2,1)S(1)}, u32[]{:S(2)}, u32[]{:S(2)}) %collective-permute-start.13) | collective-permute-done | bytes 98336 | tf_op jit(solution)/shard_map/ppermute | solution.py:23
  88.9 3.1 %while.128 = (s32[]{:T(128)}, bf16[5,512,128]{2,1,0:T(8,128)(2,1)S(1)}, s32[5,512]{1,0:T(8,128)S(1)}, bf16[1152,128]{1,0:T(8,128)(2,1)S(1)}, s32[]{:T(128)}) while((s32[]{:T(128)}, bf16[5,512,128]{2,1,0:T(8,128)(2,1)S(1)}, s32[5,512]{1,0:T(8,128)S(1)}, bf16[1152,128]{1,0:T(8,128)(2,1)S(1)}, s32[]{:T(128)}) %tuple.229), condition=%wide.region_21.22_spmd.clone, body=%wide.region_20.21_spmd.clone.sunk | while | flops 151650304 | bytes 432197 | solution.py:63
  92.0 2.5 %multiply_reduce_fusion = (f32[2304]{0:T(1024)S(1)}, f32[2304,128]{0,1:T(8,128)S(1)}) fusion(bf16[3,128,128]{2,1,0:T(8,128)(2,1)S(1)} %copy-done.21, f32[2304,128]{0,1:T(8,128)} %get-tuple-element.550, bf16[2560,128]{1,0:T(8,128)(2,1)S(1)} %bitcast.310, bf16[2560,128]{1,0:T(8,128)(2,1)S(1)} %bitcast.308, f32[2304]{0:T(1024)S(1)} %add_rsqrt_fusion.1, ...), kind=kOutput, calls=%fused_computation.110 | convolution fusion | flops 156006144 | bytes 4817920 | tf_op jit(solution)/shard_map/dot_general | solution.py:157
  96.7 16.2 %while.130 = (s32[]{:T(128)}, bf16[5,169,512]{2,1,0:T(8,128)(2,1)S(1)}, s32[2304]{0:T(1024)S(1)}, s32[5]{0:T(128)S(1)}, bf16[169,2304]{1,0:T(8,128)(2,1)}, /*index=5*/s32[]{:T(128)}) while((s32[]{:T(128)}, bf16[5,169,512]{2,1,0:T(8,128)(2,1)S(1)}, s32[2304]{0:T(1024)S(1)}, s32[5]{0:T(128)S(1)}, bf16[169,2304]{1,0:T(8,128)(2,1)}, ...), condition=%wide.region_26.27_spmd.clone, body=%wide.region_25.26_spmd.clone.sunk | while | flops 401166848 | bytes 971353 | solution.py:88
  97.3 2.7 %fusion.247 = bf16[5,169,512]{2,1,0:T(8,128)(2,1)S(1)} fusion(bf16[5,169,512]{2,1,0:T(8,128)(2,1)S(1)} %get-tuple-element.985, s32[]{:T(128)} %get-tuple-element.984, bf16[169,2304]{1,0:T(8,128)(2,1)} %get-tuple-element.994, s32[]{:T(128)} %bitcast.284, s32[2304]{0:T(1024)S(1)} %get-tuple-element.992), kind=kOutput, calls=%fused_computation.80.clone.1 | convolution fusion | flops 401166848 | bytes 971272 | tf_op jit(solution)/shard_map/while/body/eval_jaxpr/dot_general | solution.py:86
  100.5 2.7 %fusion.247 = bf16[5,169,512]{2,1,0:T(8,128)(2,1)S(1)} fusion(bf16[5,169,512]{2,1,0:T(8,128)(2,1)S(1)} %get-tuple-element.985, s32[]{:T(128)} %get-tuple-element.984, bf16[169,2304]{1,0:T(8,128)(2,1)} %get-tuple-element.994, s32[]{:T(128)} %bitcast.284, s32[2304]{0:T(1024)S(1)} %get-tuple-element.992), kind=kOutput, calls=%fused_computation.80.clone.1 | convolution fusion | flops 401166848 | bytes 971272 | tf_op jit(solution)/shard_map/while/body/eval_jaxpr/dot_general | solution.py:86
  103.8 2.7 %fusion.247 = bf16[5,169,512]{2,1,0:T(8,128)(2,1)S(1)} fusion(bf16[5,169,512]{2,1,0:T(8,128)(2,1)S(1)} %get-tuple-element.985, s32[]{:T(128)} %get-tuple-element.984, bf16[169,2304]{1,0:T(8,128)(2,1)} %get-tuple-element.994, s32[]{:T(128)} %bitcast.284, s32[2304]{0:T(1024)S(1)} %get-tuple-element.992), kind=kOutput, calls=%fused_computation.80.clone.1 | convolution fusion | flops 401166848 | bytes 971272 | tf_op jit(solution)/shard_map/while/body/eval_jaxpr/dot_general | solution.py:86
  107.0 2.7 %fusion.247 = bf16[5,169,512]{2,1,0:T(8,128)(2,1)S(1)} fusion(bf16[5,169,512]{2,1,0:T(8,128)(2,1)S(1)} %get-tuple-element.985, s32[]{:T(128)} %get-tuple-element.984, bf16[169,2304]{1,0:T(8,128)(2,1)} %get-tuple-element.994, s32[]{:T(128)} %bitcast.284, s32[2304]{0:T(1024)S(1)} %get-tuple-element.992), kind=kOutput, calls=%fused_computation.80.clone.1 | convolution fusion | flops 401166848 | bytes 971272 | tf_op jit(solution)/shard_map/while/body/eval_jaxpr/dot_general | solution.py:86
  110.2 2.7 %fusion.247 = bf16[5,169,512]{2,1,0:T(8,128)(2,1)S(1)} fusion(bf16[5,169,512]{2,1,0:T(8,128)(2,1)S(1)} %get-tuple-element.985, s32[]{:T(128)} %get-tuple-element.984, bf16[169,2304]{1,0:T(8,128)(2,1)} %get-tuple-element.994, s32[]{:T(128)} %bitcast.284, s32[2304]{0:T(1024)S(1)} %get-tuple-element.992), kind=kOutput, calls=%fused_computation.80.clone.1 | convolution fusion | flops 401166848 | bytes 971272 | tf_op jit(solution)/shard_map/while/body/eval_jaxpr/dot_general | solution.py:86
  115.8 13.4 %collective-permute-done.15 = bf16[169,3,3,128]{3,2,1,0:T(4,128)(2,1)S(1)} collective-permute-done((bf16[169,3,3,128]{3,2,1,0:T(4,128)(2,1)S(1)}, bf16[169,3,3,128]{3,2,1,0:T(4,128)(2,1)S(1)}, u32[]{:S(2)}, u32[]{:S(2)}) %collective-permute-start.15) | collective-permute-done | bytes 389408 | tf_op jit(solution)/shard_map/ppermute | solution.py:14
  130.0 2.2 %collective-permute-start.16 = (bf16[169,2,3,128]{3,2,1,0:T(4,128)(2,1)S(1)}, bf16[169,2,3,128]{3,2,1,0:T(4,128)(2,1)S(1)}, u32[]{:S(2)}, u32[]{:S(2)}) collective-permute-start(bf16[169,2,3,128]{3,2,1,0:T(4,128)(2,1)S(1)} %get-tuple-element.532), channel_id=1, source_target_pairs={{0,24},{8,0},{16,8},{24,16},{1,25},{9,1},{17,9},{25,17},{2,26},{10... | collective-permute-start | bytes 778760 | tf_op jit(solution)/shard_map/ppermute | solution.py:34
  132.2 8.4 %collective-permute-done.16 = bf16[169,2,3,128]{3,2,1,0:T(4,128)(2,1)S(1)} collective-permute-done((bf16[169,2,3,128]{3,2,1,0:T(4,128)(2,1)S(1)}, bf16[169,2,3,128]{3,2,1,0:T(4,128)(2,1)S(1)}, u32[]{:S(2)}, u32[]{:S(2)}) %collective-permute-start.16) | collective-permute-done | bytes 259616 | tf_op jit(solution)/shard_map/ppermute | solution.py:34
  140.6 7.5 %collective-permute-done.17 = bf16[169,2,3,128]{3,2,1,0:T(4,128)(2,1)S(1)} collective-permute-done((bf16[169,2,3,128]{3,2,1,0:T(4,128)(2,1)S(1)}, bf16[169,2,3,128]{3,2,1,0:T(4,128)(2,1)S(1)}, u32[]{:S(2)}, u32[]{:S(2)}) %collective-permute-start.17) | collective-permute-done | bytes 259616 | tf_op jit(solution)/shard_map/ppermute | solution.py:34
  151.6 20.1 %while.129 = (s32[]{:T(128)}, bf16[9,169,512]{2,1,0:T(8,128)(2,1)S(1)}, s32[2304]{0:T(1024)S(1)}, s32[9]{0:T(128)S(1)}, bf16[169,2304]{1,0:T(8,128)(2,1)S(1)}, /*index=5*/s32[]{:T(128)}) while((s32[]{:T(128)}, bf16[9,169,512]{2,1,0:T(8,128)(2,1)S(1)}, s32[2304]{0:T(1024)S(1)}, s32[9]{0:T(128)S(1)}, ...), condition=%wide.region_24.25_spmd.clone, body=%wide.region_23.24_spmd.clone.sunk | while | flops 401166848 | bytes 1003609 | solution.py:88
  152.2 1.6 fusion.244
  154.5 1.6 fusion.244
  156.7 1.6 fusion.244
  158.9 1.6 fusion.244
  161.2 1.6 fusion.244
  163.4 1.6 fusion.244
  165.6 1.6 fusion.244
  167.8 1.6 fusion.244
  170.1 1.6 fusion.244
  173.2 1.2 copy.78
  174.4 1.4 copy.70
  175.8 1.4 copy.71
  177.2 1.9 pad_maximum_fusion.1
  179.0 1.5 reshape.166
  180.7 19.1 %while.131 = (s32[]{:T(128)}, bf16[9,169,512]{2,1,0:T(8,128)(2,1)S(1)}, s32[9,512]{1,0:T(8,128)S(1)}, bf16[169,2304]{1,0:T(8,128)(2,1)}, s32[]{:T(128)}) while((s32[]{:T(128)}, bf16[9,169,512]{2,1,0:T(8,128)(2,1)S(1)}, s32[9,512]{1,0:T(8,128)S(1)}, bf16[169,2304]{1,0:T(8,128)(2,1)}, s32[]{:T(128)}) %tuple.224), condition=%wide.region_28.29_spmd.clone, body=%wide.region_27.28_spmd.clone.sunk | while | flops 399987200 | bytes 965189 | solution.py:75
  180.8 2.1 %fusion.249 = bf16[9,169,512]{2,1,0:T(8,128)(2,1)S(1)} fusion(bf16[9,169,512]{2,1,0:T(8,128)(2,1)S(1)} %get-tuple-element.1002, s32[]{:T(128)} %get-tuple-element.1001, bf16[169,2304]{1,0:T(8,128)(2,1)} %get-tuple-element.1009, s32[512]{0:T(512)S(1)} %bitcast.324), kind=kOutput, calls=%fused_computation.86.clone.1 | convolution fusion | flops 399987200 | bytes 961028 | tf_op jit(solution)/shard_map/while/body/eval_jaxpr/dot_general | solution.py:73
  182.9 2.1 %fusion.249 = bf16[9,169,512]{2,1,0:T(8,128)(2,1)S(1)} fusion(bf16[9,169,512]{2,1,0:T(8,128)(2,1)S(1)} %get-tuple-element.1002, s32[]{:T(128)} %get-tuple-element.1001, bf16[169,2304]{1,0:T(8,128)(2,1)} %get-tuple-element.1009, s32[512]{0:T(512)S(1)} %bitcast.324), kind=kOutput, calls=%fused_computation.86.clone.1 | convolution fusion | flops 399987200 | bytes 961028 | tf_op jit(solution)/shard_map/while/body/eval_jaxpr/dot_general | solution.py:73
  185.0 2.1 %fusion.249 = bf16[9,169,512]{2,1,0:T(8,128)(2,1)S(1)} fusion(bf16[9,169,512]{2,1,0:T(8,128)(2,1)S(1)} %get-tuple-element.1002, s32[]{:T(128)} %get-tuple-element.1001, bf16[169,2304]{1,0:T(8,128)(2,1)} %get-tuple-element.1009, s32[512]{0:T(512)S(1)} %bitcast.324), kind=kOutput, calls=%fused_computation.86.clone.1 | convolution fusion | flops 399987200 | bytes 961028 | tf_op jit(solution)/shard_map/while/body/eval_jaxpr/dot_general | solution.py:73
  187.1 2.1 %fusion.249 = bf16[9,169,512]{2,1,0:T(8,128)(2,1)S(1)} fusion(bf16[9,169,512]{2,1,0:T(8,128)(2,1)S(1)} %get-tuple-element.1002, s32[]{:T(128)} %get-tuple-element.1001, bf16[169,2304]{1,0:T(8,128)(2,1)} %get-tuple-element.1009, s32[512]{0:T(512)S(1)} %bitcast.324), kind=kOutput, calls=%fused_computation.86.clone.1 | convolution fusion | flops 399987200 | bytes 961028 | tf_op jit(solution)/shard_map/while/body/eval_jaxpr/dot_general | solution.py:73
  189.3 2.1 %fusion.249 = bf16[9,169,512]{2,1,0:T(8,128)(2,1)S(1)} fusion(bf16[9,169,512]{2,1,0:T(8,128)(2,1)S(1)} %get-tuple-element.1002, s32[]{:T(128)} %get-tuple-element.1001, bf16[169,2304]{1,0:T(8,128)(2,1)} %get-tuple-element.1009, s32[512]{0:T(512)S(1)} %bitcast.324), kind=kOutput, calls=%fused_computation.86.clone.1 | convolution fusion | flops 399987200 | bytes 961028 | tf_op jit(solution)/shard_map/while/body/eval_jaxpr/dot_general | solution.py:73
  191.4 2.1 %fusion.249 = bf16[9,169,512]{2,1,0:T(8,128)(2,1)S(1)} fusion(bf16[9,169,512]{2,1,0:T(8,128)(2,1)S(1)} %get-tuple-element.1002, s32[]{:T(128)} %get-tuple-element.1001, bf16[169,2304]{1,0:T(8,128)(2,1)} %get-tuple-element.1009, s32[512]{0:T(512)S(1)} %bitcast.324), kind=kOutput, calls=%fused_computation.86.clone.1 | convolution fusion | flops 399987200 | bytes 961028 | tf_op jit(solution)/shard_map/while/body/eval_jaxpr/dot_general | solution.py:73
  193.5 2.1 %fusion.249 = bf16[9,169,512]{2,1,0:T(8,128)(2,1)S(1)} fusion(bf16[9,169,512]{2,1,0:T(8,128)(2,1)S(1)} %get-tuple-element.1002, s32[]{:T(128)} %get-tuple-element.1001, bf16[169,2304]{1,0:T(8,128)(2,1)} %get-tuple-element.1009, s32[512]{0:T(512)S(1)} %bitcast.324), kind=kOutput, calls=%fused_computation.86.clone.1 | convolution fusion | flops 399987200 | bytes 961028 | tf_op jit(solution)/shard_map/while/body/eval_jaxpr/dot_general | solution.py:73
  195.7 2.1 %fusion.249 = bf16[9,169,512]{2,1,0:T(8,128)(2,1)S(1)} fusion(bf16[9,169,512]{2,1,0:T(8,128)(2,1)S(1)} %get-tuple-element.1002, s32[]{:T(128)} %get-tuple-element.1001, bf16[169,2304]{1,0:T(8,128)(2,1)} %get-tuple-element.1009, s32[512]{0:T(512)S(1)} %bitcast.324), kind=kOutput, calls=%fused_computation.86.clone.1 | convolution fusion | flops 399987200 | bytes 961028 | tf_op jit(solution)/shard_map/while/body/eval_jaxpr/dot_general | solution.py:73
  197.8 2.1 %fusion.249 = bf16[9,169,512]{2,1,0:T(8,128)(2,1)S(1)} fusion(bf16[9,169,512]{2,1,0:T(8,128)(2,1)S(1)} %get-tuple-element.1002, s32[]{:T(128)} %get-tuple-element.1001, bf16[169,2304]{1,0:T(8,128)(2,1)} %get-tuple-element.1009, s32[512]{0:T(512)S(1)} %bitcast.324), kind=kOutput, calls=%fused_computation.86.clone.1 | convolution fusion | flops 399987200 | bytes 961028 | tf_op jit(solution)/shard_map/while/body/eval_jaxpr/dot_general | solution.py:73
  202.6 1.5 select_select_fusion
  (272 shorter events, 62.1 us)
Async XLA Ops:
  0.0 94.6 %copy-start = (bf16[128,169]{0,1:T(8,128)(2,1)S(1)}, bf16[128,169]{0,1:T(8,128)(2,1)}, u32[]{:S(2)}) copy-start(bf16[128,169]{0,1:T(8,128)(2,1)} %param.53) | copy-start | bytes 129796
  0.0 3.7 %copy-start.1 = (s32[4608]{0:T(1024)S(1)}, s32[4608]{0:T(1024)}, u32[]{:S(2)}) copy-start(s32[4608]{0:T(1024)} %param.41) | copy-start | bytes 55300
  0.0 18.1 %collective-permute-start = (bf16[64,128]{1,0:T(8,128)(2,1)}, bf16[64,128]{1,0:T(8,128)(2,1)S(1)}, u32[]{:S(2)}, u32[]{:S(2)}) collective-permute-start(bf16[64,128]{1,0:T(8,128)(2,1)} %param.38), channel_id=1, source_target_pairs={{0,1},{1,0},{2,3},{3,2},{4,5},{5,4},{6,7},{7,6},{8,9},{9,8},{10,11... | collective-permute-start | bytes 49160 | tf_op jit(solution)/shard_map/ppermute | solution.py:14
  3.7 12.4 %copy-start.12 = (s32[2304]{0:T(1024)S(1)}, s32[2304]{0:T(1024)}, u32[]{:S(2)}) copy-start(s32[2304]{0:T(1024)} %param.43) | copy-start | bytes 27652
  3.7 12.5 %copy-start.6 = (bf16[3,128,128]{2,1,0:T(8,128)(2,1)S(1)}, bf16[3,128,128]{2,1,0:T(8,128)(2,1)}, u32[]{:S(2)}) copy-start(bf16[3,128,128]{2,1,0:T(8,128)(2,1)} %param.46) | copy-start | bytes 294916
  3.7 12.4 %copy-start.11 = (bf16[64,128]{1,0:T(8,128)(2,1)S(1)}, bf16[64,128]{1,0:T(8,128)(2,1)}, u32[]{:S(2)}) copy-start(bf16[64,128]{1,0:T(8,128)(2,1)} %param.38) | copy-start | bytes 49156
  16.1 1.9 copy-start.7
  16.1 1.9 copy-start.15
  16.1 5.9 %copy-start.20 = (f32[2,128]{1,0:T(2,128)S(1)}, f32[2,128]{1,0:T(2,128)}, u32[]{:S(2)}) copy-start(f32[2,128]{1,0:T(2,128)} %param.52) | copy-start | bytes 3076
  16.1 6.0 %copy-start.3 = (bf16[2304,128]{1,0:T(8,128)(2,1)S(1)}, bf16[2304,128]{1,0:T(8,128)(2,1)}, u32[]{:S(2)}) copy-start(bf16[2304,128]{1,0:T(8,128)(2,1)} %param.39) | copy-start | bytes 1769476
  18.0 10.3 %copy-start.9 = (bf16[2,128,128]{2,1,0:T(8,128)(2,1)S(1)}, bf16[2,128,128]{2,1,0:T(8,128)(2,1)}, u32[]{:S(2)}) copy-start(bf16[2,128,128]{2,1,0:T(8,128)(2,1)} %param.50) | copy-start | bytes 196612
  18.1 6.0 %collective-permute-start.1 = (bf16[2,1,1,64,128]{4,3,2,1,0:T(8,128)(2,1)S(1)}, bf16[2,1,1,64,128]{4,3,2,1,0:T(8,128)(2,1)S(1)}, u32[]{:S(2)}, u32[]{:S(2)}) collective-permute-start(bf16[2,1,1,64,128]{4,3,2,1,0:T(8,128)(2,1)S(1)} %maximum_bitcast_fusion), channel_id=1, source_target_pairs={{0,8},{8,16},{16,24},{24,0},{1,9},{9,17},{17,25},{25,1},{2,10},{10... | collective-permute-start | bytes 98312 | tf_op jit(solution)/shard_map/ppermute | solution.py:23
  19.7 4.4 %collective-permute-start.2 = (bf16[2,1,1,64,128]{4,3,2,1,0:T(8,128)(2,1)S(1)}, bf16[2,1,1,64,128]{4,3,2,1,0:T(8,128)(2,1)S(1)}, u32[]{:S(2)}, u32[]{:S(2)}) collective-permute-start(bf16[2,1,1,64,128]{4,3,2,1,0:T(8,128)(2,1)S(1)} %maximum_bitcast_fusion), channel_id=1, source_target_pairs={{8,0},{16,8},{24,16},{0,24},{9,1},{17,9},{25,17},{1,25},{10,2},{18... | collective-permute-start | bytes 98312 | tf_op jit(solution)/shard_map/ppermute | solution.py:26
  22.0 13.6 %copy-start.16 = (f32[128]{0:T(128)}, f32[128]{0:T(128)S(1)}, u32[]{:S(2)}) copy-start(f32[128]{0:T(128)S(1)} %get-tuple-element.542) | copy-start | bytes 1540
  24.1 4.1 %collective-permute-start.3 = (bf16[2,3,1,64,128]{4,3,2,1,0:T(8,128)(2,1)S(1)}, bf16[2,3,1,64,128]{4,3,2,1,0:T(8,128)(2,1)S(1)}, u32[]{:S(2)}, u32[]{:S(2)}) collective-permute-start(bf16[2,3,1,64,128]{4,3,2,1,0:T(8,128)(2,1)S(1)} %pad_maximum_fusion.6), channel_id=1, source_target_pairs={{0,2},{2,4},{4,6},{6,0},{1,3},{3,5},{5,7},{7,1},{8,10},{10,12},{12... | collective-permute-start | bytes 294920 | tf_op jit(solution)/shard_map/ppermute | solution.py:23
  24.2 4.1 %collective-permute-start.4 = (bf16[2,3,1,64,128]{4,3,2,1,0:T(8,128)(2,1)S(1)}, bf16[2,3,1,64,128]{4,3,2,1,0:T(8,128)(2,1)S(1)}, u32[]{:S(2)}, u32[]{:S(2)}) collective-permute-start(bf16[2,3,1,64,128]{4,3,2,1,0:T(8,128)(2,1)S(1)} %pad_maximum_fusion.6), channel_id=1, source_target_pairs={{2,0},{4,2},{6,4},{0,6},{3,1},{5,3},{7,5},{1,7},{10,8},{12,10},{14... | collective-permute-start | bytes 294920 | tf_op jit(solution)/shard_map/ppermute | solution.py:26
  34.4 0.8 copy-start.23
  35.5 1.2 copy-start.18
  36.2 13.0 %collective-permute-start.5 = (bf16[64,128]{1,0:T(8,128)(2,1)}, bf16[64,128]{1,0:T(8,128)(2,1)}, u32[]{:S(2)}, u32[]{:S(2)}) collective-permute-start(bf16[64,128]{1,0:T(8,128)(2,1)} %multiply_convert_fusion.13), channel_id=1, source_target_pairs={{0,1},{1,0},{2,3},{3,2},{4,5},{5,4},{6,7},{7,6},{8,9},{9,8},{10,11... | collective-permute-start | bytes 49160 | tf_op jit(solution)/shard_map/ppermute | solution.py:14
  41.1 8.1 %copy-start.17 = (f32[128]{0:T(128)S(1)}, f32[128]{0:T(128)}, u32[]{:S(2)}) copy-start(f32[128]{0:T(128)} %copy-done.16) | copy-start | bytes 1540
  41.1 8.1 %copy-start.19 = (f32[64]{0:T(128)S(1)}, f32[64]{0:T(128)}, u32[]{:S(2)}) copy-start(f32[64]{0:T(128)} %copy-done.18) | copy-start | bytes 772
  41.1 12.7 %copy-start.4 = (bf16[2304,128]{0,1:T(8,128)(2,1)S(1)}, bf16[2304,128]{0,1:T(8,128)(2,1)}, u32[]{:S(2)}) copy-start(bf16[2304,128]{0,1:T(8,128)(2,1)} %copy.57) | copy-start | bytes 1769476
  50.0 6.3 %collective-permute-start.6 = (bf16[2,1,1,64,128]{4,3,0,2,1:T(8,128)(2,1)S(1)}, bf16[2,1,1,64,128]{4,3,0,2,1:T(8,128)(2,1)S(1)}, u32[]{:S(2)}, u32[]{:S(2)}) collective-permute-start(bf16[2,1,1,64,128]{4,3,0,2,1:T(8,128)(2,1)S(1)} %maximum_bitcast_fusion.1), channel_id=1, source_target_pairs={{0,8},{8,16},{16,24},{24,0},{1,9},{9,17},{17,25},{25,1},{2,10},{10... | collective-permute-start | bytes 98312 | tf_op jit(solution)/shard_map/ppermute | solution.py:23
  51.1 5.2 %collective-permute-start.7 = (bf16[2,1,1,64,128]{4,3,0,2,1:T(8,128)(2,1)S(1)}, bf16[2,1,1,64,128]{4,3,0,2,1:T(8,128)(2,1)S(1)}, u32[]{:S(2)}, u32[]{:S(2)}) collective-permute-start(bf16[2,1,1,64,128]{4,3,0,2,1:T(8,128)(2,1)S(1)} %maximum_bitcast_fusion.1), channel_id=1, source_target_pairs={{8,0},{16,8},{24,16},{0,24},{9,1},{17,9},{25,17},{1,25},{10,2},{18... | collective-permute-start | bytes 98312 | tf_op jit(solution)/shard_map/ppermute | solution.py:26
  56.3 4.6 %copy-start.10 = (bf16[2,128,128]{2,1,0:T(8,128)(2,1)S(1)}, bf16[2,128,128]{2,1,0:T(8,128)(2,1)}, u32[]{:S(2)}) copy-start(bf16[2,128,128]{2,1,0:T(8,128)(2,1)} %param.50) | copy-start | bytes 196612
  56.3 4.1 %collective-permute-start.8 = (bf16[2,3,1,64,128]{4,3,0,2,1:T(8,128)(2,1)S(1)}, bf16[2,3,1,64,128]{4,3,0,2,1:T(8,128)(2,1)S(1)}, u32[]{:S(2)}, u32[]{:S(2)}) collective-permute-start(bf16[2,3,1,64,128]{4,3,0,2,1:T(8,128)(2,1)S(1)} %pad_maximum_fusion.7), channel_id=1, source_target_pairs={{0,2},{2,4},{4,6},{6,0},{1,3},{3,5},{5,7},{7,1},{8,10},{10,12},{12... | collective-permute-start | bytes 294920 | tf_op jit(solution)/shard_map/ppermute | solution.py:23
  57.1 3.7 %collective-permute-start.9 = (bf16[2,3,1,64,128]{4,3,0,2,1:T(8,128)(2,1)S(1)}, bf16[2,3,1,64,128]{4,3,0,2,1:T(8,128)(2,1)S(1)}, u32[]{:S(2)}, u32[]{:S(2)}) collective-permute-start(bf16[2,3,1,64,128]{4,3,0,2,1:T(8,128)(2,1)S(1)} %pad_maximum_fusion.7), channel_id=1, source_target_pairs={{2,0},{4,2},{6,4},{0,6},{3,1},{5,3},{7,5},{1,7},{10,8},{12,10},{14... | collective-permute-start | bytes 294920 | tf_op jit(solution)/shard_map/ppermute | solution.py:26
  67.0 0.8 copy-start.24
  67.0 4.2 %copy-start.5 = (bf16[3,128,128]{2,1,0:T(8,128)(2,1)S(1)}, bf16[3,128,128]{2,1,0:T(8,128)(2,1)}, u32[]{:S(2)}) copy-start(bf16[3,128,128]{2,1,0:T(8,128)(2,1)} %param.47) | copy-start | bytes 294916
  68.9 7.6 %collective-permute-start.10 = (bf16[64,128]{1,0:T(8,128)(2,1)S(1)}, bf16[64,128]{1,0:T(8,128)(2,1)S(1)}, u32[]{:S(2)}, u32[]{:S(2)}) collective-permute-start(bf16[64,128]{1,0:T(8,128)(2,1)S(1)} %multiply_convert_fusion.11), channel_id=1, source_target_pairs={{0,1},{1,0},{2,3},{3,2},{4,5},{5,4},{6,7},{7,6},{8,9},{9,8},{10,11... | collective-permute-start | bytes 49160 | tf_op jit(solution)/shard_map/ppermute | solution.py:14
  73.2 7.2 %copy-start.21 = (bf16[3,128,128]{2,1,0:T(8,128)(2,1)S(1)}, bf16[3,128,128]{2,1,0:T(8,128)(2,1)}, u32[]{:S(2)}) copy-start(bf16[3,128,128]{2,1,0:T(8,128)(2,1)} %param.49) | copy-start | bytes 294916
  73.2 7.1 %copy-start.22 = (bf16[3,128,128]{2,1,0:T(8,128)(2,1)S(1)}, bf16[3,128,128]{2,1,0:T(8,128)(2,1)}, u32[]{:S(2)}) copy-start(bf16[3,128,128]{2,1,0:T(8,128)(2,1)} %param.48) | copy-start | bytes 294916
  76.5 7.4 %collective-permute-start.11 = (bf16[2,1,1,64,128]{4,3,0,2,1:T(8,128)(2,1)S(1)}, bf16[2,1,1,64,128]{4,3,0,2,1:T(8,128)(2,1)S(1)}, u32[]{:S(2)}, u32[]{:S(2)}) collective-permute-start(bf16[2,1,1,64,128]{4,3,0,2,1:T(8,128)(2,1)S(1)} %maximum_bitcast_fusion.2), channel_id=1, source_target_pairs={{0,8},{8,16},{16,24},{24,0},{1,9},{9,17},{17,25},{25,1},{2,10},{10... | collective-permute-start | bytes 98312 | tf_op jit(solution)/shard_map/ppermute | solution.py:23
  77.2 6.7 %collective-permute-start.12 = (bf16[2,1,1,64,128]{4,3,0,2,1:T(8,128)(2,1)S(1)}, bf16[2,1,1,64,128]{4,3,0,2,1:T(8,128)(2,1)S(1)}, u32[]{:S(2)}, u32[]{:S(2)}) collective-permute-start(bf16[2,1,1,64,128]{4,3,0,2,1:T(8,128)(2,1)S(1)} %maximum_bitcast_fusion.2), channel_id=1, source_target_pairs={{8,0},{16,8},{24,16},{0,24},{9,1},{17,9},{25,17},{1,25},{10,2},{18... | collective-permute-start | bytes 98312 | tf_op jit(solution)/shard_map/ppermute | solution.py:26
  83.9 4.1 %collective-permute-start.13 = (bf16[2,3,1,64,128]{4,3,0,2,1:T(8,128)(2,1)S(1)}, bf16[2,3,1,64,128]{4,3,0,2,1:T(8,128)(2,1)S(1)}, u32[]{:S(2)}, u32[]{:S(2)}) collective-permute-start(bf16[2,3,1,64,128]{4,3,0,2,1:T(8,128)(2,1)S(1)} %pad_maximum_fusion.8), channel_id=1, source_target_pairs={{0,2},{2,4},{4,6},{6,0},{1,3},{3,5},{5,7},{7,1},{8,10},{10,12},{12... | collective-permute-start | bytes 294920 | tf_op jit(solution)/shard_map/ppermute | solution.py:23
  84.7 3.8 %collective-permute-start.14 = (bf16[2,3,1,64,128]{4,3,0,2,1:T(8,128)(2,1)S(1)}, bf16[2,3,1,64,128]{4,3,0,2,1:T(8,128)(2,1)S(1)}, u32[]{:S(2)}, u32[]{:S(2)}) collective-permute-start(bf16[2,3,1,64,128]{4,3,0,2,1:T(8,128)(2,1)S(1)} %pad_maximum_fusion.8), channel_id=1, source_target_pairs={{2,0},{4,2},{6,4},{0,6},{3,1},{5,3},{7,5},{1,7},{10,8},{12,10},{14... | collective-permute-start | bytes 294920 | tf_op jit(solution)/shard_map/ppermute | solution.py:26
  95.6 1.2 copy-start.2
  95.6 1.2 copy-start.25
  95.6 1.2 copy-start.26
  114.9 17.2 %copy-start.14 = (s32[4608]{0:T(1024)S(1)}, s32[4608]{0:T(1024)}, u32[]{:S(2)}) copy-start(s32[4608]{0:T(1024)} %param.45) | copy-start | bytes 55300
  115.0 17.2 %copy-start.8 = (s32[4608]{0:T(1024)S(1)}, s32[4608]{0:T(1024)}, u32[]{:S(2)}) copy-start(s32[4608]{0:T(1024)} %param.42) | copy-start | bytes 55300
  115.0 14.2 %collective-permute-start.15 = (bf16[169,3,3,128]{3,2,1,0:T(4,128)(2,1)S(1)}, bf16[169,3,3,128]{3,2,1,0:T(4,128)(2,1)S(1)}, u32[]{:S(2)}, u32[]{:S(2)}) collective-permute-start(bf16[169,3,3,128]{3,2,1,0:T(4,128)(2,1)S(1)} %get-tuple-element.536), channel_id=1, source_target_pairs={{0,1},{1,0},{2,3},{3,2},{4,5},{5,4},{6,7},{7,6},{8,9},{9,8},{10,11... | collective-permute-start | bytes 1168136 | tf_op jit(solution)/shard_map/ppermute | solution.py:14
  130.0 10.7 %collective-permute-start.16 = (bf16[169,2,3,128]{3,2,1,0:T(4,128)(2,1)S(1)}, bf16[169,2,3,128]{3,2,1,0:T(4,128)(2,1)S(1)}, u32[]{:S(2)}, u32[]{:S(2)}) collective-permute-start(bf16[169,2,3,128]{3,2,1,0:T(4,128)(2,1)S(1)} %get-tuple-element.532), channel_id=1, source_target_pairs={{0,24},{8,0},{16,8},{24,16},{1,25},{9,1},{17,9},{25,17},{2,26},{10... | collective-permute-start | bytes 778760 | tf_op jit(solution)/shard_map/ppermute | solution.py:34
  132.1 16.0 %collective-permute-start.17 = (bf16[169,2,3,128]{3,2,1,0:T(4,128)(2,1)S(1)}, bf16[169,2,3,128]{3,2,1,0:T(4,128)(2,1)S(1)}, u32[]{:S(2)}, u32[]{:S(2)}) collective-permute-start(bf16[169,2,3,128]{3,2,1,0:T(4,128)(2,1)S(1)} %get-tuple-element.533), channel_id=1, source_target_pairs={{0,8},{8,16},{16,24},{24,0},{1,9},{9,17},{17,25},{25,1},{2,10},{10... | collective-permute-start | bytes 778760 | tf_op jit(solution)/shard_map/ppermute | solution.py:34
  150.1 24.3 %collective-permute-start.18 = (bf16[169,2,3,128]{3,0,2,1:T(8,128)(2,1)S(1)}, bf16[169,2,3,128]{3,0,2,1:T(8,128)(2,1)}, u32[]{:S(2)}, u32[]{:S(2)}) collective-permute-start(bf16[169,2,3,128]{3,0,2,1:T(8,128)(2,1)S(1)} %bitcast.314), channel_id=1, source_target_pairs={{0,6},{2,0},{4,2},{6,4},{1,7},{3,1},{5,3},{7,5},{8,14},{10,8},{12,... | collective-permute-start | bytes 778760 | tf_op jit(solution)/shard_map/ppermute | solution.py:34
  150.4 1.2 copy-start.13
  151.1 24.7 %collective-permute-start.19 = (bf16[169,2,3,128]{3,0,2,1:T(8,128)(2,1)}, bf16[169,2,3,128]{3,0,2,1:T(8,128)(2,1)}, u32[]{:S(2)}, u32[]{:S(2)}) collective-permute-start(bf16[169,2,3,128]{3,0,2,1:T(8,128)(2,1)} %bitcast.220), channel_id=1, source_target_pairs={{0,2},{2,4},{4,6},{6,0},{1,3},{3,5},{5,7},{7,1},{8,10},{10,12},{12... | collective-permute-start | bytes 778760 | tf_op jit(solution)/shard_map/ppermute | solution.py:34
where the time goes:
time: 206 us; the launch traced here: 204 us
  matrix products  89.8 us (44%)
  local copies, waits for them, and re-layouts  39.1 us (19%)
  waiting for transfers between devices  37.5 us (18%)
  starting transfers between devices  25.4 us (12%)
  other arithmetic  9.6 us (5%)
    dot_general x48, matrix products, select_one_tile(): jnp.dot(picker, table, preferred_element_type=jnp.float32)  28.8 us
    dot_general x14, matrix products, place_one_tile(): jnp.dot(values, picker, preferred_element_type=jnp.float32)  27.6 us
    dot_general x9, matrix products, pick_one_tile(): jnp.dot(values, picker, preferred_element_type=jnp.float32)  18.8 us
    ppermute x4, waiting for transfers between devices, from_behind(): return lax.ppermute(value, axis, pairs)  16 us
    ppermute x4, waiting for transfers between devices, swapped(): return lax.ppermute(value, axis, pairs)  13.4 us
    gather x1, local copies, waits for them, and re-layouts, shards(): row_peer = jnp.take(neighbours, own_rows)  12.3 us
    ppermute x6, starting transfers between devices, with_halo(): lax.ppermute(lax.slice_in_dim(block, 0, width, axis=dim), axis, backward)  11.9 us
    dot_general x3, matrix products, shards(): jnp.dot(mixed_gate, w_edge_out[layer_index], preferred_element_type=jnp.f...  8.56 us
  transfers between devices with their start and end apart: 20, of which 10 were waited for; matrix products, arithmetic and copies ran while one was open for 32% of the time, Pallas kernels for 0%

commit v1 on v0

v1 whole, which is shorter than its diff:
```python
import jax
import jax.numpy as jnp
from jax import lax
from jax.experimental import pallas as pl
from jax.experimental.pallas import tpu as pltpu
from jax.sharding import PartitionSpec as P

ORB = 13
GROUPS = 4
OFFS = 18
F32 = jnp.float32
BF16 = jnp.bfloat16
VMEM_LIMIT = 48 * 1024 * 1024


def swapped(value, axis):
    return lax.ppermute(value, axis, [(0, 1), (1, 0)])


def moved(value, axis, steps):
    count = lax.axis_size(axis)
    return lax.ppermute(value, axis, [(i, (i + steps) % count) for i in range(count)])


def with_halo(block, axis, dim):
    low = moved(block, axis, 1)
    high = moved(block, axis, -1)
    return jnp.concatenate([low, block, high], axis=dim)


def ghost_table(local):
    sheets = jnp.stack([local, swapped(local, "layer")])[:, None, None]
    framed = with_halo(with_halo(sheets, "gx", 1), "gy", 2)
    return framed.reshape(-1, local.shape[1])


def deliver(outgoing):
    sheets = jnp.stack([outgoing[0], swapped(outgoing[1], "layer")])
    rows = [moved(sheets[:, i], "gx", i - 1) if i != 1 else sheets[:, i] for i in range(3)]
    shifted = jnp.stack(rows, axis=1)
    cols = [moved(shifted[:, :, i], "gy", i - 1) if i != 1 else shifted[:, :, i] for i in range(3)]
    return jnp.stack(cols, axis=2)


def dot(a, b):
    return jnp.dot(a, b, preferred_element_type=F32)


def dot_nt(a, b):
    return lax.dot_general(a, b, (((1,), (1,)), ((), ())), preferred_element_type=F32)


def one_hot(mask):
    return jnp.where(mask, 1.0, 0.0).astype(BF16)


def silu(v):
    return v * (0.5 * jnp.tanh(0.5 * v) + 0.5)


def rms_norm(v):
    return v * lax.rsqrt(jnp.mean(v * v, axis=-1, keepdims=True) + 1e-06)


def iota(shape, dim):
    return lax.broadcasted_iota(jnp.int32, shape, dim)


def fiota(shape, dim):
    return iota(shape, dim).astype(F32)


def call(body, outs, *args, scratch=(), flops=1e8, nbytes=3e6):
    return pl.pallas_call(
        body,
        out_shape=outs,
        scratch_shapes=list(scratch),
        compiler_params=pltpu.CompilerParams(vmem_limit_bytes=VMEM_LIMIT),
        cost_estimate=pl.CostEstimate(
            flops=int(flops), bytes_accessed=int(nbytes), transcendentals=0
        ),
    )(*args)


def order_body(send_ref, bond_ref, out_ref):
    owned = bond_ref.shape[0]
    bond = bond_ref[...]
    step_rows = 256

    def step(i, carry):
        start = pl.multiple_of(i * step_rows, step_rows)
        pick = one_hot(iota((step_rows, owned), 0) + start == send_ref[...])
        out_ref[pl.ds(start, step_rows), :] = dot(pick, bond).astype(BF16)
        return carry

    lax.fori_loop(0, owned // step_rows, step, 0)


def prep_body(
    send_ref, own_ref, flat_ref, pack_ref, dist_ref, wb_ref,
    idx_own_ref, idx_mir_ref, adj_ref, src_ref, place_ref, wcat_ref,
):
    atoms, fan = pack_ref.shape
    owned = send_ref.shape[1]
    slots = flat_ref.shape[1]
    cap = owned // OFFS
    send = send_ref[...]
    own = own_ref[...].astype(F32)
    atom_r = jnp.floor((own + 0.5) * (1.0 / fan))
    slot_r = own - fan * atom_r
    off_r = (send >> 7).astype(F32)
    pos_r = (send & 127).astype(F32)
    pack = pack_ref[...]
    peer = (pack & 63).astype(F32)
    off = ((pack & 2047) >> 6).astype(F32)
    kind = (pack >> 11) & 3
    pos_in = ((pack >> 13) & 127).astype(F32)

    at_atom = fiota((atoms, owned), 0) == atom_r
    at_slot = fiota((fan, owned), 0) == slot_r
    slot_hot = one_hot(at_slot)
    place_own = dot_nt(jnp.where(at_atom, pos_r + 1.0, 0.0).astype(BF16), slot_hot)
    peer_t = jnp.transpose(
        jnp.concatenate([peer, jnp.zeros((atoms, 128 - fan), F32)], axis=1)
    )[:fan]
    peer_all = dot(peer_t.astype(BF16), one_hot(at_atom))
    peer_r = jnp.sum(jnp.where(at_slot, peer_all, 0.0), axis=0, keepdims=True)
    at_off = fiota((32, owned), 0) == off_r
    values = jnp.concatenate(
        [jnp.where(at_off, atom_r, 0.0), jnp.where(at_off, peer_r, 0.0)], axis=0
    ).astype(BF16)
    idx_own_ref[...] = dot_nt(one_hot(fiota((cap, owned), 0) == pos_r), values)

    flat = flat_ref[...]
    atom_s = jnp.floor((fiota((1, slots), 1) + 0.5) * (1.0 / fan))
    peer_s = (flat & 63).astype(F32)
    off_s = jnp.where(((flat >> 11) & 3) == 2, (flat & 2047) >> 6, -1).astype(F32)
    pos_s = ((flat >> 13) & 127).astype(F32)
    at_off = fiota((32, slots), 0) == off_s
    values = jnp.concatenate(
        [jnp.where(at_off, atom_s, 0.0), jnp.where(at_off, peer_s, 0.0)], axis=0
    ).astype(BF16)
    idx_mir_ref[...] = dot_nt(one_hot(fiota((cap, slots), 0) == pos_s), values)

    src = jnp.where(kind == 1, place_own - 1.0, jnp.where(kind == 2, pos_in + cap, -1.0))
    scaled = dist_ref[...] * (1.0 / 7.0)
    env = 1.0 - scaled * scaled
    env = jnp.where(kind > 0, env * env, 0.0)
    lane = fiota((atoms, fan), 1)
    rank = jnp.zeros((atoms, fan), F32)
    for s in range(fan - 1):
        rank += jnp.where((off == off[:, s : s + 1]) & (lane > float(s)), 1.0, 0.0)
    target = off * float(GROUPS) + rank
    place_ref[...] = jnp.transpose(
        jnp.concatenate([target, jnp.zeros((atoms, 128 - fan), F32)], axis=1)
    )[:fan]
    wide = fiota((atoms, 128), 1)
    src_sorted = jnp.full((atoms, 128), -1.0, F32)
    env_sorted = jnp.zeros((atoms, 128), F32)
    peer_sorted = jnp.zeros((atoms, 128), F32)
    for s in range(fan):
        here = target[:, s : s + 1] == wide
        src_sorted = jnp.where(here, src[:, s : s + 1], src_sorted)
        env_sorted = jnp.where(here, env[:, s : s + 1], env_sorted)
        peer_sorted = jnp.where(here, peer[:, s : s + 1], peer_sorted)
    src_ref[...] = src_sorted
    for m in range(OFFS // 2):
        tile = jnp.zeros((atoms, 128), F32)
        for u in range(2 * GROUPS):
            t = 2 * GROUPS * m + u
            column = peer_sorted[:, t : t + 1] + float(atoms * (u // GROUPS))
            tile += jnp.where(column == wide, env_sorted[:, t : t + 1], 0.0)
        adj_ref[:, 128 * m : 128 * (m + 1)] = tile.astype(BF16)

    block = wb_ref.shape[1]
    row = fiota((block, block), 0)
    col = fiota((block, block), 1)
    major = jnp.floor((row + 0.5) * (1.0 / ORB))
    wb = wb_ref[...]
    wcat_ref[:, :128] = dot_nt(one_hot(row == col), wb).astype(BF16)
    wcat_ref[:, 128:] = dot_nt(
        one_hot((row - ORB * major) * ORB + major == col), wb
    ).astype(BF16)


def node_body(layer):
    def body(adj_ref, ghost_ref, h_ref, wm_ref, wu_ref, gain_ref, out_ref):
        mixed = dot(adj_ref[...], ghost_ref[...]).astype(BF16)
        summed = (dot(mixed, wm_ref[layer]) * 0.125).astype(BF16)
        updated = h_ref[...].astype(F32) + silu(dot(summed, wu_ref[layer]))
        out_ref[...] = (rms_norm(updated) * gain_ref[layer : layer + 1, :]).astype(BF16)

    return body


def edge_block(state, atom_col, peer_col, local_table, ghost_block, w_in, w_out):
    rows, atoms = state.shape[0], local_table.shape[0]
    lane = fiota((rows, atoms), 1)
    first = dot(one_hot(atom_col == lane), local_table)
    second = dot(one_hot(peer_col == lane), ghost_block)
    gate = silu(dot(state, w_in) * first * second).astype(BF16)
    return rms_norm(state.astype(F32) + dot(gate, w_out)).astype(BF16)


def reverse(o):
    return o // 9 * 9 + 8 - o % 9


def edge_body(layer, mirrored):
    def body(e_ref, idx_ref, h_ref, ghost_ref, wl_ref, wg_ref, wi_ref, wo_ref, out_ref, table):
        atoms = h_ref.shape[0]
        cap = e_ref.shape[0] // OFFS
        local = dot(h_ref[...], wl_ref[layer]).astype(BF16)
        table[...] = dot(ghost_ref[...], wg_ref[layer]).astype(BF16)
        for o in range(OFFS):
            take = reverse(o) if mirrored and layer == 0 else o
            out_ref[cap * o : cap * (o + 1), :] = edge_block(
                e_ref[cap * take : cap * (take + 1), :],
                idx_ref[:, o : o + 1],
                idx_ref[:, 32 + o : 33 + o],
                local,
                table[atoms * o : atoms * (o + 1), :],
                wi_ref[layer],
                wo_ref[layer],
            )

    return body


def final_body(layer):
    def body(
        own_ref, mir_ref, io_ref, im_ref, h_ref, ghost_ref, wl_ref, wr_ref, wi_ref, wo_ref,
        src_ref, place_ref, wcat_ref, out_ref, left, right, z_own, z_mir, rows,
    ):
        atoms = h_ref.shape[0]
        cap = own_ref.shape[0] // OFFS
        fan = place_ref.shape[0]
        near = dot(h_ref[...], wl_ref[layer]).astype(BF16)
        far = dot(h_ref[...], wr_ref[layer]).astype(BF16)
        left[...] = dot(ghost_ref[...], wl_ref[layer]).astype(BF16)
        right[...] = dot(ghost_ref[...], wr_ref[layer]).astype(BF16)
        lane = fiota((atoms, 2 * cap), 1)
        for o in range(OFFS):
            span = slice(cap * o, cap * (o + 1))
            part = slice(atoms * o, atoms * (o + 1))
            e_own = edge_block(
                own_ref[span, :], io_ref[:, o : o + 1], io_ref[:, 32 + o : 33 + o],
                near, right[part, :], wi_ref[layer], wo_ref[layer],
            )
            e_mir = edge_block(
                mir_ref[span, :], im_ref[:, o : o + 1], im_ref[:, 32 + o : 33 + o],
                far, left[part, :], wi_ref[layer], wo_ref[layer],
            )
            hot = jnp.concatenate(
                [
                    jnp.where(src_ref[:, GROUPS * o + k : GROUPS * o + k + 1] == lane, 1.0, 0.0)
                    for k in range(GROUPS)
                ],
                axis=0,
            ).astype(BF16)
            x_own = dot(hot[:, :cap], e_own)
            x_mir = dot(hot[:, cap:], e_mir)
            for k in range(GROUPS):
                to = pl.ds(GROUPS * o + k, atoms, stride=fan)
                z_own[to, :] = x_own[atoms * k : atoms * (k + 1)]
                z_mir[to, :] = x_mir[atoms * k : atoms * (k + 1)]
        wide = fiota((fan, 2 * fan), 1)
        for m in range(atoms // 2):
            span = slice(2 * fan * m, 2 * fan * (m + 1))
            perm = jnp.concatenate(
                [
                    jnp.where(place_ref[:, 2 * m : 2 * m + 1] == wide, 1.0, 0.0),
                    jnp.where(place_ref[:, 2 * m + 1 : 2 * m + 2] + float(fan) == wide, 1.0, 0.0),
                ],
                axis=0,
            ).astype(BF16)
            rows[span, :128] = dot(perm, z_own[span, :].astype(BF16)).astype(BF16)
            rows[span, 128:] = dot(perm, z_mir[span, :].astype(BF16)).astype(BF16)
        step = 16 * fan
        for g in range(atoms // 16):
            out_ref[:, step * g : step * (g + 1)] = dot_nt(
                wcat_ref[...], rows[step * g : step * (g + 1), :]
            ).astype(BF16)

    return body


def shards(
    atom_feats, bond_embed, pair_dist, neighbours, slot_kind, own_rows, send_pos, recv_pos,
    w_left, w_right, w_edge_in, w_edge_out, w_msg, w_upd, node_gain, w_block,
):
    atoms, channels = atom_feats.shape
    slots = neighbours.shape[0]
    fan = slots // atoms
    owned = own_rows.shape[0]
    cap = owned // OFFS
    block = w_block.shape[1]
    ghosts = OFFS * atoms

    def array(*shape, dtype=F32):
        return jax.ShapeDtypeStruct(shape, dtype)

    send = send_pos.reshape(1, owned)
    pack = neighbours | (slot_kind << 11) | (recv_pos << 13)
    ordered = call(
        order_body, array(owned, channels, dtype=BF16), send, bond_embed, flops=1.4e9
    )
    idx_own, idx_mir, adjacency, source, place, w_cat = call(
        prep_body,
        (
            array(cap, 64),
            array(cap, 64),
            array(atoms, ghosts, dtype=BF16),
            array(atoms, 128),
            array(fan, atoms),
            array(block, 2 * channels, dtype=BF16),
        ),
        send,
        own_rows.reshape(1, owned),
        pack.reshape(1, slots),
        pack.reshape(atoms, fan),
        pair_dist.reshape(atoms, fan),
        w_block,
    )
    mirror = deliver(ordered.reshape(2, 3, 3, cap, channels)).reshape(owned, channels)
    hidden = atom_feats
    for layer in range(2):
        ghost = ghost_table(hidden)
        new_hidden = call(
            node_body(layer),
            array(atoms, channels, dtype=BF16),
            adjacency, ghost, hidden, w_msg, w_upd, node_gain,
            flops=2e7, nbytes=5e5,
        )
        state_shape = array(owned, channels, dtype=BF16)
        table = pltpu.VMEM((ghosts, channels), BF16)
        ordered = call(
            edge_body(layer, False), state_shape,
            ordered, idx_own, hidden, ghost, w_left, w_right, w_edge_in, w_edge_out,
            scratch=[table], flops=1e9,
        )
        mirror = call(
            edge_body(layer, True), state_shape,
            mirror, idx_mir, hidden, ghost, w_right, w_left, w_edge_in, w_edge_out,
            scratch=[table], flops=1e9,
        )
        hidden = new_hidden
    ghost = ghost_table(hidden)
    return call(
        final_body(2),
        array(block, slots, dtype=BF16),
        ordered, mirror, idx_own, idx_mir, hidden, ghost, w_left, w_right, w_edge_in, w_edge_out,
        source, place, w_cat,
        scratch=[
            pltpu.VMEM((ghosts, channels), BF16),
            pltpu.VMEM((ghosts, channels), BF16),
            pltpu.VMEM((slots, channels), F32),
            pltpu.VMEM((slots, channels), F32),
            pltpu.VMEM((slots, 2 * channels), BF16),
        ],
        flops=3e9,
    )


def solution(mesh):
    axes = ("gx", "gy", "layer")
    rows = P(axes, None)
    flat = P(axes)
    placed = (rows, rows) + (flat,) * 6 + (P(),) * 8
    return jax.shard_map(
        shards,
        mesh=mesh,
        in_specs=placed,
        out_specs=P(None, axes),
        check_vma=False,
    )
```

time: 206 us -> 86 us (0.42)
  matrix products: 89.8 us -> 0 us
  Pallas kernels: 0 us -> 37.2 us
  local copies, waits for them, and re-layouts: 39.1 us -> 3.41 us
  waiting for transfers between devices: 37.5 us -> 23.8 us
  other arithmetic: 9.6 us -> 1.83 us
  starting transfers between devices: 25.4 us -> 19.1 us
    dot_general x85 -> x0, matrix products: 89.8 us -> none  [the longest x48 28.8 us: select_one_tile(): jnp.dot(picker, table, preferred_element_type=jnp.float32)]
    pallas_call x0 -> x9, Pallas kernels: none -> 37.2 us  [call(): pl.pallas_call(body, out_shape=outs, scratch_shapes=list(scratch), compil...]
    ppermute x20, waiting for transfers between devices: 37.5 us -> 23.8 us  [the longest x16 20.7 us: moved(): lax.ppermute(value, axis, [(i, (i + steps) % count) for i in range(count)])]
    gather x1 -> x0, local copies, waits for them, and re-layouts: 12.3 us -> none  [shards(): row_peer = jnp.take(neighbours, own_rows)]
    dynamic_slice x71 -> x0, local copies, waits for them, and re-layouts: 8.81 us -> none  [the longest x14 8.31 us: place_columns(): placed = lax.map(place_one_tile, jnp.arange(tiles, dtype=jnp.int32) * span)]
    ppermute x20, starting transfers between devices: 25.4 us -> 19.1 us  [the longest x16 13.3 us: moved(): lax.ppermute(value, axis, [(i, (i + steps) % count) for i in range(count)])]
    unnamed x61 -> x19, local copies, waits for them, and re-layouts: 5.32 us -> 0.93 us
    another operation x12 -> x0, local copies, waits for them, and re-layouts: 3.88 us -> none  [the longest x2 2.72 us: deliver(): return jnp.stack(along_cols, axis=3).reshape(outgoing.shape[0], -1)]
  transfers between devices with their start and end apart: 20 -> 20, of which waited for: 10 -> 11; matrix products, arithmetic and copies ran while one was open for 32% -> 5% of each run, Pallas kernels for 0% -> 19%
where the time goes in v1:
time: 86 us; the launch traced here: 85.6 us
  Pallas kernels  37.2 us (43%)
  waiting for transfers between devices  23.8 us (28%)
  starting transfers between devices  19.1 us (22%)
  local copies, waits for them, and re-layouts  3.41 us (4%)
  other arithmetic  1.83 us (2%)
    pallas_call x9, Pallas kernels, call(): pl.pallas_call(body, out_shape=outs, scratch_shapes=list(scratch), compil...  37.2 us
    ppermute x16, waiting for transfers between devices, moved(): lax.ppermute(value, axis, [(i, (i + steps) % count) for i in range(count)])  20.7 us
    ppermute x16, starting transfers between devices, moved(): lax.ppermute(value, axis, [(i, (i + steps) % count) for i in range(count)])  13.3 us
    ppermute x4, starting transfers between devices, swapped(): return lax.ppermute(value, axis, [(0, 1), (1, 0)])  5.78 us
    ppermute x4, waiting for transfers between devices, swapped(): return lax.ppermute(value, axis, [(0, 1), (1, 0)])  3.03 us
  transfers between devices with their start and end apart: 20, of which 11 were waited for; matrix products, arithmetic and copies ran while one was open for 5% of the time, Pallas kernels for 19%

profile of v1, /device:TPU:0, one launch (start us, length us, event | category | flops | bytes accessed | tf_op | source)
XLA Modules:
  0.0 85.6 jit_solution(17482834947430454377)
XLA Ops:
  0.0 3.0 %collective-permute-start = (bf16[64,128]{1,0:T(8,128)(2,1)}, bf16[64,128]{1,0:T(8,128)(2,1)S(1)}, u32[]{:S(2)}, u32[]{:S(2)}) collective-permute-start(bf16[64,128]{1,0:T(8,128)(2,1)} %h_ref.5), channel_id=1, source_target_pairs={{0,1},{1,0},{2,3},{3,2},{4,5},{5,4},{6,7},{7,6},{8,9},{9,8},{10,11... | collective-permute-start | bytes 49160 | tf_op jit(solution)/shard_map/ppermute | solution.py:17
  3.1 1.9 %collective-permute-done = bf16[64,128]{1,0:T(8,128)(2,1)S(1)} collective-permute-done((bf16[64,128]{1,0:T(8,128)(2,1)}, bf16[64,128]{1,0:T(8,128)(2,1)S(1)}, u32[]{:S(2)}, u32[]{:S(2)}) %collective-permute-start) | collective-permute-done | bytes 16416 | tf_op jit(solution)/shard_map/ppermute | solution.py:17
  5.0 0.7 maximum_bitcast_fusion
  5.7 4.1 %collective-permute-start.2 = (bf16[2,1,1,64,128]{4,3,0,2,1:T(8,128)(2,1)S(1)}, bf16[2,1,1,64,128]{4,3,0,2,1:T(8,128)(2,1)S(1)}, u32[]{:S(2)}, u32[]{:S(2)}) collective-permute-start(bf16[2,1,1,64,128]{4,3,0,2,1:T(8,128)(2,1)S(1)} %maximum_bitcast_fusion), channel_id=1, source_target_pairs={{0,24},{8,0},{16,8},{24,16},{1,25},{9,1},{17,9},{25,17},{2,26},{10... | collective-permute-start | bytes 98312 | tf_op jit(solution)/shard_map/ppermute | solution.py:22
  9.8 0.0 collective-permute-start.1
  9.8 1.6 %collective-permute-done.2 = bf16[2,1,1,64,128]{4,3,0,2,1:T(8,128)(2,1)S(1)} collective-permute-done((bf16[2,1,1,64,128]{4,3,0,2,1:T(8,128)(2,1)S(1)}, bf16[2,1,1,64,128]{4,3,0,2,1:T(8,128)(2,1)S(1)}, u32[]{:S(2)}, u32[]{:S(2)}) %collective-permute-start.2) | collective-permute-done | bytes 32800 | tf_op jit(solution)/shard_map/ppermute | solution.py:22
  11.4 4.1 %collective-permute-done.1 = bf16[2,1,1,64,128]{4,3,0,2,1:T(8,128)(2,1)S(1)} collective-permute-done((bf16[2,1,1,64,128]{4,3,0,2,1:T(8,128)(2,1)S(1)}, bf16[2,1,1,64,128]{4,3,0,2,1:T(8,128)(2,1)S(1)}, u32[]{:S(2)}, u32[]{:S(2)}) %collective-permute-start.1) | collective-permute-done | bytes 32800 | tf_op jit(solution)/shard_map/ppermute | solution.py:22
  15.5 0.1 collective-permute-start.4
  15.6 0.5 collective-permute-start.3
  16.1 0.8 shift-left_or_fusion
  16.9 0.1 reshape.34.pack_ref
  17.0 0.7 reshape.31.send_ref
  17.7 0.7 reshape.32.own_ref
  18.4 0.8 reshape.35.dist_ref
  19.2 0.9 %copy.17.wb_ref = bf16[128,169]{1,0:T(8,128)(2,1)S(1)} copy(bf16[128,169]{0,1:T(8,128)(2,1)} %param.31) | data formatting | bytes 86528 | tf_op args[15]
  20.1 5.1 %shard_map.155 = (f32[128,64]{1,0:T(8,128)S(1)}, f32[128,64]{1,0:T(8,128)S(1)}, bf16[64,1152]{1,0:T(8,128)(2,1)S(1)}, f32[64,128]{1,0:T(8,128)S(1)}, f32[72,64]{1,0:T(8,128)S(1)}, /*index=5*/bf16[169,256]{1,0:T(8,128)(2,1)S(1)}) custom-call(s32[1,2304]{1,0:T(1,128)S(1)} %reshape.31.send_ref, s32[1,2304]{1,0:T(1,128)S(1)} %reshape.32.own_ref, ...), custom_call_target="tpu_custom_call" | custom-call | flops 100000000 | bytes 3000000 | tf_op jit(solution)/shard_map/pallas_call | solution.py:74
  25.2 0.0 collective-permute-done.4
  25.2 0.0 collective-permute-done.3
  25.3 0.5 shard_map.157.h_ref
  25.9 1.6 %collective-permute-start.5 = (bf16[64,128]{1,0:T(8,128)(2,1)S(1)}, bf16[64,128]{1,0:T(8,128)(2,1)S(1)}, u32[]{:S(2)}, u32[]{:S(2)}) collective-permute-start(bf16[64,128]{1,0:T(8,128)(2,1)S(1)} %shard_map.157.h_ref), channel_id=1, source_target_pairs={{0,1},{1,0},{2,3},{3,2},{4,5},{5,4},{6,7},{7,6},{8,9},{9,8},{10,11... | collective-permute-start | bytes 49160 | tf_op jit(solution)/shard_map/ppermute | solution.py:17
  27.4 4.3 %shard_map.154.e_ref = bf16[2304,128]{1,0:T(8,128)(2,1)S(1)} custom-call(s32[1,2304]{1,0:T(1,128)S(1)} %reshape.31.send_ref, bf16[2304,128]{1,0:T(8,128)(2,1)S(1)} %copy-done.4), custom_call_target="tpu_custom_call" | custom-call | flops 1400000000 | bytes 3000000 | tf_op jit(solution)/shard_map/pallas_call | solution.py:74
  31.7 0.0 collective-permute-done.5
  31.7 0.1 collective-permute-start.7
  31.8 2.0 %collective-permute-start.6 = (bf16[2,1,1,64,128]{4,3,0,2,1:T(8,128)(2,1)S(1)}, bf16[2,1,1,64,128]{4,3,0,2,1:T(8,128)(2,1)S(1)}, u32[]{:S(2)}, u32[]{:S(2)}) collective-permute-start(bf16[2,1,1,64,128]{4,3,0,2,1:T(8,128)(2,1)S(1)} %maximum_bitcast_fusion.1), channel_id=1, source_target_pairs={{0,8},{8,16},{16,24},{24,0},{1,9},{9,17},{17,25},{25,1},{2,10},{10... | collective-permute-start | bytes 98312 | tf_op jit(solution)/shard_map/ppermute | solution.py:22
  33.9 0.0 copy-start.5
  33.9 0.0 copy-start.6
  33.9 0.0 copy-start.7
  33.9 0.0 copy-start.8
  33.9 0.6 collective-permute-start.10
  34.5 1.5 %collective-permute-done.7 = bf16[2,1,1,64,128]{4,3,0,2,1:T(8,128)(2,1)S(1)} collective-permute-done((bf16[2,1,1,64,128]{4,3,0,2,1:T(8,128)(2,1)S(1)}, bf16[2,1,1,64,128]{4,3,0,2,1:T(8,128)(2,1)S(1)}, u32[]{:S(2)}, u32[]{:S(2)}) %collective-permute-start.7) | collective-permute-done | bytes 32800 | tf_op jit(solution)/shard_map/ppermute | solution.py:22
  36.0 1.9 %collective-permute-done.6 = bf16[2,1,1,64,128]{4,3,0,2,1:T(8,128)(2,1)S(1)} collective-permute-done((bf16[2,1,1,64,128]{4,3,0,2,1:T(8,128)(2,1)S(1)}, bf16[2,1,1,64,128]{4,3,0,2,1:T(8,128)(2,1)S(1)}, u32[]{:S(2)}, u32[]{:S(2)}) %collective-permute-start.6) | collective-permute-done | bytes 32800 | tf_op jit(solution)/shard_map/ppermute | solution.py:22
  37.9 0.1 collective-permute-start.9
  37.9 0.5 collective-permute-start.8
  38.4 1.7 %collective-permute-done.9 = bf16[2,3,1,64,128]{4,3,0,2,1:T(8,128)(2,1)S(1)} collective-permute-done((bf16[2,3,1,64,128]{4,3,0,2,1:T(8,128)(2,1)S(1)}, bf16[2,3,1,64,128]{4,3,0,2,1:T(8,128)(2,1)S(1)}, u32[]{:S(2)}, u32[]{:S(2)}) %collective-permute-start.9) | collective-permute-done | bytes 98336 | tf_op jit(solution)/shard_map/ppermute | solution.py:22
  40.1 2.8 %collective-permute-done.8 = bf16[2,3,1,64,128]{4,3,0,2,1:T(8,128)(2,1)S(1)} collective-permute-done((bf16[2,3,1,64,128]{4,3,0,2,1:T(8,128)(2,1)S(1)}, bf16[2,3,1,64,128]{4,3,0,2,1:T(8,128)(2,1)S(1)}, u32[]{:S(2)}, u32[]{:S(2)}) %collective-permute-start.8) | collective-permute-done | bytes 98336 | tf_op jit(solution)/shard_map/ppermute | solution.py:22
  43.0 0.5 shard_map.161.h_ref
  43.5 0.6 collective-permute-start.15
  44.1 0.0 collective-permute-done.10
  44.1 0.1 fusion.3
  44.2 1.3 %collective-permute-start.11 = (bf16[2,3,128,128]{3,2,0,1:T(8,128)(2,1)S(1)}, bf16[2,3,128,128]{3,2,0,1:T(8,128)(2,1)S(1)}, u32[]{:S(2)}, u32[]{:S(2)}) collective-permute-start(bf16[2,3,128,128]{3,2,0,1:T(8,128)(2,1)S(1)} %get-tuple-element.20), channel_id=1, source_target_pairs={{0,24},{8,0},{16,8},{24,16},{1,25},{9,1},{17,9},{25,17},{2,26},{10... | collective-permute-start | bytes 589832 | tf_op jit(solution)/shard_map/ppermute | solution.py:22
  45.5 0.8 collective-permute-start.12
  46.3 1.1 %collective-permute-done.15 = bf16[64,128]{1,0:T(8,128)(2,1)S(1)} collective-permute-done((bf16[64,128]{1,0:T(8,128)(2,1)S(1)}, bf16[64,128]{1,0:T(8,128)(2,1)S(1)}, u32[]{:S(2)}, u32[]{:S(2)}) %collective-permute-start.15) | collective-permute-done | bytes 16416 | tf_op jit(solution)/shard_map/ppermute | solution.py:17
  47.4 2.0 %collective-permute-start.17 = (bf16[2,1,1,64,128]{4,3,0,2,1:T(8,128)(2,1)S(1)}, bf16[2,1,1,64,128]{4,3,0,2,1:T(8,128)(2,1)S(1)}, u32[]{:S(2)}, u32[]{:S(2)}) collective-permute-start(bf16[2,1,1,64,128]{4,3,0,2,1:T(8,128)(2,1)S(1)} %maximum_bitcast_fusion.2), channel_id=1, source_target_pairs={{0,24},{8,0},{16,8},{24,16},{1,25},{9,1},{17,9},{25,17},{2,26},{10... | collective-permute-start | bytes 98312 | tf_op jit(solution)/shard_map/ppermute | solution.py:22
  49.4 0.0 collective-permute-start.16
  49.4 0.0 copy-done.6
  49.4 3.2 %shard_map.156.e_ref = bf16[2304,128]{1,0:T(8,128)(2,1)S(1)} custom-call(bf16[2304,128]{1,0:T(8,128)(2,1)S(1)} %shard_map.154.e_ref, f32[128,64]{1,0:T(8,128)S(1)} %get-tuple-element.11.idx_ref.io_ref, bf16[64,128]{1,0:T(8,128)(2,1)S(1)} %copy-done.2, bf16[1152,128]{1,0:T(8,128)(2,1)S(1)} %bitcast.42, bf16[3,128,128]{2,1,0:T(8,128)(2,1)S(1)} %copy-done.5, ...), custom_call_target="tpu_custom_call" | custom-call | flops 1000000000 | bytes 3000000 | tf_op jit(solution)/shard_map/pallas_call | solution.py:74
  52.6 4.1 %collective-permute-done.17 = bf16[2,1,1,64,128]{4,3,0,2,1:T(8,128)(2,1)S(1)} collective-permute-done((bf16[2,1,1,64,128]{4,3,0,2,1:T(8,128)(2,1)S(1)}, bf16[2,1,1,64,128]{4,3,0,2,1:T(8,128)(2,1)S(1)}, u32[]{:S(2)}, u32[]{:S(2)}) %collective-permute-start.17) | collective-permute-done | bytes 32800 | tf_op jit(solution)/shard_map/ppermute | solution.py:22
  56.6 0.0 collective-permute-done.16
  56.6 0.1 collective-permute-start.19
  56.7 0.5 collective-permute-start.18
  57.2 0.0 collective-permute-done.11
  57.2 0.0 collective-permute-done.12
  57.2 0.1 pad_maximum_fusion
  57.3 1.4 %collective-permute-start.13 = (bf16[2,3,128,128]{3,2,1,0:T(8,128)(2,1)S(1)}, bf16[2,3,128,128]{3,2,1,0:T(8,128)(2,1)S(1)}, u32[]{:S(2)}, u32[]{:S(2)}) collective-permute-start(bf16[2,3,128,128]{3,2,1,0:T(8,128)(2,1)S(1)} %get-tuple-element.17), channel_id=1, source_target_pairs={{0,6},{2,0},{4,2},{6,4},{1,7},{3,1},{5,3},{7,5},{8,14},{10,8},{12,... | collective-permute-start | bytes 589832 | tf_op jit(solution)/shard_map/ppermute | solution.py:22
  58.7 0.0 collective-permute-start.14
  58.7 3.1 %shard_map.158.own_ref = bf16[2304,128]{1,0:T(8,128)(2,1)S(1)} custom-call(bf16[2304,128]{1,0:T(8,128)(2,1)S(1)} %shard_map.156.e_ref, f32[128,64]{1,0:T(8,128)S(1)} %get-tuple-element.11.idx_ref.io_ref, bf16[64,128]{1,0:T(8,128)(2,1)S(1)} %shard_map.157.h_ref, bf16[1152,128]{1,0:T(8,128)(2,1)S(1)} %bitcast.45, bf16[3,128,128]{2,1,0:T(8,128)(2,1)S(1)} %copy-done.5, ...), custom_call_target="tpu_custom_call" | custom-call | flops 1000000000 | bytes 3000000 | tf_op jit(solution)/shard_map/pallas_call | solution.py:74
  61.8 0.0 collective-permute-done.19
  61.9 0.0 collective-permute-done.18
  61.9 2.0 %collective-permute-done.13 = bf16[2,3,128,128]{3,2,1,0:T(8,128)(2,1)S(1)} collective-permute-done((bf16[2,3,128,128]{3,2,1,0:T(8,128)(2,1)S(1)}, bf16[2,3,128,128]{3,2,1,0:T(8,128)(2,1)S(1)}, u32[]{:S(2)}, u32[]{:S(2)}) %collective-permute-start.13) | collective-permute-done | bytes 196640 | tf_op jit(solution)/shard_map/ppermute | solution.py:22
  63.9 1.1 %collective-permute-done.14 = bf16[2,3,128,128]{3,2,1,0:T(8,128)(2,1)S(1)} collective-permute-done((bf16[2,3,128,128]{3,2,1,0:T(8,128)(2,1)S(1)}, bf16[2,3,128,128]{3,2,1,0:T(8,128)(2,1)S(1)}, u32[]{:S(2)}, u32[]{:S(2)}) %collective-permute-start.14) | collective-permute-done | bytes 196640 | tf_op jit(solution)/shard_map/ppermute | solution.py:22
  65.0 0.1 pad_maximum_fusion.1
  65.1 3.2 %shard_map.159.e_ref = bf16[2304,128]{1,0:T(8,128)(2,1)S(1)} custom-call(bf16[2304,128]{1,0:T(8,128)(2,1)S(1)} %bitcast.47, f32[128,64]{1,0:T(8,128)S(1)} %get-tuple-element.13.idx_ref.im_ref, bf16[64,128]{1,0:T(8,128)(2,1)S(1)} %copy-done.2, bf16[1152,128]{1,0:T(8,128)(2,1)S(1)} %bitcast.43, bf16[3,128,128]{2,1,0:T(8,128)(2,1)S(1)} %copy-done.6, ...), custom_call_target="tpu_custom_call" | custom-call | flops 1000000000 | bytes 3000000 | tf_op jit(solution)/shard_map/pallas_call | solution.py:74
  68.2 3.2 %shard_map.160.mir_ref = bf16[2304,128]{1,0:T(8,128)(2,1)S(1)} custom-call(bf16[2304,128]{1,0:T(8,128)(2,1)S(1)} %shard_map.159.e_ref, f32[128,64]{1,0:T(8,128)S(1)} %get-tuple-element.13.idx_ref.im_ref, bf16[64,128]{1,0:T(8,128)(2,1)S(1)} %shard_map.157.h_ref, bf16[1152,128]{1,0:T(8,128)(2,1)S(1)} %bitcast.46, bf16[3,128,128]{2,1,0:T(8,128)(2,1)S(1)} %copy-done.6, ...), custom_call_target="tpu_custom_call" | custom-call | flops 1000000000 | bytes 3000000 | tf_op jit(solution)/shard_map/pallas_call | solution.py:74
  71.4 14.2 %shard_map.162 = bf16[169,4608]{1,0:T(8,128)(2,1)} custom-call(bf16[2304,128]{1,0:T(8,128)(2,1)S(1)} %shard_map.158.own_ref, bf16[2304,128]{1,0:T(8,128)(2,1)S(1)} %shard_map.160.mir_ref, f32[128,64]{1,0:T(8,128)S(1)} %get-tuple-element.11.idx_ref.io_ref, f32[128,64]{1,0:T(8,128)S(1)} %get-tuple-element.13.idx_ref.im_ref, ...), custom_call_target="tpu_custom_call" | custom-call | flops 3000000000 | bytes 3000000 | tf_op jit(solution)/shard_map/pallas_call | solution.py:74
  (27 shorter events, 0.3 us)
Async XLA Ops:
  0.0 25.3 %copy-start.2 = (bf16[64,128]{1,0:T(8,128)(2,1)S(1)}, bf16[64,128]{1,0:T(8,128)(2,1)}, u32[]{:S(2)}) copy-start(bf16[64,128]{1,0:T(8,128)(2,1)} %h_ref.5) | copy-start | bytes 49156
  0.0 25.3 %copy-start.3 = (f32[2,128]{1,0:T(2,128)S(1)}, f32[2,128]{1,0:T(2,128)}, u32[]{:S(2)}) copy-start(f32[2,128]{1,0:T(2,128)} %gain_ref.3) | copy-start | bytes 3076
  0.0 25.3 %copy-start.1 = (bf16[2,128,128]{2,1,0:T(8,128)(2,1)S(1)}, bf16[2,128,128]{2,1,0:T(8,128)(2,1)}, u32[]{:S(2)}) copy-start(bf16[2,128,128]{2,1,0:T(8,128)(2,1)} %wu_ref.3) | copy-start | bytes 196612
  0.0 25.3 %copy-start = (bf16[2,128,128]{2,1,0:T(8,128)(2,1)S(1)}, bf16[2,128,128]{2,1,0:T(8,128)(2,1)}, u32[]{:S(2)}) copy-start(bf16[2,128,128]{2,1,0:T(8,128)(2,1)} %wm_ref.3) | copy-start | bytes 196612
  0.0 27.4 %copy-start.4 = (bf16[2304,128]{1,0:T(8,128)(2,1)S(1)}, bf16[2304,128]{1,0:T(8,128)(2,1)}, u32[]{:S(2)}) copy-start(bf16[2304,128]{1,0:T(8,128)(2,1)} %bond_ref.1) | copy-start | bytes 1769476
  0.0 5.0 %collective-permute-start = (bf16[64,128]{1,0:T(8,128)(2,1)}, bf16[64,128]{1,0:T(8,128)(2,1)S(1)}, u32[]{:S(2)}, u32[]{:S(2)}) collective-permute-start(bf16[64,128]{1,0:T(8,128)(2,1)} %h_ref.5), channel_id=1, source_target_pairs={{0,1},{1,0},{2,3},{3,2},{4,5},{5,4},{6,7},{7,6},{8,9},{9,8},{10,11... | collective-permute-start | bytes 49160 | tf_op jit(solution)/shard_map/ppermute | solution.py:17
  5.7 5.7 %collective-permute-start.2 = (bf16[2,1,1,64,128]{4,3,0,2,1:T(8,128)(2,1)S(1)}, bf16[2,1,1,64,128]{4,3,0,2,1:T(8,128)(2,1)S(1)}, u32[]{:S(2)}, u32[]{:S(2)}) collective-permute-start(bf16[2,1,1,64,128]{4,3,0,2,1:T(8,128)(2,1)S(1)} %maximum_bitcast_fusion), channel_id=1, source_target_pairs={{0,24},{8,0},{16,8},{24,16},{1,25},{9,1},{17,9},{25,17},{2,26},{10... | collective-permute-start | bytes 98312 | tf_op jit(solution)/shard_map/ppermute | solution.py:22
  9.8 5.7 %collective-permute-start.1 = (bf16[2,1,1,64,128]{4,3,0,2,1:T(8,128)(2,1)S(1)}, bf16[2,1,1,64,128]{4,3,0,2,1:T(8,128)(2,1)S(1)}, u32[]{:S(2)}, u32[]{:S(2)}) collective-permute-start(bf16[2,1,1,64,128]{4,3,0,2,1:T(8,128)(2,1)S(1)} %maximum_bitcast_fusion), channel_id=1, source_target_pairs={{0,8},{8,16},{16,24},{24,0},{1,9},{9,17},{17,25},{25,1},{2,10},{10... | collective-permute-start | bytes 98312 | tf_op jit(solution)/shard_map/ppermute | solution.py:22
  15.5 9.6 %collective-permute-start.4 = (bf16[2,3,1,64,128]{4,3,0,2,1:T(8,128)(2,1)S(1)}, bf16[2,3,1,64,128]{4,3,0,2,1:T(8,128)(2,1)S(1)}, u32[]{:S(2)}, u32[]{:S(2)}) collective-permute-start(bf16[2,3,1,64,128]{4,3,0,2,1:T(8,128)(2,1)S(1)} %pad_maximum_fusion.6), channel_id=1, source_target_pairs={{0,6},{2,0},{4,2},{6,4},{1,7},{3,1},{5,3},{7,5},{8,14},{10,8},{12,... | collective-permute-start | bytes 294920 | tf_op jit(solution)/shard_map/ppermute | solution.py:22
  15.6 9.6 %collective-permute-start.3 = (bf16[2,3,1,64,128]{4,3,0,2,1:T(8,128)(2,1)S(1)}, bf16[2,3,1,64,128]{4,3,0,2,1:T(8,128)(2,1)S(1)}, u32[]{:S(2)}, u32[]{:S(2)}) collective-permute-start(bf16[2,3,1,64,128]{4,3,0,2,1:T(8,128)(2,1)S(1)} %pad_maximum_fusion.6), channel_id=1, source_target_pairs={{0,2},{2,4},{4,6},{6,0},{1,3},{3,5},{5,7},{7,1},{8,10},{10,12},{12... | collective-permute-start | bytes 294920 | tf_op jit(solution)/shard_map/ppermute | solution.py:22
  25.9 5.9 %collective-permute-start.5 = (bf16[64,128]{1,0:T(8,128)(2,1)S(1)}, bf16[64,128]{1,0:T(8,128)(2,1)S(1)}, u32[]{:S(2)}, u32[]{:S(2)}) collective-permute-start(bf16[64,128]{1,0:T(8,128)(2,1)S(1)} %shard_map.157.h_ref), channel_id=1, source_target_pairs={{0,1},{1,0},{2,3},{3,2},{4,5},{5,4},{6,7},{7,6},{8,9},{9,8},{10,11... | collective-permute-start | bytes 49160 | tf_op jit(solution)/shard_map/ppermute | solution.py:17
  31.7 4.2 %collective-permute-start.7 = (bf16[2,1,1,64,128]{4,3,0,2,1:T(8,128)(2,1)S(1)}, bf16[2,1,1,64,128]{4,3,0,2,1:T(8,128)(2,1)S(1)}, u32[]{:S(2)}, u32[]{:S(2)}) collective-permute-start(bf16[2,1,1,64,128]{4,3,0,2,1:T(8,128)(2,1)S(1)} %maximum_bitcast_fusion.1), channel_id=1, source_target_pairs={{0,24},{8,0},{16,8},{24,16},{1,25},{9,1},{17,9},{25,17},{2,26},{10... | collective-permute-start | bytes 98312 | tf_op jit(solution)/shard_map/ppermute | solution.py:22
  31.8 6.0 %collective-permute-start.6 = (bf16[2,1,1,64,128]{4,3,0,2,1:T(8,128)(2,1)S(1)}, bf16[2,1,1,64,128]{4,3,0,2,1:T(8,128)(2,1)S(1)}, u32[]{:S(2)}, u32[]{:S(2)}) collective-permute-start(bf16[2,1,1,64,128]{4,3,0,2,1:T(8,128)(2,1)S(1)} %maximum_bitcast_fusion.1), channel_id=1, source_target_pairs={{0,8},{8,16},{16,24},{24,0},{1,9},{9,17},{17,25},{25,1},{2,10},{10... | collective-permute-start | bytes 98312 | tf_op jit(solution)/shard_map/ppermute | solution.py:22
  33.9 15.5 %copy-start.5 = (bf16[3,128,128]{2,1,0:T(8,128)(2,1)S(1)}, bf16[3,128,128]{2,1,0:T(8,128)(2,1)}, u32[]{:S(2)}) copy-start(bf16[3,128,128]{2,1,0:T(8,128)(2,1)} %wl_ref.9) | copy-start | bytes 294916
  33.9 15.5 %copy-start.6 = (bf16[3,128,128]{2,1,0:T(8,128)(2,1)S(1)}, bf16[3,128,128]{2,1,0:T(8,128)(2,1)}, u32[]{:S(2)}) copy-start(bf16[3,128,128]{2,1,0:T(8,128)(2,1)} %wr_ref.1) | copy-start | bytes 294916
  33.9 15.5 %copy-start.7 = (bf16[3,128,128]{2,1,0:T(8,128)(2,1)S(1)}, bf16[3,128,128]{2,1,0:T(8,128)(2,1)}, u32[]{:S(2)}) copy-start(bf16[3,128,128]{2,1,0:T(8,128)(2,1)} %wi_ref.9) | copy-start | bytes 294916
  33.9 15.5 %copy-start.8 = (bf16[3,128,128]{2,1,0:T(8,128)(2,1)S(1)}, bf16[3,128,128]{2,1,0:T(8,128)(2,1)}, u32[]{:S(2)}) copy-start(bf16[3,128,128]{2,1,0:T(8,128)(2,1)} %wo_ref.9) | copy-start | bytes 294916
  33.9 10.2 %collective-permute-start.10 = (bf16[3,3,128,128]{3,2,1,0:T(8,128)(2,1)S(1)}, bf16[3,3,128,128]{3,2,1,0:T(8,128)(2,1)S(1)}, u32[]{:S(2)}, u32[]{:S(2)}) collective-permute-start(bf16[3,3,128,128]{3,2,1,0:T(8,128)(2,1)S(1)} %bitcast.54), channel_id=1, source_target_pairs={{0,1},{1,0},{2,3},{3,2},{4,5},{5,4},{6,7},{7,6},{8,9},{9,8},{10,11... | collective-permute-start | bytes 884744 | tf_op jit(solution)/shard_map/ppermute | solution.py:17
  37.9 2.3 %collective-permute-start.9 = (bf16[2,3,1,64,128]{4,3,0,2,1:T(8,128)(2,1)S(1)}, bf16[2,3,1,64,128]{4,3,0,2,1:T(8,128)(2,1)S(1)}, u32[]{:S(2)}, u32[]{:S(2)}) collective-permute-start(bf16[2,3,1,64,128]{4,3,0,2,1:T(8,128)(2,1)S(1)} %pad_maximum_fusion.7), channel_id=1, source_target_pairs={{0,6},{2,0},{4,2},{6,4},{1,7},{3,1},{5,3},{7,5},{8,14},{10,8},{12,... | collective-permute-start | bytes 294920 | tf_op jit(solution)/shard_map/ppermute | solution.py:22
  37.9 5.0 %collective-permute-start.8 = (bf16[2,3,1,64,128]{4,3,0,2,1:T(8,128)(2,1)S(1)}, bf16[2,3,1,64,128]{4,3,0,2,1:T(8,128)(2,1)S(1)}, u32[]{:S(2)}, u32[]{:S(2)}) collective-permute-start(bf16[2,3,1,64,128]{4,3,0,2,1:T(8,128)(2,1)S(1)} %pad_maximum_fusion.7), channel_id=1, source_target_pairs={{0,2},{2,4},{4,6},{6,0},{1,3},{3,5},{5,7},{7,1},{8,10},{10,12},{12... | collective-permute-start | bytes 294920 | tf_op jit(solution)/shard_map/ppermute | solution.py:22
  43.5 3.8 %collective-permute-start.15 = (bf16[64,128]{1,0:T(8,128)(2,1)S(1)}, bf16[64,128]{1,0:T(8,128)(2,1)S(1)}, u32[]{:S(2)}, u32[]{:S(2)}) collective-permute-start(bf16[64,128]{1,0:T(8,128)(2,1)S(1)} %shard_map.161.h_ref), channel_id=1, source_target_pairs={{0,1},{1,0},{2,3},{3,2},{4,5},{5,4},{6,7},{7,6},{8,9},{9,8},{10,11... | collective-permute-start | bytes 49160 | tf_op jit(solution)/shard_map/ppermute | solution.py:17
  44.2 13.0 %collective-permute-start.11 = (bf16[2,3,128,128]{3,2,0,1:T(8,128)(2,1)S(1)}, bf16[2,3,128,128]{3,2,0,1:T(8,128)(2,1)S(1)}, u32[]{:S(2)}, u32[]{:S(2)}) collective-permute-start(bf16[2,3,128,128]{3,2,0,1:T(8,128)(2,1)S(1)} %get-tuple-element.20), channel_id=1, source_target_pairs={{0,24},{8,0},{16,8},{24,16},{1,25},{9,1},{17,9},{25,17},{2,26},{10... | collective-permute-start | bytes 589832 | tf_op jit(solution)/shard_map/ppermute | solution.py:22
  45.5 11.7 %collective-permute-start.12 = (bf16[2,3,128,128]{3,2,0,1:T(8,128)(2,1)S(1)}, bf16[2,3,128,128]{3,2,0,1:T(8,128)(2,1)S(1)}, u32[]{:S(2)}, u32[]{:S(2)}) collective-permute-start(bf16[2,3,128,128]{3,2,0,1:T(8,128)(2,1)S(1)} %get-tuple-element.21), channel_id=1, source_target_pairs={{0,8},{8,16},{16,24},{24,0},{1,9},{9,17},{17,25},{25,1},{2,10},{10... | collective-permute-start | bytes 589832 | tf_op jit(solution)/shard_map/ppermute | solution.py:22
  47.4 9.3 %collective-permute-start.17 = (bf16[2,1,1,64,128]{4,3,0,2,1:T(8,128)(2,1)S(1)}, bf16[2,1,1,64,128]{4,3,0,2,1:T(8,128)(2,1)S(1)}, u32[]{:S(2)}, u32[]{:S(2)}) collective-permute-start(bf16[2,1,1,64,128]{4,3,0,2,1:T(8,128)(2,1)S(1)} %maximum_bitcast_fusion.2), channel_id=1, source_target_pairs={{0,24},{8,0},{16,8},{24,16},{1,25},{9,1},{17,9},{25,17},{2,26},{10... | collective-permute-start | bytes 98312 | tf_op jit(solution)/shard_map/ppermute | solution.py:22
  49.4 7.3 %collective-permute-start.16 = (bf16[2,1,1,64,128]{4,3,0,2,1:T(8,128)(2,1)S(1)}, bf16[2,1,1,64,128]{4,3,0,2,1:T(8,128)(2,1)S(1)}, u32[]{:S(2)}, u32[]{:S(2)}) collective-permute-start(bf16[2,1,1,64,128]{4,3,0,2,1:T(8,128)(2,1)S(1)} %maximum_bitcast_fusion.2), channel_id=1, source_target_pairs={{0,8},{8,16},{16,24},{24,0},{1,9},{9,17},{17,25},{25,1},{2,10},{10... | collective-permute-start | bytes 98312 | tf_op jit(solution)/shard_map/ppermute | solution.py:22
  56.6 5.2 %collective-permute-start.19 = (bf16[2,3,1,64,128]{4,3,0,2,1:T(8,128)(2,1)S(1)}, bf16[2,3,1,64,128]{4,3,0,2,1:T(8,128)(2,1)S(1)}, u32[]{:S(2)}, u32[]{:S(2)}) collective-permute-start(bf16[2,3,1,64,128]{4,3,0,2,1:T(8,128)(2,1)S(1)} %pad_maximum_fusion.8), channel_id=1, source_target_pairs={{0,6},{2,0},{4,2},{6,4},{1,7},{3,1},{5,3},{7,5},{8,14},{10,8},{12,... | collective-permute-start | bytes 294920 | tf_op jit(solution)/shard_map/ppermute | solution.py:22
  56.7 5.1 %collective-permute-start.18 = (bf16[2,3,1,64,128]{4,3,0,2,1:T(8,128)(2,1)S(1)}, bf16[2,3,1,64,128]{4,3,0,2,1:T(8,128)(2,1)S(1)}, u32[]{:S(2)}, u32[]{:S(2)}) collective-permute-start(bf16[2,3,1,64,128]{4,3,0,2,1:T(8,128)(2,1)S(1)} %pad_maximum_fusion.8), channel_id=1, source_target_pairs={{0,2},{2,4},{4,6},{6,0},{1,3},{3,5},{5,7},{7,1},{8,10},{10,12},{12... | collective-permute-start | bytes 294920 | tf_op jit(solution)/shard_map/ppermute | solution.py:22
  57.3 6.6 %collective-permute-start.13 = (bf16[2,3,128,128]{3,2,1,0:T(8,128)(2,1)S(1)}, bf16[2,3,128,128]{3,2,1,0:T(8,128)(2,1)S(1)}, u32[]{:S(2)}, u32[]{:S(2)}) collective-permute-start(bf16[2,3,128,128]{3,2,1,0:T(8,128)(2,1)S(1)} %get-tuple-element.17), channel_id=1, source_target_pairs={{0,6},{2,0},{4,2},{6,4},{1,7},{3,1},{5,3},{7,5},{8,14},{10,8},{12,... | collective-permute-start | bytes 589832 | tf_op jit(solution)/shard_map/ppermute | solution.py:22
  58.7 6.3 %collective-permute-start.14 = (bf16[2,3,128,128]{3,2,1,0:T(8,128)(2,1)S(1)}, bf16[2,3,128,128]{3,2,1,0:T(8,128)(2,1)S(1)}, u32[]{:S(2)}, u32[]{:S(2)}) collective-permute-start(bf16[2,3,128,128]{3,2,1,0:T(8,128)(2,1)S(1)} %get-tuple-element.18), channel_id=1, source_target_pairs={{0,2},{2,4},{4,6},{6,0},{1,3},{3,5},{5,7},{7,1},{8,10},{10,12},{12... | collective-permute-start | bytes 589832 | tf_op jit(solution)/shard_map/ppermute | solution.py:22

commit v2 on v1

v2 whole, which is shorter than its diff:
```python
import jax
import jax.numpy as jnp
from jax import lax
from jax.experimental import pallas as pl
from jax.experimental.pallas import tpu as pltpu
from jax.sharding import PartitionSpec as P

ORB = 13
GROUPS = 4
OFFS = 18
F32 = jnp.float32
BF16 = jnp.bfloat16
VMEM_LIMIT = 48 * 1024 * 1024


def swapped(value, axis):
    return lax.ppermute(value, axis, [(0, 1), (1, 0)])


def moved(value, axis, steps):
    count = lax.axis_size(axis)
    return lax.ppermute(value, axis, [(i, (i + steps) % count) for i in range(count)])


def with_halo(block, axis, dim):
    low = moved(block, axis, 1)
    high = moved(block, axis, -1)
    return jnp.concatenate([low, block, high], axis=dim)


def ghosts_of(sheets):
    framed = with_halo(with_halo(sheets, "gx", 1), "gy", 2)
    return framed.reshape(-1, sheets.shape[-1])


def deliver(outgoing):
    sheets = jnp.stack([outgoing[0], swapped(outgoing[1], "layer")])
    rows = [moved(sheets[:, i], "gx", i - 1) if i != 1 else sheets[:, i] for i in (2, 1, 0)]
    shifted = jnp.stack(rows, axis=1)
    cols = [moved(shifted[:, :, i], "gy", i - 1) if i != 1 else shifted[:, :, i] for i in (2, 1, 0)]
    return jnp.stack(cols, axis=2)


def dot(a, b):
    return jnp.dot(a, b, preferred_element_type=F32)


def dot_nt(a, b):
    return lax.dot_general(a, b, (((1,), (1,)), ((), ())), preferred_element_type=F32)


def one_hot(mask):
    return jnp.where(mask, 1.0, 0.0).astype(BF16)


def silu(v):
    return v * (0.5 * jnp.tanh(0.5 * v) + 0.5)


def rms_norm(v):
    return v * lax.rsqrt(jnp.mean(v * v, axis=-1, keepdims=True) + 1e-06)


def iota(shape, dim):
    return lax.broadcasted_iota(jnp.int32, shape, dim)


def fiota(shape, dim):
    return iota(shape, dim).astype(F32)


def call(body, outs, *args, scratch=(), us=1.0):
    return pl.pallas_call(
        body,
        out_shape=outs,
        scratch_shapes=list(scratch),
        compiler_params=pltpu.CompilerParams(vmem_limit_bytes=VMEM_LIMIT),
        cost_estimate=pl.CostEstimate(
            flops=int(us * 1.1e9), bytes_accessed=int(us * 3.6e6), transcendentals=0
        ),
    )(*args)


def as_row(tiles):
    return jnp.concatenate([tiles[i : i + 1] for i in range(tiles.shape[0])], axis=1)


def folded(row, count, fan):
    return jnp.concatenate([row[:, fan * n : fan * (n + 1)] for n in range(count)], axis=0)


def transposed(values):
    rows, cols = values.shape
    filler = jnp.zeros((rows, 128 - cols), F32)
    return jnp.transpose(jnp.concatenate([values, filler], axis=1))[:cols]


def order_body(send_ref, bond_ref, h_ref, out_ref, h_out_ref):
    owned = bond_ref.shape[0]
    cap = owned // OFFS
    bond = bond_ref[...]
    h_out_ref[...] = h_ref[...]
    send = as_row(send_ref[...])
    low = one_hot(iota((cap, owned), 0) == (send & 127))
    high = send >> 7

    def masked(o):
        mask = jnp.where(high == o, 1.0, 0.0)
        mask = jnp.broadcast_to(mask, (16, owned)).astype(BF16)
        return [low[16 * i : 16 * (i + 1)] * mask for i in range(cap // 16)]

    def step(i, carry):
        start = pl.multiple_of(2 * cap * i, 2 * cap)
        pick = jnp.concatenate(masked(2 * i) + masked(2 * i + 1), axis=0)
        out_ref[pl.ds(start, 2 * cap), :] = dot(pick, bond).astype(BF16)
        return carry

    lax.fori_loop(0, OFFS // 2, step, 0)


def slots_body(nb_ref, kind_ref, recv_ref, dist_ref, adj_ref, pack_ref, rank_ref):
    atoms, fan = pack_ref.shape
    flat = nb_ref[...] | (kind_ref[...] << 11) | (recv_ref[...] << 13)
    pack = folded(as_row(flat), atoms, fan)
    dist = folded(as_row(dist_ref[...]), atoms, fan)
    pack_ref[...] = pack
    peer = (pack & 63).astype(F32)
    off = ((pack & 2047) >> 6).astype(F32)
    scaled = dist * (1.0 / 7.0)
    env = 1.0 - scaled * scaled
    env = jnp.where(((pack >> 11) & 3) > 0, env * env, 0.0)
    lane = fiota((atoms, fan), 1)
    rank = jnp.zeros((atoms, fan), F32)
    for s in range(fan - 1):
        rank += jnp.where((off == off[:, s : s + 1]) & (lane > float(s)), 1.0, 0.0)
    rank_ref[...] = rank
    target = off * float(GROUPS) + rank
    wide = fiota((atoms, 128), 1)
    env_sorted = jnp.zeros((atoms, 128), F32)
    peer_sorted = jnp.zeros((atoms, 128), F32)
    for s in range(fan):
        here = target[:, s : s + 1] == wide
        env_sorted = jnp.where(here, env[:, s : s + 1], env_sorted)
        peer_sorted = jnp.where(here, peer[:, s : s + 1], peer_sorted)
    for m in range(OFFS // 2):
        tile = jnp.zeros((atoms, 128), F32)
        for u in range(2 * GROUPS):
            t = 2 * GROUPS * m + u
            column = peer_sorted[:, t : t + 1] + float(atoms * (u // GROUPS))
            tile += jnp.where(column == wide, env_sorted[:, t : t + 1], 0.0)
        adj_ref[:, 128 * m : 128 * (m + 1)] = tile.astype(BF16)


def write_hots(out_ref, index):
    cap = index.shape[0]
    lane = fiota((cap, 128), 1)
    for o in range(OFFS):
        hot = (lane == index[:, o : o + 1]) | (lane == index[:, 32 + o : 33 + o] + 64.0)
        out_ref[cap * o : cap * (o + 1), :] = one_hot(hot)


def pairs_body(
    send_ref, own_ref, nb_ref, kind_ref, recv_ref, pack_ref, hot_own_ref, hot_mir_ref, place_ref
):
    atoms, fan = pack_ref.shape
    cap = hot_own_ref.shape[0] // OFFS
    send = as_row(send_ref[...])
    own = as_row(own_ref[...]).astype(F32)
    owned = send.shape[1]
    atom_r = jnp.floor((own + 0.5) * (1.0 / fan))
    slot_r = own - fan * atom_r
    off_r = (send >> 7).astype(F32)
    pos_r = (send & 127).astype(F32)
    peer = (pack_ref[...] & 63).astype(F32)
    at_atom = fiota((atoms, owned), 0) == atom_r
    at_slot = fiota((fan, owned), 0) == slot_r
    place_ref[...] = dot_nt(
        jnp.where(at_atom, pos_r + 1.0, 0.0).astype(BF16), one_hot(at_slot)
    )
    peer_all = dot(transposed(peer).astype(BF16), one_hot(at_atom))
    peer_r = jnp.sum(jnp.where(at_slot, peer_all, 0.0), axis=0, keepdims=True)
    at_off = fiota((32, owned), 0) == off_r
    values = jnp.concatenate(
        [jnp.where(at_off, atom_r, 0.0), jnp.where(at_off, peer_r, 0.0)], axis=0
    ).astype(BF16)
    write_hots(hot_own_ref, dot_nt(one_hot(fiota((cap, owned), 0) == pos_r), values))

    ids = as_row(jnp.where(kind_ref[...] == 2, nb_ref[...], 64 * 31))
    slots = ids.shape[1]
    atom_s = jnp.floor((fiota((1, slots), 1) + 0.5) * (1.0 / fan))
    peer_s = (ids & 63).astype(F32)
    off_s = (ids >> 6).astype(F32)
    pos_s = as_row(recv_ref[...] & 127).astype(F32)
    at_off = fiota((32, slots), 0) == off_s
    values = jnp.concatenate(
        [jnp.where(at_off, atom_s, 0.0), jnp.where(at_off, peer_s, 0.0)], axis=0
    ).astype(BF16)
    write_hots(hot_mir_ref, dot_nt(one_hot(fiota((cap, slots), 0) == pos_s), values))


def places_body(pack_ref, rank_ref, place_ref, wb_ref, pick_ref, perm_ref, wcat_ref):
    atoms, fan = pack_ref.shape
    rows = pick_ref.shape[0] // OFFS
    cap = rows // 2
    pack = pack_ref[...]
    off = ((pack & 2047) >> 6).astype(F32)
    kind = (pack >> 11) & 3
    pos_in = ((pack >> 13) & 127).astype(F32)
    rank = rank_ref[...]
    src = jnp.where(kind == 1, place_ref[...], jnp.where(kind == 2, pos_in + (cap + 1.0), 0.0))
    target = off * float(GROUPS) + rank
    wide = fiota((atoms, 128), 1)
    sorted_src = jnp.zeros((atoms, 128), F32)
    for s in range(fan):
        sorted_src = jnp.where(target[:, s : s + 1] == wide, src[:, s : s + 1], sorted_src)
    row = iota((rows, atoms), 0)
    spread = one_hot((row >> 2) == iota((rows, atoms), 1))
    spread = dot(spread, sorted_src.astype(BF16))
    keep = (iota((rows, 128), 1) & 3) == (iota((rows, 128), 0) & 3)
    fold = one_hot((iota((128, 32), 0) >> 2) == iota((128, 32), 1))
    index = dot(jnp.where(keep, spread, 0.0).astype(BF16), fold) - 1.0
    lane = fiota((rows, rows), 1)
    for o in range(OFFS):
        pick_ref[rows * o : rows * (o + 1), :] = one_hot(index[:, o : o + 1] == lane)

    member = (iota((atoms, fan), 0) & 3).astype(F32)
    spot = transposed(off * 16.0 + member * 4.0 + rank)
    lane = fiota((fan, 4 * fan), 1)
    for q in range(atoms // 4):
        perm_ref[4 * fan * q : 4 * fan * (q + 1), :] = jnp.concatenate(
            [jnp.where(spot[:, 4 * q + i : 4 * q + i + 1] == lane, 1.0, 0.0) for i in range(4)],
            axis=0,
        ).astype(BF16)

    block = wb_ref.shape[0]
    row = fiota((block, block), 0)
    col = fiota((block, block), 1)
    major = jnp.floor((row + 0.5) * (1.0 / ORB))
    wcat_ref[:, :128] = wb_ref[...]
    wcat_ref[:, 128:] = dot(
        one_hot((row - ORB * major) * ORB + major == col), wb_ref[...]
    ).astype(BF16)


def node_body(layer):
    def body(adj_ref, other_ref, ghost_ref, wm_ref, wu_ref, gain_ref, out_ref):
        ghosts = ghost_ref.shape[0]
        half = ghosts // 2
        atoms = ghosts // OFFS
        mixed = dot(adj_ref[...], ghost_ref[...])
        other = dot(other_ref[:, :half], ghost_ref[half:, :])
        other += dot(other_ref[:, half:], ghost_ref[:half, :])
        mixed = jnp.concatenate([mixed, other], axis=0).astype(BF16)
        hidden = jnp.concatenate(
            [ghost_ref[atoms * 4 : atoms * 5, :], ghost_ref[atoms * 13 : atoms * 14, :]], axis=0
        )
        summed = (dot(mixed, wm_ref[layer]) * 0.125).astype(BF16)
        updated = hidden.astype(F32) + silu(dot(summed, wu_ref[layer]))
        out_ref[...] = (rms_norm(updated) * gain_ref[layer : layer + 1, :]).astype(BF16)

    return body


CHUNK = 6


def edge_all(e_ref, hot_ref, ghost_ref, w_local, w_ghost, w_in, w_out, table, out_ref):
    atoms = ghost_ref.shape[0] // OFFS
    cap = e_ref.shape[0] // OFFS
    local = dot(ghost_ref[atoms * 4 : atoms * 5, :], w_local).astype(BF16)
    distant = dot(ghost_ref[...], w_ghost).astype(BF16)
    blank = jnp.zeros((atoms, 128), BF16)
    for o in range(OFFS):
        base = 2 * atoms * o
        table[base : base + atoms, :128] = local
        table[base : base + atoms, 128:] = blank
        table[base + atoms : base + 2 * atoms, :128] = blank
        table[base + atoms : base + 2 * atoms, 128:] = distant[atoms * o : atoms * (o + 1)]
    for c in range(OFFS // CHUNK):
        span = slice(CHUNK * cap * c, CHUNK * cap * (c + 1))
        chosen = jnp.concatenate(
            [
                dot(
                    hot_ref[cap * o : cap * (o + 1), :],
                    table[2 * atoms * o : 2 * atoms * (o + 1), :],
                )
                for o in range(CHUNK * c, CHUNK * (c + 1))
            ],
            axis=0,
        )
        state = e_ref[span, :]
        gate = silu(dot(state, w_in) * chosen[:, :128] * chosen[:, 128:]).astype(BF16)
        out_ref[span, :] = rms_norm(state.astype(F32) + dot(gate, w_out)).astype(BF16)


def edge_body(layer):
    def body(e_ref, hot_ref, ghost_ref, wl_ref, wg_ref, wi_ref, wo_ref, out_ref, table):
        edge_all(
            e_ref, hot_ref, ghost_ref, wl_ref[layer], wg_ref[layer], wi_ref[layer], wo_ref[layer],
            table, out_ref,
        )

    return body


def final_body(layer):
    def body(
        own_ref, mir_ref, ho_ref, hm_ref, ghost_ref, wl_ref, wr_ref, wi_ref, wo_ref,
        pick_ref, perm_ref, wcat_ref, out_ref, table_own, table_mir, e_own, e_mir, ranked, rows,
    ):
        atoms = ghost_ref.shape[0] // OFFS
        cap = own_ref.shape[0] // OFFS
        fan = out_ref.shape[1] // atoms
        w_in, w_out = wi_ref[layer], wo_ref[layer]
        edge_all(
            own_ref, ho_ref, ghost_ref, wl_ref[layer], wr_ref[layer], w_in, w_out, table_own, e_own
        )
        edge_all(
            mir_ref, hm_ref, ghost_ref, wr_ref[layer], wl_ref[layer], w_in, w_out, table_mir, e_mir
        )
        for o in range(OFFS):
            span = slice(cap * o, cap * (o + 1))
            wide = slice(2 * cap * o, 2 * cap * (o + 1))
            ranked[wide, :128] = dot(pick_ref[wide, :cap], e_own[span, :]).astype(BF16)
            ranked[wide, 128:] = dot(pick_ref[wide, cap:], e_mir[span, :]).astype(BF16)
        for q in range(atoms // 4):
            span = slice(4 * fan * q, 4 * fan * (q + 1))
            tiles = jnp.concatenate(
                [
                    ranked[2 * cap * o + 16 * q : 2 * cap * o + 16 * (q + 1), :]
                    for o in range(OFFS)
                ],
                axis=0,
            )
            rows[span, :] = dot(perm_ref[span, :], tiles).astype(BF16)
        step = 16 * fan
        for g in range(atoms // 16):
            out_ref[:, step * g : step * (g + 1)] = dot_nt(
                wcat_ref[...], rows[step * g : step * (g + 1), :]
            ).astype(BF16)

    return body


def shards(
    atom_feats, bond_embed, pair_dist, neighbours, slot_kind, own_rows, send_pos, recv_pos,
    w_left, w_right, w_edge_in, w_edge_out, w_msg, w_upd, node_gain, w_block,
):
    atoms, channels = atom_feats.shape
    slots = neighbours.shape[0]
    fan = slots // atoms
    owned = own_rows.shape[0]
    cap = owned // OFFS
    block = w_block.shape[1]
    ghosts = OFFS * atoms

    def array(*shape, dtype=BF16):
        return jax.ShapeDtypeStruct(shape, dtype)

    def tiles(values):
        return values.reshape(-1, 128)

    send, own = tiles(send_pos), tiles(own_rows)
    nb, kind, recv, dist = map(tiles, (neighbours, slot_kind, recv_pos, pair_dist))
    opposite = swapped(atom_feats, "layer")
    ordered, hidden = call(
        order_body,
        (array(owned, channels), array(atoms, channels)),
        send, bond_embed, atom_feats,
        us=3.5,
    )
    adjacency, pack, rank = call(
        slots_body,
        (array(atoms, ghosts), array(atoms, fan, dtype=jnp.int32), array(atoms, fan, dtype=F32)),
        nb, kind, recv, dist,
        us=2.0,
    )
    hot_own, hot_mir, place = call(
        pairs_body,
        (array(owned, 128), array(owned, 128), array(atoms, fan, dtype=F32)),
        send, own, nb, kind, recv, pack,
        us=2.5,
    )
    pick, perm, w_cat = call(
        places_body,
        (array(2 * owned, 2 * cap), array(slots, 4 * fan), array(block, 2 * channels)),
        pack, rank, place, w_block.T,
        us=2.5,
    )
    mirror = deliver(ordered.reshape(2, 3, 3, cap, channels)).reshape(owned, channels)
    other = swapped(adjacency, "layer")
    sheets = jnp.stack([hidden, opposite])
    table = pltpu.VMEM((2 * ghosts, 2 * channels), BF16)
    state = pltpu.VMEM((owned, channels), BF16)
    for layer in range(2):
        ghost = ghosts_of(sheets.reshape(2, 1, 1, atoms, channels))
        sheets = call(
            node_body(layer),
            array(2 * atoms, channels),
            adjacency, other, ghost, w_msg, w_upd, node_gain,
            us=0.6,
        )
        ordered = call(
            edge_body(layer),
            array(owned, channels),
            ordered, hot_own, ghost, w_left, w_right, w_edge_in, w_edge_out,
            scratch=[table],
            us=2.5,
        )
        mirror = call(
            edge_body(layer),
            array(owned, channels),
            mirror, hot_mir, ghost, w_right, w_left, w_edge_in, w_edge_out,
            scratch=[table],
            us=2.5,
        )
    ghost = ghosts_of(sheets.reshape(2, 1, 1, atoms, channels))
    wide = pltpu.VMEM((slots, 2 * channels), BF16)
    return call(
        final_body(2),
        array(block, slots),
        ordered, mirror, hot_own, hot_mir, ghost, w_left, w_right, w_edge_in, w_edge_out,
        pick, perm, w_cat,
        scratch=[table, table, state, state, wide, wide],
        us=8.0,
    )


def solution(mesh):
    axes = ("gx", "gy", "layer")
    rows = P(axes, None)
    flat = P(axes)
    placed = (rows, rows) + (flat,) * 6 + (P(),) * 8
    return jax.shard_map(
        shards,
        mesh=mesh,
        in_specs=placed,
        out_specs=P(None, axes),
        check_vma=False,
    )
```

time: 86 us -> 73.5 us (0.85)
  Pallas kernels: 37.2 us -> 29.1 us
  waiting for transfers between devices: 23.8 us -> 17.8 us
  starting transfers between devices: 19.1 us -> 21.1 us
  other arithmetic: 1.83 us -> 0.34 us
  local copies, waits for them, and re-layouts: 3.41 us -> 4.39 us
    pallas_call x9 -> x11, Pallas kernels: 37.2 us -> 29.1 us  [call(): pl.pallas_call(body, out_shape=outs, scratch_shapes=list(scratch), compil...]
    unnamed x19 -> x34, local copies, waits for them, and re-layouts: 0.93 us -> 4.28 us
    ppermute x16, starting transfers between devices: 13.3 us -> 16.5 us  [moved(): lax.ppermute(value, axis, [(i, (i + steps) % count) for i in range(count)])]
    ppermute x4 -> x3, waiting for transfers between devices: 3.03 us -> 0.01 us  [swapped(): return lax.ppermute(value, axis, [(0, 1), (1, 0)])]
    ppermute x16, waiting for transfers between devices: 20.7 us -> 17.8 us  [moved(): lax.ppermute(value, axis, [(i, (i + steps) % count) for i in range(count)])]
    reshape x5 -> x0, local copies, waits for them, and re-layouts: 2.33 us -> none  [the longest x1 0.81 us: shards(): pair_dist.reshape(atoms, fan)]
    ppermute x4 -> x3, starting transfers between devices: 5.78 us -> 4.56 us  [swapped(): return lax.ppermute(value, axis, [(0, 1), (1, 0)])]
  transfers between devices with their start and end apart: 20 -> 19, of which waited for: 11 -> 8; matrix products, arithmetic and copies ran while one was open for 5% -> 1% of each run, Pallas kernels for 19% -> 25%
where the time goes in v2:
time: 73.5 us; the launch traced here: 73.1 us
  Pallas kernels  29.1 us (40%)
  starting transfers between devices  21.1 us (29%)
  waiting for transfers between devices  17.8 us (24%)
  local copies, waits for them, and re-layouts  4.39 us (6%)
    pallas_call x11, Pallas kernels, call(): pl.pallas_call(body, out_shape=outs, scratch_shapes=list(scratch), compil...  29.1 us
    ppermute x16, waiting for transfers between devices, moved(): lax.ppermute(value, axis, [(i, (i + steps) % count) for i in range(count)])  17.8 us
    ppermute x16, starting transfers between devices, moved(): lax.ppermute(value, axis, [(i, (i + steps) % count) for i in range(count)])  16.5 us
    ppermute x3, starting transfers between devices, swapped(): return lax.ppermute(value, axis, [(0, 1), (1, 0)])  4.56 us
    unnamed x34, local copies, waits for them, and re-layouts  4.28 us
  transfers between devices with their start and end apart: 19, of which 8 were waited for; matrix products, arithmetic and copies ran while one was open for 1% of the time, Pallas kernels for 25%

profile of v2, /device:TPU:0, one launch (start us, length us, event | category | flops | bytes accessed | tf_op | source)
XLA Modules:
  0.0 73.1 jit_solution(18165113980785360446)
XLA Ops:
  0.0 3.0 %collective-permute-start = (bf16[64,128]{1,0:T(8,128)(2,1)}, bf16[64,128]{1,0:T(8,128)(2,1)S(1)}, u32[]{:S(2)}, u32[]{:S(2)}) collective-permute-start(bf16[64,128]{1,0:T(8,128)(2,1)} %h_ref.1), channel_id=1, source_target_pairs={{0,1},{1,0},{2,3},{3,2},{4,5},{5,4},{6,7},{7,6},{8,9},{9,8},{10,11... | collective-permute-start | bytes 49160 | tf_op jit(solution)/shard_map/ppermute | solution.py:17
  3.0 1.1 %copy-done = bf16[2304,128]{1,0:T(8,128)(2,1)S(1)} copy-done((bf16[2304,128]{1,0:T(8,128)(2,1)S(1)}, bf16[2304,128]{1,0:T(8,128)(2,1)}, u32[]{:S(2)}) %copy-start) | copy-done | bytes 589848
  4.0 0.7 copy-done.12
  4.8 0.7 copy-done.13
  5.5 4.5 %shard_map.154 = (bf16[2304,128]{1,0:T(8,128)(2,1)S(1)}, bf16[64,128]{1,0:T(8,128)(2,1)S(1)}) custom-call(s32[18,128]{1,0:T(8,128)S(1)} %bitcast.71, bf16[2304,128]{1,0:T(8,128)(2,1)S(1)} %copy-done, bf16[64,128]{1,0:T(8,128)(2,1)S(1)} %copy-done.12), custom_call_target="tpu_custom_call" | custom-call | flops 3849999872 | bytes 12600000 | tf_op jit(solution)/shard_map/pallas_call | solution.py:73
  10.0 0.0 collective-permute-done
  10.0 3.6 %collective-permute-start.2 = (bf16[2,1,1,64,128]{4,3,0,2,1:T(8,128)(2,1)S(1)}, bf16[2,1,1,64,128]{4,3,0,2,1:T(8,128)(2,1)S(1)}, u32[]{:S(2)}, u32[]{:S(2)}) collective-permute-start(bf16[2,1,1,64,128]{4,3,0,2,1:T(8,128)(2,1)S(1)} %maximum_bitcast_fusion), channel_id=1, source_target_pairs={{0,24},{8,0},{16,8},{24,16},{1,25},{9,1},{17,9},{25,17},{2,26},{10... | collective-permute-start | bytes 98312 | tf_op jit(solution)/shard_map/ppermute | solution.py:22
  13.6 0.0 collective-permute-start.1
  13.7 0.0 copy-done.8
  13.7 0.0 copy-done.9
  13.7 0.0 copy-done.10
  13.7 0.0 copy-done.11
  13.7 4.5 %shard_map.155 = (bf16[64,1152]{1,0:T(8,128)(2,1)S(1)}, s32[64,72]{1,0:T(8,128)S(1)}, f32[64,72]{1,0:T(8,128)S(1)}) custom-call(s32[36,128]{1,0:T(8,128)S(1)} %bitcast.65, s32[36,128]{1,0:T(8,128)S(1)} %bitcast.67, s32[36,128]{1,0:T(8,128)S(1)} %bitcast.69, f32[36,128]{1,0:T(8,128)S(1)} %bitcast.64), custom_call_target="tpu_custom_call" | custom-call | flops 2200000000 | bytes 7200000 | tf_op jit(solution)/shard_map/pallas_call | solution.py:73
  18.2 0.0 copy-start.5
  18.2 0.0 copy-start.6
  18.2 0.0 copy-start.15
  18.2 0.6 collective-permute-start.5
  18.8 0.0 collective-permute-done.2
  18.8 0.6 collective-permute-done.1
  19.4 0.1 collective-permute-start.4
  19.4 0.5 collective-permute-start.3
  20.0 1.0 %collective-permute-start.10 = (bf16[3,3,128,128]{3,2,1,0:T(8,128)(2,1)S(1)}, bf16[3,3,128,128]{3,2,1,0:T(8,128)(2,1)S(1)}, u32[]{:S(2)}, u32[]{:S(2)}) collective-permute-start(bf16[3,3,128,128]{3,2,1,0:T(8,128)(2,1)S(1)} %bitcast.76), channel_id=1, source_target_pairs={{0,1},{1,0},{2,3},{3,2},{4,5},{5,4},{6,7},{7,6},{8,9},{9,8},{10,11... | collective-permute-start | bytes 884744 | tf_op jit(solution)/shard_map/ppermute | solution.py:17
  21.0 0.6 collective-permute-done.4
  21.6 2.9 %collective-permute-done.3 = bf16[2,3,1,64,128]{4,3,0,2,1:T(8,128)(2,1)S(1)} collective-permute-done((bf16[2,3,1,64,128]{4,3,0,2,1:T(8,128)(2,1)S(1)}, bf16[2,3,1,64,128]{4,3,0,2,1:T(8,128)(2,1)S(1)}, u32[]{:S(2)}, u32[]{:S(2)}) %collective-permute-start.3) | collective-permute-done | bytes 98336 | tf_op jit(solution)/shard_map/ppermute | solution.py:22
  24.7 0.0 collective-permute-done.5.other_ref
  24.7 0.0 copy-done.5
  24.7 0.6 shard_map.158
  25.3 3.3 %collective-permute-start.7 = (bf16[2,1,1,64,128]{4,3,2,1,0:T(8,128)(2,1)S(1)}, bf16[2,1,1,64,128]{4,3,2,1,0:T(8,128)(2,1)S(1)}, u32[]{:S(2)}, u32[]{:S(2)}) collective-permute-start(bf16[2,1,1,64,128]{4,3,2,1,0:T(8,128)(2,1)S(1)} %bitcast.58), channel_id=1, source_target_pairs={{0,24},{8,0},{16,8},{24,16},{1,25},{9,1},{17,9},{25,17},{2,26},{10... | collective-permute-start | bytes 98312 | tf_op jit(solution)/shard_map/ppermute | solution.py:22
  28.6 0.0 collective-permute-start.6
  28.6 2.3 %shard_map.156 = (bf16[2304,128]{1,0:T(8,128)(2,1)S(1)}, bf16[2304,128]{1,0:T(8,128)(2,1)S(1)}, f32[64,72]{1,0:T(8,128)S(1)}) custom-call(s32[18,128]{1,0:T(8,128)S(1)} %bitcast.72, s32[18,128]{1,0:T(8,128)S(1)} %bitcast.73, s32[36,128]{1,0:T(8,128)S(1)} %bitcast.66, s32[36,128]{1,0:T(8,128)S(1)} %bitcast.68, s32[36,128]{1,0:T(8,128)S(1)} %bitcast.70, ...), custom_call_target="tpu_custom_call" | custom-call | flops 2750000128 | bytes 9000000 | tf_op jit(solution)/shard_map/pallas_call | solution.py:73
  30.9 0.0 collective-permute-done.7
  30.9 3.4 %collective-permute-done.6 = bf16[2,1,1,64,128]{4,3,2,1,0:T(8,128)(2,1)S(1)} collective-permute-done((bf16[2,1,1,64,128]{4,3,2,1,0:T(8,128)(2,1)S(1)}, bf16[2,1,1,64,128]{4,3,2,1,0:T(8,128)(2,1)S(1)}, u32[]{:S(2)}, u32[]{:S(2)}) %collective-permute-start.6) | collective-permute-done | bytes 32800 | tf_op jit(solution)/shard_map/ppermute | solution.py:22
  34.3 0.1 collective-permute-start.9
  34.4 0.5 collective-permute-start.8
  34.9 2.8 %shard_map.163 = (bf16[4608,256]{1,0:T(8,128)(2,1)S(1)}, bf16[4608,288]{1,0:T(8,128)(2,1)S(1)}, bf16[169,256]{1,0:T(8,128)(2,1)S(1)}) custom-call(s32[64,72]{1,0:T(8,128)S(1)} %get-tuple-element.17.pack_ref, f32[64,72]{1,0:T(8,128)S(1)} %get-tuple-element.22.rank_ref, f32[64,72]{1,0:T(8,128)S(1)} %get-tuple-element.23.place_ref, bf16[169,128]{1,0:T(8,128)(2,1)S(1)} %bitcast.63), custom_call_target="tpu_custom_call" | custom-call | flops 2750000128 | bytes 9000000 | tf_op jit(solution)/shard_map/pallas_call | solution.py:73
  37.7 1.7 %copy-done.16 = bf16[4608,288]{1,0:T(8,128)(2,1)} copy-done((bf16[4608,288]{1,0:T(8,128)(2,1)}, bf16[4608,288]{1,0:T(8,128)(2,1)S(1)}, u32[]{:S(2)}) %copy-start.16) | copy-done | bytes 2654232
  39.5 0.0 collective-permute-done.9
  39.5 0.2 collective-permute-done.8
  39.7 0.6 shard_map.162
  40.4 0.5 collective-permute-start.16
  40.8 1.6 %collective-permute-start.15 = (bf16[2,1,1,64,128]{4,3,2,1,0:T(8,128)(2,1)S(1)}, bf16[2,1,1,64,128]{4,3,2,1,0:T(8,128)(2,1)S(1)}, u32[]{:S(2)}, u32[]{:S(2)}) collective-permute-start(bf16[2,1,1,64,128]{4,3,2,1,0:T(8,128)(2,1)S(1)} %bitcast.55), channel_id=1, source_target_pairs={{0,8},{8,16},{16,24},{24,0},{1,9},{9,17},{17,25},{25,1},{2,10},{10... | collective-permute-start | bytes 98312 | tf_op jit(solution)/shard_map/ppermute | solution.py:22
  42.4 0.0 collective-permute-done.10
  42.4 0.1 fusion.3
  42.5 0.2 collective-permute-start.11
  42.8 3.8 %collective-permute-start.12 = (bf16[2,3,128,128]{3,2,0,1:T(8,128)(2,1)S(1)}, bf16[2,3,128,128]{3,2,0,1:T(8,128)(2,1)S(1)}, u32[]{:S(2)}, u32[]{:S(2)}) collective-permute-start(bf16[2,3,128,128]{3,2,0,1:T(8,128)(2,1)S(1)} %get-tuple-element.31), channel_id=1, source_target_pairs={{0,24},{8,0},{16,8},{24,16},{1,25},{9,1},{17,9},{25,17},{2,26},{10... | collective-permute-start | bytes 589832 | tf_op jit(solution)/shard_map/ppermute | solution.py:22
  46.6 1.4 %shard_map.157.e_ref = bf16[2304,128]{1,0:T(8,128)(2,1)S(1)} custom-call(bf16[2304,128]{1,0:T(8,128)(2,1)S(1)} %get-tuple-element.16.e_ref, bf16[2304,128]{1,0:T(8,128)(2,1)S(1)} %get-tuple-element.18.hot_ref.ho_ref, bf16[1152,128]{1,0:T(8,128)(2,1)S(1)} %bitcast.48, bf16[3,128,128]{2,1,0:T(8,128)(2,1)S(1)} %copy-done.1, bf16[3,128,128]{2,1,0:T(8,128)(2,1)S(1)} %copy-done.2, ...), custom_call_target="tpu_custom_call" | custom-call | flops 2750000128 | bytes 9000000 | tf_op jit(solution)/shard_map/pallas_call | solution.py:73
  48.0 0.0 collective-permute-done.16
  48.0 0.0 collective-permute-done.15
  48.0 0.4 collective-permute-start.18
  48.4 0.2 collective-permute-start.17
  48.6 3.9 %collective-permute-done.11 = bf16[2,3,128,128]{3,2,0,1:T(8,128)(2,1)S(1)} collective-permute-done((bf16[2,3,128,128]{3,2,0,1:T(8,128)(2,1)S(1)}, bf16[2,3,128,128]{3,2,0,1:T(8,128)(2,1)S(1)}, u32[]{:S(2)}, u32[]{:S(2)}) %collective-permute-start.11) | collective-permute-done | bytes 196640 | tf_op jit(solution)/shard_map/ppermute | solution.py:22
  52.5 2.9 %collective-permute-done.12 = bf16[2,3,128,128]{3,2,0,1:T(8,128)(2,1)S(1)} collective-permute-done((bf16[2,3,128,128]{3,2,0,1:T(8,128)(2,1)S(1)}, bf16[2,3,128,128]{3,2,0,1:T(8,128)(2,1)S(1)}, u32[]{:S(2)}, u32[]{:S(2)}) %collective-permute-start.12) | collective-permute-done | bytes 196640 | tf_op jit(solution)/shard_map/ppermute | solution.py:22
  55.3 0.1 pad_maximum_fusion
  55.4 0.2 collective-permute-start.13
  55.6 1.6 %collective-permute-start.14 = (bf16[2,3,128,128]{3,2,1,0:T(8,128)(2,1)S(1)}, bf16[2,3,128,128]{3,2,1,0:T(8,128)(2,1)S(1)}, u32[]{:S(2)}, u32[]{:S(2)}) collective-permute-start(bf16[2,3,128,128]{3,2,1,0:T(8,128)(2,1)S(1)} %get-tuple-element.28), channel_id=1, source_target_pairs={{0,6},{2,0},{4,2},{6,4},{1,7},{3,1},{5,3},{7,5},{8,14},{10,8},{12,... | collective-permute-start | bytes 589832 | tf_op jit(solution)/shard_map/ppermute | solution.py:22
  57.2 1.4 %shard_map.159.own_ref = bf16[2304,128]{1,0:T(8,128)(2,1)S(1)} custom-call(bf16[2304,128]{1,0:T(8,128)(2,1)S(1)} %shard_map.157.e_ref, bf16[2304,128]{1,0:T(8,128)(2,1)S(1)} %get-tuple-element.18.hot_ref.ho_ref, bf16[1152,128]{1,0:T(8,128)(2,1)S(1)} %bitcast.51, bf16[3,128,128]{2,1,0:T(8,128)(2,1)S(1)} %copy-done.1, bf16[3,128,128]{2,1,0:T(8,128)(2,1)S(1)} %copy-done.2, ...), custom_call_target="tpu_custom_call" | custom-call | flops 2750000128 | bytes 9000000 | tf_op jit(solution)/shard_map/pallas_call | solution.py:73
  58.6 0.0 collective-permute-done.18
  58.6 0.0 collective-permute-done.17
  58.7 3.2 %collective-permute-done.13 = bf16[2,3,128,128]{3,2,1,0:T(8,128)(2,1)S(1)} collective-permute-done((bf16[2,3,128,128]{3,2,1,0:T(8,128)(2,1)S(1)}, bf16[2,3,128,128]{3,2,1,0:T(8,128)(2,1)S(1)}, u32[]{:S(2)}, u32[]{:S(2)}) %collective-permute-start.13) | collective-permute-done | bytes 196640 | tf_op jit(solution)/shard_map/ppermute | solution.py:22
  61.9 0.0 collective-permute-done.14
  61.9 0.1 pad_maximum_fusion.1
  62.0 1.4 %shard_map.160.e_ref = bf16[2304,128]{1,0:T(8,128)(2,1)S(1)} custom-call(bf16[2304,128]{1,0:T(8,128)(2,1)S(1)} %bitcast.46, bf16[2304,128]{1,0:T(8,128)(2,1)S(1)} %get-tuple-element.21.hot_ref.hm_ref, bf16[1152,128]{1,0:T(8,128)(2,1)S(1)} %bitcast.49, bf16[3,128,128]{2,1,0:T(8,128)(2,1)S(1)} %copy-done.2, bf16[3,128,128]{2,1,0:T(8,128)(2,1)S(1)} %copy-done.1, ...), custom_call_target="tpu_custom_call" | custom-call | flops 2750000128 | bytes 9000000 | tf_op jit(solution)/shard_map/pallas_call | solution.py:73
  63.4 1.4 %shard_map.161.mir_ref = bf16[2304,128]{1,0:T(8,128)(2,1)S(1)} custom-call(bf16[2304,128]{1,0:T(8,128)(2,1)S(1)} %shard_map.160.e_ref, bf16[2304,128]{1,0:T(8,128)(2,1)S(1)} %get-tuple-element.21.hot_ref.hm_ref, bf16[1152,128]{1,0:T(8,128)(2,1)S(1)} %bitcast.52, bf16[3,128,128]{2,1,0:T(8,128)(2,1)S(1)} %copy-done.2, bf16[3,128,128]{2,1,0:T(8,128)(2,1)S(1)} %copy-done.1, ...), custom_call_target="tpu_custom_call" | custom-call | flops 2750000128 | bytes 9000000 | tf_op jit(solution)/shard_map/pallas_call | solution.py:73
  64.8 8.3 %shard_map.164 = bf16[169,4608]{1,0:T(8,128)(2,1)} custom-call(bf16[2304,128]{1,0:T(8,128)(2,1)S(1)} %shard_map.159.own_ref, bf16[2304,128]{1,0:T(8,128)(2,1)S(1)} %shard_map.161.mir_ref, bf16[2304,128]{1,0:T(8,128)(2,1)S(1)} %get-tuple-element.18.hot_ref.ho_ref, bf16[2304,128]{1,0:T(8,128)(2,1)S(1)} %get-tuple-element.21.hot_ref.hm_ref, ...), custom_call_target="tpu_custom_call" | custom-call | flops 8800000000 | bytes 28800000 | tf_op jit(solution)/shard_map/pallas_call | solution.py:73
  (32 shorter events, 0.3 us)
Async XLA Ops:
  0.0 10.0 %collective-permute-start = (bf16[64,128]{1,0:T(8,128)(2,1)}, bf16[64,128]{1,0:T(8,128)(2,1)S(1)}, u32[]{:S(2)}, u32[]{:S(2)}) collective-permute-start(bf16[64,128]{1,0:T(8,128)(2,1)} %h_ref.1), channel_id=1, source_target_pairs={{0,1},{1,0},{2,3},{3,2},{4,5},{5,4},{6,7},{7,6},{8,9},{9,8},{10,11... | collective-permute-start | bytes 49160 | tf_op jit(solution)/shard_map/ppermute | solution.py:17
  3.0 1.1 %copy-start = (bf16[2304,128]{1,0:T(8,128)(2,1)S(1)}, bf16[2304,128]{1,0:T(8,128)(2,1)}, u32[]{:S(2)}) copy-start(bf16[2304,128]{1,0:T(8,128)(2,1)} %bond_ref.1) | copy-start | bytes 1769476
  4.0 0.7 copy-start.12
  4.8 0.7 copy-start.13
  5.5 8.2 %copy-start.8 = (f32[4608]{0:T(1024)S(1)}, f32[4608]{0:T(1024)}, u32[]{:S(2)}) copy-start(f32[4608]{0:T(1024)} %param.18) | copy-start | bytes 55300
  5.5 8.2 %copy-start.9 = (s32[4608]{0:T(1024)S(1)}, s32[4608]{0:T(1024)}, u32[]{:S(2)}) copy-start(s32[4608]{0:T(1024)} %param.19) | copy-start | bytes 55300
  5.5 8.2 %copy-start.10 = (s32[4608]{0:T(1024)S(1)}, s32[4608]{0:T(1024)}, u32[]{:S(2)}) copy-start(s32[4608]{0:T(1024)} %param.20) | copy-start | bytes 55300
  5.5 8.2 %copy-start.11 = (s32[4608]{0:T(1024)S(1)}, s32[4608]{0:T(1024)}, u32[]{:S(2)}) copy-start(s32[4608]{0:T(1024)} %param.23) | copy-start | bytes 55300
  10.0 8.8 %collective-permute-start.2 = (bf16[2,1,1,64,128]{4,3,0,2,1:T(8,128)(2,1)S(1)}, bf16[2,1,1,64,128]{4,3,0,2,1:T(8,128)(2,1)S(1)}, u32[]{:S(2)}, u32[]{:S(2)}) collective-permute-start(bf16[2,1,1,64,128]{4,3,0,2,1:T(8,128)(2,1)S(1)} %maximum_bitcast_fusion), channel_id=1, source_target_pairs={{0,24},{8,0},{16,8},{24,16},{1,25},{9,1},{17,9},{25,17},{2,26},{10... | collective-permute-start | bytes 98312 | tf_op jit(solution)/shard_map/ppermute | solution.py:22
  13.6 5.7 %collective-permute-start.1 = (bf16[2,1,1,64,128]{4,3,0,2,1:T(8,128)(2,1)S(1)}, bf16[2,1,1,64,128]{4,3,0,2,1:T(8,128)(2,1)S(1)}, u32[]{:S(2)}, u32[]{:S(2)}) collective-permute-start(bf16[2,1,1,64,128]{4,3,0,2,1:T(8,128)(2,1)S(1)} %maximum_bitcast_fusion), channel_id=1, source_target_pairs={{0,8},{8,16},{16,24},{24,0},{1,9},{9,17},{17,25},{25,1},{2,10},{10... | collective-permute-start | bytes 98312 | tf_op jit(solution)/shard_map/ppermute | solution.py:22
  18.2 6.5 %copy-start.5 = (bf16[2,128,128]{2,1,0:T(8,128)(2,1)S(1)}, bf16[2,128,128]{2,1,0:T(8,128)(2,1)}, u32[]{:S(2)}) copy-start(bf16[2,128,128]{2,1,0:T(8,128)(2,1)} %wm_ref.3) | copy-start | bytes 196612
  18.2 6.5 %copy-start.6 = (bf16[2,128,128]{2,1,0:T(8,128)(2,1)S(1)}, bf16[2,128,128]{2,1,0:T(8,128)(2,1)}, u32[]{:S(2)}) copy-start(bf16[2,128,128]{2,1,0:T(8,128)(2,1)} %wu_ref.3) | copy-start | bytes 196612
  18.2 6.5 %copy-start.15 = (f32[2,128]{1,0:T(2,128)S(1)}, f32[2,128]{1,0:T(2,128)}, u32[]{:S(2)}) copy-start(f32[2,128]{1,0:T(2,128)} %gain_ref.3) | copy-start | bytes 3076
  18.2 6.4 %collective-permute-start.5 = (bf16[64,1152]{1,0:T(8,128)(2,1)S(1)}, bf16[64,1152]{1,0:T(8,128)(2,1)S(1)}, u32[]{:S(2)}, u32[]{:S(2)}) collective-permute-start(bf16[64,1152]{1,0:T(8,128)(2,1)S(1)} %get-tuple-element.20.adj_ref), channel_id=1, source_target_pairs={{0,1},{1,0},{2,3},{3,2},{4,5},{5,4},{6,7},{7,6},{8,9},{9,8},{10,11... | collective-permute-start | bytes 442376 | tf_op jit(solution)/shard_map/ppermute | solution.py:17
  19.4 2.3 %collective-permute-start.4 = (bf16[2,3,1,64,128]{4,3,0,2,1:T(8,128)(2,1)S(1)}, bf16[2,3,1,64,128]{4,3,0,2,1:T(8,128)(2,1)S(1)}, u32[]{:S(2)}, u32[]{:S(2)}) collective-permute-start(bf16[2,3,1,64,128]{4,3,0,2,1:T(8,128)(2,1)S(1)} %pad_maximum_fusion.6), channel_id=1, source_target_pairs={{0,6},{2,0},{4,2},{6,4},{1,7},{3,1},{5,3},{7,5},{8,14},{10,8},{12,... | collective-permute-start | bytes 294920 | tf_op jit(solution)/shard_map/ppermute | solution.py:22
  19.4 5.1 %collective-permute-start.3 = (bf16[2,3,1,64,128]{4,3,0,2,1:T(8,128)(2,1)S(1)}, bf16[2,3,1,64,128]{4,3,0,2,1:T(8,128)(2,1)S(1)}, u32[]{:S(2)}, u32[]{:S(2)}) collective-permute-start(bf16[2,3,1,64,128]{4,3,0,2,1:T(8,128)(2,1)S(1)} %pad_maximum_fusion.6), channel_id=1, source_target_pairs={{0,2},{2,4},{4,6},{6,0},{1,3},{3,5},{5,7},{7,1},{8,10},{10,12},{12... | collective-permute-start | bytes 294920 | tf_op jit(solution)/shard_map/ppermute | solution.py:22
  19.9 8.7 %copy-start.14 = (s32[2304]{0:T(1024)S(1)}, s32[2304]{0:T(1024)}, u32[]{:S(2)}) copy-start(s32[2304]{0:T(1024)} %param.21) | copy-start | bytes 27652
  20.0 22.5 %collective-permute-start.10 = (bf16[3,3,128,128]{3,2,1,0:T(8,128)(2,1)S(1)}, bf16[3,3,128,128]{3,2,1,0:T(8,128)(2,1)S(1)}, u32[]{:S(2)}, u32[]{:S(2)}) collective-permute-start(bf16[3,3,128,128]{3,2,1,0:T(8,128)(2,1)S(1)} %bitcast.76), channel_id=1, source_target_pairs={{0,1},{1,0},{2,3},{3,2},{4,5},{5,4},{6,7},{7,6},{8,9},{9,8},{10,11... | collective-permute-start | bytes 884744 | tf_op jit(solution)/shard_map/ppermute | solution.py:17
  25.3 5.6 %collective-permute-start.7 = (bf16[2,1,1,64,128]{4,3,2,1,0:T(8,128)(2,1)S(1)}, bf16[2,1,1,64,128]{4,3,2,1,0:T(8,128)(2,1)S(1)}, u32[]{:S(2)}, u32[]{:S(2)}) collective-permute-start(bf16[2,1,1,64,128]{4,3,2,1,0:T(8,128)(2,1)S(1)} %bitcast.58), channel_id=1, source_target_pairs={{0,24},{8,0},{16,8},{24,16},{1,25},{9,1},{17,9},{25,17},{2,26},{10... | collective-permute-start | bytes 98312 | tf_op jit(solution)/shard_map/ppermute | solution.py:22
  28.6 5.7 %collective-permute-start.6 = (bf16[2,1,1,64,128]{4,3,2,1,0:T(8,128)(2,1)S(1)}, bf16[2,1,1,64,128]{4,3,2,1,0:T(8,128)(2,1)S(1)}, u32[]{:S(2)}, u32[]{:S(2)}) collective-permute-start(bf16[2,1,1,64,128]{4,3,2,1,0:T(8,128)(2,1)S(1)} %bitcast.59), channel_id=1, source_target_pairs={{0,8},{8,16},{16,24},{24,0},{1,9},{9,17},{17,25},{25,1},{2,10},{10... | collective-permute-start | bytes 98312 | tf_op jit(solution)/shard_map/ppermute | solution.py:22
  28.6 6.3 %copy-start.7 = (bf16[128,169]{0,1:T(8,128)(2,1)S(1)}, bf16[128,169]{0,1:T(8,128)(2,1)}, u32[]{:S(2)}) copy-start(bf16[128,169]{0,1:T(8,128)(2,1)} %param.31) | copy-start | bytes 129796
  34.3 5.1 %collective-permute-start.9 = (bf16[2,3,1,64,128]{4,3,2,1,0:T(8,128)(2,1)S(1)}, bf16[2,3,1,64,128]{4,3,2,1,0:T(8,128)(2,1)S(1)}, u32[]{:S(2)}, u32[]{:S(2)}) collective-permute-start(bf16[2,3,1,64,128]{4,3,2,1,0:T(8,128)(2,1)S(1)} %pad_maximum_fusion.7), channel_id=1, source_target_pairs={{0,6},{2,0},{4,2},{6,4},{1,7},{3,1},{5,3},{7,5},{8,14},{10,8},{12,... | collective-permute-start | bytes 294920 | tf_op jit(solution)/shard_map/ppermute | solution.py:22
  34.4 5.3 %collective-permute-start.8 = (bf16[2,3,1,64,128]{4,3,2,1,0:T(8,128)(2,1)S(1)}, bf16[2,3,1,64,128]{4,3,2,1,0:T(8,128)(2,1)S(1)}, u32[]{:S(2)}, u32[]{:S(2)}) collective-permute-start(bf16[2,3,1,64,128]{4,3,2,1,0:T(8,128)(2,1)S(1)} %pad_maximum_fusion.7), channel_id=1, source_target_pairs={{0,2},{2,4},{4,6},{6,0},{1,3},{3,5},{5,7},{7,1},{8,10},{10,12},{12... | collective-permute-start | bytes 294920 | tf_op jit(solution)/shard_map/ppermute | solution.py:22
  37.7 1.7 %copy-start.16 = (bf16[4608,288]{1,0:T(8,128)(2,1)}, bf16[4608,288]{1,0:T(8,128)(2,1)S(1)}, u32[]{:S(2)}) copy-start(bf16[4608,288]{1,0:T(8,128)(2,1)S(1)} %get-tuple-element.25.perm_ref) | copy-start | bytes 7962628
  39.5 7.1 %copy-start.1 = (bf16[3,128,128]{2,1,0:T(8,128)(2,1)S(1)}, bf16[3,128,128]{2,1,0:T(8,128)(2,1)}, u32[]{:S(2)}) copy-start(bf16[3,128,128]{2,1,0:T(8,128)(2,1)} %wl_ref.9) | copy-start | bytes 294916
  39.5 7.1 %copy-start.2 = (bf16[3,128,128]{2,1,0:T(8,128)(2,1)S(1)}, bf16[3,128,128]{2,1,0:T(8,128)(2,1)}, u32[]{:S(2)}) copy-start(bf16[3,128,128]{2,1,0:T(8,128)(2,1)} %wr_ref.1) | copy-start | bytes 294916
  39.5 7.1 %copy-start.3 = (bf16[3,128,128]{2,1,0:T(8,128)(2,1)S(1)}, bf16[3,128,128]{2,1,0:T(8,128)(2,1)}, u32[]{:S(2)}) copy-start(bf16[3,128,128]{2,1,0:T(8,128)(2,1)} %wi_ref.9) | copy-start | bytes 294916
  39.5 7.1 %copy-start.4 = (bf16[3,128,128]{2,1,0:T(8,128)(2,1)S(1)}, bf16[3,128,128]{2,1,0:T(8,128)(2,1)}, u32[]{:S(2)}) copy-start(bf16[3,128,128]{2,1,0:T(8,128)(2,1)} %wo_ref.9) | copy-start | bytes 294916
  40.4 7.6 %collective-permute-start.16 = (bf16[2,1,1,64,128]{4,3,2,1,0:T(8,128)(2,1)S(1)}, bf16[2,1,1,64,128]{4,3,2,1,0:T(8,128)(2,1)S(1)}, u32[]{:S(2)}, u32[]{:S(2)}) collective-permute-start(bf16[2,1,1,64,128]{4,3,2,1,0:T(8,128)(2,1)S(1)} %bitcast.54), channel_id=1, source_target_pairs={{0,24},{8,0},{16,8},{24,16},{1,25},{9,1},{17,9},{25,17},{2,26},{10... | collective-permute-start | bytes 98312 | tf_op jit(solution)/shard_map/ppermute | solution.py:22
  40.8 7.2 %collective-permute-start.15 = (bf16[2,1,1,64,128]{4,3,2,1,0:T(8,128)(2,1)S(1)}, bf16[2,1,1,64,128]{4,3,2,1,0:T(8,128)(2,1)S(1)}, u32[]{:S(2)}, u32[]{:S(2)}) collective-permute-start(bf16[2,1,1,64,128]{4,3,2,1,0:T(8,128)(2,1)S(1)} %bitcast.55), channel_id=1, source_target_pairs={{0,8},{8,16},{16,24},{24,0},{1,9},{9,17},{17,25},{25,1},{2,10},{10... | collective-permute-start | bytes 98312 | tf_op jit(solution)/shard_map/ppermute | solution.py:22
  42.5 9.9 %collective-permute-start.11 = (bf16[2,3,128,128]{3,2,0,1:T(8,128)(2,1)S(1)}, bf16[2,3,128,128]{3,2,0,1:T(8,128)(2,1)S(1)}, u32[]{:S(2)}, u32[]{:S(2)}) collective-permute-start(bf16[2,3,128,128]{3,2,0,1:T(8,128)(2,1)S(1)} %get-tuple-element.30), channel_id=1, source_target_pairs={{0,8},{8,16},{16,24},{24,0},{1,9},{9,17},{17,25},{25,1},{2,10},{10... | collective-permute-start | bytes 589832 | tf_op jit(solution)/shard_map/ppermute | solution.py:22
  42.8 12.6 %collective-permute-start.12 = (bf16[2,3,128,128]{3,2,0,1:T(8,128)(2,1)S(1)}, bf16[2,3,128,128]{3,2,0,1:T(8,128)(2,1)S(1)}, u32[]{:S(2)}, u32[]{:S(2)}) collective-permute-start(bf16[2,3,128,128]{3,2,0,1:T(8,128)(2,1)S(1)} %get-tuple-element.31), channel_id=1, source_target_pairs={{0,24},{8,0},{16,8},{24,16},{1,25},{9,1},{17,9},{25,17},{2,26},{10... | collective-permute-start | bytes 589832 | tf_op jit(solution)/shard_map/ppermute | solution.py:22
  48.0 10.6 %collective-permute-start.18 = (bf16[2,3,1,64,128]{4,3,2,1,0:T(8,128)(2,1)S(1)}, bf16[2,3,1,64,128]{4,3,2,1,0:T(8,128)(2,1)S(1)}, u32[]{:S(2)}, u32[]{:S(2)}) collective-permute-start(bf16[2,3,1,64,128]{4,3,2,1,0:T(8,128)(2,1)S(1)} %pad_maximum_fusion.8), channel_id=1, source_target_pairs={{0,6},{2,0},{4,2},{6,4},{1,7},{3,1},{5,3},{7,5},{8,14},{10,8},{12,... | collective-permute-start | bytes 294920 | tf_op jit(solution)/shard_map/ppermute | solution.py:22
  48.4 10.2 %collective-permute-start.17 = (bf16[2,3,1,64,128]{4,3,2,1,0:T(8,128)(2,1)S(1)}, bf16[2,3,1,64,128]{4,3,2,1,0:T(8,128)(2,1)S(1)}, u32[]{:S(2)}, u32[]{:S(2)}) collective-permute-start(bf16[2,3,1,64,128]{4,3,2,1,0:T(8,128)(2,1)S(1)} %pad_maximum_fusion.8), channel_id=1, source_target_pairs={{0,2},{2,4},{4,6},{6,0},{1,3},{3,5},{5,7},{7,1},{8,10},{10,12},{12... | collective-permute-start | bytes 294920 | tf_op jit(solution)/shard_map/ppermute | solution.py:22
  55.4 6.5 %collective-permute-start.13 = (bf16[2,3,128,128]{3,2,1,0:T(8,128)(2,1)S(1)}, bf16[2,3,128,128]{3,2,1,0:T(8,128)(2,1)S(1)}, u32[]{:S(2)}, u32[]{:S(2)}) collective-permute-start(bf16[2,3,128,128]{3,2,1,0:T(8,128)(2,1)S(1)} %get-tuple-element.27), channel_id=1, source_target_pairs={{0,2},{2,4},{4,6},{6,0},{1,3},{3,5},{5,7},{7,1},{8,10},{10,12},{12... | collective-permute-start | bytes 589832 | tf_op jit(solution)/shard_map/ppermute | solution.py:22
  55.6 6.3 %collective-permute-start.14 = (bf16[2,3,128,128]{3,2,1,0:T(8,128)(2,1)S(1)}, bf16[2,3,128,128]{3,2,1,0:T(8,128)(2,1)S(1)}, u32[]{:S(2)}, u32[]{:S(2)}) collective-permute-start(bf16[2,3,128,128]{3,2,1,0:T(8,128)(2,1)S(1)} %get-tuple-element.28), channel_id=1, source_target_pairs={{0,6},{2,0},{4,2},{6,4},{1,7},{3,1},{5,3},{7,5},{8,14},{10,8},{12,... | collective-permute-start | bytes 589832 | tf_op jit(solution)/shard_map/ppermute | solution.py:22

commit v3 on v2

v3 whole, which is shorter than its diff:
```python
import jax
import jax.numpy as jnp
from jax import lax
from jax.experimental import pallas as pl
from jax.experimental.pallas import tpu as pltpu
from jax.sharding import PartitionSpec as P

ORB = 13
GROUPS = 4
OFFS = 18
F32 = jnp.float32
BF16 = jnp.bfloat16
VMEM_LIMIT = 24 * 1024 * 1024


def swapped(value, axis):
    return lax.ppermute(value, axis, [(0, 1), (1, 0)])


def moved(value, axis, steps):
    count = lax.axis_size(axis)
    return lax.ppermute(value, axis, [(i, (i + steps) % count) for i in range(count)])


def with_halo(block, axis, dim):
    low = moved(block, axis, 1)
    high = moved(block, axis, -1)
    return jnp.concatenate([low, block, high], axis=dim)


def ghosts_of(sheets, centre=None):
    low, high = moved(sheets, "gx", 1), moved(sheets, "gx", -1)
    centre = sheets if centre is None else centre
    framed = with_halo(jnp.concatenate([low, centre, high], axis=1), "gy", 2)
    return framed.reshape(-1, sheets.shape[-1])


def across_rows(outgoing, crossed):
    sheets = jnp.stack([outgoing[0], crossed])
    rows = [moved(sheets[:, i], "gx", i - 1) if i != 1 else sheets[:, i] for i in (2, 1, 0)]
    return jnp.stack(rows, axis=1)


def across_columns(shifted):
    cols = [moved(shifted[:, :, i], "gy", i - 1) if i != 1 else shifted[:, :, i] for i in (2, 1, 0)]
    return jnp.stack(cols, axis=2)


def dot(a, b):
    return jnp.dot(a, b, preferred_element_type=F32)


def dot_nt(a, b):
    return lax.dot_general(a, b, (((1,), (1,)), ((), ())), preferred_element_type=F32)


def one_hot(mask):
    return jnp.where(mask, 1.0, 0.0).astype(BF16)


def silu(v):
    return v * (0.5 * jnp.tanh(0.5 * v) + 0.5)


def rms_norm(v):
    return v * lax.rsqrt(jnp.mean(v * v, axis=-1, keepdims=True) + 1e-06)


def iota(shape, dim):
    return lax.broadcasted_iota(jnp.int32, shape, dim)


def fiota(shape, dim):
    return iota(shape, dim).astype(F32)


def call(body, outs, *args, after=(), scratch=(), us=1.0):
    used = len(args)

    def ordered_body(*refs):
        body(*refs[:used], *refs[used + len(after) :])

    return pl.pallas_call(
        ordered_body if after else body,
        out_shape=outs,
        in_specs=[pl.BlockSpec(memory_space=pltpu.VMEM)] * used
        + [pl.BlockSpec(memory_space=pl.ANY)] * len(after),
        scratch_shapes=list(scratch),
        compiler_params=pltpu.CompilerParams(vmem_limit_bytes=VMEM_LIMIT),
        cost_estimate=pl.CostEstimate(
            flops=int(us * 1.1e9), bytes_accessed=int(us * 3.6e6), transcendentals=0
        ),
    )(*args, *after)


def as_row(tiles):
    return jnp.concatenate([tiles[i : i + 1] for i in range(tiles.shape[0])], axis=1)


def folded(row, count, fan):
    return jnp.concatenate([row[:, fan * n : fan * (n + 1)] for n in range(count)], axis=0)


def transposed(values):
    rows, cols = values.shape
    filler = jnp.zeros((rows, 128 - cols), F32)
    return jnp.transpose(jnp.concatenate([values, filler], axis=1))[:cols]


def order_body(send_ref, bond_ref, h_ref, out_ref, h_out_ref):
    owned = bond_ref.shape[0]
    half = owned // 2
    cap = owned // OFFS
    h_out_ref[...] = h_ref[...]
    bond = jnp.concatenate([bond_ref[:half, :], bond_ref[half:, :]], axis=1)
    send = as_row(send_ref[...])
    low = one_hot(iota((cap, owned), 0) == (send & 127))
    high = send >> 7
    late = iota((32, owned), 1) >= half
    late = dot_nt(low, one_hot((iota((32, owned), 0) == high) & late))

    def masked(o):
        mask = jnp.where(high == o, 1.0, 0.0)
        mask = jnp.broadcast_to(mask, (16, owned)).astype(BF16)
        kept = [low[16 * i : 16 * (i + 1)] * mask for i in range(cap // 16)]
        return [k[:, :half] + k[:, half:] for k in kept]

    for i in range(OFFS // 2):
        both = dot(jnp.concatenate(masked(2 * i) + masked(2 * i + 1), axis=0), bond)
        column = jnp.concatenate([late[:, 2 * i : 2 * i + 1], late[:, 2 * i + 1 : 2 * i + 2]], axis=0)
        out_ref[2 * cap * i : 2 * cap * (i + 1), :] = jnp.where(
            column > 0.5, both[:, 128:], both[:, :128]
        ).astype(BF16)


def slots_body(nb_ref, kind_ref, recv_ref, dist_ref, h_ref, adj_ref, pack_ref, h_out_ref):
    fan, atoms = pack_ref.shape
    h_out_ref[...] = h_ref[...]
    flat = nb_ref[...] | (kind_ref[...] << 11) | ((recv_ref[...] & 127) << 13)
    pack = transposed(folded(as_row(flat.astype(F32)), atoms, fan)).astype(jnp.int32)
    dist = transposed(folded(as_row(dist_ref[...]), atoms, fan))
    pack_ref[...] = pack
    peer = (pack & 63).astype(F32)
    off = ((pack & 2047) >> 6).astype(F32)
    scaled = dist * (1.0 / 7.0)
    env = 1.0 - scaled * scaled
    env = jnp.where(((pack >> 11) & 3) > 0, env * env, 0.0)
    row = fiota((fan, atoms), 0)
    target = off * float(GROUPS) + ranked_among(off)
    env_sorted = jnp.zeros((fan, atoms), F32)
    peer_sorted = jnp.zeros((fan, atoms), F32)
    for s in range(fan):
        here = target[s : s + 1, :] == row
        env_sorted = jnp.where(here, env[s : s + 1, :], env_sorted)
        peer_sorted = jnp.where(here, peer[s : s + 1, :], peer_sorted)
    which = fiota((atoms, atoms), 0)
    parts = []
    for o in range(OFFS):
        part = jnp.zeros((atoms, atoms), F32)
        for t in range(GROUPS * o, GROUPS * (o + 1)):
            part += jnp.where(peer_sorted[t : t + 1, :] == which, env_sorted[t : t + 1, :], 0.0)
        parts.append(part)
    for m in range(OFFS // 2):
        pair = jnp.concatenate([parts[2 * m], parts[2 * m + 1]], axis=0)
        pair = jnp.concatenate([pair, jnp.zeros_like(pair)], axis=1)
        adj_ref[:, 128 * m : 128 * (m + 1)] = jnp.transpose(pair)[:atoms].astype(BF16)


def ranked_among(key):
    fan = key.shape[0]
    row = fiota(key.shape, 0)
    rank = jnp.zeros(key.shape, F32)
    for s in range(fan - 1):
        rank += jnp.where((key == key[s : s + 1, :]) & (row > float(s)), 1.0, 0.0)
    return rank


def write_hots(out_ref, index):
    cap = index.shape[0]
    lane = fiota((cap, 128), 1)
    for o in range(OFFS):
        hot = (lane == index[:, o : o + 1]) | (lane == index[:, 32 + o : 33 + o] + 64.0)
        out_ref[cap * o : cap * (o + 1), :] = one_hot(hot)


def pairs_body(
    send_ref, own_ref, nb_ref, kind_ref, recv_ref, pack_ref, hot_own_ref, hot_mir_ref, place_ref
):
    fan, atoms = pack_ref.shape
    cap = hot_own_ref.shape[0] // OFFS
    send = as_row(send_ref[...])
    own = as_row(own_ref[...]).astype(F32)
    owned = send.shape[1]
    atom_r = jnp.floor((own + 0.5) * (1.0 / fan))
    slot_r = own - fan * atom_r
    off_r = (send >> 7).astype(F32)
    pos_r = (send & 127).astype(F32)
    peer = (pack_ref[...] & 63).astype(F32)
    at_atom = fiota((atoms, owned), 0) == atom_r
    at_slot = fiota((fan, owned), 0) == slot_r
    place_ref[...] = dot_nt(
        one_hot(at_slot), jnp.where(at_atom, pos_r + 1.0, 0.0).astype(BF16)
    )
    peer_all = dot(peer.astype(BF16), one_hot(at_atom))
    peer_r = jnp.sum(jnp.where(at_slot, peer_all, 0.0), axis=0, keepdims=True)
    at_off = fiota((32, owned), 0) == off_r
    values = jnp.concatenate(
        [jnp.where(at_off, atom_r, 0.0), jnp.where(at_off, peer_r, 0.0)], axis=0
    ).astype(BF16)
    write_hots(hot_own_ref, dot_nt(one_hot(fiota((cap, owned), 0) == pos_r), values))

    ids = as_row(jnp.where(kind_ref[...] == 2, nb_ref[...], 64 * 31))
    slots = ids.shape[1]
    atom_s = jnp.floor((fiota((1, slots), 1) + 0.5) * (1.0 / fan))
    peer_s = (ids & 63).astype(F32)
    off_s = (ids >> 6).astype(F32)
    pos_s = as_row(recv_ref[...] & 127).astype(F32)
    at_off = fiota((32, slots), 0) == off_s
    values = jnp.concatenate(
        [jnp.where(at_off, atom_s, 0.0), jnp.where(at_off, peer_s, 0.0)], axis=0
    ).astype(BF16)
    write_hots(hot_mir_ref, dot_nt(one_hot(fiota((cap, slots), 0) == pos_s), values))


def places_body(
    pack_ref, place_ref, wb_ref, pick_own_ref, pick_mir_ref, perm_ref, owned_ref, wcat_ref
):
    fan, atoms = pack_ref.shape
    cap = pick_own_ref.shape[0] // OFFS
    pack = pack_ref[...]
    off = ((pack & 2047) >> 6).astype(F32)
    kind = (pack >> 11) & 3
    pos_in = (pack >> 13).astype(F32)
    place = place_ref[...]
    owned = jnp.where(place > 0.5, 1.0, 0.0)
    owned_ref[...] = owned
    src = jnp.where(kind == 1, place, jnp.where(kind == 2, pos_in + 1.0, 0.0))
    rank = ranked_among(off * 2.0 + owned)
    target = off * float(GROUPS) + (2.0 - 2.0 * owned) + rank
    row = fiota((fan, atoms), 0)
    sorted_src = jnp.zeros((fan, atoms), F32)
    for s in range(fan):
        sorted_src = jnp.where(target[s : s + 1, :] == row, src[s : s + 1, :], sorted_src)
    spread = one_hot((iota((cap, atoms), 0) >> 1) == iota((cap, atoms), 1))
    spread = dot_nt(spread, sorted_src.astype(BF16))
    member = iota((cap, fan), 1) & 3
    parity = iota((cap, fan), 0) & 1
    fold = one_hot((iota((fan, 32), 0) >> 2) == iota((fan, 32), 1))
    lane = fiota((cap, cap), 1)
    for shift, pick_ref in ((0, pick_own_ref), (2, pick_mir_ref)):
        kept = jnp.where(member == parity + shift, spread, 0.0).astype(BF16)
        index = dot(kept, fold) - 1.0
        for o in range(OFFS):
            pick_ref[cap * o : cap * (o + 1), :] = one_hot(index[:, o : o + 1] == lane)

    spot = off * 8.0 + (iota((fan, atoms), 1) & 3).astype(F32) * 2.0 + rank
    lane = fiota((fan, 2 * fan), 1)
    for q in range(atoms // 4):
        perm_ref[4 * fan * q : 4 * fan * (q + 1), :] = jnp.concatenate(
            [jnp.where(spot[:, 4 * q + i : 4 * q + i + 1] == lane, 1.0, 0.0) for i in range(4)],
            axis=0,
        ).astype(BF16)

    block = wb_ref.shape[0]
    row = fiota((block, block), 0)
    col = fiota((block, block), 1)
    major = jnp.floor((row + 0.5) * (1.0 / ORB))
    wcat_ref[:, :128] = wb_ref[...]
    wcat_ref[:, 128:] = dot(
        one_hot((row - ORB * major) * ORB + major == col), wb_ref[...]
    ).astype(BF16)


def node_body(layer):
    def body(adj_ref, other_ref, ghost_ref, wm_ref, wu_ref, gain_ref, out_ref):
        ghosts = ghost_ref.shape[0]
        half = ghosts // 2
        atoms = ghosts // OFFS
        mixed = dot(adj_ref[...], ghost_ref[...])
        other = dot(other_ref[:, :half], ghost_ref[half:, :])
        other += dot(other_ref[:, half:], ghost_ref[:half, :])
        mixed = jnp.concatenate([mixed, other], axis=0).astype(BF16)
        hidden = jnp.concatenate(
            [ghost_ref[atoms * 4 : atoms * 5, :], ghost_ref[atoms * 13 : atoms * 14, :]], axis=0
        )
        summed = (dot(mixed, wm_ref[layer]) * 0.125).astype(BF16)
        updated = hidden.astype(F32) + silu(dot(summed, wu_ref[layer]))
        out_ref[...] = (rms_norm(updated) * gain_ref[layer : layer + 1, :]).astype(BF16)

    return body


CHUNK = 6


def fill_table(ghost_ref, w_local, w_ghost, table):
    atoms = ghost_ref.shape[0] // OFFS
    local = dot(ghost_ref[atoms * 4 : atoms * 5, :], w_local).astype(BF16)
    distant = dot(ghost_ref[...], w_ghost).astype(BF16)
    blank = jnp.zeros((atoms, 128), BF16)
    for o in range(OFFS):
        base = 2 * atoms * o
        table[base : base + atoms, :128] = local
        table[base : base + atoms, 128:] = blank
        table[base + atoms : base + 2 * atoms, :128] = blank
        table[base + atoms : base + 2 * atoms, 128:] = distant[atoms * o : atoms * (o + 1)]


def chosen_product(hot_ref, table, c):
    cap = hot_ref.shape[0] // OFFS
    chosen = jnp.concatenate(
        [
            dot(hot_ref[cap * o : cap * (o + 1), :], table[cap * o : cap * (o + 1), :])
            for o in range(CHUNK * c, CHUNK * (c + 1))
        ],
        axis=0,
    )
    return chosen[:, :128] * chosen[:, 128:]


def edge_all(e_ref, hot_ref, ghost_ref, w_local, w_ghost, w_in, w_out, table, out_ref):
    cap = e_ref.shape[0] // OFFS
    fill_table(ghost_ref, w_local, w_ghost, table)
    for c in range(OFFS // CHUNK):
        span = slice(CHUNK * cap * c, CHUNK * cap * (c + 1))
        state = e_ref[span, :]
        gate = silu(dot(state, w_in) * chosen_product(hot_ref, table, c)).astype(BF16)
        out_ref[span, :] = rms_norm(state.astype(F32) + dot(gate, w_out)).astype(BF16)


def edge_body(layer):
    def body(e_ref, hot_ref, ghost_ref, wl_ref, wg_ref, wi_ref, wo_ref, out_ref, table):
        edge_all(
            e_ref, hot_ref, ghost_ref, wl_ref[layer], wg_ref[layer], wi_ref[layer], wo_ref[layer],
            table, out_ref,
        )

    return body


def twice(weight):
    blank = jnp.zeros_like(weight)
    return jnp.concatenate(
        [
            jnp.concatenate([weight, blank], axis=1),
            jnp.concatenate([blank, weight], axis=1),
        ],
        axis=0,
    )


def final_body(layer):
    def body(
        own_ref, mir_ref, ho_ref, hm_ref, ghost_ref, wl_ref, wr_ref, wi_ref, wo_ref,
        po_ref, pm_ref, perm_ref, owned_ref, wcat_ref,
        out_ref, table_own, table_mir, ranked, rows,
    ):
        atoms = ghost_ref.shape[0] // OFFS
        cap = own_ref.shape[0] // OFFS
        fan = out_ref.shape[1] // atoms
        w_in, w_out = twice(wi_ref[layer]), twice(wo_ref[layer])
        fill_table(ghost_ref, wl_ref[layer], wr_ref[layer], table_own)
        fill_table(ghost_ref, wr_ref[layer], wl_ref[layer], table_mir)
        for c in range(OFFS // CHUNK):
            span = slice(CHUNK * cap * c, CHUNK * cap * (c + 1))
            state = jnp.concatenate([own_ref[span, :], mir_ref[span, :]], axis=1)
            chosen = jnp.concatenate(
                [chosen_product(ho_ref, table_own, c), chosen_product(hm_ref, table_mir, c)],
                axis=1,
            )
            gate = silu(dot(state, w_in) * chosen).astype(BF16)
            renewed = state.astype(F32) + dot(gate, w_out)
            e_own = rms_norm(renewed[:, :128]).astype(BF16)
            e_mir = rms_norm(renewed[:, 128:]).astype(BF16)
            for i in range(CHUNK):
                o = CHUNK * c + i
                here = slice(cap * i, cap * (i + 1))
                span = slice(cap * o, cap * (o + 1))
                ranked[span, :128] = dot(po_ref[span, :], e_own[here])
                ranked[span, 128:] = dot(pm_ref[span, :], e_mir[here])
        for q in range(atoms // 4):
            span = slice(4 * fan * q, 4 * fan * (q + 1))
            tiles = jnp.concatenate(
                [ranked[cap * o + 8 * q : cap * o + 8 * (q + 1), :] for o in range(OFFS)], axis=0
            ).astype(BF16)
            spread = dot(perm_ref[span, :], tiles)
            mine = jnp.concatenate(
                [owned_ref[:, 4 * q + i : 4 * q + i + 1] for i in range(4)], axis=0
            )
            mine = mine > 0.5
            rows[span, :128] = jnp.where(mine, spread[:, :128], 0.0).astype(BF16)
            rows[span, 128:] = jnp.where(mine, 0.0, spread[:, 128:]).astype(BF16)
        step = 16 * fan
        for g in range(atoms // 16):
            out_ref[:, step * g : step * (g + 1)] = dot_nt(
                wcat_ref[...], rows[step * g : step * (g + 1), :]
            ).astype(BF16)

    return body


def shards(
    atom_feats, bond_embed, pair_dist, neighbours, slot_kind, own_rows, send_pos, recv_pos,
    w_left, w_right, w_edge_in, w_edge_out, w_msg, w_upd, node_gain, w_block,
):
    atoms, channels = atom_feats.shape
    slots = neighbours.shape[0]
    fan = slots // atoms
    owned = own_rows.shape[0]
    cap = owned // OFFS
    block = w_block.shape[1]
    ghosts = OFFS * atoms

    def array(*shape, dtype=BF16):
        return jax.ShapeDtypeStruct(shape, dtype)

    def tiles(values):
        return values.reshape(-1, 128)

    send, own = tiles(send_pos), tiles(own_rows)
    nb, kind, recv, dist = map(tiles, (neighbours, slot_kind, recv_pos, pair_dist))
    opposite = swapped(atom_feats, "layer")
    adjacency, pack, hidden = call(
        slots_body,
        (array(atoms, ghosts), array(fan, atoms, dtype=jnp.int32), array(atoms, channels)),
        nb, kind, recv, dist, atom_feats,
        us=3.0,
    )
    other = swapped(adjacency, "layer")
    sheets = jnp.concatenate([hidden, opposite], axis=0)
    ordered, centre = call(
        order_body,
        (array(owned, channels), array(2 * atoms, channels)),
        send, bond_embed, sheets,
        us=3.5,
    )
    outgoing = ordered.reshape(2, 3, 3, cap, channels)
    crossed = swapped(outgoing[1], "layer")
    shifted = across_rows(outgoing, crossed)
    mirror = across_columns(shifted).reshape(owned, channels)
    hot_own, hot_mir, place = call(
        pairs_body,
        (array(owned, 128), array(owned, 128), array(fan, atoms, dtype=F32)),
        send, own, nb, kind, recv, pack,
        us=2.5,
    )
    pick_own, pick_mir, perm, mine, w_cat = call(
        places_body,
        (
            array(owned, cap),
            array(owned, cap),
            array(slots, 2 * fan),
            array(fan, atoms, dtype=F32),
            array(block, 2 * channels),
        ),
        pack, place, w_block.T,
        us=2.5,
    )
    centre = centre.reshape(2, 1, 1, atoms, channels)
    table = pltpu.VMEM((2 * ghosts, 2 * channels), BF16)
    for layer in range(2):
        ghost = ghosts_of(sheets.reshape(2, 1, 1, atoms, channels), centre)
        centre = None
        sheets = call(
            node_body(layer),
            array(2 * atoms, channels),
            adjacency, other, ghost, w_msg, w_upd, node_gain,
            after=(shifted, perm) if layer else (crossed,),
            us=0.6,
        )
        ordered = call(
            edge_body(layer),
            array(owned, channels),
            ordered, hot_own, ghost, w_left, w_right, w_edge_in, w_edge_out,
            scratch=[table],
            us=1.4,
        )
        mirror = call(
            edge_body(layer),
            array(owned, channels),
            mirror, hot_mir, ghost, w_right, w_left, w_edge_in, w_edge_out,
            scratch=[table],
            us=1.4,
        )
    ghost = ghosts_of(sheets.reshape(2, 1, 1, atoms, channels))
    return call(
        final_body(2),
        array(block, slots),
        ordered, mirror, hot_own, hot_mir, ghost, w_left, w_right, w_edge_in, w_edge_out,
        pick_own, pick_mir, perm, mine, w_cat,
        scratch=[
            table,
            table,
            pltpu.VMEM((owned, 2 * channels), F32),
            pltpu.VMEM((slots, 2 * channels), BF16),
        ],
        us=7.0,
    )


def solution(mesh):
    axes = ("gx", "gy", "layer")
    rows = P(axes, None)
    flat = P(axes)
    placed = (rows, rows) + (flat,) * 6 + (P(),) * 8
    return jax.shard_map(
        shards,
        mesh=mesh,
        in_specs=placed,
        out_specs=P(None, axes),
        check_vma=False,
    )
```

time: 73.5 us -> 62.6 us (0.85)
  Pallas kernels: 29.1 us -> 20.2 us
  waiting for transfers between devices: 17.8 us -> 16 us
    pallas_call x11, Pallas kernels: 29.1 us -> 20.2 us  [call(): pl.pallas_call(ordered_body if after else body, out_shape=outs, in_specs=...]
    ppermute x16, waiting for transfers between devices: 17.8 us -> 16 us  [moved(): lax.ppermute(value, axis, [(i, (i + steps) % count) for i in range(count)])]
    unnamed x34 -> x33, local copies, waits for them, and re-layouts: 4.28 us -> 3.68 us
  transfers between devices with their start and end apart: 19 -> 19, of which waited for: 8 -> 8; matrix products, arithmetic and copies ran while one was open for 1% -> 0% of each run, Pallas kernels for 25% -> 17%
where the time goes in v3:
time: 62.6 us; the launch traced here: 62.2 us
  starting transfers between devices  21.4 us (34%)
  Pallas kernels  20.2 us (32%)
  waiting for transfers between devices  16 us (26%)
  local copies, waits for them, and re-layouts  3.83 us (6%)
    pallas_call x11, Pallas kernels, call(): pl.pallas_call(ordered_body if after else body, out_shape=outs, in_specs=...  20.2 us
    ppermute x16, starting transfers between devices, moved(): lax.ppermute(value, axis, [(i, (i + steps) % count) for i in range(count)])  16.7 us
    ppermute x16, waiting for transfers between devices, moved(): lax.ppermute(value, axis, [(i, (i + steps) % count) for i in range(count)])  16 us
    ppermute x3, starting transfers between devices, swapped(): return lax.ppermute(value, axis, [(0, 1), (1, 0)])  4.62 us
    unnamed x33, local copies, waits for them, and re-layouts  3.68 us
  transfers between devices with their start and end apart: 19, of which 8 were waited for; matrix products, arithmetic and copies ran while one was open for 0% of the time, Pallas kernels for 17%

profile of v3, /device:TPU:0, one launch (start us, length us, event | category | flops | bytes accessed | tf_op | source)
XLA Modules:
  0.0 62.2 jit_solution(9576271441655071023)
XLA Ops:
  0.0 3.0 %collective-permute-start = (bf16[64,128]{1,0:T(8,128)(2,1)}, bf16[64,128]{1,0:T(8,128)(2,1)S(1)}, u32[]{:S(2)}, u32[]{:S(2)}) collective-permute-start(bf16[64,128]{1,0:T(8,128)(2,1)} %h_ref.1), channel_id=1, source_target_pairs={{0,1},{1,0},{2,3},{3,2},{4,5},{5,4},{6,7},{7,6},{8,9},{9,8},{10,11... | collective-permute-start | bytes 49160 | tf_op jit(solution)/shard_map/ppermute | solution.py:17
  3.0 0.7 %copy-done.9 = f32[4608]{0:T(1024)S(1)} copy-done((f32[4608]{0:T(1024)S(1)}, f32[4608]{0:T(1024)}, u32[]{:S(2)}) %copy-start.9) | copy-done | bytes 18456
  3.7 0.7 %copy-done.10 = s32[4608]{0:T(1024)S(1)} copy-done((s32[4608]{0:T(1024)S(1)}, s32[4608]{0:T(1024)}, u32[]{:S(2)}) %copy-start.10) | copy-done | bytes 18456
  4.4 0.7 %copy-done.11 = s32[4608]{0:T(1024)S(1)} copy-done((s32[4608]{0:T(1024)S(1)}, s32[4608]{0:T(1024)}, u32[]{:S(2)}) %copy-start.11) | copy-done | bytes 18456
  5.2 0.7 %copy-done.12 = s32[4608]{0:T(1024)S(1)} copy-done((s32[4608]{0:T(1024)S(1)}, s32[4608]{0:T(1024)}, u32[]{:S(2)}) %copy-start.12) | copy-done | bytes 18456
  5.9 0.7 %copy-done.13 = bf16[64,128]{1,0:T(8,128)(2,1)S(1)} copy-done((bf16[64,128]{1,0:T(8,128)(2,1)S(1)}, bf16[64,128]{1,0:T(8,128)(2,1)}, u32[]{:S(2)}) %copy-start.13) | copy-done | bytes 16408
  6.6 1.4 %shard_map.154 = (bf16[64,1152]{1,0:T(8,128)(2,1)S(1)}, s32[72,64]{1,0:T(8,128)S(1)}, bf16[64,128]{1,0:T(8,128)(2,1)S(1)}) custom-call(s32[36,128]{1,0:T(8,128)S(1)} %bitcast.69, s32[36,128]{1,0:T(8,128)S(1)} %bitcast.71, s32[36,128]{1,0:T(8,128)S(1)} %bitcast.73, f32[36,128]{1,0:T(8,128)S(1)} %bitcast.68, bf16[64,128]{1,0:T(8,128)(2,1)S(1)} %copy-done.13), custom_call_target="tpu_custom_call" | custom-call | flops 3300000000 | bytes 10800000 | tf_op jit(solution)/shard_map/pallas_call | solution.py:83
  8.0 0.1 collective-permute-start.5
  8.1 0.0 copy-done.14
  8.1 0.0 copy-start.3
  8.1 2.2 %shard_map.156 = (bf16[2304,128]{1,0:T(8,128)(2,1)S(1)}, bf16[2304,128]{1,0:T(8,128)(2,1)S(1)}, f32[72,64]{1,0:T(8,128)S(1)}) custom-call(s32[18,128]{1,0:T(8,128)S(1)} %bitcast.76, s32[18,128]{1,0:T(8,128)S(1)} %bitcast.75, s32[36,128]{1,0:T(8,128)S(1)} %bitcast.70, s32[36,128]{1,0:T(8,128)S(1)} %bitcast.72, s32[36,128]{1,0:T(8,128)S(1)} %bitcast.74, ...), custom_call_target="tpu_custom_call" | custom-call | flops 2750000128 | bytes 9000000 | tf_op jit(solution)/shard_map/pallas_call | solution.py:83
  10.3 0.0 collective-permute-done
  10.3 0.0 copy-start.8
  10.3 4.1 %collective-permute-start.2 = (bf16[2,1,1,64,128]{4,3,2,1,0:T(8,128)(2,1)S(1)}, bf16[2,1,1,64,128]{4,3,2,1,0:T(8,128)(2,1)S(1)}, u32[]{:S(2)}, u32[]{:S(2)}) collective-permute-start(bf16[2,1,1,64,128]{4,3,2,1,0:T(8,128)(2,1)S(1)} %bitcast.65), channel_id=1, source_target_pairs={{0,24},{8,0},{16,8},{24,16},{1,25},{9,1},{17,9},{25,17},{2,26},{10... | collective-permute-start | bytes 98312 | tf_op jit(solution)/shard_map/ppermute | solution.py:22
  14.5 0.0 collective-permute-start.1
  14.5 1.9 %shard_map.155 = (bf16[2304,128]{1,0:T(8,128)(2,1)S(1)}, bf16[128,128]{1,0:T(8,128)(2,1)S(1)}) custom-call(s32[18,128]{1,0:T(8,128)S(1)} %bitcast.77, bf16[2304,128]{1,0:T(8,128)(2,1)S(1)} %copy-done.3, bf16[128,128]{1,0:T(8,128)(2,1)S(1)} %constant_dynamic-update-slice_fusion.h_ref), custom_call_target="tpu_custom_call" | custom-call | flops 3849999872 | bytes 12600000 | tf_op jit(solution)/shard_map/pallas_call | solution.py:83
  16.4 1.6 %collective-permute-start.6 = (bf16[3,3,128,128]{3,2,1,0:T(8,128)(2,1)S(1)}, bf16[3,3,128,128]{3,2,1,0:T(8,128)(2,1)S(1)}, u32[]{:S(2)}, u32[]{:S(2)}) collective-permute-start(bf16[3,3,128,128]{3,2,1,0:T(8,128)(2,1)S(1)} %bitcast.79), channel_id=1, source_target_pairs={{0,1},{1,0},{2,3},{3,2},{4,5},{5,4},{6,7},{7,6},{8,9},{9,8},{10,11... | collective-permute-start | bytes 884744 | tf_op jit(solution)/shard_map/ppermute | solution.py:17
  18.0 0.0 collective-permute-done.2
  18.0 2.1 %collective-permute-done.1 = bf16[2,1,1,64,128]{4,3,2,1,0:T(8,128)(2,1)S(1)} collective-permute-done((bf16[2,1,1,64,128]{4,3,2,1,0:T(8,128)(2,1)S(1)}, bf16[2,1,1,64,128]{4,3,2,1,0:T(8,128)(2,1)S(1)}, u32[]{:S(2)}, u32[]{:S(2)}) %collective-permute-start.1) | collective-permute-done | bytes 32800 | tf_op jit(solution)/shard_map/ppermute | solution.py:22
  20.2 0.1 collective-permute-start.4
  20.2 0.5 collective-permute-start.3
  20.8 2.4 %shard_map.162 = (bf16[2304,128]{1,0:T(8,128)(2,1)S(1)}, bf16[2304,128]{1,0:T(8,128)(2,1)S(1)}, bf16[4608,144]{1,0:T(8,128)(2,1)S(1)}, f32[72,64]{1,0:T(8,128)S(1)}, bf16[169,256]{1,0:T(8,128)(2,1)S(1)}) custom-call(s32[72,64]{1,0:T(8,128)S(1)} %get-tuple-element.20.pack_ref, f32[72,64]{1,0:T(8,128)S(1)} %get-tuple-element.25.place_ref, ...), custom_call_target="tpu_custom_call" | custom-call | flops 2750000128 | bytes 9000000 | tf_op jit(solution)/shard_map/pallas_call | solution.py:83
  23.2 0.0 copy-start.4
  23.2 0.0 copy-start.5
  23.2 0.0 copy-start.6
  23.2 0.0 copy-start.7
  23.2 0.0 collective-permute-done.4
  23.3 2.1 %collective-permute-done.3 = bf16[2,3,1,64,128]{4,3,2,1,0:T(8,128)(2,1)S(1)} collective-permute-done((bf16[2,3,1,64,128]{4,3,2,1,0:T(8,128)(2,1)S(1)}, bf16[2,3,1,64,128]{4,3,2,1,0:T(8,128)(2,1)S(1)}, u32[]{:S(2)}, u32[]{:S(2)}) %collective-permute-start.3) | collective-permute-done | bytes 98336 | tf_op jit(solution)/shard_map/ppermute | solution.py:22
  25.4 0.0 collective-permute-done.5.refs_1_
  25.4 0.0 collective-permute-done.6.refs_6_
  25.5 0.6 shard_map.158
  26.1 2.5 %collective-permute-start.8 = (bf16[2,1,1,64,128]{4,3,2,1,0:T(8,128)(2,1)S(1)}, bf16[2,1,1,64,128]{4,3,2,1,0:T(8,128)(2,1)S(1)}, u32[]{:S(2)}, u32[]{:S(2)}) collective-permute-start(bf16[2,1,1,64,128]{4,3,2,1,0:T(8,128)(2,1)S(1)} %bitcast.59), channel_id=1, source_target_pairs={{0,24},{8,0},{16,8},{24,16},{1,25},{9,1},{17,9},{25,17},{2,26},{10... | collective-permute-start | bytes 98312 | tf_op jit(solution)/shard_map/ppermute | solution.py:22
  28.6 0.0 collective-permute-start.7
  28.6 0.1 fusion.3
  28.7 0.1 collective-permute-start.11
  28.8 3.9 %collective-permute-start.12 = (bf16[2,3,128,128]{3,2,1,0:T(8,128)(2,1)S(1)}, bf16[2,3,128,128]{3,2,1,0:T(8,128)(2,1)S(1)}, u32[]{:S(2)}, u32[]{:S(2)}) collective-permute-start(bf16[2,3,128,128]{3,2,1,0:T(8,128)(2,1)S(1)} %get-tuple-element.35), channel_id=1, source_target_pairs={{0,24},{8,0},{16,8},{24,16},{1,25},{9,1},{17,9},{25,17},{2,26},{10... | collective-permute-start | bytes 589832 | tf_op jit(solution)/shard_map/ppermute | solution.py:22
  32.6 0.0 collective-permute-done.8
  32.6 2.3 %collective-permute-done.7 = bf16[2,1,1,64,128]{4,3,2,1,0:T(8,128)(2,1)S(1)} collective-permute-done((bf16[2,1,1,64,128]{4,3,2,1,0:T(8,128)(2,1)S(1)}, bf16[2,1,1,64,128]{4,3,2,1,0:T(8,128)(2,1)S(1)}, u32[]{:S(2)}, u32[]{:S(2)}) %collective-permute-start.7) | collective-permute-done | bytes 32800 | tf_op jit(solution)/shard_map/ppermute | solution.py:22
  34.9 0.1 collective-permute-start.10
  35.0 0.5 collective-permute-start.9
  35.5 1.3 %shard_map.157.e_ref = bf16[2304,128]{1,0:T(8,128)(2,1)S(1)} custom-call(bf16[2304,128]{1,0:T(8,128)(2,1)S(1)} %get-tuple-element.19.e_ref, bf16[2304,128]{1,0:T(8,128)(2,1)S(1)} %get-tuple-element.21.hot_ref.ho_ref, bf16[1152,128]{1,0:T(8,128)(2,1)S(1)} %bitcast.55, bf16[3,128,128]{2,1,0:T(8,128)(2,1)S(1)} %copy-done.4, bf16[3,128,128]{2,1,0:T(8,128)(2,1)S(1)} %copy-done.5, ...), custom_call_target="tpu_custom_call" | custom-call | flops 1540000000 | bytes 5040000 | tf_op jit(solution)/shard_map/pallas_call | solution.py:83
  36.8 0.6 collective-permute-done.10
  37.4 2.6 %collective-permute-done.9 = bf16[2,3,1,64,128]{4,3,2,1,0:T(8,128)(2,1)S(1)} collective-permute-done((bf16[2,3,1,64,128]{4,3,2,1,0:T(8,128)(2,1)S(1)}, bf16[2,3,1,64,128]{4,3,2,1,0:T(8,128)(2,1)S(1)}, u32[]{:S(2)}, u32[]{:S(2)}) %collective-permute-start.9) | collective-permute-done | bytes 98336 | tf_op jit(solution)/shard_map/ppermute | solution.py:22
  40.0 0.0 collective-permute-done.11
  40.0 0.0 collective-permute-done.12
  40.0 0.1 pad_maximum_fusion.refs_6_
  40.1 0.6 shard_map.163
  40.7 2.7 %collective-permute-start.16 = (bf16[2,1,1,64,128]{4,3,2,1,0:T(8,128)(2,1)S(1)}, bf16[2,1,1,64,128]{4,3,2,1,0:T(8,128)(2,1)S(1)}, u32[]{:S(2)}, u32[]{:S(2)}) collective-permute-start(bf16[2,1,1,64,128]{4,3,2,1,0:T(8,128)(2,1)S(1)} %bitcast.50), channel_id=1, source_target_pairs={{0,24},{8,0},{16,8},{24,16},{1,25},{9,1},{17,9},{25,17},{2,26},{10... | collective-permute-start | bytes 98312 | tf_op jit(solution)/shard_map/ppermute | solution.py:22
  43.4 0.0 collective-permute-start.15
  43.5 0.1 collective-permute-start.13
  43.5 1.7 %collective-permute-start.14 = (bf16[2,3,128,128]{3,2,1,0:T(8,128)(2,1)S(1)}, bf16[2,3,128,128]{3,2,1,0:T(8,128)(2,1)S(1)}, u32[]{:S(2)}, u32[]{:S(2)}) collective-permute-start(bf16[2,3,128,128]{3,2,1,0:T(8,128)(2,1)S(1)} %get-tuple-element.32), channel_id=1, source_target_pairs={{0,6},{2,0},{4,2},{6,4},{1,7},{3,1},{5,3},{7,5},{8,14},{10,8},{12,... | collective-permute-start | bytes 589832 | tf_op jit(solution)/shard_map/ppermute | solution.py:22
  45.3 0.0 collective-permute-done.16
  45.3 3.9 %collective-permute-done.15 = bf16[2,1,1,64,128]{4,3,2,1,0:T(8,128)(2,1)S(1)} collective-permute-done((bf16[2,1,1,64,128]{4,3,2,1,0:T(8,128)(2,1)S(1)}, bf16[2,1,1,64,128]{4,3,2,1,0:T(8,128)(2,1)S(1)}, u32[]{:S(2)}, u32[]{:S(2)}) %collective-permute-start.15) | collective-permute-done | bytes 32800 | tf_op jit(solution)/shard_map/ppermute | solution.py:22
  49.1 0.1 collective-permute-start.18
  49.2 0.5 collective-permute-start.17
  49.7 1.3 %shard_map.159.own_ref = bf16[2304,128]{1,0:T(8,128)(2,1)S(1)} custom-call(bf16[2304,128]{1,0:T(8,128)(2,1)S(1)} %shard_map.157.e_ref, bf16[2304,128]{1,0:T(8,128)(2,1)S(1)} %get-tuple-element.21.hot_ref.ho_ref, bf16[1152,128]{1,0:T(8,128)(2,1)S(1)} %bitcast.47, bf16[3,128,128]{2,1,0:T(8,128)(2,1)S(1)} %copy-done.4, bf16[3,128,128]{2,1,0:T(8,128)(2,1)S(1)} %copy-done.5, ...), custom_call_target="tpu_custom_call" | custom-call | flops 1540000000 | bytes 5040000 | tf_op jit(solution)/shard_map/pallas_call | solution.py:83
  51.0 1.4 %collective-permute-done.18 = bf16[2,3,1,64,128]{4,3,2,1,0:T(8,128)(2,1)S(1)} collective-permute-done((bf16[2,3,1,64,128]{4,3,2,1,0:T(8,128)(2,1)S(1)}, bf16[2,3,1,64,128]{4,3,2,1,0:T(8,128)(2,1)S(1)}, u32[]{:S(2)}, u32[]{:S(2)}) %collective-permute-start.18) | collective-permute-done | bytes 98336 | tf_op jit(solution)/shard_map/ppermute | solution.py:22
  52.4 1.1 %collective-permute-done.17 = bf16[2,3,1,64,128]{4,3,2,1,0:T(8,128)(2,1)S(1)} collective-permute-done((bf16[2,3,1,64,128]{4,3,2,1,0:T(8,128)(2,1)S(1)}, bf16[2,3,1,64,128]{4,3,2,1,0:T(8,128)(2,1)S(1)}, u32[]{:S(2)}, u32[]{:S(2)}) %collective-permute-start.17) | collective-permute-done | bytes 98336 | tf_op jit(solution)/shard_map/ppermute | solution.py:22
  53.5 0.0 collective-permute-done.13
  53.5 0.0 collective-permute-done.14
  53.5 0.1 pad_maximum_fusion.1
  53.7 1.3 %shard_map.160.e_ref = bf16[2304,128]{1,0:T(8,128)(2,1)S(1)} custom-call(bf16[2304,128]{1,0:T(8,128)(2,1)S(1)} %bitcast.49, bf16[2304,128]{1,0:T(8,128)(2,1)S(1)} %get-tuple-element.24.hot_ref.hm_ref, bf16[1152,128]{1,0:T(8,128)(2,1)S(1)} %bitcast.56, bf16[3,128,128]{2,1,0:T(8,128)(2,1)S(1)} %copy-done.5, bf16[3,128,128]{2,1,0:T(8,128)(2,1)S(1)} %copy-done.4, ...), custom_call_target="tpu_custom_call" | custom-call | flops 1540000000 | bytes 5040000 | tf_op jit(solution)/shard_map/pallas_call | solution.py:83
  55.0 1.3 %shard_map.161.mir_ref = bf16[2304,128]{1,0:T(8,128)(2,1)S(1)} custom-call(bf16[2304,128]{1,0:T(8,128)(2,1)S(1)} %shard_map.160.e_ref, bf16[2304,128]{1,0:T(8,128)(2,1)S(1)} %get-tuple-element.24.hot_ref.hm_ref, bf16[1152,128]{1,0:T(8,128)(2,1)S(1)} %bitcast.48, bf16[3,128,128]{2,1,0:T(8,128)(2,1)S(1)} %copy-done.5, bf16[3,128,128]{2,1,0:T(8,128)(2,1)S(1)} %copy-done.4, ...), custom_call_target="tpu_custom_call" | custom-call | flops 1540000000 | bytes 5040000 | tf_op jit(solution)/shard_map/pallas_call | solution.py:83
  56.3 5.9 %shard_map.164 = bf16[169,4608]{1,0:T(8,128)(2,1)} custom-call(bf16[2304,128]{1,0:T(8,128)(2,1)S(1)} %shard_map.159.own_ref, bf16[2304,128]{1,0:T(8,128)(2,1)S(1)} %shard_map.161.mir_ref, bf16[2304,128]{1,0:T(8,128)(2,1)S(1)} %get-tuple-element.21.hot_ref.ho_ref, bf16[2304,128]{1,0:T(8,128)(2,1)S(1)} %get-tuple-element.24.hot_ref.hm_ref, ...), custom_call_target="tpu_custom_call" | custom-call | flops 7699999744 | bytes 25200000 | tf_op jit(solution)/shard_map/pallas_call | solution.py:83
  (31 shorter events, 0.3 us)
Async XLA Ops:
  0.0 10.3 %collective-permute-start = (bf16[64,128]{1,0:T(8,128)(2,1)}, bf16[64,128]{1,0:T(8,128)(2,1)S(1)}, u32[]{:S(2)}, u32[]{:S(2)}) collective-permute-start(bf16[64,128]{1,0:T(8,128)(2,1)} %h_ref.1), channel_id=1, source_target_pairs={{0,1},{1,0},{2,3},{3,2},{4,5},{5,4},{6,7},{7,6},{8,9},{9,8},{10,11... | collective-permute-start | bytes 49160 | tf_op jit(solution)/shard_map/ppermute | solution.py:17
  3.0 0.7 %copy-start.9 = (f32[4608]{0:T(1024)S(1)}, f32[4608]{0:T(1024)}, u32[]{:S(2)}) copy-start(f32[4608]{0:T(1024)} %param.18) | copy-start | bytes 55300
  3.7 0.7 %copy-start.10 = (s32[4608]{0:T(1024)S(1)}, s32[4608]{0:T(1024)}, u32[]{:S(2)}) copy-start(s32[4608]{0:T(1024)} %param.19) | copy-start | bytes 55300
  4.4 0.7 %copy-start.11 = (s32[4608]{0:T(1024)S(1)}, s32[4608]{0:T(1024)}, u32[]{:S(2)}) copy-start(s32[4608]{0:T(1024)} %param.20) | copy-start | bytes 55300
  5.2 0.7 %copy-start.12 = (s32[4608]{0:T(1024)S(1)}, s32[4608]{0:T(1024)}, u32[]{:S(2)}) copy-start(s32[4608]{0:T(1024)} %param.23) | copy-start | bytes 55300
  5.9 0.7 %copy-start.13 = (bf16[64,128]{1,0:T(8,128)(2,1)S(1)}, bf16[64,128]{1,0:T(8,128)(2,1)}, u32[]{:S(2)}) copy-start(bf16[64,128]{1,0:T(8,128)(2,1)} %h_ref.1) | copy-start | bytes 49156
  6.6 1.5 %copy-start.14 = (s32[2304]{0:T(1024)S(1)}, s32[2304]{0:T(1024)}, u32[]{:S(2)}) copy-start(s32[2304]{0:T(1024)} %param.21) | copy-start | bytes 27652
  6.6 1.5 %copy-start.15 = (s32[2304]{0:T(1024)S(1)}, s32[2304]{0:T(1024)}, u32[]{:S(2)}) copy-start(s32[2304]{0:T(1024)} %param.22) | copy-start | bytes 27652
  8.0 17.4 %collective-permute-start.5 = (bf16[64,1152]{1,0:T(8,128)(2,1)S(1)}, bf16[64,1152]{1,0:T(8,128)(2,1)S(1)}, u32[]{:S(2)}, u32[]{:S(2)}) collective-permute-start(bf16[64,1152]{1,0:T(8,128)(2,1)S(1)} %get-tuple-element.23.refs_0_), channel_id=1, source_target_pairs={{0,1},{1,0},{2,3},{3,2},{4,5},{5,4},{6,7},{7,6},{8,9},{9,8},{10,11... | collective-permute-start | bytes 442376 | tf_op jit(solution)/shard_map/ppermute | solution.py:17
  8.1 6.4 %copy-start.3 = (bf16[2304,128]{1,0:T(8,128)(2,1)S(1)}, bf16[2304,128]{1,0:T(8,128)(2,1)}, u32[]{:S(2)}) copy-start(bf16[2304,128]{1,0:T(8,128)(2,1)} %bond_ref.1) | copy-start | bytes 1769476
  10.3 10.4 %copy-start.8 = (bf16[128,169]{0,1:T(8,128)(2,1)S(1)}, bf16[128,169]{0,1:T(8,128)(2,1)}, u32[]{:S(2)}) copy-start(bf16[128,169]{0,1:T(8,128)(2,1)} %param.31) | copy-start | bytes 129796
  10.3 7.7 %collective-permute-start.2 = (bf16[2,1,1,64,128]{4,3,2,1,0:T(8,128)(2,1)S(1)}, bf16[2,1,1,64,128]{4,3,2,1,0:T(8,128)(2,1)S(1)}, u32[]{:S(2)}, u32[]{:S(2)}) collective-permute-start(bf16[2,1,1,64,128]{4,3,2,1,0:T(8,128)(2,1)S(1)} %bitcast.65), channel_id=1, source_target_pairs={{0,24},{8,0},{16,8},{24,16},{1,25},{9,1},{17,9},{25,17},{2,26},{10... | collective-permute-start | bytes 98312 | tf_op jit(solution)/shard_map/ppermute | solution.py:22
  14.5 5.7 %collective-permute-start.1 = (bf16[2,1,1,64,128]{4,3,2,1,0:T(8,128)(2,1)S(1)}, bf16[2,1,1,64,128]{4,3,2,1,0:T(8,128)(2,1)S(1)}, u32[]{:S(2)}, u32[]{:S(2)}) collective-permute-start(bf16[2,1,1,64,128]{4,3,2,1,0:T(8,128)(2,1)S(1)} %bitcast.66), channel_id=1, source_target_pairs={{0,8},{8,16},{16,24},{24,0},{1,9},{9,17},{17,25},{25,1},{2,10},{10... | collective-permute-start | bytes 98312 | tf_op jit(solution)/shard_map/ppermute | solution.py:22
  16.4 9.0 %collective-permute-start.6 = (bf16[3,3,128,128]{3,2,1,0:T(8,128)(2,1)S(1)}, bf16[3,3,128,128]{3,2,1,0:T(8,128)(2,1)S(1)}, u32[]{:S(2)}, u32[]{:S(2)}) collective-permute-start(bf16[3,3,128,128]{3,2,1,0:T(8,128)(2,1)S(1)} %bitcast.79), channel_id=1, source_target_pairs={{0,1},{1,0},{2,3},{3,2},{4,5},{5,4},{6,7},{7,6},{8,9},{9,8},{10,11... | collective-permute-start | bytes 884744 | tf_op jit(solution)/shard_map/ppermute | solution.py:17
  20.2 3.1 %collective-permute-start.4 = (bf16[2,3,1,64,128]{4,3,2,1,0:T(8,128)(2,1)S(1)}, bf16[2,3,1,64,128]{4,3,2,1,0:T(8,128)(2,1)S(1)}, u32[]{:S(2)}, u32[]{:S(2)}) collective-permute-start(bf16[2,3,1,64,128]{4,3,2,1,0:T(8,128)(2,1)S(1)} %pad_maximum_fusion.6), channel_id=1, source_target_pairs={{0,6},{2,0},{4,2},{6,4},{1,7},{3,1},{5,3},{7,5},{8,14},{10,8},{12,... | collective-permute-start | bytes 294920 | tf_op jit(solution)/shard_map/ppermute | solution.py:22
  20.2 5.1 %collective-permute-start.3 = (bf16[2,3,1,64,128]{4,3,2,1,0:T(8,128)(2,1)S(1)}, bf16[2,3,1,64,128]{4,3,2,1,0:T(8,128)(2,1)S(1)}, u32[]{:S(2)}, u32[]{:S(2)}) collective-permute-start(bf16[2,3,1,64,128]{4,3,2,1,0:T(8,128)(2,1)S(1)} %pad_maximum_fusion.6), channel_id=1, source_target_pairs={{0,2},{2,4},{4,6},{6,0},{1,3},{3,5},{5,7},{7,1},{8,10},{10,12},{12... | collective-permute-start | bytes 294920 | tf_op jit(solution)/shard_map/ppermute | solution.py:22
  20.7 4.7 %copy-start = (bf16[2,128,128]{2,1,0:T(8,128)(2,1)S(1)}, bf16[2,128,128]{2,1,0:T(8,128)(2,1)}, u32[]{:S(2)}) copy-start(bf16[2,128,128]{2,1,0:T(8,128)(2,1)} %refs_3_.3) | copy-start | bytes 196612
  20.8 4.7 %copy-start.1 = (bf16[2,128,128]{2,1,0:T(8,128)(2,1)S(1)}, bf16[2,128,128]{2,1,0:T(8,128)(2,1)}, u32[]{:S(2)}) copy-start(bf16[2,128,128]{2,1,0:T(8,128)(2,1)} %refs_4_.3) | copy-start | bytes 196612
  20.8 4.7 %copy-start.2 = (f32[2,128]{1,0:T(2,128)S(1)}, f32[2,128]{1,0:T(2,128)}, u32[]{:S(2)}) copy-start(f32[2,128]{1,0:T(2,128)} %refs_5_.3) | copy-start | bytes 3076
  23.2 12.3 %copy-start.4 = (bf16[3,128,128]{2,1,0:T(8,128)(2,1)S(1)}, bf16[3,128,128]{2,1,0:T(8,128)(2,1)}, u32[]{:S(2)}) copy-start(bf16[3,128,128]{2,1,0:T(8,128)(2,1)} %wl_ref.9) | copy-start | bytes 294916
  23.2 12.3 %copy-start.5 = (bf16[3,128,128]{2,1,0:T(8,128)(2,1)S(1)}, bf16[3,128,128]{2,1,0:T(8,128)(2,1)}, u32[]{:S(2)}) copy-start(bf16[3,128,128]{2,1,0:T(8,128)(2,1)} %wr_ref.1) | copy-start | bytes 294916
  23.2 12.3 %copy-start.6 = (bf16[3,128,128]{2,1,0:T(8,128)(2,1)S(1)}, bf16[3,128,128]{2,1,0:T(8,128)(2,1)}, u32[]{:S(2)}) copy-start(bf16[3,128,128]{2,1,0:T(8,128)(2,1)} %wi_ref.9) | copy-start | bytes 294916
  23.2 12.3 %copy-start.7 = (bf16[3,128,128]{2,1,0:T(8,128)(2,1)S(1)}, bf16[3,128,128]{2,1,0:T(8,128)(2,1)}, u32[]{:S(2)}) copy-start(bf16[3,128,128]{2,1,0:T(8,128)(2,1)} %wo_ref.9) | copy-start | bytes 294916
  26.1 6.5 %collective-permute-start.8 = (bf16[2,1,1,64,128]{4,3,2,1,0:T(8,128)(2,1)S(1)}, bf16[2,1,1,64,128]{4,3,2,1,0:T(8,128)(2,1)S(1)}, u32[]{:S(2)}, u32[]{:S(2)}) collective-permute-start(bf16[2,1,1,64,128]{4,3,2,1,0:T(8,128)(2,1)S(1)} %bitcast.59), channel_id=1, source_target_pairs={{0,24},{8,0},{16,8},{24,16},{1,25},{9,1},{17,9},{25,17},{2,26},{10... | collective-permute-start | bytes 98312 | tf_op jit(solution)/shard_map/ppermute | solution.py:22
  28.6 6.3 %collective-permute-start.7 = (bf16[2,1,1,64,128]{4,3,2,1,0:T(8,128)(2,1)S(1)}, bf16[2,1,1,64,128]{4,3,2,1,0:T(8,128)(2,1)S(1)}, u32[]{:S(2)}, u32[]{:S(2)}) collective-permute-start(bf16[2,1,1,64,128]{4,3,2,1,0:T(8,128)(2,1)S(1)} %bitcast.60), channel_id=1, source_target_pairs={{0,8},{8,16},{16,24},{24,0},{1,9},{9,17},{17,25},{25,1},{2,10},{10... | collective-permute-start | bytes 98312 | tf_op jit(solution)/shard_map/ppermute | solution.py:22
  28.7 11.3 %collective-permute-start.11 = (bf16[2,3,128,128]{3,2,1,0:T(8,128)(2,1)S(1)}, bf16[2,3,128,128]{3,2,1,0:T(8,128)(2,1)S(1)}, u32[]{:S(2)}, u32[]{:S(2)}) collective-permute-start(bf16[2,3,128,128]{3,2,1,0:T(8,128)(2,1)S(1)} %get-tuple-element.34), channel_id=1, source_target_pairs={{0,8},{8,16},{16,24},{24,0},{1,9},{9,17},{17,25},{25,1},{2,10},{10... | collective-permute-start | bytes 589832 | tf_op jit(solution)/shard_map/ppermute | solution.py:22
  28.8 11.3 %collective-permute-start.12 = (bf16[2,3,128,128]{3,2,1,0:T(8,128)(2,1)S(1)}, bf16[2,3,128,128]{3,2,1,0:T(8,128)(2,1)S(1)}, u32[]{:S(2)}, u32[]{:S(2)}) collective-permute-start(bf16[2,3,128,128]{3,2,1,0:T(8,128)(2,1)S(1)} %get-tuple-element.35), channel_id=1, source_target_pairs={{0,24},{8,0},{16,8},{24,16},{1,25},{9,1},{17,9},{25,17},{2,26},{10... | collective-permute-start | bytes 589832 | tf_op jit(solution)/shard_map/ppermute | solution.py:22
  34.9 2.4 %collective-permute-start.10 = (bf16[2,3,1,64,128]{4,3,2,1,0:T(8,128)(2,1)S(1)}, bf16[2,3,1,64,128]{4,3,2,1,0:T(8,128)(2,1)S(1)}, u32[]{:S(2)}, u32[]{:S(2)}) collective-permute-start(bf16[2,3,1,64,128]{4,3,2,1,0:T(8,128)(2,1)S(1)} %pad_maximum_fusion.7), channel_id=1, source_target_pairs={{0,6},{2,0},{4,2},{6,4},{1,7},{3,1},{5,3},{7,5},{8,14},{10,8},{12,... | collective-permute-start | bytes 294920 | tf_op jit(solution)/shard_map/ppermute | solution.py:22
  35.0 5.0 %collective-permute-start.9 = (bf16[2,3,1,64,128]{4,3,2,1,0:T(8,128)(2,1)S(1)}, bf16[2,3,1,64,128]{4,3,2,1,0:T(8,128)(2,1)S(1)}, u32[]{:S(2)}, u32[]{:S(2)}) collective-permute-start(bf16[2,3,1,64,128]{4,3,2,1,0:T(8,128)(2,1)S(1)} %pad_maximum_fusion.7), channel_id=1, source_target_pairs={{0,2},{2,4},{4,6},{6,0},{1,3},{3,5},{5,7},{7,1},{8,10},{10,12},{12... | collective-permute-start | bytes 294920 | tf_op jit(solution)/shard_map/ppermute | solution.py:22
  40.7 4.5 %collective-permute-start.16 = (bf16[2,1,1,64,128]{4,3,2,1,0:T(8,128)(2,1)S(1)}, bf16[2,1,1,64,128]{4,3,2,1,0:T(8,128)(2,1)S(1)}, u32[]{:S(2)}, u32[]{:S(2)}) collective-permute-start(bf16[2,1,1,64,128]{4,3,2,1,0:T(8,128)(2,1)S(1)} %bitcast.50), channel_id=1, source_target_pairs={{0,24},{8,0},{16,8},{24,16},{1,25},{9,1},{17,9},{25,17},{2,26},{10... | collective-permute-start | bytes 98312 | tf_op jit(solution)/shard_map/ppermute | solution.py:22
  43.4 5.7 %collective-permute-start.15 = (bf16[2,1,1,64,128]{4,3,2,1,0:T(8,128)(2,1)S(1)}, bf16[2,1,1,64,128]{4,3,2,1,0:T(8,128)(2,1)S(1)}, u32[]{:S(2)}, u32[]{:S(2)}) collective-permute-start(bf16[2,1,1,64,128]{4,3,2,1,0:T(8,128)(2,1)S(1)} %bitcast.51), channel_id=1, source_target_pairs={{0,8},{8,16},{16,24},{24,0},{1,9},{9,17},{17,25},{25,1},{2,10},{10... | collective-permute-start | bytes 98312 | tf_op jit(solution)/shard_map/ppermute | solution.py:22
  43.5 10.1 %collective-permute-start.13 = (bf16[2,3,128,128]{3,2,1,0:T(8,128)(2,1)S(1)}, bf16[2,3,128,128]{3,2,1,0:T(8,128)(2,1)S(1)}, u32[]{:S(2)}, u32[]{:S(2)}) collective-permute-start(bf16[2,3,128,128]{3,2,1,0:T(8,128)(2,1)S(1)} %get-tuple-element.31), channel_id=1, source_target_pairs={{0,2},{2,4},{4,6},{6,0},{1,3},{3,5},{5,7},{7,1},{8,10},{10,12},{12... | collective-permute-start | bytes 589832 | tf_op jit(solution)/shard_map/ppermute | solution.py:22
  43.5 10.0 %collective-permute-start.14 = (bf16[2,3,128,128]{3,2,1,0:T(8,128)(2,1)S(1)}, bf16[2,3,128,128]{3,2,1,0:T(8,128)(2,1)S(1)}, u32[]{:S(2)}, u32[]{:S(2)}) collective-permute-start(bf16[2,3,128,128]{3,2,1,0:T(8,128)(2,1)S(1)} %get-tuple-element.32), channel_id=1, source_target_pairs={{0,6},{2,0},{4,2},{6,4},{1,7},{3,1},{5,3},{7,5},{8,14},{10,8},{12,... | collective-permute-start | bytes 589832 | tf_op jit(solution)/shard_map/ppermute | solution.py:22
  49.1 3.2 %collective-permute-start.18 = (bf16[2,3,1,64,128]{4,3,2,1,0:T(8,128)(2,1)S(1)}, bf16[2,3,1,64,128]{4,3,2,1,0:T(8,128)(2,1)S(1)}, u32[]{:S(2)}, u32[]{:S(2)}) collective-permute-start(bf16[2,3,1,64,128]{4,3,2,1,0:T(8,128)(2,1)S(1)} %pad_maximum_fusion.8), channel_id=1, source_target_pairs={{0,6},{2,0},{4,2},{6,4},{1,7},{3,1},{5,3},{7,5},{8,14},{10,8},{12,... | collective-permute-start | bytes 294920 | tf_op jit(solution)/shard_map/ppermute | solution.py:22
  49.2 4.3 %collective-permute-start.17 = (bf16[2,3,1,64,128]{4,3,2,1,0:T(8,128)(2,1)S(1)}, bf16[2,3,1,64,128]{4,3,2,1,0:T(8,128)(2,1)S(1)}, u32[]{:S(2)}, u32[]{:S(2)}) collective-permute-start(bf16[2,3,1,64,128]{4,3,2,1,0:T(8,128)(2,1)S(1)} %pad_maximum_fusion.8), channel_id=1, source_target_pairs={{0,2},{2,4},{4,6},{6,0},{1,3},{3,5},{5,7},{7,1},{8,10},{10,12},{12... | collective-permute-start | bytes 294920 | tf_op jit(solution)/shard_map/ppermute | solution.py:22

commit v4 on v3

--- a/solution.py
+++ b/solution.py
@@ -17,33 +17,38 @@
     return lax.ppermute(value, axis, [(0, 1), (1, 0)])
 
 
-def moved(value, axis, steps):
-    count = lax.axis_size(axis)
-    return lax.ppermute(value, axis, [(i, (i + steps) % count) for i in range(count)])
-
-
-def with_halo(block, axis, dim):
-    low = moved(block, axis, 1)
-    high = moved(block, axis, -1)
-    return jnp.concatenate([low, block, high], axis=dim)
+def moved(value, row_step, col_step):
+    rows, cols = lax.axis_size("gx"), lax.axis_size("gy")
+    pairs = [
+        (x * cols + y, (x + row_step) % rows * cols + (y + col_step) % cols)
+        for x in range(rows)
+        for y in range(cols)
+    ]
+    return lax.ppermute(value, ("gx", "gy"), pairs)
+
+
+STEPS = [(1, 1), (1, -1), (-1, 1), (-1, -1), (1, 0), (-1, 0), (0, 1), (0, -1)]
+
+
+def framed(pieces, centre):
+    pieces = {**pieces, (0, 0): centre}
+    return jnp.stack(
+        [jnp.stack([pieces[(i, j)] for j in (1, 0, -1)], axis=1) for i in (1, 0, -1)], axis=1
+    )
 
 
 def ghosts_of(sheets, centre=None):
-    low, high = moved(sheets, "gx", 1), moved(sheets, "gx", -1)
+    pieces = {step: moved(sheets, *step) for step in STEPS}
     centre = sheets if centre is None else centre
-    framed = with_halo(jnp.concatenate([low, centre, high], axis=1), "gy", 2)
-    return framed.reshape(-1, sheets.shape[-1])
-
-
-def across_rows(outgoing, crossed):
+    apart = {step: p.reshape(2, -1, p.shape[1]) for step, p in pieces.items()}
+    table = framed(apart, centre.reshape(2, -1, centre.shape[1]))
+    return table.reshape(-1, sheets.shape[1])
+
+
+def deliver(outgoing, crossed):
     sheets = jnp.stack([outgoing[0], crossed])
-    rows = [moved(sheets[:, i], "gx", i - 1) if i != 1 else sheets[:, i] for i in (2, 1, 0)]
-    return jnp.stack(rows, axis=1)
-
-
-def across_columns(shifted):
-    cols = [moved(shifted[:, :, i], "gy", i - 1) if i != 1 else shifted[:, :, i] for i in (2, 1, 0)]
-    return jnp.stack(cols, axis=2)
+    pieces = {(i, j): moved(sheets[:, i + 1, j + 1], i, j) for i, j in STEPS}
+    return framed(pieces, sheets[:, 1, 1])
 
 
 def dot(a, b):
@@ -74,7 +79,7 @@
     return iota(shape, dim).astype(F32)
 
 
-def call(body, outs, *args, after=(), scratch=(), us=1.0):
+def call(body, outs, *args, after=(), space=pltpu.VMEM, scratch=(), us=1.0):
     used = len(args)
 
     def ordered_body(*refs):
@@ -83,7 +88,7 @@
     return pl.pallas_call(
         ordered_body if after else body,
         out_shape=outs,
-        in_specs=[pl.BlockSpec(memory_space=pltpu.VMEM)] * used
+        in_specs=[pl.BlockSpec(memory_space=space)] * used
         + [pl.BlockSpec(memory_space=pl.ANY)] * len(after),
         scratch_shapes=list(scratch),
         compiler_params=pltpu.CompilerParams(vmem_limit_bytes=VMEM_LIMIT),
@@ -133,12 +138,11 @@
         ).astype(BF16)
 
 
-def slots_body(nb_ref, kind_ref, recv_ref, dist_ref, h_ref, adj_ref, pack_ref, h_out_ref):
+def slots_body(both_ref, adj_ref, pack_ref):
     fan, atoms = pack_ref.shape
-    h_out_ref[...] = h_ref[...]
-    flat = nb_ref[...] | (kind_ref[...] << 11) | ((recv_ref[...] & 127) << 13)
-    pack = transposed(folded(as_row(flat.astype(F32)), atoms, fan)).astype(jnp.int32)
-    dist = transposed(folded(as_row(dist_ref[...]), atoms, fan))
+    half = both_ref.shape[0] // 2
+    pack = transposed(folded(as_row(both_ref[:half, :]), atoms, fan)).astype(jnp.int32)
+    dist = transposed(folded(as_row(both_ref[half:, :]), atoms, fan))
     pack_ref[...] = pack
     peer = (pack & 63).astype(F32)
     off = ((pack & 2047) >> 6).astype(F32)
@@ -328,8 +332,12 @@
         out_ref[span, :] = rms_norm(state.astype(F32) + dot(gate, w_out)).astype(BF16)
 
 
-def edge_body(layer):
-    def body(e_ref, hot_ref, ghost_ref, wl_ref, wg_ref, wi_ref, wo_ref, out_ref, table):
+def edge_body(layer, hand_on=False):
+    def body(e_ref, hot_ref, ghost_ref, wl_ref, wg_ref, wi_ref, wo_ref, *refs):
+        if hand_on:
+            refs[2][...] = refs[0][...]
+            refs = (refs[1], refs[3])
+        out_ref, table = refs
         edge_all(
             e_ref, hot_ref, ghost_ref, wl_ref[layer], wg_ref[layer], wi_ref[layer], wo_ref[layer],
             table, out_ref,
@@ -420,24 +428,27 @@
     send, own = tiles(send_pos), tiles(own_rows)
     nb, kind, recv, dist = map(tiles, (neighbours, slot_kind, recv_pos, pair_dist))
     opposite = swapped(atom_feats, "layer")
-    adjacency, pack, hidden = call(
+    both = jnp.concatenate(
+        [(nb | (kind << 11) | ((recv & 127) << 13)).astype(F32), dist], axis=0
+    )
+    adjacency, pack = call(
         slots_body,
-        (array(atoms, ghosts), array(fan, atoms, dtype=jnp.int32), array(atoms, channels)),
-        nb, kind, recv, dist, atom_feats,
-        us=3.0,
+        (array(atoms, ghosts), array(fan, atoms, dtype=jnp.int32)),
+        both,
+        us=2.0,
+    )
+    ordered, hidden = call(
+        order_body,
+        (array(owned, channels), array(atoms, channels)),
+        send, bond_embed, atom_feats,
+        after=(pack,),
+        us=2.0,
     )
     other = swapped(adjacency, "layer")
     sheets = jnp.concatenate([hidden, opposite], axis=0)
-    ordered, centre = call(
-        order_body,
-        (array(owned, channels), array(2 * atoms, channels)),
-        send, bond_embed, sheets,
-        us=3.5,
-    )
     outgoing = ordered.reshape(2, 3, 3, cap, channels)
     crossed = swapped(outgoing[1], "layer")
-    shifted = across_rows(outgoing, crossed)
-    mirror = across_columns(shifted).reshape(owned, channels)
+    mirror = deliver(outgoing, crossed).reshape(owned, channels)
     hot_own, hot_mir, place = call(
         pairs_body,
         (array(owned, 128), array(owned, 128), array(fan, atoms, dtype=F32)),
@@ -456,16 +467,16 @@
         pack, place, w_block.T,
         us=2.5,
     )
-    centre = centre.reshape(2, 1, 1, atoms, channels)
     table = pltpu.VMEM((2 * ghosts, 2 * channels), BF16)
+    mirror_ghosts = []
     for layer in range(2):
-        ghost = ghosts_of(sheets.reshape(2, 1, 1, atoms, channels), centre)
-        centre = None
+        ghost = ghosts_of(sheets)
+        mirror_ghosts.append(ghost)
         sheets = call(
             node_body(layer),
             array(2 * atoms, channels),
             adjacency, other, ghost, w_msg, w_upd, node_gain,
-            after=(shifted, perm) if layer else (crossed,),
+            after=(perm,) if layer else (crossed,),
             us=0.6,
         )
         ordered = call(
@@ -475,14 +486,16 @@
             scratch=[table],
             us=1.4,
         )
-        mirror = call(
-            edge_body(layer),
-            array(owned, channels),
-            mirror, hot_mir, ghost, w_right, w_left, w_edge_in, w_edge_out,
+    centre = sheets
+    for layer in range(2):
+        mirror, centre = call(
+            edge_body(layer, True),
+            (array(owned, channels), array(2 * atoms, channels)),
+            mirror, hot_mir, mirror_ghosts[layer], w_right, w_left, w_edge_in, w_edge_out, centre,
             scratch=[table],
             us=1.4,
         )
-    ghost = ghosts_of(sheets.reshape(2, 1, 1, atoms, channels))
+    ghost = ghosts_of(sheets, centre)
     return call(
         final_body(2),
         array(block, slots),

time: 62.6 us -> 77 us (1.23)
  starting transfers between devices: 21.4 us -> 38.6 us
  local copies, waits for them, and re-layouts: 3.83 us -> 0.18 us
  other arithmetic: 0.34 us -> 1.93 us
    ppermute x16 -> x32, starting transfers between devices: 16.7 us -> 33.5 us  [moved(): return lax.ppermute(value, ('gx', 'gy'), pairs)]
    unnamed x33 -> x31, local copies, waits for them, and re-layouts: 3.68 us -> 0.08 us
    convert_element_type x0 -> x1, other arithmetic: none -> 0.77 us  [shards(): (nb | kind << 11 | (recv & 127) << 13).astype(F32)]
    ppermute x16 -> x32, waiting for transfers between devices: 16 us -> 15.3 us  [moved(): return lax.ppermute(value, ('gx', 'gy'), pairs)]
  transfers between devices with their start and end apart: 19 -> 35, of which waited for: 8 -> 11; matrix products, arithmetic and copies ran while one was open for 0% -> 3% of each run, Pallas kernels for 17% -> 18%
where the time goes in v4:
time: 77 us; the launch traced here: 76.7 us
  starting transfers between devices  38.6 us (50%)
  Pallas kernels  20.2 us (26%)
  waiting for transfers between devices  15.3 us (20%)
  other arithmetic  1.93 us (3%)
    ppermute x32, starting transfers between devices, moved(): return lax.ppermute(value, ('gx', 'gy'), pairs)  33.5 us
    pallas_call x11, Pallas kernels, call(): pl.pallas_call(ordered_body if after else body, out_shape=outs, in_specs=...  20.2 us
    ppermute x32, waiting for transfers between devices, moved(): return lax.ppermute(value, ('gx', 'gy'), pairs)  15.3 us
    ppermute x3, starting transfers between devices, swapped(): return lax.ppermute(value, axis, [(0, 1), (1, 0)])  5.09 us
  transfers between devices with their start and end apart: 35, of which 11 were waited for; matrix products, arithmetic and copies ran while one was open for 3% of the time, Pallas kernels for 18%

profile of v4, /device:TPU:0, one launch (start us, length us, event | category | flops | bytes accessed | tf_op | source)
XLA Modules:
  0.0 76.7 jit_solution(5863144383911365377)
XLA Ops:
  0.0 3.0 %collective-permute-start = (bf16[64,128]{1,0:T(8,128)(2,1)}, bf16[64,128]{1,0:T(8,128)(2,1)S(1)}, u32[]{:S(2)}, u32[]{:S(2)}) collective-permute-start(bf16[64,128]{1,0:T(8,128)(2,1)} %refs_2_.1), channel_id=1, source_target_pairs={{0,1},{1,0},{2,3},{3,2},{4,5},{5,4},{6,7},{7,6},{8,9},{9,8},{10,11... | collective-permute-start | bytes 49160 | tf_op jit(solution)/shard_map/ppermute | solution.py:17
  3.0 0.8 %or_convert_fusion = f32[36,128]{1,0:T(8,128)S(1)} fusion(s32[4608]{0:T(1024)} %param.23, s32[4608]{0:T(1024)} %param.20, s32[4608]{0:T(1024)} %param.19), kind=kLoop, calls=%fused_computation.51 | loop fusion | flops 27648 | bytes 73728 | tf_op jit(solution)/shard_map/convert_element_type | solution.py:432
  3.7 0.7 pad_maximum_fusion.5.both_ref
  4.5 0.0 copy-start.13
  4.5 1.4 %shard_map.154 = (bf16[64,1152]{1,0:T(8,128)(2,1)S(1)}, s32[72,64]{1,0:T(8,128)S(1)}) custom-call(f32[72,128]{1,0:T(8,128)S(1)} %pad_maximum_fusion.5.both_ref), custom_call_target="tpu_custom_call" | custom-call | flops 2200000000 | bytes 7200000 | tf_op jit(solution)/shard_map/pallas_call | solution.py:88
  5.9 0.1 collective-permute-start.9
  6.0 0.0 copy-start.2
  6.0 0.0 copy-start.3
  6.0 0.0 copy-start.4
  6.0 0.0 copy-start.14
  6.0 1.9 %shard_map.155 = (bf16[2304,128]{1,0:T(8,128)(2,1)S(1)}, bf16[64,128]{1,0:T(8,128)(2,1)S(1)}) custom-call(s32[18,128]{1,0:T(8,128)S(1)} %bitcast.179, bf16[2304,128]{1,0:T(8,128)(2,1)S(1)} %copy-done.6, bf16[64,128]{1,0:T(8,128)(2,1)S(1)} %copy-done.12, s32[72,64]{1,0:T(8,128)S(1)} %get-tuple-element.21.refs_3_.pack_ref), custom_call_target="tpu_custom_call" | custom-call | flops 2200000000 | bytes 7200000 | tf_op jit(solution)/shard_map/pallas_call | solution.py:88
  8.0 2.1 %collective-permute-start.10 = (bf16[3,3,128,128]{3,2,1,0:T(8,128)(2,1)S(1)}, bf16[3,3,128,128]{3,2,1,0:T(8,128)(2,1)S(1)}, u32[]{:S(2)}, u32[]{:S(2)}) collective-permute-start(bf16[3,3,128,128]{3,2,1,0:T(8,128)(2,1)S(1)} %bitcast.183), channel_id=1, source_target_pairs={{0,1},{1,0},{2,3},{3,2},{4,5},{5,4},{6,7},{7,6},{8,9},{9,8},{10,11... | collective-permute-start | bytes 884744 | tf_op jit(solution)/shard_map/ppermute | solution.py:17
  10.0 0.0 copy-start.11
  10.1 2.2 %shard_map.156 = (bf16[2304,128]{1,0:T(8,128)(2,1)S(1)}, bf16[2304,128]{1,0:T(8,128)(2,1)S(1)}, f32[72,64]{1,0:T(8,128)S(1)}) custom-call(s32[18,128]{1,0:T(8,128)S(1)} %bitcast.180, s32[18,128]{1,0:T(8,128)S(1)} %bitcast.181, s32[36,128]{1,0:T(8,128)S(1)} %bitcast.177, s32[36,128]{1,0:T(8,128)S(1)} %bitcast.176, s32[36,128]{1,0:T(8,128)S(1)} %bitcast.175, ...), custom_call_target="tpu_custom_call" | custom-call | flops 2750000128 | bytes 9000000 | tf_op jit(solution)/shard_map/pallas_call | solution.py:88
  12.3 3.2 %collective-permute-start.8 = (bf16[128,128]{1,0:T(8,128)(2,1)S(1)}, bf16[128,128]{1,0:T(8,128)(2,1)S(1)}, u32[]{:S(2)}, u32[]{:S(2)}) collective-permute-start(bf16[128,128]{1,0:T(8,128)(2,1)S(1)} %constant_dynamic-update-slice_fusion), channel_id=1, source_target_pairs={{0,30},{2,24},{4,26},{6,28},{8,6},{10,0},{12,2},{14,4},{16,14},{18... | collective-permute-start | bytes 98312 | tf_op jit(solution)/shard_map/ppermute | solution.py:27
  15.5 0.5 collective-permute-start.7
  16.0 0.3 collective-permute-start.6
  16.3 2.4 %shard_map.160 = (bf16[2304,128]{1,0:T(8,128)(2,1)S(1)}, bf16[2304,128]{1,0:T(8,128)(2,1)S(1)}, bf16[4608,144]{1,0:T(8,128)(2,1)S(1)}, f32[72,64]{1,0:T(8,128)S(1)}, bf16[169,256]{1,0:T(8,128)(2,1)S(1)}) custom-call(s32[72,64]{1,0:T(8,128)S(1)} %get-tuple-element.21.refs_3_.pack_ref, f32[72,64]{1,0:T(8,128)S(1)} %get-tuple-element.27.place_ref, ...), custom_call_target="tpu_custom_call" | custom-call | flops 2750000128 | bytes 9000000 | tf_op jit(solution)/shard_map/pallas_call | solution.py:88
  18.8 1.4 %collective-permute-start.5 = (bf16[128,128]{1,0:T(8,128)(2,1)S(1)}, bf16[128,128]{1,0:T(8,128)(2,1)S(1)}, u32[]{:S(2)}, u32[]{:S(2)}) collective-permute-start(bf16[128,128]{1,0:T(8,128)(2,1)S(1)} %constant_dynamic-update-slice_fusion), channel_id=1, source_target_pairs={{0,6},{2,0},{4,2},{6,4},{8,14},{10,8},{12,10},{14,12},{16,22},{18,... | collective-permute-start | bytes 98312 | tf_op jit(solution)/shard_map/ppermute | solution.py:27
  20.2 0.1 collective-permute-done.6
  20.3 2.6 %collective-permute-start.3 = (bf16[128,128]{1,0:T(8,128)(2,1)S(1)}, bf16[128,128]{1,0:T(8,128)(2,1)S(1)}, u32[]{:S(2)}, u32[]{:S(2)}) collective-permute-start(bf16[128,128]{1,0:T(8,128)(2,1)S(1)} %constant_dynamic-update-slice_fusion), channel_id=1, source_target_pairs={{0,14},{2,8},{4,10},{6,12},{8,22},{10,16},{12,18},{14,20},{16,30},... | collective-permute-start | bytes 98312 | tf_op jit(solution)/shard_map/ppermute | solution.py:27
  23.0 1.5 %collective-permute-start.2 = (bf16[128,128]{1,0:T(8,128)(2,1)S(1)}, bf16[128,128]{1,0:T(8,128)(2,1)S(1)}, u32[]{:S(2)}, u32[]{:S(2)}) collective-permute-start(bf16[128,128]{1,0:T(8,128)(2,1)S(1)} %constant_dynamic-update-slice_fusion), channel_id=1, source_target_pairs={{0,8},{2,10},{4,12},{6,14},{8,16},{10,18},{12,20},{14,22},{16,24},... | collective-permute-start | bytes 98312 | tf_op jit(solution)/shard_map/ppermute | solution.py:27
  24.5 0.6 collective-permute-start.1
  25.2 0.3 collective-permute-done.3
  25.4 3.6 %collective-permute-done.2 = bf16[128,128]{1,0:T(8,128)(2,1)S(1)} collective-permute-done((bf16[128,128]{1,0:T(8,128)(2,1)S(1)}, bf16[128,128]{1,0:T(8,128)(2,1)S(1)}, u32[]{:S(2)}, u32[]{:S(2)}) %collective-permute-start.2) | collective-permute-done | bytes 32800 | tf_op jit(solution)/shard_map/ppermute | solution.py:27
  29.0 1.5 %collective-permute-done.1 = bf16[128,128]{1,0:T(8,128)(2,1)S(1)} collective-permute-done((bf16[128,128]{1,0:T(8,128)(2,1)S(1)}, bf16[128,128]{1,0:T(8,128)(2,1)S(1)}, u32[]{:S(2)}, u32[]{:S(2)}) %collective-permute-start.1) | collective-permute-done | bytes 32800 | tf_op jit(solution)/shard_map/ppermute | solution.py:27
  30.7 0.0 copy-start.1
  30.7 0.0 copy-start.5
  30.7 1.3 %shard_map.157.e_ref = bf16[2304,128]{1,0:T(8,128)(2,1)S(1)} custom-call(bf16[2304,128]{1,0:T(8,128)(2,1)S(1)} %get-tuple-element.22.e_ref, bf16[2304,128]{1,0:T(8,128)(2,1)S(1)} %get-tuple-element.23.hot_ref.ho_ref, bf16[1152,128]{1,0:T(8,128)(2,1)S(1)} %bitcast.168, bf16[3,128,128]{2,1,0:T(8,128)(2,1)S(1)} %copy-done.7, ...), custom_call_target="tpu_custom_call" | custom-call | flops 1540000000 | bytes 5040000 | tf_op jit(solution)/shard_map/pallas_call | solution.py:88
  32.0 0.6 shard_map.158
  32.6 0.1 collective-permute-start.18
  32.7 0.6 collective-permute-start.17
  33.3 0.9 %collective-permute-start.16 = (bf16[128,128]{1,0:T(8,128)(2,1)S(1)}, bf16[128,128]{1,0:T(8,128)(2,1)S(1)}, u32[]{:S(2)}, u32[]{:S(2)}) collective-permute-start(bf16[128,128]{1,0:T(8,128)(2,1)S(1)} %shard_map.158), channel_id=1, source_target_pairs={{0,26},{2,28},{4,30},{6,24},{8,2},{10,4},{12,6},{14,0},{16,10},{18... | collective-permute-start | bytes 98312 | tf_op jit(solution)/shard_map/ppermute | solution.py:27
  34.1 2.0 %collective-permute-start.15 = (bf16[128,128]{1,0:T(8,128)(2,1)S(1)}, bf16[128,128]{1,0:T(8,128)(2,1)S(1)}, u32[]{:S(2)}, u32[]{:S(2)}) collective-permute-start(bf16[128,128]{1,0:T(8,128)(2,1)S(1)} %shard_map.158), channel_id=1, source_target_pairs={{0,6},{2,0},{4,2},{6,4},{8,14},{10,8},{12,10},{14,12},{16,22},{18,... | collective-permute-start | bytes 98312 | tf_op jit(solution)/shard_map/ppermute | solution.py:27
  36.2 0.1 fusion.15
  36.3 1.5 %collective-permute-start.13 = (bf16[128,128]{1,0:T(8,128)(2,1)S(1)}, bf16[128,128]{1,0:T(8,128)(2,1)S(1)}, u32[]{:S(2)}, u32[]{:S(2)}) collective-permute-start(bf16[128,128]{1,0:T(8,128)(2,1)S(1)} %shard_map.158), channel_id=1, source_target_pairs={{0,14},{2,8},{4,10},{6,12},{8,22},{10,16},{12,18},{14,20},{16,30},... | collective-permute-start | bytes 98312 | tf_op jit(solution)/shard_map/ppermute | solution.py:27
  37.8 1.5 %collective-permute-start.12 = (bf16[128,128]{1,0:T(8,128)(2,1)S(1)}, bf16[128,128]{1,0:T(8,128)(2,1)S(1)}, u32[]{:S(2)}, u32[]{:S(2)}) collective-permute-start(bf16[128,128]{1,0:T(8,128)(2,1)S(1)} %shard_map.158), channel_id=1, source_target_pairs={{0,8},{2,10},{4,12},{6,14},{8,16},{10,18},{12,20},{14,22},{16,24},... | collective-permute-start | bytes 98312 | tf_op jit(solution)/shard_map/ppermute | solution.py:27
  39.4 3.1 %collective-permute-start.19 = (bf16[2,128,128]{2,1,0:T(8,128)(2,1)S(1)}, bf16[2,128,128]{2,1,0:T(8,128)(2,1)S(1)}, u32[]{:S(2)}, u32[]{:S(2)}) collective-permute-start(bf16[2,128,128]{2,1,0:T(8,128)(2,1)S(1)} %get-tuple-element.37), channel_id=1, source_target_pairs={{0,10},{2,12},{4,14},{6,8},{8,18},{10,20},{12,22},{14,16},{16,26},... | collective-permute-start | bytes 196616 | tf_op jit(solution)/shard_map/ppermute | solution.py:27
  42.4 1.3 %collective-permute-start.20 = (bf16[2,128,128]{2,1,0:T(8,128)(2,1)S(1)}, bf16[2,128,128]{2,1,0:T(8,128)(2,1)S(1)}, u32[]{:S(2)}, u32[]{:S(2)}) collective-permute-start(bf16[2,128,128]{2,1,0:T(8,128)(2,1)S(1)} %get-tuple-element.38), channel_id=1, source_target_pairs={{0,8},{2,10},{4,12},{6,14},{8,16},{10,18},{12,20},{14,22},{16,24},... | collective-permute-start | bytes 196616 | tf_op jit(solution)/shard_map/ppermute | solution.py:27
  43.8 1.6 %collective-permute-done.11 = bf16[128,128]{1,0:T(8,128)(2,1)S(1)} collective-permute-done((bf16[128,128]{1,0:T(8,128)(2,1)S(1)}, bf16[128,128]{1,0:T(8,128)(2,1)S(1)}, u32[]{:S(2)}, u32[]{:S(2)}) %collective-permute-start.11) | collective-permute-done | bytes 32800 | tf_op jit(solution)/shard_map/ppermute | solution.py:27
  45.5 0.6 shard_map.161.refs_0_
  46.1 0.1 collective-permute-start.34
  46.2 1.0 %collective-permute-start.33 = (bf16[128,128]{1,0:T(8,128)(2,1)S(1)}, bf16[128,128]{1,0:T(8,128)(2,1)S(1)}, u32[]{:S(2)}, u32[]{:S(2)}) collective-permute-start(bf16[128,128]{1,0:T(8,128)(2,1)S(1)} %shard_map.161.refs_0_), channel_id=1, source_target_pairs={{0,24},{2,26},{4,28},{6,30},{8,0},{10,2},{12,4},{14,6},{16,8},{18,... | collective-permute-start | bytes 98312 | tf_op jit(solution)/shard_map/ppermute | solution.py:27
  47.2 1.1 %collective-permute-start.32 = (bf16[128,128]{1,0:T(8,128)(2,1)S(1)}, bf16[128,128]{1,0:T(8,128)(2,1)S(1)}, u32[]{:S(2)}, u32[]{:S(2)}) collective-permute-start(bf16[128,128]{1,0:T(8,128)(2,1)S(1)} %shard_map.161.refs_0_), channel_id=1, source_target_pairs={{0,26},{2,28},{4,30},{6,24},{8,2},{10,4},{12,6},{14,0},{16,10},{18... | collective-permute-start | bytes 98312 | tf_op jit(solution)/shard_map/ppermute | solution.py:27
  48.3 1.3 %shard_map.159.own_ref = bf16[2304,128]{1,0:T(8,128)(2,1)S(1)} custom-call(bf16[2304,128]{1,0:T(8,128)(2,1)S(1)} %shard_map.157.e_ref, bf16[2304,128]{1,0:T(8,128)(2,1)S(1)} %get-tuple-element.23.hot_ref.ho_ref, bf16[1152,128]{1,0:T(8,128)(2,1)S(1)} %bitcast.165, bf16[3,128,128]{2,1,0:T(8,128)(2,1)S(1)} %copy-done.7, bf16[3,128,128]{2,1,0:T(8,128)(2,1)S(1)} %copy-done.8, ...), custom_call_target="tpu_custom_call" | custom-call | flops 1540000000 | bytes 5040000 | tf_op jit(solution)/shard_map/pallas_call | solution.py:88
  49.6 1.6 %collective-permute-start.29 = (bf16[128,128]{1,0:T(8,128)(2,1)S(1)}, bf16[128,128]{1,0:T(8,128)(2,1)S(1)}, u32[]{:S(2)}, u32[]{:S(2)}) collective-permute-start(bf16[128,128]{1,0:T(8,128)(2,1)S(1)} %shard_map.161.refs_0_), channel_id=1, source_target_pairs={{0,14},{2,8},{4,10},{6,12},{8,22},{10,16},{12,18},{14,20},{16,30},... | collective-permute-start | bytes 98312 | tf_op jit(solution)/shard_map/ppermute | solution.py:27
  51.2 1.0 %collective-permute-start.28 = (bf16[128,128]{1,0:T(8,128)(2,1)S(1)}, bf16[128,128]{1,0:T(8,128)(2,1)S(1)}, u32[]{:S(2)}, u32[]{:S(2)}) collective-permute-start(bf16[128,128]{1,0:T(8,128)(2,1)S(1)} %shard_map.161.refs_0_), channel_id=1, source_target_pairs={{0,8},{2,10},{4,12},{6,14},{8,16},{10,18},{12,20},{14,22},{16,24},... | collective-permute-start | bytes 98312 | tf_op jit(solution)/shard_map/ppermute | solution.py:27
  52.3 0.6 collective-permute-start.27
  52.9 1.9 %collective-permute-done.29 = bf16[128,128]{1,0:T(8,128)(2,1)S(1)} collective-permute-done((bf16[128,128]{1,0:T(8,128)(2,1)S(1)}, bf16[128,128]{1,0:T(8,128)(2,1)S(1)}, u32[]{:S(2)}, u32[]{:S(2)}) %collective-permute-start.29) | collective-permute-done | bytes 32800 | tf_op jit(solution)/shard_map/ppermute | solution.py:27
  54.8 1.2 %collective-permute-start.21 = (bf16[2,128,128]{2,1,0:T(8,128)(2,1)S(1)}, bf16[2,128,128]{2,1,0:T(8,128)(2,1)S(1)}, u32[]{:S(2)}, u32[]{:S(2)}) collective-permute-start(bf16[2,128,128]{2,1,0:T(8,128)(2,1)S(1)} %get-tuple-element.39), channel_id=1, source_target_pairs={{0,14},{2,8},{4,10},{6,12},{8,22},{10,16},{12,18},{14,20},{16,30},... | collective-permute-start | bytes 196616 | tf_op jit(solution)/shard_map/ppermute | solution.py:27
  56.0 0.9 %collective-permute-done.28 = bf16[128,128]{1,0:T(8,128)(2,1)S(1)} collective-permute-done((bf16[128,128]{1,0:T(8,128)(2,1)S(1)}, bf16[128,128]{1,0:T(8,128)(2,1)S(1)}, u32[]{:S(2)}, u32[]{:S(2)}) %collective-permute-start.28) | collective-permute-done | bytes 32800 | tf_op jit(solution)/shard_map/ppermute | solution.py:27
  56.9 1.4 %collective-permute-done.27 = bf16[128,128]{1,0:T(8,128)(2,1)S(1)} collective-permute-done((bf16[128,128]{1,0:T(8,128)(2,1)S(1)}, bf16[128,128]{1,0:T(8,128)(2,1)S(1)}, u32[]{:S(2)}, u32[]{:S(2)}) %collective-permute-start.27) | collective-permute-done | bytes 32800 | tf_op jit(solution)/shard_map/ppermute | solution.py:27
  58.3 0.4 collective-permute-start.23
  58.7 2.4 %collective-permute-start.24 = (bf16[2,128,128]{2,1,0:T(8,128)(2,1)S(1)}, bf16[2,128,128]{2,1,0:T(8,128)(2,1)S(1)}, u32[]{:S(2)}, u32[]{:S(2)}) collective-permute-start(bf16[2,128,128]{2,1,0:T(8,128)(2,1)S(1)} %get-tuple-element.43), channel_id=1, source_target_pairs={{0,26},{2,28},{4,30},{6,24},{8,2},{10,4},{12,6},{14,0},{16,10},{18... | collective-permute-start | bytes 196616 | tf_op jit(solution)/shard_map/ppermute | solution.py:27
  61.1 0.8 %collective-permute-start.26 = (bf16[2,128,128]{2,1,0:T(8,128)(2,1)S(1)}, bf16[2,128,128]{2,1,0:T(8,128)(2,1)S(1)}, u32[]{:S(2)}, u32[]{:S(2)}) collective-permute-start(bf16[2,128,128]{2,1,0:T(8,128)(2,1)S(1)} %get-tuple-element.44), channel_id=1, source_target_pairs={{0,30},{2,24},{4,26},{6,28},{8,6},{10,0},{12,2},{14,4},{16,14},{18... | collective-permute-start | bytes 196616 | tf_op jit(solution)/shard_map/ppermute | solution.py:27
  61.9 0.6 collective-permute-start.25
  62.5 1.4 %collective-permute-start.31 = (bf16[128,128]{1,0:T(8,128)(2,1)S(1)}, bf16[128,128]{1,0:T(8,128)(2,1)S(1)}, u32[]{:S(2)}, u32[]{:S(2)}) collective-permute-start(bf16[128,128]{1,0:T(8,128)(2,1)S(1)} %shard_map.161.refs_0_), channel_id=1, source_target_pairs={{0,6},{2,0},{4,2},{6,4},{8,14},{10,8},{12,10},{14,12},{16,22},{18,... | collective-permute-start | bytes 98312 | tf_op jit(solution)/shard_map/ppermute | solution.py:27
  64.0 0.4 collective-permute-done.24
  64.4 0.5 collective-permute-done.26
  64.9 3.1 %collective-permute-done.25 = bf16[2,128,128]{2,1,0:T(8,128)(2,1)S(1)} collective-permute-done((bf16[2,128,128]{2,1,0:T(8,128)(2,1)S(1)}, bf16[2,128,128]{2,1,0:T(8,128)(2,1)S(1)}, u32[]{:S(2)}, u32[]{:S(2)}) %collective-permute-start.25) | collective-permute-done | bytes 65568 | tf_op jit(solution)/shard_map/ppermute | solution.py:27
  68.0 0.1 pad_maximum_fusion
  68.1 1.3 %shard_map.162 = (bf16[2304,128]{1,0:T(8,128)(2,1)S(1)}, bf16[128,128]{1,0:T(8,128)(2,1)S(1)}) custom-call(bf16[2304,128]{1,0:T(8,128)(2,1)S(1)} %bitcast.167, bf16[2304,128]{1,0:T(8,128)(2,1)S(1)} %get-tuple-element.26.hot_ref.hm_ref, bf16[1152,128]{1,0:T(8,128)(2,1)S(1)} %bitcast.170, bf16[3,128,128]{2,1,0:T(8,128)(2,1)S(1)} %copy-done.8, ...), custom_call_target="tpu_custom_call" | custom-call | flops 1540000000 | bytes 5040000 | tf_op jit(solution)/shard_map/pallas_call | solution.py:88
  69.4 1.3 %shard_map.163 = (bf16[2304,128]{1,0:T(8,128)(2,1)S(1)}, bf16[128,128]{1,0:T(8,128)(2,1)S(1)}) custom-call(bf16[2304,128]{1,0:T(8,128)(2,1)S(1)} %get-tuple-element.29.e_ref, bf16[2304,128]{1,0:T(8,128)(2,1)S(1)} %get-tuple-element.26.hot_ref.hm_ref, bf16[1152,128]{1,0:T(8,128)(2,1)S(1)} %bitcast.166, bf16[3,128,128]{2,1,0:T(8,128)(2,1)S(1)} %copy-done.8, ...), custom_call_target="tpu_custom_call" | custom-call | flops 1540000000 | bytes 5040000 | tf_op jit(solution)/shard_map/pallas_call | solution.py:88
  70.8 5.9 %shard_map.164 = bf16[169,4608]{1,0:T(8,128)(2,1)} custom-call(bf16[2304,128]{1,0:T(8,128)(2,1)S(1)} %shard_map.159.own_ref, bf16[2304,128]{1,0:T(8,128)(2,1)S(1)} %get-tuple-element.31.mir_ref, bf16[2304,128]{1,0:T(8,128)(2,1)S(1)} %get-tuple-element.23.hot_ref.ho_ref, bf16[2304,128]{1,0:T(8,128)(2,1)S(1)} %get-tuple-element.26.hot_ref.hm_ref, ...), custom_call_target="tpu_custom_call" | custom-call | flops 7699999744 | bytes 25200000 | tf_op jit(solution)/shard_map/pallas_call | solution.py:88
  (70 shorter events, 0.5 us)
Async XLA Ops:
  0.0 12.3 %collective-permute-start = (bf16[64,128]{1,0:T(8,128)(2,1)}, bf16[64,128]{1,0:T(8,128)(2,1)S(1)}, u32[]{:S(2)}, u32[]{:S(2)}) collective-permute-start(bf16[64,128]{1,0:T(8,128)(2,1)} %refs_2_.1), channel_id=1, source_target_pairs={{0,1},{1,0},{2,3},{3,2},{4,5},{5,4},{6,7},{7,6},{8,9},{9,8},{10,11... | collective-permute-start | bytes 49160 | tf_op jit(solution)/shard_map/ppermute | solution.py:17
  4.5 1.5 %copy-start.6 = (bf16[2304,128]{1,0:T(8,128)(2,1)S(1)}, bf16[2304,128]{1,0:T(8,128)(2,1)}, u32[]{:S(2)}) copy-start(bf16[2304,128]{1,0:T(8,128)(2,1)} %refs_1_.1) | copy-start | bytes 1769476
  4.5 1.5 %copy-start.12 = (bf16[64,128]{1,0:T(8,128)(2,1)S(1)}, bf16[64,128]{1,0:T(8,128)(2,1)}, u32[]{:S(2)}) copy-start(bf16[64,128]{1,0:T(8,128)(2,1)} %refs_2_.1) | copy-start | bytes 49156
  4.5 1.5 %copy-start.13 = (s32[2304]{0:T(1024)S(1)}, s32[2304]{0:T(1024)}, u32[]{:S(2)}) copy-start(s32[2304]{0:T(1024)} %param.22) | copy-start | bytes 27652
  5.9 26.1 %collective-permute-start.9 = (bf16[64,1152]{1,0:T(8,128)(2,1)S(1)}, bf16[64,1152]{1,0:T(8,128)(2,1)S(1)}, u32[]{:S(2)}, u32[]{:S(2)}) collective-permute-start(bf16[64,1152]{1,0:T(8,128)(2,1)S(1)} %get-tuple-element.25.refs_0_), channel_id=1, source_target_pairs={{0,1},{1,0},{2,3},{3,2},{4,5},{5,4},{6,7},{7,6},{8,9},{9,8},{10,11... | collective-permute-start | bytes 442376 | tf_op jit(solution)/shard_map/ppermute | solution.py:17
  6.0 4.1 %copy-start.2 = (s32[4608]{0:T(1024)S(1)}, s32[4608]{0:T(1024)}, u32[]{:S(2)}) copy-start(s32[4608]{0:T(1024)} %param.23) | copy-start | bytes 55300
  6.0 4.0 %copy-start.3 = (s32[4608]{0:T(1024)S(1)}, s32[4608]{0:T(1024)}, u32[]{:S(2)}) copy-start(s32[4608]{0:T(1024)} %param.20) | copy-start | bytes 55300
  6.0 4.0 %copy-start.4 = (s32[4608]{0:T(1024)S(1)}, s32[4608]{0:T(1024)}, u32[]{:S(2)}) copy-start(s32[4608]{0:T(1024)} %param.19) | copy-start | bytes 55300
  6.0 4.0 %copy-start.14 = (s32[2304]{0:T(1024)S(1)}, s32[2304]{0:T(1024)}, u32[]{:S(2)}) copy-start(s32[2304]{0:T(1024)} %param.21) | copy-start | bytes 27652
  8.0 24.0 %collective-permute-start.10 = (bf16[3,3,128,128]{3,2,1,0:T(8,128)(2,1)S(1)}, bf16[3,3,128,128]{3,2,1,0:T(8,128)(2,1)S(1)}, u32[]{:S(2)}, u32[]{:S(2)}) collective-permute-start(bf16[3,3,128,128]{3,2,1,0:T(8,128)(2,1)S(1)} %bitcast.183), channel_id=1, source_target_pairs={{0,1},{1,0},{2,3},{3,2},{4,5},{5,4},{6,7},{7,6},{8,9},{9,8},{10,11... | collective-permute-start | bytes 884744 | tf_op jit(solution)/shard_map/ppermute | solution.py:17
  10.0 6.2 %copy-start.11 = (bf16[128,169]{0,1:T(8,128)(2,1)S(1)}, bf16[128,169]{0,1:T(8,128)(2,1)}, u32[]{:S(2)}) copy-start(bf16[128,169]{0,1:T(8,128)(2,1)} %param.31) | copy-start | bytes 129796
  12.3 6.5 %collective-permute-start.8 = (bf16[128,128]{1,0:T(8,128)(2,1)S(1)}, bf16[128,128]{1,0:T(8,128)(2,1)S(1)}, u32[]{:S(2)}, u32[]{:S(2)}) collective-permute-start(bf16[128,128]{1,0:T(8,128)(2,1)S(1)} %constant_dynamic-update-slice_fusion), channel_id=1, source_target_pairs={{0,30},{2,24},{4,26},{6,28},{8,6},{10,0},{12,2},{14,4},{16,14},{18... | collective-permute-start | bytes 98312 | tf_op jit(solution)/shard_map/ppermute | solution.py:27
  15.5 4.7 %collective-permute-start.7 = (bf16[128,128]{1,0:T(8,128)(2,1)S(1)}, bf16[128,128]{1,0:T(8,128)(2,1)S(1)}, u32[]{:S(2)}, u32[]{:S(2)}) collective-permute-start(bf16[128,128]{1,0:T(8,128)(2,1)S(1)} %constant_dynamic-update-slice_fusion), channel_id=1, source_target_pairs={{0,24},{2,26},{4,28},{6,30},{8,0},{10,2},{12,4},{14,6},{16,8},{18,... | collective-permute-start | bytes 98312 | tf_op jit(solution)/shard_map/ppermute | solution.py:27
  16.0 4.3 %collective-permute-start.6 = (bf16[128,128]{1,0:T(8,128)(2,1)S(1)}, bf16[128,128]{1,0:T(8,128)(2,1)S(1)}, u32[]{:S(2)}, u32[]{:S(2)}) collective-permute-start(bf16[128,128]{1,0:T(8,128)(2,1)S(1)} %constant_dynamic-update-slice_fusion), channel_id=1, source_target_pairs={{0,26},{2,28},{4,30},{6,24},{8,2},{10,4},{12,6},{14,0},{16,10},{18... | collective-permute-start | bytes 98312 | tf_op jit(solution)/shard_map/ppermute | solution.py:27
  16.3 14.3 %copy-start.7 = (bf16[3,128,128]{2,1,0:T(8,128)(2,1)S(1)}, bf16[3,128,128]{2,1,0:T(8,128)(2,1)}, u32[]{:S(2)}) copy-start(bf16[3,128,128]{2,1,0:T(8,128)(2,1)} %wl_ref.9) | copy-start | bytes 294916
  16.3 14.3 %copy-start.8 = (bf16[3,128,128]{2,1,0:T(8,128)(2,1)S(1)}, bf16[3,128,128]{2,1,0:T(8,128)(2,1)}, u32[]{:S(2)}) copy-start(bf16[3,128,128]{2,1,0:T(8,128)(2,1)} %wr_ref.1) | copy-start | bytes 294916
  16.3 14.3 %copy-start.9 = (bf16[3,128,128]{2,1,0:T(8,128)(2,1)S(1)}, bf16[3,128,128]{2,1,0:T(8,128)(2,1)}, u32[]{:S(2)}) copy-start(bf16[3,128,128]{2,1,0:T(8,128)(2,1)} %wi_ref.9) | copy-start | bytes 294916
  16.3 14.3 %copy-start.10 = (bf16[3,128,128]{2,1,0:T(8,128)(2,1)S(1)}, bf16[3,128,128]{2,1,0:T(8,128)(2,1)}, u32[]{:S(2)}) copy-start(bf16[3,128,128]{2,1,0:T(8,128)(2,1)} %wo_ref.9) | copy-start | bytes 294916
  18.8 4.2 %collective-permute-start.5 = (bf16[128,128]{1,0:T(8,128)(2,1)S(1)}, bf16[128,128]{1,0:T(8,128)(2,1)S(1)}, u32[]{:S(2)}, u32[]{:S(2)}) collective-permute-start(bf16[128,128]{1,0:T(8,128)(2,1)S(1)} %constant_dynamic-update-slice_fusion), channel_id=1, source_target_pairs={{0,6},{2,0},{4,2},{6,4},{8,14},{10,8},{12,10},{14,12},{16,22},{18,... | collective-permute-start | bytes 98312 | tf_op jit(solution)/shard_map/ppermute | solution.py:27
  20.2 4.3 %collective-permute-start.4 = (bf16[128,128]{1,0:T(8,128)(2,1)S(1)}, bf16[128,128]{1,0:T(8,128)(2,1)S(1)}, u32[]{:S(2)}, u32[]{:S(2)}) collective-permute-start(bf16[128,128]{1,0:T(8,128)(2,1)S(1)} %constant_dynamic-update-slice_fusion), channel_id=1, source_target_pairs={{0,2},{2,4},{4,6},{6,0},{8,10},{10,12},{12,14},{14,8},{16,18},{18,... | collective-permute-start | bytes 98312 | tf_op jit(solution)/shard_map/ppermute | solution.py:27
  20.3 5.1 %collective-permute-start.3 = (bf16[128,128]{1,0:T(8,128)(2,1)S(1)}, bf16[128,128]{1,0:T(8,128)(2,1)S(1)}, u32[]{:S(2)}, u32[]{:S(2)}) collective-permute-start(bf16[128,128]{1,0:T(8,128)(2,1)S(1)} %constant_dynamic-update-slice_fusion), channel_id=1, source_target_pairs={{0,14},{2,8},{4,10},{6,12},{8,22},{10,16},{12,18},{14,20},{16,30},... | collective-permute-start | bytes 98312 | tf_op jit(solution)/shard_map/ppermute | solution.py:27
  23.0 6.1 %collective-permute-start.2 = (bf16[128,128]{1,0:T(8,128)(2,1)S(1)}, bf16[128,128]{1,0:T(8,128)(2,1)S(1)}, u32[]{:S(2)}, u32[]{:S(2)}) collective-permute-start(bf16[128,128]{1,0:T(8,128)(2,1)S(1)} %constant_dynamic-update-slice_fusion), channel_id=1, source_target_pairs={{0,8},{2,10},{4,12},{6,14},{8,16},{10,18},{12,20},{14,22},{16,24},... | collective-permute-start | bytes 98312 | tf_op jit(solution)/shard_map/ppermute | solution.py:27
  24.5 6.0 %collective-permute-start.1 = (bf16[128,128]{1,0:T(8,128)(2,1)S(1)}, bf16[128,128]{1,0:T(8,128)(2,1)S(1)}, u32[]{:S(2)}, u32[]{:S(2)}) collective-permute-start(bf16[128,128]{1,0:T(8,128)(2,1)S(1)} %constant_dynamic-update-slice_fusion), channel_id=1, source_target_pairs={{0,10},{2,12},{4,14},{6,8},{8,18},{10,20},{12,22},{14,16},{16,26},... | collective-permute-start | bytes 98312 | tf_op jit(solution)/shard_map/ppermute | solution.py:27
  30.6 1.4 %copy-start = (bf16[2,128,128]{2,1,0:T(8,128)(2,1)S(1)}, bf16[2,128,128]{2,1,0:T(8,128)(2,1)}, u32[]{:S(2)}) copy-start(bf16[2,128,128]{2,1,0:T(8,128)(2,1)} %refs_3_.3) | copy-start | bytes 196612
  30.7 1.4 %copy-start.1 = (bf16[2,128,128]{2,1,0:T(8,128)(2,1)S(1)}, bf16[2,128,128]{2,1,0:T(8,128)(2,1)}, u32[]{:S(2)}) copy-start(bf16[2,128,128]{2,1,0:T(8,128)(2,1)} %refs_4_.3) | copy-start | bytes 196612
  30.7 1.4 %copy-start.5 = (f32[2,128]{1,0:T(2,128)S(1)}, f32[2,128]{1,0:T(2,128)}, u32[]{:S(2)}) copy-start(f32[2,128]{1,0:T(2,128)} %refs_5_.3) | copy-start | bytes 3076
  32.6 3.6 %collective-permute-start.18 = (bf16[128,128]{1,0:T(8,128)(2,1)S(1)}, bf16[128,128]{1,0:T(8,128)(2,1)S(1)}, u32[]{:S(2)}, u32[]{:S(2)}) collective-permute-start(bf16[128,128]{1,0:T(8,128)(2,1)S(1)} %shard_map.158), channel_id=1, source_target_pairs={{0,30},{2,24},{4,26},{6,28},{8,6},{10,0},{12,2},{14,4},{16,14},{18... | collective-permute-start | bytes 98312 | tf_op jit(solution)/shard_map/ppermute | solution.py:27
  32.7 5.1 %collective-permute-start.17 = (bf16[128,128]{1,0:T(8,128)(2,1)S(1)}, bf16[128,128]{1,0:T(8,128)(2,1)S(1)}, u32[]{:S(2)}, u32[]{:S(2)}) collective-permute-start(bf16[128,128]{1,0:T(8,128)(2,1)S(1)} %shard_map.158), channel_id=1, source_target_pairs={{0,24},{2,26},{4,28},{6,30},{8,0},{10,2},{12,4},{14,6},{16,8},{18,... | collective-permute-start | bytes 98312 | tf_op jit(solution)/shard_map/ppermute | solution.py:27
  33.3 6.0 %collective-permute-start.16 = (bf16[128,128]{1,0:T(8,128)(2,1)S(1)}, bf16[128,128]{1,0:T(8,128)(2,1)S(1)}, u32[]{:S(2)}, u32[]{:S(2)}) collective-permute-start(bf16[128,128]{1,0:T(8,128)(2,1)S(1)} %shard_map.158), channel_id=1, source_target_pairs={{0,26},{2,28},{4,30},{6,24},{8,2},{10,4},{12,6},{14,0},{16,10},{18... | collective-permute-start | bytes 98312 | tf_op jit(solution)/shard_map/ppermute | solution.py:27
  34.1 5.2 %collective-permute-start.15 = (bf16[128,128]{1,0:T(8,128)(2,1)S(1)}, bf16[128,128]{1,0:T(8,128)(2,1)S(1)}, u32[]{:S(2)}, u32[]{:S(2)}) collective-permute-start(bf16[128,128]{1,0:T(8,128)(2,1)S(1)} %shard_map.158), channel_id=1, source_target_pairs={{0,6},{2,0},{4,2},{6,4},{8,14},{10,8},{12,10},{14,12},{16,22},{18,... | collective-permute-start | bytes 98312 | tf_op jit(solution)/shard_map/ppermute | solution.py:27
  36.2 6.2 %collective-permute-start.14 = (bf16[128,128]{1,0:T(8,128)(2,1)S(1)}, bf16[128,128]{1,0:T(8,128)(2,1)S(1)}, u32[]{:S(2)}, u32[]{:S(2)}) collective-permute-start(bf16[128,128]{1,0:T(8,128)(2,1)S(1)} %shard_map.158), channel_id=1, source_target_pairs={{0,2},{2,4},{4,6},{6,0},{8,10},{10,12},{12,14},{14,8},{16,18},{18,... | collective-permute-start | bytes 98312 | tf_op jit(solution)/shard_map/ppermute | solution.py:27
  36.3 7.5 %collective-permute-start.13 = (bf16[128,128]{1,0:T(8,128)(2,1)S(1)}, bf16[128,128]{1,0:T(8,128)(2,1)S(1)}, u32[]{:S(2)}, u32[]{:S(2)}) collective-permute-start(bf16[128,128]{1,0:T(8,128)(2,1)S(1)} %shard_map.158), channel_id=1, source_target_pairs={{0,14},{2,8},{4,10},{6,12},{8,22},{10,16},{12,18},{14,20},{16,30},... | collective-permute-start | bytes 98312 | tf_op jit(solution)/shard_map/ppermute | solution.py:27
  37.8 6.0 %collective-permute-start.12 = (bf16[128,128]{1,0:T(8,128)(2,1)S(1)}, bf16[128,128]{1,0:T(8,128)(2,1)S(1)}, u32[]{:S(2)}, u32[]{:S(2)}) collective-permute-start(bf16[128,128]{1,0:T(8,128)(2,1)S(1)} %shard_map.158), channel_id=1, source_target_pairs={{0,8},{2,10},{4,12},{6,14},{8,16},{10,18},{12,20},{14,22},{16,24},... | collective-permute-start | bytes 98312 | tf_op jit(solution)/shard_map/ppermute | solution.py:27
  39.3 6.1 %collective-permute-start.11 = (bf16[128,128]{1,0:T(8,128)(2,1)S(1)}, bf16[128,128]{1,0:T(8,128)(2,1)S(1)}, u32[]{:S(2)}, u32[]{:S(2)}) collective-permute-start(bf16[128,128]{1,0:T(8,128)(2,1)S(1)} %shard_map.158), channel_id=1, source_target_pairs={{0,10},{2,12},{4,14},{6,8},{8,18},{10,20},{12,22},{14,16},{16,26},... | collective-permute-start | bytes 98312 | tf_op jit(solution)/shard_map/ppermute | solution.py:27
  39.4 19.3 %collective-permute-start.19 = (bf16[2,128,128]{2,1,0:T(8,128)(2,1)S(1)}, bf16[2,128,128]{2,1,0:T(8,128)(2,1)S(1)}, u32[]{:S(2)}, u32[]{:S(2)}) collective-permute-start(bf16[2,128,128]{2,1,0:T(8,128)(2,1)S(1)} %get-tuple-element.37), channel_id=1, source_target_pairs={{0,10},{2,12},{4,14},{6,8},{8,18},{10,20},{12,22},{14,16},{16,26},... | collective-permute-start | bytes 196616 | tf_op jit(solution)/shard_map/ppermute | solution.py:27
  42.4 18.6 %collective-permute-start.20 = (bf16[2,128,128]{2,1,0:T(8,128)(2,1)S(1)}, bf16[2,128,128]{2,1,0:T(8,128)(2,1)S(1)}, u32[]{:S(2)}, u32[]{:S(2)}) collective-permute-start(bf16[2,128,128]{2,1,0:T(8,128)(2,1)S(1)} %get-tuple-element.38), channel_id=1, source_target_pairs={{0,8},{2,10},{4,12},{6,14},{8,16},{10,18},{12,20},{14,22},{16,24},... | collective-permute-start | bytes 196616 | tf_op jit(solution)/shard_map/ppermute | solution.py:27
  46.1 3.5 %collective-permute-start.34 = (bf16[128,128]{1,0:T(8,128)(2,1)S(1)}, bf16[128,128]{1,0:T(8,128)(2,1)S(1)}, u32[]{:S(2)}, u32[]{:S(2)}) collective-permute-start(bf16[128,128]{1,0:T(8,128)(2,1)S(1)} %shard_map.161.refs_0_), channel_id=1, source_target_pairs={{0,30},{2,24},{4,26},{6,28},{8,6},{10,0},{12,2},{14,4},{16,14},{18... | collective-permute-start | bytes 98312 | tf_op jit(solution)/shard_map/ppermute | solution.py:27
  46.2 5.0 %collective-permute-start.33 = (bf16[128,128]{1,0:T(8,128)(2,1)S(1)}, bf16[128,128]{1,0:T(8,128)(2,1)S(1)}, u32[]{:S(2)}, u32[]{:S(2)}) collective-permute-start(bf16[128,128]{1,0:T(8,128)(2,1)S(1)} %shard_map.161.refs_0_), channel_id=1, source_target_pairs={{0,24},{2,26},{4,28},{6,30},{8,0},{10,2},{12,4},{14,6},{16,8},{18,... | collective-permute-start | bytes 98312 | tf_op jit(solution)/shard_map/ppermute | solution.py:27
  47.2 5.1 %collective-permute-start.32 = (bf16[128,128]{1,0:T(8,128)(2,1)S(1)}, bf16[128,128]{1,0:T(8,128)(2,1)S(1)}, u32[]{:S(2)}, u32[]{:S(2)}) collective-permute-start(bf16[128,128]{1,0:T(8,128)(2,1)S(1)} %shard_map.161.refs_0_), channel_id=1, source_target_pairs={{0,26},{2,28},{4,30},{6,24},{8,2},{10,4},{12,6},{14,0},{16,10},{18... | collective-permute-start | bytes 98312 | tf_op jit(solution)/shard_map/ppermute | solution.py:27
  49.6 5.2 %collective-permute-start.29 = (bf16[128,128]{1,0:T(8,128)(2,1)S(1)}, bf16[128,128]{1,0:T(8,128)(2,1)S(1)}, u32[]{:S(2)}, u32[]{:S(2)}) collective-permute-start(bf16[128,128]{1,0:T(8,128)(2,1)S(1)} %shard_map.161.refs_0_), channel_id=1, source_target_pairs={{0,14},{2,8},{4,10},{6,12},{8,22},{10,16},{12,18},{14,20},{16,30},... | collective-permute-start | bytes 98312 | tf_op jit(solution)/shard_map/ppermute | solution.py:27
  51.2 5.7 %collective-permute-start.28 = (bf16[128,128]{1,0:T(8,128)(2,1)S(1)}, bf16[128,128]{1,0:T(8,128)(2,1)S(1)}, u32[]{:S(2)}, u32[]{:S(2)}) collective-permute-start(bf16[128,128]{1,0:T(8,128)(2,1)S(1)} %shard_map.161.refs_0_), channel_id=1, source_target_pairs={{0,8},{2,10},{4,12},{6,14},{8,16},{10,18},{12,20},{14,22},{16,24},... | collective-permute-start | bytes 98312 | tf_op jit(solution)/shard_map/ppermute | solution.py:27
  52.3 6.0 %collective-permute-start.27 = (bf16[128,128]{1,0:T(8,128)(2,1)S(1)}, bf16[128,128]{1,0:T(8,128)(2,1)S(1)}, u32[]{:S(2)}, u32[]{:S(2)}) collective-permute-start(bf16[128,128]{1,0:T(8,128)(2,1)S(1)} %shard_map.161.refs_0_), channel_id=1, source_target_pairs={{0,10},{2,12},{4,14},{6,8},{8,18},{10,20},{12,22},{14,16},{16,26},... | collective-permute-start | bytes 98312 | tf_op jit(solution)/shard_map/ppermute | solution.py:27
  54.8 7.1 %collective-permute-start.21 = (bf16[2,128,128]{2,1,0:T(8,128)(2,1)S(1)}, bf16[2,128,128]{2,1,0:T(8,128)(2,1)S(1)}, u32[]{:S(2)}, u32[]{:S(2)}) collective-permute-start(bf16[2,128,128]{2,1,0:T(8,128)(2,1)S(1)} %get-tuple-element.39), channel_id=1, source_target_pairs={{0,14},{2,8},{4,10},{6,12},{8,22},{10,16},{12,18},{14,20},{16,30},... | collective-permute-start | bytes 196616 | tf_op jit(solution)/shard_map/ppermute | solution.py:27
  56.9 5.6 %collective-permute-start.22 = (bf16[2,128,128]{2,1,0:T(8,128)(2,1)S(1)}, bf16[2,128,128]{2,1,0:T(8,128)(2,1)S(1)}, u32[]{:S(2)}, u32[]{:S(2)}) collective-permute-start(bf16[2,128,128]{2,1,0:T(8,128)(2,1)S(1)} %get-tuple-element.40), channel_id=1, source_target_pairs={{0,2},{2,4},{4,6},{6,0},{8,10},{10,12},{12,14},{14,8},{16,18},{18,... | collective-permute-start | bytes 196616 | tf_op jit(solution)/shard_map/ppermute | solution.py:27
  58.3 5.6 %collective-permute-start.23 = (bf16[2,128,128]{2,1,0:T(8,128)(2,1)S(1)}, bf16[2,128,128]{2,1,0:T(8,128)(2,1)S(1)}, u32[]{:S(2)}, u32[]{:S(2)}) collective-permute-start(bf16[2,128,128]{2,1,0:T(8,128)(2,1)S(1)} %get-tuple-element.42), channel_id=1, source_target_pairs={{0,6},{2,0},{4,2},{6,4},{8,14},{10,8},{12,10},{14,12},{16,22},{18,... | collective-permute-start | bytes 196616 | tf_op jit(solution)/shard_map/ppermute | solution.py:27
  58.7 5.7 %collective-permute-start.24 = (bf16[2,128,128]{2,1,0:T(8,128)(2,1)S(1)}, bf16[2,128,128]{2,1,0:T(8,128)(2,1)S(1)}, u32[]{:S(2)}, u32[]{:S(2)}) collective-permute-start(bf16[2,128,128]{2,1,0:T(8,128)(2,1)S(1)} %get-tuple-element.43), channel_id=1, source_target_pairs={{0,26},{2,28},{4,30},{6,24},{8,2},{10,4},{12,6},{14,0},{16,10},{18... | collective-permute-start | bytes 196616 | tf_op jit(solution)/shard_map/ppermute | solution.py:27
  61.1 3.8 %collective-permute-start.26 = (bf16[2,128,128]{2,1,0:T(8,128)(2,1)S(1)}, bf16[2,128,128]{2,1,0:T(8,128)(2,1)S(1)}, u32[]{:S(2)}, u32[]{:S(2)}) collective-permute-start(bf16[2,128,128]{2,1,0:T(8,128)(2,1)S(1)} %get-tuple-element.44), channel_id=1, source_target_pairs={{0,30},{2,24},{4,26},{6,28},{8,6},{10,0},{12,2},{14,4},{16,14},{18... | collective-permute-start | bytes 196616 | tf_op jit(solution)/shard_map/ppermute | solution.py:27
  61.9 6.1 %collective-permute-start.25 = (bf16[2,128,128]{2,1,0:T(8,128)(2,1)S(1)}, bf16[2,128,128]{2,1,0:T(8,128)(2,1)S(1)}, u32[]{:S(2)}, u32[]{:S(2)}) collective-permute-start(bf16[2,128,128]{2,1,0:T(8,128)(2,1)S(1)} %get-tuple-element.45), channel_id=1, source_target_pairs={{0,24},{2,26},{4,28},{6,30},{8,0},{10,2},{12,4},{14,6},{16,8},{18,... | collective-permute-start | bytes 196616 | tf_op jit(solution)/shard_map/ppermute | solution.py:27
  62.5 8.2 %collective-permute-start.31 = (bf16[128,128]{1,0:T(8,128)(2,1)S(1)}, bf16[128,128]{1,0:T(8,128)(2,1)S(1)}, u32[]{:S(2)}, u32[]{:S(2)}) collective-permute-start(bf16[128,128]{1,0:T(8,128)(2,1)S(1)} %shard_map.161.refs_0_), channel_id=1, source_target_pairs={{0,6},{2,0},{4,2},{6,4},{8,14},{10,8},{12,10},{14,12},{16,22},{18,... | collective-permute-start | bytes 98312 | tf_op jit(solution)/shard_map/ppermute | solution.py:27
  63.9 6.8 %collective-permute-start.30 = (bf16[128,128]{1,0:T(8,128)(2,1)S(1)}, bf16[128,128]{1,0:T(8,128)(2,1)S(1)}, u32[]{:S(2)}, u32[]{:S(2)}) collective-permute-start(bf16[128,128]{1,0:T(8,128)(2,1)S(1)} %shard_map.161.refs_0_), channel_id=1, source_target_pairs={{0,2},{2,4},{4,6},{6,0},{8,10},{10,12},{12,14},{14,8},{16,18},{18,... | collective-permute-start | bytes 98312 | tf_op jit(solution)/shard_map/ppermute | solution.py:27

commit v5 on v3

--- a/solution.py
+++ b/solution.py
@@ -8,6 +8,7 @@
 ORB = 13
 GROUPS = 4
 OFFS = 18
+AXES = ("gx", "gy", "layer")
 F32 = jnp.float32
 BF16 = jnp.bfloat16
 VMEM_LIMIT = 24 * 1024 * 1024
@@ -20,19 +21,6 @@
 def moved(value, axis, steps):
     count = lax.axis_size(axis)
     return lax.ppermute(value, axis, [(i, (i + steps) % count) for i in range(count)])
-
-
-def with_halo(block, axis, dim):
-    low = moved(block, axis, 1)
-    high = moved(block, axis, -1)
-    return jnp.concatenate([low, block, high], axis=dim)
-
-
-def ghosts_of(sheets, centre=None):
-    low, high = moved(sheets, "gx", 1), moved(sheets, "gx", -1)
-    centre = sheets if centre is None else centre
-    framed = with_halo(jnp.concatenate([low, centre, high], axis=1), "gy", 2)
-    return framed.reshape(-1, sheets.shape[-1])
 
 
 def across_rows(outgoing, crossed):
@@ -46,6 +34,15 @@
     return jnp.stack(cols, axis=2)
 
 
+def partner_domains():
+    offset = jnp.arange(OFFS, dtype=jnp.int32)
+    rows, cols, sheets = (lax.axis_size(a) for a in AXES)
+    x, y, sheet = (lax.axis_index(a) for a in AXES)
+    x = (x + offset % 9 // 3 - 1) % rows
+    y = (y + offset % 3 - 1) % cols
+    return ((x * cols + y) * sheets + (sheet + offset // 9) % sheets).astype(jnp.int32)
+
+
 def dot(a, b):
     return jnp.dot(a, b, preferred_element_type=F32)
 
@@ -74,8 +71,9 @@
     return iota(shape, dim).astype(F32)
 
 
-def call(body, outs, *args, after=(), scratch=(), us=1.0):
-    used = len(args)
+def call(body, outs, *args, after=(), domains=None, scratch=(), us=1.0):
+    head = () if domains is None else (domains,)
+    used = len(head) + len(args)
 
     def ordered_body(*refs):
         body(*refs[:used], *refs[used + len(after) :])
@@ -83,14 +81,15 @@
     return pl.pallas_call(
         ordered_body if after else body,
         out_shape=outs,
-        in_specs=[pl.BlockSpec(memory_space=pltpu.VMEM)] * used
+        in_specs=[pl.BlockSpec(memory_space=pltpu.SMEM)] * len(head)
+        + [pl.BlockSpec(memory_space=pltpu.VMEM)] * len(args)
         + [pl.BlockSpec(memory_space=pl.ANY)] * len(after),
         scratch_shapes=list(scratch),
         compiler_params=pltpu.CompilerParams(vmem_limit_bytes=VMEM_LIMIT),
         cost_estimate=pl.CostEstimate(
             flops=int(us * 1.1e9), bytes_accessed=int(us * 3.6e6), transcendentals=0
         ),
-    )(*args, *after)
+    )(*head, *args, *after)
 
 
 def as_row(tiles):
@@ -107,11 +106,10 @@
     return jnp.transpose(jnp.concatenate([values, filler], axis=1))[:cols]
 
 
-def order_body(send_ref, bond_ref, h_ref, out_ref, h_out_ref):
+def order_body(send_ref, bond_ref, out_ref):
     owned = bond_ref.shape[0]
     half = owned // 2
     cap = owned // OFFS
-    h_out_ref[...] = h_ref[...]
     bond = jnp.concatenate([bond_ref[:half, :], bond_ref[half:, :]], axis=1)
     send = as_row(send_ref[...])
     low = one_hot(iota((cap, owned), 0) == (send & 127))
@@ -133,12 +131,11 @@
         ).astype(BF16)
 
 
-def slots_body(nb_ref, kind_ref, recv_ref, dist_ref, h_ref, adj_ref, pack_ref, h_out_ref):
+def slots_body(both_ref, adj_ref, pack_ref):
     fan, atoms = pack_ref.shape
-    h_out_ref[...] = h_ref[...]
-    flat = nb_ref[...] | (kind_ref[...] << 11) | ((recv_ref[...] & 127) << 13)
-    pack = transposed(folded(as_row(flat.astype(F32)), atoms, fan)).astype(jnp.int32)
-    dist = transposed(folded(as_row(dist_ref[...]), atoms, fan))
+    half = both_ref.shape[0] // 2
+    pack = transposed(folded(as_row(both_ref[:half, :]), atoms, fan)).astype(jnp.int32)
+    dist = transposed(folded(as_row(both_ref[half:, :]), atoms, fan))
     pack_ref[...] = pack
     peer = (pack & 63).astype(F32)
     off = ((pack & 2047) >> 6).astype(F32)
@@ -271,20 +268,18 @@
     ).astype(BF16)
 
 
+def blocks_of(domain_ref, all_ref, atoms=64):
+    return [
+        all_ref[pl.ds(pl.multiple_of(domain_ref[o] * atoms, atoms), atoms), :] for o in range(OFFS)
+    ]
+
+
 def node_body(layer):
-    def body(adj_ref, other_ref, ghost_ref, wm_ref, wu_ref, gain_ref, out_ref):
-        ghosts = ghost_ref.shape[0]
-        half = ghosts // 2
-        atoms = ghosts // OFFS
-        mixed = dot(adj_ref[...], ghost_ref[...])
-        other = dot(other_ref[:, :half], ghost_ref[half:, :])
-        other += dot(other_ref[:, half:], ghost_ref[:half, :])
-        mixed = jnp.concatenate([mixed, other], axis=0).astype(BF16)
-        hidden = jnp.concatenate(
-            [ghost_ref[atoms * 4 : atoms * 5, :], ghost_ref[atoms * 13 : atoms * 14, :]], axis=0
-        )
+    def body(domain_ref, adj_ref, all_ref, wm_ref, wu_ref, gain_ref, out_ref):
+        ghosts = blocks_of(domain_ref, all_ref)
+        mixed = dot(adj_ref[...], jnp.concatenate(ghosts, axis=0)).astype(BF16)
         summed = (dot(mixed, wm_ref[layer]) * 0.125).astype(BF16)
-        updated = hidden.astype(F32) + silu(dot(summed, wu_ref[layer]))
+        updated = ghosts[4].astype(F32) + silu(dot(summed, wu_ref[layer]))
         out_ref[...] = (rms_norm(updated) * gain_ref[layer : layer + 1, :]).astype(BF16)
 
     return body
@@ -293,10 +288,10 @@
 CHUNK = 6
 
 
-def fill_table(ghost_ref, w_local, w_ghost, table):
-    atoms = ghost_ref.shape[0] // OFFS
-    local = dot(ghost_ref[atoms * 4 : atoms * 5, :], w_local).astype(BF16)
-    distant = dot(ghost_ref[...], w_ghost).astype(BF16)
+def fill_table(ghosts, w_local, w_ghost, table):
+    atoms = ghosts[0].shape[0]
+    local = dot(ghosts[4], w_local).astype(BF16)
+    distant = dot(jnp.concatenate(ghosts, axis=0), w_ghost).astype(BF16)
     blank = jnp.zeros((atoms, 128), BF16)
     for o in range(OFFS):
         base = 2 * atoms * o
@@ -318,9 +313,9 @@
     return chosen[:, :128] * chosen[:, 128:]
 
 
-def edge_all(e_ref, hot_ref, ghost_ref, w_local, w_ghost, w_in, w_out, table, out_ref):
+def edge_all(e_ref, hot_ref, ghosts, w_local, w_ghost, w_in, w_out, table, out_ref):
     cap = e_ref.shape[0] // OFFS
-    fill_table(ghost_ref, w_local, w_ghost, table)
+    fill_table(ghosts, w_local, w_ghost, table)
     for c in range(OFFS // CHUNK):
         span = slice(CHUNK * cap * c, CHUNK * cap * (c + 1))
         state = e_ref[span, :]
@@ -329,10 +324,12 @@
 
 
 def edge_body(layer):
-    def body(e_ref, hot_ref, ghost_ref, wl_ref, wg_ref, wi_ref, wo_ref, out_ref, table):
+    def body(
+        domain_ref, e_ref, hot_ref, all_ref, wl_ref, wg_ref, wi_ref, wo_ref, out_ref, table
+    ):
         edge_all(
-            e_ref, hot_ref, ghost_ref, wl_ref[layer], wg_ref[layer], wi_ref[layer], wo_ref[layer],
-            table, out_ref,
+            e_ref, hot_ref, blocks_of(domain_ref, all_ref), wl_ref[layer], wg_ref[layer],
+            wi_ref[layer], wo_ref[layer], table, out_ref,
         )
 
     return body
@@ -351,16 +348,17 @@
 
 def final_body(layer):
     def body(
-        own_ref, mir_ref, ho_ref, hm_ref, ghost_ref, wl_ref, wr_ref, wi_ref, wo_ref,
+        domain_ref, own_ref, mir_ref, ho_ref, hm_ref, all_ref, wl_ref, wr_ref, wi_ref, wo_ref,
         po_ref, pm_ref, perm_ref, owned_ref, wcat_ref,
         out_ref, table_own, table_mir, ranked, rows,
     ):
-        atoms = ghost_ref.shape[0] // OFFS
+        ghosts = blocks_of(domain_ref, all_ref)
+        atoms = ghosts[0].shape[0]
         cap = own_ref.shape[0] // OFFS
         fan = out_ref.shape[1] // atoms
         w_in, w_out = twice(wi_ref[layer]), twice(wo_ref[layer])
-        fill_table(ghost_ref, wl_ref[layer], wr_ref[layer], table_own)
-        fill_table(ghost_ref, wr_ref[layer], wl_ref[layer], table_mir)
+        fill_table(ghosts, wl_ref[layer], wr_ref[layer], table_own)
+        fill_table(ghosts, wr_ref[layer], wl_ref[layer], table_mir)
         for c in range(OFFS // CHUNK):
             span = slice(CHUNK * cap * c, CHUNK * cap * (c + 1))
             state = jnp.concatenate([own_ref[span, :], mir_ref[span, :]], axis=1)
@@ -419,20 +417,23 @@
 
     send, own = tiles(send_pos), tiles(own_rows)
     nb, kind, recv, dist = map(tiles, (neighbours, slot_kind, recv_pos, pair_dist))
-    opposite = swapped(atom_feats, "layer")
-    adjacency, pack, hidden = call(
+    gathered = lax.all_gather(atom_feats, AXES, tiled=True)
+    domains = partner_domains()
+    both = jnp.concatenate(
+        [(nb | (kind << 11) | ((recv & 127) << 13)).astype(F32), dist], axis=0
+    )
+    adjacency, pack = call(
         slots_body,
-        (array(atoms, ghosts), array(fan, atoms, dtype=jnp.int32), array(atoms, channels)),
-        nb, kind, recv, dist, atom_feats,
-        us=3.0,
-    )
-    other = swapped(adjacency, "layer")
-    sheets = jnp.concatenate([hidden, opposite], axis=0)
-    ordered, centre = call(
+        (array(atoms, ghosts), array(fan, atoms, dtype=jnp.int32)),
+        both,
+        us=2.0,
+    )
+    ordered = call(
         order_body,
-        (array(owned, channels), array(2 * atoms, channels)),
-        send, bond_embed, sheets,
-        us=3.5,
+        array(owned, channels),
+        send, bond_embed,
+        after=(pack,),
+        us=2.0,
     )
     outgoing = ordered.reshape(2, 3, 3, cap, channels)
     crossed = swapped(outgoing[1], "layer")
@@ -456,38 +457,39 @@
         pack, place, w_block.T,
         us=2.5,
     )
-    centre = centre.reshape(2, 1, 1, atoms, channels)
     table = pltpu.VMEM((2 * ghosts, 2 * channels), BF16)
     for layer in range(2):
-        ghost = ghosts_of(sheets.reshape(2, 1, 1, atoms, channels), centre)
-        centre = None
-        sheets = call(
+        hidden = call(
             node_body(layer),
-            array(2 * atoms, channels),
-            adjacency, other, ghost, w_msg, w_upd, node_gain,
+            array(atoms, channels),
+            adjacency, gathered, w_msg, w_upd, node_gain,
+            domains=domains,
             after=(shifted, perm) if layer else (crossed,),
             us=0.6,
         )
         ordered = call(
             edge_body(layer),
             array(owned, channels),
-            ordered, hot_own, ghost, w_left, w_right, w_edge_in, w_edge_out,
+            ordered, hot_own, gathered, w_left, w_right, w_edge_in, w_edge_out,
+            domains=domains,
             scratch=[table],
             us=1.4,
         )
         mirror = call(
             edge_body(layer),
             array(owned, channels),
-            mirror, hot_mir, ghost, w_right, w_left, w_edge_in, w_edge_out,
+            mirror, hot_mir, gathered, w_right, w_left, w_edge_in, w_edge_out,
+            domains=domains,
             scratch=[table],
             us=1.4,
         )
-    ghost = ghosts_of(sheets.reshape(2, 1, 1, atoms, channels))
+        gathered = lax.all_gather(hidden, AXES, tiled=True)
     return call(
         final_body(2),
         array(block, slots),
-        ordered, mirror, hot_own, hot_mir, ghost, w_left, w_right, w_edge_in, w_edge_out,
+        ordered, mirror, hot_own, hot_mir, gathered, w_left, w_right, w_edge_in, w_edge_out,
         pick_own, pick_mir, perm, mine, w_cat,
+        domains=domains,
         scratch=[
             table,
             table,

time: 62.6 us -> 241 us (3.85)
  blocking collectives: 0 us -> 206 us
  waiting for transfers between devices: 16 us -> 0.01 us
  starting transfers between devices: 21.4 us -> 8.69 us
  local copies, waits for them, and re-layouts: 3.83 us -> 0.22 us
  Pallas kernels: 20.2 us -> 23.8 us
    all_gather x0 -> x3, blocking collectives: none -> 206 us  [the longest x2 135 us: shards(): gathered = lax.all_gather(hidden, AXES, tiled=True)]
    ppermute x16 -> x4, waiting for transfers between devices: 16 us -> 0.01 us  [moved(): lax.ppermute(value, axis, [(i, (i + steps) % count) for i in range(count)])]
    ppermute x16 -> x4, starting transfers between devices: 16.7 us -> 5.66 us  [moved(): lax.ppermute(value, axis, [(i, (i + steps) % count) for i in range(count)])]
    unnamed x33 -> x30, local copies, waits for them, and re-layouts: 3.68 us -> 0.09 us
    pallas_call x11, Pallas kernels: 20.2 us -> 23.8 us  [call(): pl.pallas_call(ordered_body if after else body, out_shape=outs, in_specs=...]
  transfers between devices with their start and end apart: 19 -> 5, of which waited for: 8 -> 0; matrix products, arithmetic and copies ran while one was open for 0% -> 0% of each run, Pallas kernels for 17% -> 4%
where the time goes in v5:
time: 241 us; the launch traced here: 240 us
  blocking collectives  206 us (85%)
  Pallas kernels  23.8 us (10%)
  starting transfers between devices  8.69 us (4%)
    all_gather x2, blocking collectives, shards(): gathered = lax.all_gather(hidden, AXES, tiled=True)  135 us
    all_gather x1, blocking collectives, shards(): gathered = lax.all_gather(atom_feats, AXES, tiled=True)  71 us
    pallas_call x11, Pallas kernels, call(): pl.pallas_call(ordered_body if after else body, out_shape=outs, in_specs=...  23.8 us
    ppermute x4, starting transfers between devices, moved(): lax.ppermute(value, axis, [(i, (i + steps) % count) for i in range(count)])  5.66 us
  transfers between devices with their start and end apart: 5, of which 0 were waited for; matrix products, arithmetic and copies ran while one was open for 0% of the time, Pallas kernels for 4%

profile of v5, /device:TPU:0, one launch (start us, length us, event | category | flops | bytes accessed | tf_op | source)
XLA Modules:
  0.0 240.5 jit_solution(4917023381134213372)
XLA Ops:
  0.0 0.8 or_convert_fusion
  0.8 0.7 pad_maximum_fusion.3.both_ref
  1.5 0.0 copy-start.6
  1.5 0.0 copy-start.12
  1.5 1.4 shard_map.154
  2.9 0.0 copy-done.6
  2.9 0.0 copy-done.12
  2.9 0.0 copy-start.14
  2.9 0.0 copy-start.2
  2.9 0.0 copy-start.3
  2.9 0.0 copy-start.4
  3.0 0.0 copy-start.13
  3.0 1.9 shard_map.155.e_ref
  4.9 3.0 %collective-permute-start = (bf16[3,3,128,128]{3,2,1,0:T(8,128)(2,1)S(1)}, bf16[3,3,128,128]{3,2,1,0:T(8,128)(2,1)S(1)}, u32[]{:S(2)}, u32[]{:S(2)}) collective-permute-start(bf16[3,3,128,128]{3,2,1,0:T(8,128)(2,1)S(1)} %bitcast.44), channel_id=1, source_target_pairs={{0,1},{1,0},{2,3},{3,2},{4,5},{5,4},{6,7},{7,6},{8,9},{9,8},{10,11... | collective-permute-start | bytes 884744 | tf_op jit(solution)/shard_map/ppermute | solution.py:18
  8.0 0.0 copy-done.14
  8.0 71.0 %all_gather.9.all_ref.refs_2_ = bf16[2048,128]{1,0:T(8,128)(2,1)S(1)} all-gather(bf16[64,128]{1,0:T(8,128)(2,1)S(1)} %copy-done.14), channel_id=1, replica_groups=mesh['gx'=4,'gy'=4,'layer'=2] {'gx','gy','layer'}, dimensions={0}, use_global_device_ids=true | all-gather | bytes 540672 | tf_op jit(solution)/shard_map/all_gather | solution.py:420
  79.0 0.0 copy-done.2
  79.0 0.0 copy-done.3
  79.0 0.0 copy-done.4
  79.0 0.0 copy-done.13
  79.0 0.0 copy-start.7
  79.1 0.0 copy-start.8
  79.1 0.0 copy-start.9
  79.1 0.0 copy-start.10
  79.1 2.2 shard_map.156
  81.3 0.0 copy-done.7
  81.3 0.0 copy-done.8
  81.3 0.0 copy-done.9
  81.3 0.0 copy-done.10
  81.3 0.0 copy-start.11
  81.3 1.8 shard_map.157.e_ref
  83.2 0.0 copy-done.11
  83.2 0.0 copy-start
  83.2 0.0 copy-start.1
  83.2 0.0 copy-start.5
  83.2 2.4 %shard_map.162 = (bf16[2304,128]{1,0:T(8,128)(2,1)S(1)}, bf16[2304,128]{1,0:T(8,128)(2,1)S(1)}, bf16[4608,144]{1,0:T(8,128)(2,1)S(1)}, f32[72,64]{1,0:T(8,128)S(1)}, bf16[169,256]{1,0:T(8,128)(2,1)S(1)}) custom-call(s32[72,64]{1,0:T(8,128)S(1)} %get-tuple-element.15.refs_2_.pack_ref, f32[72,64]{1,0:T(8,128)S(1)} %get-tuple-element.19.place_ref, ...), custom_call_target="tpu_custom_call" | custom-call | flops 2750000128 | bytes 9000000 | tf_op jit(solution)/shard_map/pallas_call | solution.py:81
  85.7 0.0 collective-permute-done.refs_6_
  85.7 0.1 fusion.3
  85.7 0.1 collective-permute-start.1
  85.8 3.8 %collective-permute-start.2 = (bf16[2,3,128,128]{3,2,1,0:T(8,128)(2,1)S(1)}, bf16[2,3,128,128]{3,2,1,0:T(8,128)(2,1)S(1)}, u32[]{:S(2)}, u32[]{:S(2)}) collective-permute-start(bf16[2,3,128,128]{3,2,1,0:T(8,128)(2,1)S(1)} %get-tuple-element.29), channel_id=1, source_target_pairs={{0,24},{8,0},{16,8},{24,16},{1,25},{9,1},{17,9},{25,17},{2,26},{10... | collective-permute-start | bytes 589832 | tf_op jit(solution)/shard_map/ppermute | solution.py:23
  89.6 0.0 copy-done
  89.6 0.0 copy-done.1
  89.6 0.0 copy-done.5
  89.6 1.1 shard_map.158
  90.7 66.5 %all_gather.10.all_ref.refs_2_ = bf16[2048,128]{1,0:T(8,128)(2,1)S(1)} all-gather(bf16[64,128]{1,0:T(8,128)(2,1)S(1)} %shard_map.158), channel_id=1, replica_groups=mesh['gx'=4,'gy'=4,'layer'=2] {'gx','gy','layer'}, dimensions={0}, use_global_device_ids=true | all-gather | bytes 540672 | tf_op jit(solution)/shard_map/all_gather | solution.py:486
  157.2 1.8 shard_map.159.own_ref
  159.0 0.0 collective-permute-done.1
  159.0 0.0 collective-permute-done.2
  159.0 0.1 pad_maximum_fusion.refs_6_
  159.1 0.1 collective-permute-start.3
  159.2 1.7 collective-permute-start.4
  160.9 1.1 shard_map.163
  162.0 68.2 %all_gather.11.all_ref = bf16[2048,128]{1,0:T(8,128)(2,1)S(1)} all-gather(bf16[64,128]{1,0:T(8,128)(2,1)S(1)} %shard_map.163), channel_id=1, replica_groups=mesh['gx'=4,'gy'=4,'layer'=2] {'gx','gy','layer'}, dimensions={0}, use_global_device_ids=true | all-gather | bytes 540672 | tf_op jit(solution)/shard_map/all_gather | solution.py:486
  230.2 0.0 collective-permute-done.3
  230.2 0.0 collective-permute-done.4
  230.3 0.1 pad_maximum_fusion.1
  230.4 1.8 shard_map.160.e_ref
  232.2 1.8 shard_map.161.mir_ref
  234.0 6.4 %shard_map.164 = bf16[169,4608]{1,0:T(8,128)(2,1)} custom-call(s32[18]{0:T(128)S(1)} %fusion.6.domain_ref.refs_0_, bf16[2304,128]{1,0:T(8,128)(2,1)S(1)} %shard_map.159.own_ref, bf16[2304,128]{1,0:T(8,128)(2,1)S(1)} %shard_map.161.mir_ref, bf16[2304,128]{1,0:T(8,128)(2,1)S(1)} %get-tuple-element.16.hot_ref.ho_ref, ...), custom_call_target="tpu_custom_call" | custom-call | flops 7699999744 | bytes 25200000 | tf_op jit(solution)/shard_map/pallas_call | solution.py:81
  (4 shorter events, 0.2 us)
Async XLA Ops:
  1.5 1.4 copy-start.6
  1.5 1.4 copy-start.12
  2.9 5.1 %copy-start.14 = (bf16[64,128]{1,0:T(8,128)(2,1)S(1)}, bf16[64,128]{1,0:T(8,128)(2,1)}, u32[]{:S(2)}) copy-start(bf16[64,128]{1,0:T(8,128)(2,1)} %param.16) | copy-start | bytes 49156
  2.9 76.1 %copy-start.2 = (s32[4608]{0:T(1024)S(1)}, s32[4608]{0:T(1024)}, u32[]{:S(2)}) copy-start(s32[4608]{0:T(1024)} %param.23) | copy-start | bytes 55300
  2.9 76.1 %copy-start.3 = (s32[4608]{0:T(1024)S(1)}, s32[4608]{0:T(1024)}, u32[]{:S(2)}) copy-start(s32[4608]{0:T(1024)} %param.20) | copy-start | bytes 55300
  2.9 76.1 %copy-start.4 = (s32[4608]{0:T(1024)S(1)}, s32[4608]{0:T(1024)}, u32[]{:S(2)}) copy-start(s32[4608]{0:T(1024)} %param.19) | copy-start | bytes 55300
  3.0 76.1 %copy-start.13 = (s32[2304]{0:T(1024)S(1)}, s32[2304]{0:T(1024)}, u32[]{:S(2)}) copy-start(s32[2304]{0:T(1024)} %param.21) | copy-start | bytes 27652
  4.9 80.7 %collective-permute-start = (bf16[3,3,128,128]{3,2,1,0:T(8,128)(2,1)S(1)}, bf16[3,3,128,128]{3,2,1,0:T(8,128)(2,1)S(1)}, u32[]{:S(2)}, u32[]{:S(2)}) collective-permute-start(bf16[3,3,128,128]{3,2,1,0:T(8,128)(2,1)S(1)} %bitcast.44), channel_id=1, source_target_pairs={{0,1},{1,0},{2,3},{3,2},{4,5},{5,4},{6,7},{7,6},{8,9},{9,8},{10,11... | collective-permute-start | bytes 884744 | tf_op jit(solution)/shard_map/ppermute | solution.py:18
  79.0 2.2 copy-start.7
  79.1 2.2 copy-start.8
  79.1 2.2 copy-start.9
  79.1 2.2 copy-start.10
  81.3 1.9 copy-start.11
  83.2 6.4 %copy-start = (bf16[2,128,128]{2,1,0:T(8,128)(2,1)S(1)}, bf16[2,128,128]{2,1,0:T(8,128)(2,1)}, u32[]{:S(2)}) copy-start(bf16[2,128,128]{2,1,0:T(8,128)(2,1)} %refs_3_.3) | copy-start | bytes 196612
  83.2 6.4 %copy-start.1 = (bf16[2,128,128]{2,1,0:T(8,128)(2,1)S(1)}, bf16[2,128,128]{2,1,0:T(8,128)(2,1)}, u32[]{:S(2)}) copy-start(bf16[2,128,128]{2,1,0:T(8,128)(2,1)} %refs_4_.3) | copy-start | bytes 196612
  83.2 6.4 %copy-start.5 = (f32[2,128]{1,0:T(2,128)S(1)}, f32[2,128]{1,0:T(2,128)}, u32[]{:S(2)}) copy-start(f32[2,128]{1,0:T(2,128)} %refs_5_.3) | copy-start | bytes 3076
  85.7 73.3 %collective-permute-start.1 = (bf16[2,3,128,128]{3,2,1,0:T(8,128)(2,1)S(1)}, bf16[2,3,128,128]{3,2,1,0:T(8,128)(2,1)S(1)}, u32[]{:S(2)}, u32[]{:S(2)}) collective-permute-start(bf16[2,3,128,128]{3,2,1,0:T(8,128)(2,1)S(1)} %get-tuple-element.28), channel_id=1, source_target_pairs={{0,8},{8,16},{16,24},{24,0},{1,9},{9,17},{17,25},{25,1},{2,10},{10... | collective-permute-start | bytes 589832 | tf_op jit(solution)/shard_map/ppermute | solution.py:23
  85.8 73.2 %collective-permute-start.2 = (bf16[2,3,128,128]{3,2,1,0:T(8,128)(2,1)S(1)}, bf16[2,3,128,128]{3,2,1,0:T(8,128)(2,1)S(1)}, u32[]{:S(2)}, u32[]{:S(2)}) collective-permute-start(bf16[2,3,128,128]{3,2,1,0:T(8,128)(2,1)S(1)} %get-tuple-element.29), channel_id=1, source_target_pairs={{0,24},{8,0},{16,8},{24,16},{1,25},{9,1},{17,9},{25,17},{2,26},{10... | collective-permute-start | bytes 589832 | tf_op jit(solution)/shard_map/ppermute | solution.py:23
  159.1 71.1 %collective-permute-start.3 = (bf16[2,3,128,128]{3,2,1,0:T(8,128)(2,1)S(1)}, bf16[2,3,128,128]{3,2,1,0:T(8,128)(2,1)S(1)}, u32[]{:S(2)}, u32[]{:S(2)}) collective-permute-start(bf16[2,3,128,128]{3,2,1,0:T(8,128)(2,1)S(1)} %get-tuple-element.25), channel_id=1, source_target_pairs={{0,2},{2,4},{4,6},{6,0},{1,3},{3,5},{5,7},{7,1},{8,10},{10,12},{12... | collective-permute-start | bytes 589832 | tf_op jit(solution)/shard_map/ppermute | solution.py:23
  159.2 71.0 %collective-permute-start.4 = (bf16[2,3,128,128]{3,2,1,0:T(8,128)(2,1)S(1)}, bf16[2,3,128,128]{3,2,1,0:T(8,128)(2,1)S(1)}, u32[]{:S(2)}, u32[]{:S(2)}) collective-permute-start(bf16[2,3,128,128]{3,2,1,0:T(8,128)(2,1)S(1)} %get-tuple-element.26), channel_id=1, source_target_pairs={{0,6},{2,0},{4,2},{6,4},{1,7},{3,1},{5,3},{7,5},{8,14},{10,8},{12,... | collective-permute-start | bytes 589832 | tf_op jit(solution)/shard_map/ppermute | solution.py:23

commit v6 on v3

--- a/solution.py
+++ b/solution.py
@@ -133,12 +133,12 @@
         ).astype(BF16)
 
 
-def slots_body(nb_ref, kind_ref, recv_ref, dist_ref, h_ref, adj_ref, pack_ref, h_out_ref):
+def slots_body(both_ref, h_ref, adj_ref, pack_ref, h_out_ref):
     fan, atoms = pack_ref.shape
+    half = both_ref.shape[0] // 2
     h_out_ref[...] = h_ref[...]
-    flat = nb_ref[...] | (kind_ref[...] << 11) | ((recv_ref[...] & 127) << 13)
-    pack = transposed(folded(as_row(flat.astype(F32)), atoms, fan)).astype(jnp.int32)
-    dist = transposed(folded(as_row(dist_ref[...]), atoms, fan))
+    pack = transposed(folded(as_row(both_ref[:half, :]), atoms, fan)).astype(jnp.int32)
+    dist = transposed(folded(as_row(both_ref[half:, :]), atoms, fan))
     pack_ref[...] = pack
     peer = (pack & 63).astype(F32)
     off = ((pack & 2047) >> 6).astype(F32)
@@ -328,8 +328,12 @@
         out_ref[span, :] = rms_norm(state.astype(F32) + dot(gate, w_out)).astype(BF16)
 
 
-def edge_body(layer):
-    def body(e_ref, hot_ref, ghost_ref, wl_ref, wg_ref, wi_ref, wo_ref, out_ref, table):
+def edge_body(layer, hand_on=False):
+    def body(e_ref, hot_ref, ghost_ref, wl_ref, wg_ref, wi_ref, wo_ref, *refs):
+        if hand_on:
+            refs[2][...] = refs[0][...]
+            refs = (refs[1], refs[3])
+        out_ref, table = refs
         edge_all(
             e_ref, hot_ref, ghost_ref, wl_ref[layer], wg_ref[layer], wi_ref[layer], wo_ref[layer],
             table, out_ref,
@@ -420,11 +424,14 @@
     send, own = tiles(send_pos), tiles(own_rows)
     nb, kind, recv, dist = map(tiles, (neighbours, slot_kind, recv_pos, pair_dist))
     opposite = swapped(atom_feats, "layer")
+    both = jnp.concatenate(
+        [(nb | (kind << 11) | ((recv & 127) << 13)).astype(F32), dist], axis=0
+    )
     adjacency, pack, hidden = call(
         slots_body,
         (array(atoms, ghosts), array(fan, atoms, dtype=jnp.int32), array(atoms, channels)),
-        nb, kind, recv, dist, atom_feats,
-        us=3.0,
+        both, atom_feats,
+        us=2.0,
     )
     other = swapped(adjacency, "layer")
     sheets = jnp.concatenate([hidden, opposite], axis=0)
@@ -432,7 +439,7 @@
         order_body,
         (array(owned, channels), array(2 * atoms, channels)),
         send, bond_embed, sheets,
-        us=3.5,
+        us=2.0,
     )
     outgoing = ordered.reshape(2, 3, 3, cap, channels)
     crossed = swapped(outgoing[1], "layer")
@@ -442,6 +449,7 @@
         pairs_body,
         (array(owned, 128), array(owned, 128), array(fan, atoms, dtype=F32)),
         send, own, nb, kind, recv, pack,
+        after=(ordered,),
         us=2.5,
     )
     pick_own, pick_mir, perm, mine, w_cat = call(
@@ -456,33 +464,43 @@
         pack, place, w_block.T,
         us=2.5,
     )
-    centre = centre.reshape(2, 1, 1, atoms, channels)
     table = pltpu.VMEM((2 * ghosts, 2 * channels), BF16)
-    for layer in range(2):
-        ghost = ghosts_of(sheets.reshape(2, 1, 1, atoms, channels), centre)
-        centre = None
-        sheets = call(
-            node_body(layer),
-            array(2 * atoms, channels),
-            adjacency, other, ghost, w_msg, w_upd, node_gain,
-            after=(shifted, perm) if layer else (crossed,),
-            us=0.6,
-        )
-        ordered = call(
-            edge_body(layer),
-            array(owned, channels),
-            ordered, hot_own, ghost, w_left, w_right, w_edge_in, w_edge_out,
+    state = array(owned, channels)
+
+    def framed_sheets(value):
+        return value.reshape(2, 1, 1, atoms, channels)
+
+    def edge(layer, own, after=(), hand_on=()):
+        values = (ordered, hot_own) if own else (mirror, hot_mir)
+        weights = (w_left, w_right) if own else (w_right, w_left)
+        outs = (state, array(2 * atoms, channels)) if hand_on else state
+        return call(
+            edge_body(layer, bool(hand_on)),
+            outs,
+            *values, ghosts_at[layer], *weights, w_edge_in, w_edge_out, *hand_on,
+            after=after,
             scratch=[table],
             us=1.4,
         )
-        mirror = call(
-            edge_body(layer),
-            array(owned, channels),
-            mirror, hot_mir, ghost, w_right, w_left, w_edge_in, w_edge_out,
-            scratch=[table],
-            us=1.4,
+
+    def node(layer, after):
+        return call(
+            node_body(layer),
+            array(2 * atoms, channels),
+            adjacency, other, ghosts_at[layer], w_msg, w_upd, node_gain,
+            after=after,
+            us=0.6,
         )
-    ghost = ghosts_of(sheets.reshape(2, 1, 1, atoms, channels))
+
+    ghosts_at = [ghosts_of(framed_sheets(sheets), framed_sheets(centre))]
+    sheets = node(0, (crossed,))
+    ghosts_at.append(ghosts_of(framed_sheets(sheets)))
+    ordered = edge(0, True)
+    sheets = node(1, (perm, ordered, shifted))
+    ordered = edge(1, True)
+    mirror, centre = edge(0, False, hand_on=(sheets,))
+    mirror = edge(1, False)
+    ghost = ghosts_of(framed_sheets(sheets), framed_sheets(centre))
     return call(
         final_body(2),
         array(block, slots),

time: 62.6 us -> 58.2 us (0.930)
  waiting for transfers between devices: 16 us -> 7.47 us
  starting transfers between devices: 21.4 us -> 26.6 us
  local copies, waits for them, and re-layouts: 3.83 us -> 0.93 us
  other arithmetic: 0.34 us -> 1.84 us
    ppermute x16, waiting for transfers between devices: 16 us -> 7.46 us  [moved(): lax.ppermute(value, axis, [(i, (i + steps) % count) for i in range(count)])]
    ppermute x16, starting transfers between devices: 16.7 us -> 21.8 us  [moved(): lax.ppermute(value, axis, [(i, (i + steps) % count) for i in range(count)])]
    unnamed x33 -> x31, local copies, waits for them, and re-layouts: 3.68 us -> 0.79 us
    convert_element_type x0 -> x1, other arithmetic: none -> 0.77 us  [shards(): (nb | kind << 11 | (recv & 127) << 13).astype(F32)]
    concatenate x0 -> x1, other arithmetic: none -> 0.73 us  [shards(): jnp.concatenate([(nb | kind << 11 | (recv & 127) << 13).astype(F32), dist...]
  transfers between devices with their start and end apart: 19 -> 19, of which waited for: 8 -> 6; matrix products, arithmetic and copies ran while one was open for 0% -> 3% of each run, Pallas kernels for 17% -> 24%
where the time goes in v6:
time: 58.2 us; the launch traced here: 57.5 us
  starting transfers between devices  26.6 us (46%)
  Pallas kernels  20.2 us (35%)
  waiting for transfers between devices  7.47 us (13%)
  other arithmetic  1.84 us (3%)
  local copies, waits for them, and re-layouts  0.93 us (2%)
    ppermute x16, starting transfers between devices, moved(): lax.ppermute(value, axis, [(i, (i + steps) % count) for i in range(count)])  21.8 us
    pallas_call x11, Pallas kernels, call(): pl.pallas_call(ordered_body if after else body, out_shape=outs, in_specs=...  20.2 us
    ppermute x16, waiting for transfers between devices, moved(): lax.ppermute(value, axis, [(i, (i + steps) % count) for i in range(count)])  7.46 us
    ppermute x3, starting transfers between devices, swapped(): return lax.ppermute(value, axis, [(0, 1), (1, 0)])  4.78 us
  transfers between devices with their start and end apart: 19, of which 6 were waited for; matrix products, arithmetic and copies ran while one was open for 3% of the time, Pallas kernels for 24%

profile of v6, /device:TPU:0, one launch (start us, length us, event | category | flops | bytes accessed | tf_op | source)
XLA Modules:
  0.0 57.5 jit_solution(16271024103029162584)
XLA Ops:
  0.0 3.0 %collective-permute-start = (bf16[64,128]{1,0:T(8,128)(2,1)}, bf16[64,128]{1,0:T(8,128)(2,1)S(1)}, u32[]{:S(2)}, u32[]{:S(2)}) collective-permute-start(bf16[64,128]{1,0:T(8,128)(2,1)} %h_ref.1), channel_id=1, source_target_pairs={{0,1},{1,0},{2,3},{3,2},{4,5},{5,4},{6,7},{7,6},{8,9},{9,8},{10,11... | collective-permute-start | bytes 49160 | tf_op jit(solution)/shard_map/ppermute | solution.py:17
  3.0 0.8 %or_convert_fusion = f32[36,128]{1,0:T(8,128)S(1)} fusion(s32[4608]{0:T(1024)} %param.23, s32[4608]{0:T(1024)} %param.20, s32[4608]{0:T(1024)} %param.19), kind=kLoop, calls=%fused_computation.22 | loop fusion | flops 27648 | bytes 73728 | tf_op jit(solution)/shard_map/convert_element_type | solution.py:428
  3.7 0.7 %pad_maximum_fusion.9.both_ref = f32[72,128]{1,0:T(8,128)S(1)} fusion(f32[36,128]{1,0:T(8,128)} %bitcast.86, f32[36,128]{1,0:T(8,128)S(1)} %or_convert_fusion), kind=kLoop, calls=%fused_computation.21 | loop fusion | flops 9216 | bytes 73728 | tf_op jit(solution)/shard_map/concatenate | solution.py:427
  4.5 0.7 %copy-done.12 = bf16[64,128]{1,0:T(8,128)(2,1)S(1)} copy-done((bf16[64,128]{1,0:T(8,128)(2,1)S(1)}, bf16[64,128]{1,0:T(8,128)(2,1)}, u32[]{:S(2)}) %copy-start.12) | copy-done | bytes 16408
  5.2 1.4 %shard_map.154 = (bf16[64,1152]{1,0:T(8,128)(2,1)S(1)}, s32[72,64]{1,0:T(8,128)S(1)}, bf16[64,128]{1,0:T(8,128)(2,1)S(1)}) custom-call(f32[72,128]{1,0:T(8,128)S(1)} %pad_maximum_fusion.9.both_ref, bf16[64,128]{1,0:T(8,128)(2,1)S(1)} %copy-done.12), custom_call_target="tpu_custom_call" | custom-call | flops 2200000000 | bytes 7200000 | tf_op jit(solution)/shard_map/pallas_call | solution.py:83
  6.6 0.1 collective-permute-start.5
  6.7 0.0 collective-permute-done
  6.7 2.1 %collective-permute-start.1 = (bf16[2,1,1,64,128]{4,3,2,1,0:T(8,128)(2,1)S(1)}, bf16[2,1,1,64,128]{4,3,2,1,0:T(8,128)(2,1)S(1)}, u32[]{:S(2)}, u32[]{:S(2)}) collective-permute-start(bf16[2,1,1,64,128]{4,3,2,1,0:T(8,128)(2,1)S(1)} %bitcast.74), channel_id=1, source_target_pairs={{0,8},{8,16},{16,24},{24,0},{1,9},{9,17},{17,25},{25,1},{2,10},{10... | collective-permute-start | bytes 98312 | tf_op jit(solution)/shard_map/ppermute | solution.py:22
  8.8 2.1 %collective-permute-start.2 = (bf16[2,1,1,64,128]{4,3,2,1,0:T(8,128)(2,1)S(1)}, bf16[2,1,1,64,128]{4,3,2,1,0:T(8,128)(2,1)S(1)}, u32[]{:S(2)}, u32[]{:S(2)}) collective-permute-start(bf16[2,1,1,64,128]{4,3,2,1,0:T(8,128)(2,1)S(1)} %bitcast.75), channel_id=1, source_target_pairs={{0,24},{8,0},{16,8},{24,16},{1,25},{9,1},{17,9},{25,17},{2,26},{10... | collective-permute-start | bytes 98312 | tf_op jit(solution)/shard_map/ppermute | solution.py:22
  10.9 0.0 copy-start.4
  10.9 0.0 copy-start.14
  10.9 1.9 %shard_map.155 = (bf16[2304,128]{1,0:T(8,128)(2,1)S(1)}, bf16[128,128]{1,0:T(8,128)(2,1)S(1)}) custom-call(s32[18,128]{1,0:T(8,128)S(1)} %bitcast.77, bf16[2304,128]{1,0:T(8,128)(2,1)S(1)} %copy-done.6, bf16[128,128]{1,0:T(8,128)(2,1)S(1)} %constant_dynamic-update-slice_fusion.h_ref), custom_call_target="tpu_custom_call" | custom-call | flops 2200000000 | bytes 7200000 | tf_op jit(solution)/shard_map/pallas_call | solution.py:83
  12.9 1.7 %collective-permute-start.6 = (bf16[3,3,128,128]{3,2,1,0:T(8,128)(2,1)S(1)}, bf16[3,3,128,128]{3,2,1,0:T(8,128)(2,1)S(1)}, u32[]{:S(2)}, u32[]{:S(2)}) collective-permute-start(bf16[3,3,128,128]{3,2,1,0:T(8,128)(2,1)S(1)} %bitcast.81), channel_id=1, source_target_pairs={{0,1},{1,0},{2,3},{3,2},{4,5},{5,4},{6,7},{7,6},{8,9},{9,8},{10,11... | collective-permute-start | bytes 884744 | tf_op jit(solution)/shard_map/ppermute | solution.py:17
  14.6 0.0 copy-done.3
  14.6 0.0 copy-start.11
  14.7 2.2 %shard_map.156 = (bf16[2304,128]{1,0:T(8,128)(2,1)S(1)}, bf16[2304,128]{1,0:T(8,128)(2,1)S(1)}, f32[72,64]{1,0:T(8,128)S(1)}) custom-call(s32[18,128]{1,0:T(8,128)S(1)} %bitcast.78, s32[18,128]{1,0:T(8,128)S(1)} %bitcast.79, s32[36,128]{1,0:T(8,128)S(1)} %bitcast.73, s32[36,128]{1,0:T(8,128)S(1)} %bitcast.72, s32[36,128]{1,0:T(8,128)S(1)} %bitcast.71, ...), custom_call_target="tpu_custom_call" | custom-call | flops 2750000128 | bytes 9000000 | tf_op jit(solution)/shard_map/pallas_call | solution.py:83
  16.9 0.0 collective-permute-done.1
  16.9 0.0 collective-permute-done.2
  16.9 0.1 collective-permute-start.3
  17.0 1.7 %collective-permute-start.4 = (bf16[2,3,1,64,128]{4,3,2,1,0:T(8,128)(2,1)S(1)}, bf16[2,3,1,64,128]{4,3,2,1,0:T(8,128)(2,1)S(1)}, u32[]{:S(2)}, u32[]{:S(2)}) collective-permute-start(bf16[2,3,1,64,128]{4,3,2,1,0:T(8,128)(2,1)S(1)} %pad_maximum_fusion.6), channel_id=1, source_target_pairs={{0,6},{2,0},{4,2},{6,4},{1,7},{3,1},{5,3},{7,5},{8,14},{10,8},{12,... | collective-permute-start | bytes 294920 | tf_op jit(solution)/shard_map/ppermute | solution.py:22
  18.7 2.4 %shard_map.160 = (bf16[2304,128]{1,0:T(8,128)(2,1)S(1)}, bf16[2304,128]{1,0:T(8,128)(2,1)S(1)}, bf16[4608,144]{1,0:T(8,128)(2,1)S(1)}, f32[72,64]{1,0:T(8,128)S(1)}, bf16[169,256]{1,0:T(8,128)(2,1)S(1)}) custom-call(s32[72,64]{1,0:T(8,128)S(1)} %get-tuple-element.22.refs_5_.pack_ref, f32[72,64]{1,0:T(8,128)S(1)} %get-tuple-element.27.place_ref, ...), custom_call_target="tpu_custom_call" | custom-call | flops 2750000128 | bytes 9000000 | tf_op jit(solution)/shard_map/pallas_call | solution.py:83
  21.2 0.0 copy-start.7
  21.2 0.0 copy-start.8
  21.2 0.0 copy-start.9
  21.2 0.0 copy-start.10
  21.2 0.0 collective-permute-done.3
  21.2 0.0 collective-permute-done.4
  21.3 0.0 collective-permute-done.5.refs_1_
  21.3 0.0 collective-permute-done.6.refs_6_
  21.3 0.0 copy-done
  21.3 0.6 %shard_map.158 = bf16[128,128]{1,0:T(8,128)(2,1)S(1)} custom-call(bf16[64,1152]{1,0:T(8,128)(2,1)S(1)} %get-tuple-element.25.refs_0_, bf16[64,1152]{1,0:T(8,128)(2,1)S(1)} %collective-permute-done.5.refs_1_, bf16[1152,128]{1,0:T(8,128)(2,1)S(1)} %bitcast.56, bf16[2,128,128]{2,1,0:T(8,128)(2,1)S(1)} %copy-done, bf16[2,128,128]{2,1,0:T(8,128)(2,1)S(1)} %copy-done.1, ...), custom_call_target="tpu_custom_call" | custom-call | flops 660000000 | bytes 2160000 | tf_op jit(solution)/shard_map/pallas_call | solution.py:83
  21.9 0.1 collective-permute-start.7
  22.0 3.8 %collective-permute-start.8 = (bf16[2,1,1,64,128]{4,3,2,1,0:T(8,128)(2,1)S(1)}, bf16[2,1,1,64,128]{4,3,2,1,0:T(8,128)(2,1)S(1)}, u32[]{:S(2)}, u32[]{:S(2)}) collective-permute-start(bf16[2,1,1,64,128]{4,3,2,1,0:T(8,128)(2,1)S(1)} %bitcast.64), channel_id=1, source_target_pairs={{0,24},{8,0},{16,8},{24,16},{1,25},{9,1},{17,9},{25,17},{2,26},{10... | collective-permute-start | bytes 98312 | tf_op jit(solution)/shard_map/ppermute | solution.py:22
  25.8 0.1 fusion.3
  25.9 0.1 collective-permute-start.11
  25.9 3.8 %collective-permute-start.12 = (bf16[2,3,128,128]{3,2,1,0:T(8,128)(2,1)S(1)}, bf16[2,3,128,128]{3,2,1,0:T(8,128)(2,1)S(1)}, u32[]{:S(2)}, u32[]{:S(2)}) collective-permute-start(bf16[2,3,128,128]{3,2,1,0:T(8,128)(2,1)S(1)} %get-tuple-element.39), channel_id=1, source_target_pairs={{0,24},{8,0},{16,8},{24,16},{1,25},{9,1},{17,9},{25,17},{2,26},{10... | collective-permute-start | bytes 589832 | tf_op jit(solution)/shard_map/ppermute | solution.py:22
  29.7 0.0 collective-permute-done.7
  29.7 0.0 collective-permute-done.8
  29.8 0.7 %collective-permute-start.10 = (bf16[2,3,1,64,128]{4,3,2,1,0:T(8,128)(2,1)S(1)}, bf16[2,3,1,64,128]{4,3,2,1,0:T(8,128)(2,1)S(1)}, u32[]{:S(2)}, u32[]{:S(2)}) collective-permute-start(bf16[2,3,1,64,128]{4,3,2,1,0:T(8,128)(2,1)S(1)} %pad_maximum_fusion.7), channel_id=1, source_target_pairs={{0,6},{2,0},{4,2},{6,4},{1,7},{3,1},{5,3},{7,5},{8,14},{10,8},{12,... | collective-permute-start | bytes 294920 | tf_op jit(solution)/shard_map/ppermute | solution.py:22
  30.4 0.0 collective-permute-start.9
  30.5 1.3 %shard_map.157.e_ref.refs_7_ = bf16[2304,128]{1,0:T(8,128)(2,1)S(1)} custom-call(bf16[2304,128]{1,0:T(8,128)(2,1)S(1)} %get-tuple-element.21.refs_6_.e_ref, bf16[2304,128]{1,0:T(8,128)(2,1)S(1)} %get-tuple-element.23.hot_ref.ho_ref, bf16[1152,128]{1,0:T(8,128)(2,1)S(1)} %bitcast.57, bf16[3,128,128]{2,1,0:T(8,128)(2,1)S(1)} %copy-done.7, ...), custom_call_target="tpu_custom_call" | custom-call | flops 1540000000 | bytes 5040000 | tf_op jit(solution)/shard_map/pallas_call | solution.py:83
  31.8 1.2 %collective-permute-done.10 = bf16[2,3,1,64,128]{4,3,2,1,0:T(8,128)(2,1)S(1)} collective-permute-done((bf16[2,3,1,64,128]{4,3,2,1,0:T(8,128)(2,1)S(1)}, bf16[2,3,1,64,128]{4,3,2,1,0:T(8,128)(2,1)S(1)}, u32[]{:S(2)}, u32[]{:S(2)}) %collective-permute-start.10) | collective-permute-done | bytes 98336 | tf_op jit(solution)/shard_map/ppermute | solution.py:22
  33.0 2.4 %collective-permute-done.9 = bf16[2,3,1,64,128]{4,3,2,1,0:T(8,128)(2,1)S(1)} collective-permute-done((bf16[2,3,1,64,128]{4,3,2,1,0:T(8,128)(2,1)S(1)}, bf16[2,3,1,64,128]{4,3,2,1,0:T(8,128)(2,1)S(1)}, u32[]{:S(2)}, u32[]{:S(2)}) %collective-permute-start.9) | collective-permute-done | bytes 98336 | tf_op jit(solution)/shard_map/ppermute | solution.py:22
  35.4 0.2 collective-permute-done.11
  35.5 2.3 %collective-permute-done.12 = bf16[2,3,128,128]{3,2,1,0:T(8,128)(2,1)S(1)} collective-permute-done((bf16[2,3,128,128]{3,2,1,0:T(8,128)(2,1)S(1)}, bf16[2,3,128,128]{3,2,1,0:T(8,128)(2,1)S(1)}, u32[]{:S(2)}, u32[]{:S(2)}) %collective-permute-start.12) | collective-permute-done | bytes 196640 | tf_op jit(solution)/shard_map/ppermute | solution.py:22
  37.8 0.1 pad_maximum_fusion.refs_8_
  37.9 0.1 collective-permute-start.13
  38.0 1.7 %collective-permute-start.14 = (bf16[2,3,128,128]{3,2,1,0:T(8,128)(2,1)S(1)}, bf16[2,3,128,128]{3,2,1,0:T(8,128)(2,1)S(1)}, u32[]{:S(2)}, u32[]{:S(2)}) collective-permute-start(bf16[2,3,128,128]{3,2,1,0:T(8,128)(2,1)S(1)} %get-tuple-element.36), channel_id=1, source_target_pairs={{0,6},{2,0},{4,2},{6,4},{1,7},{3,1},{5,3},{7,5},{8,14},{10,8},{12,... | collective-permute-start | bytes 589832 | tf_op jit(solution)/shard_map/ppermute | solution.py:22
  39.7 1.3 %shard_map.159.own_ref = bf16[2304,128]{1,0:T(8,128)(2,1)S(1)} custom-call(bf16[2304,128]{1,0:T(8,128)(2,1)S(1)} %shard_map.157.e_ref.refs_7_, bf16[2304,128]{1,0:T(8,128)(2,1)S(1)} %get-tuple-element.23.hot_ref.ho_ref, bf16[1152,128]{1,0:T(8,128)(2,1)S(1)} %bitcast.52, bf16[3,128,128]{2,1,0:T(8,128)(2,1)S(1)} %copy-done.7, ...), custom_call_target="tpu_custom_call" | custom-call | flops 1540000000 | bytes 5040000 | tf_op jit(solution)/shard_map/pallas_call | solution.py:83
  41.0 0.6 %shard_map.161.refs_0_ = bf16[128,128]{1,0:T(8,128)(2,1)S(1)} custom-call(bf16[64,1152]{1,0:T(8,128)(2,1)S(1)} %get-tuple-element.25.refs_0_, bf16[64,1152]{1,0:T(8,128)(2,1)S(1)} %collective-permute-done.5.refs_1_, bf16[1152,128]{1,0:T(8,128)(2,1)S(1)} %bitcast.53, bf16[2,128,128]{2,1,0:T(8,128)(2,1)S(1)} %copy-done, bf16[2,128,128]{2,1,0:T(8,128)(2,1)S(1)} %copy-done.1, ...), custom_call_target="tpu_custom_call" | custom-call | flops 660000000 | bytes 2160000 | tf_op jit(solution)/shard_map/pallas_call | solution.py:83
  41.6 0.1 collective-permute-start.15
  41.7 3.8 %collective-permute-start.16 = (bf16[2,1,1,64,128]{4,3,2,1,0:T(8,128)(2,1)S(1)}, bf16[2,1,1,64,128]{4,3,2,1,0:T(8,128)(2,1)S(1)}, u32[]{:S(2)}, u32[]{:S(2)}) collective-permute-start(bf16[2,1,1,64,128]{4,3,2,1,0:T(8,128)(2,1)S(1)} %bitcast.70), channel_id=1, source_target_pairs={{0,24},{8,0},{16,8},{24,16},{1,25},{9,1},{17,9},{25,17},{2,26},{10... | collective-permute-start | bytes 98312 | tf_op jit(solution)/shard_map/ppermute | solution.py:22
  45.5 0.0 collective-permute-done.13
  45.5 0.0 collective-permute-done.14
  45.5 0.1 pad_maximum_fusion.1
  45.7 1.3 %shard_map.162 = (bf16[2304,128]{1,0:T(8,128)(2,1)S(1)}, bf16[128,128]{1,0:T(8,128)(2,1)S(1)}) custom-call(bf16[2304,128]{1,0:T(8,128)(2,1)S(1)} %bitcast.55, bf16[2304,128]{1,0:T(8,128)(2,1)S(1)} %get-tuple-element.26.hot_ref.hm_ref, bf16[1152,128]{1,0:T(8,128)(2,1)S(1)} %bitcast.58, bf16[3,128,128]{2,1,0:T(8,128)(2,1)S(1)} %copy-done.8, ...), custom_call_target="tpu_custom_call" | custom-call | flops 1540000000 | bytes 5040000 | tf_op jit(solution)/shard_map/pallas_call | solution.py:83
  47.0 0.4 collective-permute-done.15
  47.4 0.0 collective-permute-done.16
  47.4 0.1 collective-permute-start.17
  47.5 1.7 %collective-permute-start.18 = (bf16[2,3,1,64,128]{4,3,2,1,0:T(8,128)(2,1)S(1)}, bf16[2,3,1,64,128]{4,3,2,1,0:T(8,128)(2,1)S(1)}, u32[]{:S(2)}, u32[]{:S(2)}) collective-permute-start(bf16[2,3,1,64,128]{4,3,2,1,0:T(8,128)(2,1)S(1)} %pad_maximum_fusion.8), channel_id=1, source_target_pairs={{0,6},{2,0},{4,2},{6,4},{1,7},{3,1},{5,3},{7,5},{8,14},{10,8},{12,... | collective-permute-start | bytes 294920 | tf_op jit(solution)/shard_map/ppermute | solution.py:22
  49.2 1.3 %shard_map.163.mir_ref = bf16[2304,128]{1,0:T(8,128)(2,1)S(1)} custom-call(bf16[2304,128]{1,0:T(8,128)(2,1)S(1)} %get-tuple-element.29.e_ref, bf16[2304,128]{1,0:T(8,128)(2,1)S(1)} %get-tuple-element.26.hot_ref.hm_ref, bf16[1152,128]{1,0:T(8,128)(2,1)S(1)} %bitcast.54, bf16[3,128,128]{2,1,0:T(8,128)(2,1)S(1)} %copy-done.8, ...), custom_call_target="tpu_custom_call" | custom-call | flops 1540000000 | bytes 5040000 | tf_op jit(solution)/shard_map/pallas_call | solution.py:83
  50.5 1.0 %collective-permute-done.17 = bf16[2,3,1,64,128]{4,3,2,1,0:T(8,128)(2,1)S(1)} collective-permute-done((bf16[2,3,1,64,128]{4,3,2,1,0:T(8,128)(2,1)S(1)}, bf16[2,3,1,64,128]{4,3,2,1,0:T(8,128)(2,1)S(1)}, u32[]{:S(2)}, u32[]{:S(2)}) %collective-permute-start.17) | collective-permute-done | bytes 98336 | tf_op jit(solution)/shard_map/ppermute | solution.py:22
  51.5 0.0 collective-permute-done.18
  51.6 5.9 %shard_map.164 = bf16[169,4608]{1,0:T(8,128)(2,1)} custom-call(bf16[2304,128]{1,0:T(8,128)(2,1)S(1)} %shard_map.159.own_ref, bf16[2304,128]{1,0:T(8,128)(2,1)S(1)} %shard_map.163.mir_ref, bf16[2304,128]{1,0:T(8,128)(2,1)S(1)} %get-tuple-element.23.hot_ref.ho_ref, bf16[2304,128]{1,0:T(8,128)(2,1)S(1)} %get-tuple-element.26.hot_ref.hm_ref, ...), custom_call_target="tpu_custom_call" | custom-call | flops 7699999744 | bytes 25200000 | tf_op jit(solution)/shard_map/pallas_call | solution.py:83
  (31 shorter events, 0.3 us)
Async XLA Ops:
  0.0 6.7 %collective-permute-start = (bf16[64,128]{1,0:T(8,128)(2,1)}, bf16[64,128]{1,0:T(8,128)(2,1)S(1)}, u32[]{:S(2)}, u32[]{:S(2)}) collective-permute-start(bf16[64,128]{1,0:T(8,128)(2,1)} %h_ref.1), channel_id=1, source_target_pairs={{0,1},{1,0},{2,3},{3,2},{4,5},{5,4},{6,7},{7,6},{8,9},{9,8},{10,11... | collective-permute-start | bytes 49160 | tf_op jit(solution)/shard_map/ppermute | solution.py:17
  4.5 0.7 %copy-start.12 = (bf16[64,128]{1,0:T(8,128)(2,1)S(1)}, bf16[64,128]{1,0:T(8,128)(2,1)}, u32[]{:S(2)}) copy-start(bf16[64,128]{1,0:T(8,128)(2,1)} %h_ref.1) | copy-start | bytes 49156
  5.2 5.7 %copy-start.6 = (bf16[2304,128]{1,0:T(8,128)(2,1)S(1)}, bf16[2304,128]{1,0:T(8,128)(2,1)}, u32[]{:S(2)}) copy-start(bf16[2304,128]{1,0:T(8,128)(2,1)} %bond_ref.1) | copy-start | bytes 1769476
  5.2 5.7 %copy-start.13 = (s32[2304]{0:T(1024)S(1)}, s32[2304]{0:T(1024)}, u32[]{:S(2)}) copy-start(s32[2304]{0:T(1024)} %param.22) | copy-start | bytes 27652
  6.6 14.7 %collective-permute-start.5 = (bf16[64,1152]{1,0:T(8,128)(2,1)S(1)}, bf16[64,1152]{1,0:T(8,128)(2,1)S(1)}, u32[]{:S(2)}, u32[]{:S(2)}) collective-permute-start(bf16[64,1152]{1,0:T(8,128)(2,1)S(1)} %get-tuple-element.25.refs_0_), channel_id=1, source_target_pairs={{0,1},{1,0},{2,3},{3,2},{4,5},{5,4},{6,7},{7,6},{8,9},{9,8},{10,11... | collective-permute-start | bytes 442376 | tf_op jit(solution)/shard_map/ppermute | solution.py:17
  6.7 10.2 %collective-permute-start.1 = (bf16[2,1,1,64,128]{4,3,2,1,0:T(8,128)(2,1)S(1)}, bf16[2,1,1,64,128]{4,3,2,1,0:T(8,128)(2,1)S(1)}, u32[]{:S(2)}, u32[]{:S(2)}) collective-permute-start(bf16[2,1,1,64,128]{4,3,2,1,0:T(8,128)(2,1)S(1)} %bitcast.74), channel_id=1, source_target_pairs={{0,8},{8,16},{16,24},{24,0},{1,9},{9,17},{17,25},{25,1},{2,10},{10... | collective-permute-start | bytes 98312 | tf_op jit(solution)/shard_map/ppermute | solution.py:22
  8.8 8.1 %collective-permute-start.2 = (bf16[2,1,1,64,128]{4,3,2,1,0:T(8,128)(2,1)S(1)}, bf16[2,1,1,64,128]{4,3,2,1,0:T(8,128)(2,1)S(1)}, u32[]{:S(2)}, u32[]{:S(2)}) collective-permute-start(bf16[2,1,1,64,128]{4,3,2,1,0:T(8,128)(2,1)S(1)} %bitcast.75), channel_id=1, source_target_pairs={{0,24},{8,0},{16,8},{24,16},{1,25},{9,1},{17,9},{25,17},{2,26},{10... | collective-permute-start | bytes 98312 | tf_op jit(solution)/shard_map/ppermute | solution.py:22
  10.9 3.8 %copy-start.2 = (s32[4608]{0:T(1024)S(1)}, s32[4608]{0:T(1024)}, u32[]{:S(2)}) copy-start(s32[4608]{0:T(1024)} %param.23) | copy-start | bytes 55300
  10.9 3.8 %copy-start.3 = (s32[4608]{0:T(1024)S(1)}, s32[4608]{0:T(1024)}, u32[]{:S(2)}) copy-start(s32[4608]{0:T(1024)} %param.20) | copy-start | bytes 55300
  10.9 3.8 %copy-start.4 = (s32[4608]{0:T(1024)S(1)}, s32[4608]{0:T(1024)}, u32[]{:S(2)}) copy-start(s32[4608]{0:T(1024)} %param.19) | copy-start | bytes 55300
  10.9 3.7 %copy-start.14 = (s32[2304]{0:T(1024)S(1)}, s32[2304]{0:T(1024)}, u32[]{:S(2)}) copy-start(s32[2304]{0:T(1024)} %param.21) | copy-start | bytes 27652
  12.9 8.4 %collective-permute-start.6 = (bf16[3,3,128,128]{3,2,1,0:T(8,128)(2,1)S(1)}, bf16[3,3,128,128]{3,2,1,0:T(8,128)(2,1)S(1)}, u32[]{:S(2)}, u32[]{:S(2)}) collective-permute-start(bf16[3,3,128,128]{3,2,1,0:T(8,128)(2,1)S(1)} %bitcast.81), channel_id=1, source_target_pairs={{0,1},{1,0},{2,3},{3,2},{4,5},{5,4},{6,7},{7,6},{8,9},{9,8},{10,11... | collective-permute-start | bytes 884744 | tf_op jit(solution)/shard_map/ppermute | solution.py:17
  14.6 4.1 %copy-start.11 = (bf16[128,169]{0,1:T(8,128)(2,1)S(1)}, bf16[128,169]{0,1:T(8,128)(2,1)}, u32[]{:S(2)}) copy-start(bf16[128,169]{0,1:T(8,128)(2,1)} %param.31) | copy-start | bytes 129796
  16.9 4.3 %collective-permute-start.3 = (bf16[2,3,1,64,128]{4,3,2,1,0:T(8,128)(2,1)S(1)}, bf16[2,3,1,64,128]{4,3,2,1,0:T(8,128)(2,1)S(1)}, u32[]{:S(2)}, u32[]{:S(2)}) collective-permute-start(bf16[2,3,1,64,128]{4,3,2,1,0:T(8,128)(2,1)S(1)} %pad_maximum_fusion.6), channel_id=1, source_target_pairs={{0,2},{2,4},{4,6},{6,0},{1,3},{3,5},{5,7},{7,1},{8,10},{10,12},{12... | collective-permute-start | bytes 294920 | tf_op jit(solution)/shard_map/ppermute | solution.py:22
  17.0 4.2 %collective-permute-start.4 = (bf16[2,3,1,64,128]{4,3,2,1,0:T(8,128)(2,1)S(1)}, bf16[2,3,1,64,128]{4,3,2,1,0:T(8,128)(2,1)S(1)}, u32[]{:S(2)}, u32[]{:S(2)}) collective-permute-start(bf16[2,3,1,64,128]{4,3,2,1,0:T(8,128)(2,1)S(1)} %pad_maximum_fusion.6), channel_id=1, source_target_pairs={{0,6},{2,0},{4,2},{6,4},{1,7},{3,1},{5,3},{7,5},{8,14},{10,8},{12,... | collective-permute-start | bytes 294920 | tf_op jit(solution)/shard_map/ppermute | solution.py:22
  18.7 2.6 %copy-start = (bf16[2,128,128]{2,1,0:T(8,128)(2,1)S(1)}, bf16[2,128,128]{2,1,0:T(8,128)(2,1)}, u32[]{:S(2)}) copy-start(bf16[2,128,128]{2,1,0:T(8,128)(2,1)} %refs_3_.3) | copy-start | bytes 196612
  18.7 2.6 %copy-start.1 = (bf16[2,128,128]{2,1,0:T(8,128)(2,1)S(1)}, bf16[2,128,128]{2,1,0:T(8,128)(2,1)}, u32[]{:S(2)}) copy-start(bf16[2,128,128]{2,1,0:T(8,128)(2,1)} %refs_4_.3) | copy-start | bytes 196612
  18.7 2.6 %copy-start.5 = (f32[2,128]{1,0:T(2,128)S(1)}, f32[2,128]{1,0:T(2,128)}, u32[]{:S(2)}) copy-start(f32[2,128]{1,0:T(2,128)} %refs_5_.3) | copy-start | bytes 3076
  21.2 9.3 %copy-start.7 = (bf16[3,128,128]{2,1,0:T(8,128)(2,1)S(1)}, bf16[3,128,128]{2,1,0:T(8,128)(2,1)}, u32[]{:S(2)}) copy-start(bf16[3,128,128]{2,1,0:T(8,128)(2,1)} %wl_ref.9) | copy-start | bytes 294916
  21.2 9.3 %copy-start.8 = (bf16[3,128,128]{2,1,0:T(8,128)(2,1)S(1)}, bf16[3,128,128]{2,1,0:T(8,128)(2,1)}, u32[]{:S(2)}) copy-start(bf16[3,128,128]{2,1,0:T(8,128)(2,1)} %wr_ref.1) | copy-start | bytes 294916
  21.2 9.3 %copy-start.9 = (bf16[3,128,128]{2,1,0:T(8,128)(2,1)S(1)}, bf16[3,128,128]{2,1,0:T(8,128)(2,1)}, u32[]{:S(2)}) copy-start(bf16[3,128,128]{2,1,0:T(8,128)(2,1)} %wi_ref.9) | copy-start | bytes 294916
  21.2 9.3 %copy-start.10 = (bf16[3,128,128]{2,1,0:T(8,128)(2,1)S(1)}, bf16[3,128,128]{2,1,0:T(8,128)(2,1)}, u32[]{:S(2)}) copy-start(bf16[3,128,128]{2,1,0:T(8,128)(2,1)} %wo_ref.9) | copy-start | bytes 294916
  21.9 7.8 %collective-permute-start.7 = (bf16[2,1,1,64,128]{4,3,2,1,0:T(8,128)(2,1)S(1)}, bf16[2,1,1,64,128]{4,3,2,1,0:T(8,128)(2,1)S(1)}, u32[]{:S(2)}, u32[]{:S(2)}) collective-permute-start(bf16[2,1,1,64,128]{4,3,2,1,0:T(8,128)(2,1)S(1)} %bitcast.63), channel_id=1, source_target_pairs={{0,8},{8,16},{16,24},{24,0},{1,9},{9,17},{17,25},{25,1},{2,10},{10... | collective-permute-start | bytes 98312 | tf_op jit(solution)/shard_map/ppermute | solution.py:22
  22.0 7.7 %collective-permute-start.8 = (bf16[2,1,1,64,128]{4,3,2,1,0:T(8,128)(2,1)S(1)}, bf16[2,1,1,64,128]{4,3,2,1,0:T(8,128)(2,1)S(1)}, u32[]{:S(2)}, u32[]{:S(2)}) collective-permute-start(bf16[2,1,1,64,128]{4,3,2,1,0:T(8,128)(2,1)S(1)} %bitcast.64), channel_id=1, source_target_pairs={{0,24},{8,0},{16,8},{24,16},{1,25},{9,1},{17,9},{25,17},{2,26},{10... | collective-permute-start | bytes 98312 | tf_op jit(solution)/shard_map/ppermute | solution.py:22
  25.9 9.7 %collective-permute-start.11 = (bf16[2,3,128,128]{3,2,1,0:T(8,128)(2,1)S(1)}, bf16[2,3,128,128]{3,2,1,0:T(8,128)(2,1)S(1)}, u32[]{:S(2)}, u32[]{:S(2)}) collective-permute-start(bf16[2,3,128,128]{3,2,1,0:T(8,128)(2,1)S(1)} %get-tuple-element.38), channel_id=1, source_target_pairs={{0,8},{8,16},{16,24},{24,0},{1,9},{9,17},{17,25},{25,1},{2,10},{10... | collective-permute-start | bytes 589832 | tf_op jit(solution)/shard_map/ppermute | solution.py:22
  25.9 11.9 %collective-permute-start.12 = (bf16[2,3,128,128]{3,2,1,0:T(8,128)(2,1)S(1)}, bf16[2,3,128,128]{3,2,1,0:T(8,128)(2,1)S(1)}, u32[]{:S(2)}, u32[]{:S(2)}) collective-permute-start(bf16[2,3,128,128]{3,2,1,0:T(8,128)(2,1)S(1)} %get-tuple-element.39), channel_id=1, source_target_pairs={{0,24},{8,0},{16,8},{24,16},{1,25},{9,1},{17,9},{25,17},{2,26},{10... | collective-permute-start | bytes 589832 | tf_op jit(solution)/shard_map/ppermute | solution.py:22
  29.8 3.2 %collective-permute-start.10 = (bf16[2,3,1,64,128]{4,3,2,1,0:T(8,128)(2,1)S(1)}, bf16[2,3,1,64,128]{4,3,2,1,0:T(8,128)(2,1)S(1)}, u32[]{:S(2)}, u32[]{:S(2)}) collective-permute-start(bf16[2,3,1,64,128]{4,3,2,1,0:T(8,128)(2,1)S(1)} %pad_maximum_fusion.7), channel_id=1, source_target_pairs={{0,6},{2,0},{4,2},{6,4},{1,7},{3,1},{5,3},{7,5},{8,14},{10,8},{12,... | collective-permute-start | bytes 294920 | tf_op jit(solution)/shard_map/ppermute | solution.py:22
  30.4 4.9 %collective-permute-start.9 = (bf16[2,3,1,64,128]{4,3,2,1,0:T(8,128)(2,1)S(1)}, bf16[2,3,1,64,128]{4,3,2,1,0:T(8,128)(2,1)S(1)}, u32[]{:S(2)}, u32[]{:S(2)}) collective-permute-start(bf16[2,3,1,64,128]{4,3,2,1,0:T(8,128)(2,1)S(1)} %pad_maximum_fusion.7), channel_id=1, source_target_pairs={{0,2},{2,4},{4,6},{6,0},{1,3},{3,5},{5,7},{7,1},{8,10},{10,12},{12... | collective-permute-start | bytes 294920 | tf_op jit(solution)/shard_map/ppermute | solution.py:22
  37.9 7.6 %collective-permute-start.13 = (bf16[2,3,128,128]{3,2,1,0:T(8,128)(2,1)S(1)}, bf16[2,3,128,128]{3,2,1,0:T(8,128)(2,1)S(1)}, u32[]{:S(2)}, u32[]{:S(2)}) collective-permute-start(bf16[2,3,128,128]{3,2,1,0:T(8,128)(2,1)S(1)} %get-tuple-element.35), channel_id=1, source_target_pairs={{0,2},{2,4},{4,6},{6,0},{1,3},{3,5},{5,7},{7,1},{8,10},{10,12},{12... | collective-permute-start | bytes 589832 | tf_op jit(solution)/shard_map/ppermute | solution.py:22
  38.0 7.5 %collective-permute-start.14 = (bf16[2,3,128,128]{3,2,1,0:T(8,128)(2,1)S(1)}, bf16[2,3,128,128]{3,2,1,0:T(8,128)(2,1)S(1)}, u32[]{:S(2)}, u32[]{:S(2)}) collective-permute-start(bf16[2,3,128,128]{3,2,1,0:T(8,128)(2,1)S(1)} %get-tuple-element.36), channel_id=1, source_target_pairs={{0,6},{2,0},{4,2},{6,4},{1,7},{3,1},{5,3},{7,5},{8,14},{10,8},{12,... | collective-permute-start | bytes 589832 | tf_op jit(solution)/shard_map/ppermute | solution.py:22
  41.6 5.8 %collective-permute-start.15 = (bf16[2,1,1,64,128]{4,3,2,1,0:T(8,128)(2,1)S(1)}, bf16[2,1,1,64,128]{4,3,2,1,0:T(8,128)(2,1)S(1)}, u32[]{:S(2)}, u32[]{:S(2)}) collective-permute-start(bf16[2,1,1,64,128]{4,3,2,1,0:T(8,128)(2,1)S(1)} %bitcast.69), channel_id=1, source_target_pairs={{0,8},{8,16},{16,24},{24,0},{1,9},{9,17},{17,25},{25,1},{2,10},{10... | collective-permute-start | bytes 98312 | tf_op jit(solution)/shard_map/ppermute | solution.py:22
  41.7 5.7 %collective-permute-start.16 = (bf16[2,1,1,64,128]{4,3,2,1,0:T(8,128)(2,1)S(1)}, bf16[2,1,1,64,128]{4,3,2,1,0:T(8,128)(2,1)S(1)}, u32[]{:S(2)}, u32[]{:S(2)}) collective-permute-start(bf16[2,1,1,64,128]{4,3,2,1,0:T(8,128)(2,1)S(1)} %bitcast.70), channel_id=1, source_target_pairs={{0,24},{8,0},{16,8},{24,16},{1,25},{9,1},{17,9},{25,17},{2,26},{10... | collective-permute-start | bytes 98312 | tf_op jit(solution)/shard_map/ppermute | solution.py:22
  47.4 4.1 %collective-permute-start.17 = (bf16[2,3,1,64,128]{4,3,2,1,0:T(8,128)(2,1)S(1)}, bf16[2,3,1,64,128]{4,3,2,1,0:T(8,128)(2,1)S(1)}, u32[]{:S(2)}, u32[]{:S(2)}) collective-permute-start(bf16[2,3,1,64,128]{4,3,2,1,0:T(8,128)(2,1)S(1)} %pad_maximum_fusion.8), channel_id=1, source_target_pairs={{0,2},{2,4},{4,6},{6,0},{1,3},{3,5},{5,7},{7,1},{8,10},{10,12},{12... | collective-permute-start | bytes 294920 | tf_op jit(solution)/shard_map/ppermute | solution.py:22
  47.5 4.0 %collective-permute-start.18 = (bf16[2,3,1,64,128]{4,3,2,1,0:T(8,128)(2,1)S(1)}, bf16[2,3,1,64,128]{4,3,2,1,0:T(8,128)(2,1)S(1)}, u32[]{:S(2)}, u32[]{:S(2)}) collective-permute-start(bf16[2,3,1,64,128]{4,3,2,1,0:T(8,128)(2,1)S(1)} %pad_maximum_fusion.8), channel_id=1, source_target_pairs={{0,6},{2,0},{4,2},{6,4},{1,7},{3,1},{5,3},{7,5},{8,14},{10,8},{12,... | collective-permute-start | bytes 294920 | tf_op jit(solution)/shard_map/ppermute | solution.py:22

commit v7 on v6

--- a/solution.py
+++ b/solution.py
@@ -496,9 +496,9 @@
     sheets = node(0, (crossed,))
     ghosts_at.append(ghosts_of(framed_sheets(sheets)))
     ordered = edge(0, True)
-    sheets = node(1, (perm, ordered, shifted))
-    ordered = edge(1, True)
-    mirror, centre = edge(0, False, hand_on=(sheets,))
+    sheets = node(1, (perm, ordered))
+    ordered, centre = edge(1, True, after=(shifted,), hand_on=(sheets,))
+    mirror = edge(0, False)
     mirror = edge(1, False)
     ghost = ghosts_of(framed_sheets(sheets), framed_sheets(centre))
     return call(

time: 58.2 us -> 61.6 us (1.058)
  waiting for transfers between devices: 7.47 us -> 15.9 us
  starting transfers between devices: 26.6 us -> 22.1 us
    ppermute x16, waiting for transfers between devices: 7.46 us -> 15.9 us  [moved(): lax.ppermute(value, axis, [(i, (i + steps) % count) for i in range(count)])]
    ppermute x16, starting transfers between devices: 21.8 us -> 17.5 us  [moved(): lax.ppermute(value, axis, [(i, (i + steps) % count) for i in range(count)])]
  transfers between devices with their start and end apart: 19 -> 19, of which waited for: 6 -> 8; matrix products, arithmetic and copies ran while one was open for 3% -> 3% of each run, Pallas kernels for 24% -> 18%
where the time goes in v7:
time: 61.6 us; the launch traced here: 61.4 us
  starting transfers between devices  22.1 us (36%)
  Pallas kernels  20.2 us (33%)
  waiting for transfers between devices  15.9 us (26%)
  other arithmetic  1.84 us (3%)
  local copies, waits for them, and re-layouts  0.94 us (2%)
    pallas_call x11, Pallas kernels, call(): pl.pallas_call(ordered_body if after else body, out_shape=outs, in_specs=...  20.2 us
    ppermute x16, starting transfers between devices, moved(): lax.ppermute(value, axis, [(i, (i + steps) % count) for i in range(count)])  17.5 us
    ppermute x16, waiting for transfers between devices, moved(): lax.ppermute(value, axis, [(i, (i + steps) % count) for i in range(count)])  15.9 us
    ppermute x3, starting transfers between devices, swapped(): return lax.ppermute(value, axis, [(0, 1), (1, 0)])  4.62 us
  transfers between devices with their start and end apart: 19, of which 8 were waited for; matrix products, arithmetic and copies ran while one was open for 3% of the time, Pallas kernels for 18%

profile of v7, /device:TPU:0, one launch (start us, length us, event | category | flops | bytes accessed | tf_op | source)
XLA Modules:
  0.0 61.4 jit_solution(1479606987243597093)
XLA Ops:
  0.0 3.0 %collective-permute-start = (bf16[64,128]{1,0:T(8,128)(2,1)}, bf16[64,128]{1,0:T(8,128)(2,1)S(1)}, u32[]{:S(2)}, u32[]{:S(2)}) collective-permute-start(bf16[64,128]{1,0:T(8,128)(2,1)} %h_ref.1), channel_id=1, source_target_pairs={{0,1},{1,0},{2,3},{3,2},{4,5},{5,4},{6,7},{7,6},{8,9},{9,8},{10,11... | collective-permute-start | bytes 49160 | tf_op jit(solution)/shard_map/ppermute | solution.py:17
  3.0 0.8 %or_convert_fusion = f32[36,128]{1,0:T(8,128)S(1)} fusion(s32[4608]{0:T(1024)} %param.23, s32[4608]{0:T(1024)} %param.20, s32[4608]{0:T(1024)} %param.19), kind=kLoop, calls=%fused_computation.22 | loop fusion | flops 27648 | bytes 73728 | tf_op jit(solution)/shard_map/convert_element_type | solution.py:428
  3.7 0.7 %pad_maximum_fusion.9.both_ref = f32[72,128]{1,0:T(8,128)S(1)} fusion(f32[36,128]{1,0:T(8,128)} %bitcast.86, f32[36,128]{1,0:T(8,128)S(1)} %or_convert_fusion), kind=kLoop, calls=%fused_computation.21 | loop fusion | flops 9216 | bytes 73728 | tf_op jit(solution)/shard_map/concatenate | solution.py:427
  4.5 0.7 %copy-done.12 = bf16[64,128]{1,0:T(8,128)(2,1)S(1)} copy-done((bf16[64,128]{1,0:T(8,128)(2,1)S(1)}, bf16[64,128]{1,0:T(8,128)(2,1)}, u32[]{:S(2)}) %copy-start.12) | copy-done | bytes 16408
  5.2 1.4 %shard_map.154 = (bf16[64,1152]{1,0:T(8,128)(2,1)S(1)}, s32[72,64]{1,0:T(8,128)S(1)}, bf16[64,128]{1,0:T(8,128)(2,1)S(1)}) custom-call(f32[72,128]{1,0:T(8,128)S(1)} %pad_maximum_fusion.9.both_ref, bf16[64,128]{1,0:T(8,128)(2,1)S(1)} %copy-done.12), custom_call_target="tpu_custom_call" | custom-call | flops 2200000000 | bytes 7200000 | tf_op jit(solution)/shard_map/pallas_call | solution.py:83
  6.6 0.1 collective-permute-start.5
  6.7 0.0 collective-permute-done
  6.7 4.1 %collective-permute-start.2 = (bf16[2,1,1,64,128]{4,3,2,1,0:T(8,128)(2,1)S(1)}, bf16[2,1,1,64,128]{4,3,2,1,0:T(8,128)(2,1)S(1)}, u32[]{:S(2)}, u32[]{:S(2)}) collective-permute-start(bf16[2,1,1,64,128]{4,3,2,1,0:T(8,128)(2,1)S(1)} %bitcast.74), channel_id=1, source_target_pairs={{0,24},{8,0},{16,8},{24,16},{1,25},{9,1},{17,9},{25,17},{2,26},{10... | collective-permute-start | bytes 98312 | tf_op jit(solution)/shard_map/ppermute | solution.py:22
  10.8 0.0 collective-permute-start.1
  10.8 0.0 copy-start.2
  10.8 0.0 copy-start.3
  10.8 0.0 copy-start.4
  10.9 0.0 copy-start.14
  10.9 1.9 %shard_map.155 = (bf16[2304,128]{1,0:T(8,128)(2,1)S(1)}, bf16[128,128]{1,0:T(8,128)(2,1)S(1)}) custom-call(s32[18,128]{1,0:T(8,128)S(1)} %bitcast.77, bf16[2304,128]{1,0:T(8,128)(2,1)S(1)} %copy-done.6, bf16[128,128]{1,0:T(8,128)(2,1)S(1)} %constant_dynamic-update-slice_fusion.h_ref), custom_call_target="tpu_custom_call" | custom-call | flops 2200000000 | bytes 7200000 | tf_op jit(solution)/shard_map/pallas_call | solution.py:83
  12.9 1.6 %collective-permute-start.6 = (bf16[3,3,128,128]{3,2,1,0:T(8,128)(2,1)S(1)}, bf16[3,3,128,128]{3,2,1,0:T(8,128)(2,1)S(1)}, u32[]{:S(2)}, u32[]{:S(2)}) collective-permute-start(bf16[3,3,128,128]{3,2,1,0:T(8,128)(2,1)S(1)} %bitcast.81), channel_id=1, source_target_pairs={{0,1},{1,0},{2,3},{3,2},{4,5},{5,4},{6,7},{7,6},{8,9},{9,8},{10,11... | collective-permute-start | bytes 884744 | tf_op jit(solution)/shard_map/ppermute | solution.py:17
  14.4 0.0 copy-start.11
  14.5 2.2 %shard_map.156 = (bf16[2304,128]{1,0:T(8,128)(2,1)S(1)}, bf16[2304,128]{1,0:T(8,128)(2,1)S(1)}, f32[72,64]{1,0:T(8,128)S(1)}) custom-call(s32[18,128]{1,0:T(8,128)S(1)} %bitcast.78, s32[18,128]{1,0:T(8,128)S(1)} %bitcast.79, s32[36,128]{1,0:T(8,128)S(1)} %bitcast.73, s32[36,128]{1,0:T(8,128)S(1)} %bitcast.72, s32[36,128]{1,0:T(8,128)S(1)} %bitcast.71, ...), custom_call_target="tpu_custom_call" | custom-call | flops 2750000128 | bytes 9000000 | tf_op jit(solution)/shard_map/pallas_call | solution.py:83
  16.7 0.0 collective-permute-done.2
  16.7 0.0 collective-permute-done.1
  16.7 0.1 collective-permute-start.4
  16.8 0.5 collective-permute-start.3
  17.3 2.4 %shard_map.159 = (bf16[2304,128]{1,0:T(8,128)(2,1)S(1)}, bf16[2304,128]{1,0:T(8,128)(2,1)S(1)}, bf16[4608,144]{1,0:T(8,128)(2,1)S(1)}, f32[72,64]{1,0:T(8,128)S(1)}, bf16[169,256]{1,0:T(8,128)(2,1)S(1)}) custom-call(s32[72,64]{1,0:T(8,128)S(1)} %get-tuple-element.22.refs_5_.pack_ref, f32[72,64]{1,0:T(8,128)S(1)} %get-tuple-element.26.place_ref, ...), custom_call_target="tpu_custom_call" | custom-call | flops 2750000128 | bytes 9000000 | tf_op jit(solution)/shard_map/pallas_call | solution.py:83
  19.7 0.0 copy-start.7
  19.7 0.0 copy-start.8
  19.7 0.0 copy-start.9
  19.7 0.0 copy-start.10
  19.8 0.0 collective-permute-done.4
  19.8 2.1 %collective-permute-done.3 = bf16[2,3,1,64,128]{4,3,2,1,0:T(8,128)(2,1)S(1)} collective-permute-done((bf16[2,3,1,64,128]{4,3,2,1,0:T(8,128)(2,1)S(1)}, bf16[2,3,1,64,128]{4,3,2,1,0:T(8,128)(2,1)S(1)}, u32[]{:S(2)}, u32[]{:S(2)}) %collective-permute-start.3) | collective-permute-done | bytes 98336 | tf_op jit(solution)/shard_map/ppermute | solution.py:22
  21.9 0.0 collective-permute-done.5.refs_1_
  21.9 0.0 collective-permute-done.6.refs_6_
  22.0 0.6 %shard_map.158 = bf16[128,128]{1,0:T(8,128)(2,1)S(1)} custom-call(bf16[64,1152]{1,0:T(8,128)(2,1)S(1)} %get-tuple-element.25.refs_0_, bf16[64,1152]{1,0:T(8,128)(2,1)S(1)} %collective-permute-done.5.refs_1_, bf16[1152,128]{1,0:T(8,128)(2,1)S(1)} %bitcast.56, bf16[2,128,128]{2,1,0:T(8,128)(2,1)S(1)} %copy-done, bf16[2,128,128]{2,1,0:T(8,128)(2,1)S(1)} %copy-done.1, ...), custom_call_target="tpu_custom_call" | custom-call | flops 660000000 | bytes 2160000 | tf_op jit(solution)/shard_map/pallas_call | solution.py:83
  22.6 3.9 %collective-permute-start.8 = (bf16[2,1,1,64,128]{4,3,2,1,0:T(8,128)(2,1)S(1)}, bf16[2,1,1,64,128]{4,3,2,1,0:T(8,128)(2,1)S(1)}, u32[]{:S(2)}, u32[]{:S(2)}) collective-permute-start(bf16[2,1,1,64,128]{4,3,2,1,0:T(8,128)(2,1)S(1)} %bitcast.63), channel_id=1, source_target_pairs={{0,24},{8,0},{16,8},{24,16},{1,25},{9,1},{17,9},{25,17},{2,26},{10... | collective-permute-start | bytes 98312 | tf_op jit(solution)/shard_map/ppermute | solution.py:22
  26.5 0.0 collective-permute-start.7
  26.5 0.1 fusion.3
  26.5 0.1 collective-permute-start.11
  26.6 3.9 %collective-permute-start.12 = (bf16[2,3,128,128]{3,2,1,0:T(8,128)(2,1)S(1)}, bf16[2,3,128,128]{3,2,1,0:T(8,128)(2,1)S(1)}, u32[]{:S(2)}, u32[]{:S(2)}) collective-permute-start(bf16[2,3,128,128]{3,2,1,0:T(8,128)(2,1)S(1)} %get-tuple-element.39), channel_id=1, source_target_pairs={{0,24},{8,0},{16,8},{24,16},{1,25},{9,1},{17,9},{25,17},{2,26},{10... | collective-permute-start | bytes 589832 | tf_op jit(solution)/shard_map/ppermute | solution.py:22
  30.5 0.0 collective-permute-done.8
  30.5 2.2 %collective-permute-done.7 = bf16[2,1,1,64,128]{4,3,2,1,0:T(8,128)(2,1)S(1)} collective-permute-done((bf16[2,1,1,64,128]{4,3,2,1,0:T(8,128)(2,1)S(1)}, bf16[2,1,1,64,128]{4,3,2,1,0:T(8,128)(2,1)S(1)}, u32[]{:S(2)}, u32[]{:S(2)}) %collective-permute-start.7) | collective-permute-done | bytes 32800 | tf_op jit(solution)/shard_map/ppermute | solution.py:22
  32.7 0.1 collective-permute-start.10
  32.8 0.5 collective-permute-start.9
  33.3 1.3 %shard_map.157.refs_7_.refs_0_ = bf16[2304,128]{1,0:T(8,128)(2,1)S(1)} custom-call(bf16[2304,128]{1,0:T(8,128)(2,1)S(1)} %get-tuple-element.21.refs_6_.e_ref, bf16[2304,128]{1,0:T(8,128)(2,1)S(1)} %get-tuple-element.23.hot_ref.refs_1_.ho_ref, bf16[1152,128]{1,0:T(8,128)(2,1)S(1)} %bitcast.57, bf16[3,128,128]{2,1,0:T(8,128)(2,1)S(1)} %copy-done.7, ...), custom_call_target="tpu_custom_call" | custom-call | flops 1540000000 | bytes 5040000 | tf_op jit(solution)/shard_map/pallas_call | solution.py:83
  34.6 1.3 %collective-permute-done.10 = bf16[2,3,1,64,128]{4,3,2,1,0:T(8,128)(2,1)S(1)} collective-permute-done((bf16[2,3,1,64,128]{4,3,2,1,0:T(8,128)(2,1)S(1)}, bf16[2,3,1,64,128]{4,3,2,1,0:T(8,128)(2,1)S(1)}, u32[]{:S(2)}, u32[]{:S(2)}) %collective-permute-start.10) | collective-permute-done | bytes 98336 | tf_op jit(solution)/shard_map/ppermute | solution.py:22
  35.9 1.0 %collective-permute-done.9 = bf16[2,3,1,64,128]{4,3,2,1,0:T(8,128)(2,1)S(1)} collective-permute-done((bf16[2,3,1,64,128]{4,3,2,1,0:T(8,128)(2,1)S(1)}, bf16[2,3,1,64,128]{4,3,2,1,0:T(8,128)(2,1)S(1)}, u32[]{:S(2)}, u32[]{:S(2)}) %collective-permute-start.9) | collective-permute-done | bytes 98336 | tf_op jit(solution)/shard_map/ppermute | solution.py:22
  37.0 0.6 shard_map.160.refs_7_
  37.6 0.1 collective-permute-start.16
  37.7 2.0 %collective-permute-start.15 = (bf16[2,1,1,64,128]{4,3,2,1,0:T(8,128)(2,1)S(1)}, bf16[2,1,1,64,128]{4,3,2,1,0:T(8,128)(2,1)S(1)}, u32[]{:S(2)}, u32[]{:S(2)}) collective-permute-start(bf16[2,1,1,64,128]{4,3,2,1,0:T(8,128)(2,1)S(1)} %bitcast.70), channel_id=1, source_target_pairs={{0,8},{8,16},{16,24},{24,0},{1,9},{9,17},{17,25},{25,1},{2,10},{10... | collective-permute-start | bytes 98312 | tf_op jit(solution)/shard_map/ppermute | solution.py:22
  39.7 0.0 collective-permute-done.11
  39.7 0.0 collective-permute-done.12
  39.7 0.1 pad_maximum_fusion.refs_8_
  39.8 1.3 %shard_map.161 = (bf16[2304,128]{1,0:T(8,128)(2,1)S(1)}, bf16[128,128]{1,0:T(8,128)(2,1)S(1)}) custom-call(bf16[2304,128]{1,0:T(8,128)(2,1)S(1)} %shard_map.157.refs_7_.refs_0_, bf16[2304,128]{1,0:T(8,128)(2,1)S(1)} %get-tuple-element.23.hot_ref.refs_1_.ho_ref, bf16[1152,128]{1,0:T(8,128)(2,1)S(1)} %bitcast.53, bf16[3,128,128]{2,1,0:T(8,128)(2,1)S(1)} %copy-done.7, ...), custom_call_target="tpu_custom_call" | custom-call | flops 1540000000 | bytes 5040000 | tf_op jit(solution)/shard_map/pallas_call | solution.py:83
  41.1 0.8 %collective-permute-done.16 = bf16[2,1,1,64,128]{4,3,2,1,0:T(8,128)(2,1)S(1)} collective-permute-done((bf16[2,1,1,64,128]{4,3,2,1,0:T(8,128)(2,1)S(1)}, bf16[2,1,1,64,128]{4,3,2,1,0:T(8,128)(2,1)S(1)}, u32[]{:S(2)}, u32[]{:S(2)}) %collective-permute-start.16) | collective-permute-done | bytes 32800 | tf_op jit(solution)/shard_map/ppermute | solution.py:22
  41.9 1.7 %collective-permute-done.15 = bf16[2,1,1,64,128]{4,3,2,1,0:T(8,128)(2,1)S(1)} collective-permute-done((bf16[2,1,1,64,128]{4,3,2,1,0:T(8,128)(2,1)S(1)}, bf16[2,1,1,64,128]{4,3,2,1,0:T(8,128)(2,1)S(1)}, u32[]{:S(2)}, u32[]{:S(2)}) %collective-permute-start.15) | collective-permute-done | bytes 32800 | tf_op jit(solution)/shard_map/ppermute | solution.py:22
  43.7 0.1 collective-permute-start.18
  43.7 0.5 collective-permute-start.17
  44.3 1.2 %collective-permute-start.13 = (bf16[2,3,128,128]{3,2,1,0:T(8,128)(2,1)S(1)}, bf16[2,3,128,128]{3,2,1,0:T(8,128)(2,1)S(1)}, u32[]{:S(2)}, u32[]{:S(2)}) collective-permute-start(bf16[2,3,128,128]{3,2,1,0:T(8,128)(2,1)S(1)} %get-tuple-element.35), channel_id=1, source_target_pairs={{0,2},{2,4},{4,6},{6,0},{1,3},{3,5},{5,7},{7,1},{8,10},{10,12},{12... | collective-permute-start | bytes 589832 | tf_op jit(solution)/shard_map/ppermute | solution.py:22
  45.5 0.6 collective-permute-start.14
  46.1 0.0 collective-permute-done.18
  46.1 2.8 %collective-permute-done.17 = bf16[2,3,1,64,128]{4,3,2,1,0:T(8,128)(2,1)S(1)} collective-permute-done((bf16[2,3,1,64,128]{4,3,2,1,0:T(8,128)(2,1)S(1)}, bf16[2,3,1,64,128]{4,3,2,1,0:T(8,128)(2,1)S(1)}, u32[]{:S(2)}, u32[]{:S(2)}) %collective-permute-start.17) | collective-permute-done | bytes 98336 | tf_op jit(solution)/shard_map/ppermute | solution.py:22
  48.9 3.9 %collective-permute-done.13 = bf16[2,3,128,128]{3,2,1,0:T(8,128)(2,1)S(1)} collective-permute-done((bf16[2,3,128,128]{3,2,1,0:T(8,128)(2,1)S(1)}, bf16[2,3,128,128]{3,2,1,0:T(8,128)(2,1)S(1)}, u32[]{:S(2)}, u32[]{:S(2)}) %collective-permute-start.13) | collective-permute-done | bytes 196640 | tf_op jit(solution)/shard_map/ppermute | solution.py:22
  52.7 0.0 collective-permute-done.14
  52.7 0.1 pad_maximum_fusion.1
  52.9 1.3 %shard_map.162.e_ref = bf16[2304,128]{1,0:T(8,128)(2,1)S(1)} custom-call(bf16[2304,128]{1,0:T(8,128)(2,1)S(1)} %bitcast.55, bf16[2304,128]{1,0:T(8,128)(2,1)S(1)} %get-tuple-element.29.hot_ref.hm_ref, bf16[1152,128]{1,0:T(8,128)(2,1)S(1)} %bitcast.58, bf16[3,128,128]{2,1,0:T(8,128)(2,1)S(1)} %copy-done.8, bf16[3,128,128]{2,1,0:T(8,128)(2,1)S(1)} %copy-done.7, ...), custom_call_target="tpu_custom_call" | custom-call | flops 1540000000 | bytes 5040000 | tf_op jit(solution)/shard_map/pallas_call | solution.py:83
  54.2 1.3 %shard_map.163.mir_ref = bf16[2304,128]{1,0:T(8,128)(2,1)S(1)} custom-call(bf16[2304,128]{1,0:T(8,128)(2,1)S(1)} %shard_map.162.e_ref, bf16[2304,128]{1,0:T(8,128)(2,1)S(1)} %get-tuple-element.29.hot_ref.hm_ref, bf16[1152,128]{1,0:T(8,128)(2,1)S(1)} %bitcast.54, bf16[3,128,128]{2,1,0:T(8,128)(2,1)S(1)} %copy-done.8, bf16[3,128,128]{2,1,0:T(8,128)(2,1)S(1)} %copy-done.7, ...), custom_call_target="tpu_custom_call" | custom-call | flops 1540000000 | bytes 5040000 | tf_op jit(solution)/shard_map/pallas_call | solution.py:83
  55.5 5.9 %shard_map.164 = bf16[169,4608]{1,0:T(8,128)(2,1)} custom-call(bf16[2304,128]{1,0:T(8,128)(2,1)S(1)} %get-tuple-element.28.own_ref, bf16[2304,128]{1,0:T(8,128)(2,1)S(1)} %shard_map.163.mir_ref, bf16[2304,128]{1,0:T(8,128)(2,1)S(1)} %get-tuple-element.23.hot_ref.refs_1_.ho_ref, bf16[2304,128]{1,0:T(8,128)(2,1)S(1)} %get-tuple-element.29.hot_ref.hm_ref, ...), custom_call_target="tpu_custom_call" | custom-call | flops 7699999744 | bytes 25200000 | tf_op jit(solution)/shard_map/pallas_call | solution.py:83
  (31 shorter events, 0.3 us)
Async XLA Ops:
  0.0 6.7 %collective-permute-start = (bf16[64,128]{1,0:T(8,128)(2,1)}, bf16[64,128]{1,0:T(8,128)(2,1)S(1)}, u32[]{:S(2)}, u32[]{:S(2)}) collective-permute-start(bf16[64,128]{1,0:T(8,128)(2,1)} %h_ref.1), channel_id=1, source_target_pairs={{0,1},{1,0},{2,3},{3,2},{4,5},{5,4},{6,7},{7,6},{8,9},{9,8},{10,11... | collective-permute-start | bytes 49160 | tf_op jit(solution)/shard_map/ppermute | solution.py:17
  4.5 0.7 %copy-start.12 = (bf16[64,128]{1,0:T(8,128)(2,1)S(1)}, bf16[64,128]{1,0:T(8,128)(2,1)}, u32[]{:S(2)}) copy-start(bf16[64,128]{1,0:T(8,128)(2,1)} %h_ref.1) | copy-start | bytes 49156
  5.2 5.6 %copy-start.6 = (bf16[2304,128]{1,0:T(8,128)(2,1)S(1)}, bf16[2304,128]{1,0:T(8,128)(2,1)}, u32[]{:S(2)}) copy-start(bf16[2304,128]{1,0:T(8,128)(2,1)} %bond_ref.1) | copy-start | bytes 1769476
  5.2 5.6 %copy-start.13 = (s32[2304]{0:T(1024)S(1)}, s32[2304]{0:T(1024)}, u32[]{:S(2)}) copy-start(s32[2304]{0:T(1024)} %param.22) | copy-start | bytes 27652
  6.6 15.4 %collective-permute-start.5 = (bf16[64,1152]{1,0:T(8,128)(2,1)S(1)}, bf16[64,1152]{1,0:T(8,128)(2,1)S(1)}, u32[]{:S(2)}, u32[]{:S(2)}) collective-permute-start(bf16[64,1152]{1,0:T(8,128)(2,1)S(1)} %get-tuple-element.25.refs_0_), channel_id=1, source_target_pairs={{0,1},{1,0},{2,3},{3,2},{4,5},{5,4},{6,7},{7,6},{8,9},{9,8},{10,11... | collective-permute-start | bytes 442376 | tf_op jit(solution)/shard_map/ppermute | solution.py:17
  6.7 10.0 %collective-permute-start.2 = (bf16[2,1,1,64,128]{4,3,2,1,0:T(8,128)(2,1)S(1)}, bf16[2,1,1,64,128]{4,3,2,1,0:T(8,128)(2,1)S(1)}, u32[]{:S(2)}, u32[]{:S(2)}) collective-permute-start(bf16[2,1,1,64,128]{4,3,2,1,0:T(8,128)(2,1)S(1)} %bitcast.74), channel_id=1, source_target_pairs={{0,24},{8,0},{16,8},{24,16},{1,25},{9,1},{17,9},{25,17},{2,26},{10... | collective-permute-start | bytes 98312 | tf_op jit(solution)/shard_map/ppermute | solution.py:22
  10.8 5.9 %collective-permute-start.1 = (bf16[2,1,1,64,128]{4,3,2,1,0:T(8,128)(2,1)S(1)}, bf16[2,1,1,64,128]{4,3,2,1,0:T(8,128)(2,1)S(1)}, u32[]{:S(2)}, u32[]{:S(2)}) collective-permute-start(bf16[2,1,1,64,128]{4,3,2,1,0:T(8,128)(2,1)S(1)} %bitcast.75), channel_id=1, source_target_pairs={{0,8},{8,16},{16,24},{24,0},{1,9},{9,17},{17,25},{25,1},{2,10},{10... | collective-permute-start | bytes 98312 | tf_op jit(solution)/shard_map/ppermute | solution.py:22
  10.8 3.6 %copy-start.2 = (s32[4608]{0:T(1024)S(1)}, s32[4608]{0:T(1024)}, u32[]{:S(2)}) copy-start(s32[4608]{0:T(1024)} %param.23) | copy-start | bytes 55300
  10.8 3.6 %copy-start.3 = (s32[4608]{0:T(1024)S(1)}, s32[4608]{0:T(1024)}, u32[]{:S(2)}) copy-start(s32[4608]{0:T(1024)} %param.20) | copy-start | bytes 55300
  10.8 3.6 %copy-start.4 = (s32[4608]{0:T(1024)S(1)}, s32[4608]{0:T(1024)}, u32[]{:S(2)}) copy-start(s32[4608]{0:T(1024)} %param.19) | copy-start | bytes 55300
  10.9 3.6 %copy-start.14 = (s32[2304]{0:T(1024)S(1)}, s32[2304]{0:T(1024)}, u32[]{:S(2)}) copy-start(s32[2304]{0:T(1024)} %param.21) | copy-start | bytes 27652
  12.9 9.1 %collective-permute-start.6 = (bf16[3,3,128,128]{3,2,1,0:T(8,128)(2,1)S(1)}, bf16[3,3,128,128]{3,2,1,0:T(8,128)(2,1)S(1)}, u32[]{:S(2)}, u32[]{:S(2)}) collective-permute-start(bf16[3,3,128,128]{3,2,1,0:T(8,128)(2,1)S(1)} %bitcast.81), channel_id=1, source_target_pairs={{0,1},{1,0},{2,3},{3,2},{4,5},{5,4},{6,7},{7,6},{8,9},{9,8},{10,11... | collective-permute-start | bytes 884744 | tf_op jit(solution)/shard_map/ppermute | solution.py:17
  14.4 2.8 %copy-start.11 = (bf16[128,169]{0,1:T(8,128)(2,1)S(1)}, bf16[128,169]{0,1:T(8,128)(2,1)}, u32[]{:S(2)}) copy-start(bf16[128,169]{0,1:T(8,128)(2,1)} %param.31) | copy-start | bytes 129796
  16.7 3.1 %collective-permute-start.4 = (bf16[2,3,1,64,128]{4,3,2,1,0:T(8,128)(2,1)S(1)}, bf16[2,3,1,64,128]{4,3,2,1,0:T(8,128)(2,1)S(1)}, u32[]{:S(2)}, u32[]{:S(2)}) collective-permute-start(bf16[2,3,1,64,128]{4,3,2,1,0:T(8,128)(2,1)S(1)} %pad_maximum_fusion.6), channel_id=1, source_target_pairs={{0,6},{2,0},{4,2},{6,4},{1,7},{3,1},{5,3},{7,5},{8,14},{10,8},{12,... | collective-permute-start | bytes 294920 | tf_op jit(solution)/shard_map/ppermute | solution.py:22
  16.8 5.1 %collective-permute-start.3 = (bf16[2,3,1,64,128]{4,3,2,1,0:T(8,128)(2,1)S(1)}, bf16[2,3,1,64,128]{4,3,2,1,0:T(8,128)(2,1)S(1)}, u32[]{:S(2)}, u32[]{:S(2)}) collective-permute-start(bf16[2,3,1,64,128]{4,3,2,1,0:T(8,128)(2,1)S(1)} %pad_maximum_fusion.6), channel_id=1, source_target_pairs={{0,2},{2,4},{4,6},{6,0},{1,3},{3,5},{5,7},{7,1},{8,10},{10,12},{12... | collective-permute-start | bytes 294920 | tf_op jit(solution)/shard_map/ppermute | solution.py:22
  17.3 4.7 %copy-start = (bf16[2,128,128]{2,1,0:T(8,128)(2,1)S(1)}, bf16[2,128,128]{2,1,0:T(8,128)(2,1)}, u32[]{:S(2)}) copy-start(bf16[2,128,128]{2,1,0:T(8,128)(2,1)} %refs_3_.4) | copy-start | bytes 196612
  17.3 4.7 %copy-start.1 = (bf16[2,128,128]{2,1,0:T(8,128)(2,1)S(1)}, bf16[2,128,128]{2,1,0:T(8,128)(2,1)}, u32[]{:S(2)}) copy-start(bf16[2,128,128]{2,1,0:T(8,128)(2,1)} %refs_4_.4) | copy-start | bytes 196612
  17.3 4.7 %copy-start.5 = (f32[2,128]{1,0:T(2,128)S(1)}, f32[2,128]{1,0:T(2,128)}, u32[]{:S(2)}) copy-start(f32[2,128]{1,0:T(2,128)} %refs_5_.4) | copy-start | bytes 3076
  19.7 13.6 %copy-start.7 = (bf16[3,128,128]{2,1,0:T(8,128)(2,1)S(1)}, bf16[3,128,128]{2,1,0:T(8,128)(2,1)}, u32[]{:S(2)}) copy-start(bf16[3,128,128]{2,1,0:T(8,128)(2,1)} %wl_ref.7) | copy-start | bytes 294916
  19.7 13.6 %copy-start.8 = (bf16[3,128,128]{2,1,0:T(8,128)(2,1)S(1)}, bf16[3,128,128]{2,1,0:T(8,128)(2,1)}, u32[]{:S(2)}) copy-start(bf16[3,128,128]{2,1,0:T(8,128)(2,1)} %wr_ref.1) | copy-start | bytes 294916
  19.7 13.5 %copy-start.9 = (bf16[3,128,128]{2,1,0:T(8,128)(2,1)S(1)}, bf16[3,128,128]{2,1,0:T(8,128)(2,1)}, u32[]{:S(2)}) copy-start(bf16[3,128,128]{2,1,0:T(8,128)(2,1)} %wi_ref.7) | copy-start | bytes 294916
  19.7 13.5 %copy-start.10 = (bf16[3,128,128]{2,1,0:T(8,128)(2,1)S(1)}, bf16[3,128,128]{2,1,0:T(8,128)(2,1)}, u32[]{:S(2)}) copy-start(bf16[3,128,128]{2,1,0:T(8,128)(2,1)} %wo_ref.7) | copy-start | bytes 294916
  22.6 7.9 %collective-permute-start.8 = (bf16[2,1,1,64,128]{4,3,2,1,0:T(8,128)(2,1)S(1)}, bf16[2,1,1,64,128]{4,3,2,1,0:T(8,128)(2,1)S(1)}, u32[]{:S(2)}, u32[]{:S(2)}) collective-permute-start(bf16[2,1,1,64,128]{4,3,2,1,0:T(8,128)(2,1)S(1)} %bitcast.63), channel_id=1, source_target_pairs={{0,24},{8,0},{16,8},{24,16},{1,25},{9,1},{17,9},{25,17},{2,26},{10... | collective-permute-start | bytes 98312 | tf_op jit(solution)/shard_map/ppermute | solution.py:22
  26.5 6.2 %collective-permute-start.7 = (bf16[2,1,1,64,128]{4,3,2,1,0:T(8,128)(2,1)S(1)}, bf16[2,1,1,64,128]{4,3,2,1,0:T(8,128)(2,1)S(1)}, u32[]{:S(2)}, u32[]{:S(2)}) collective-permute-start(bf16[2,1,1,64,128]{4,3,2,1,0:T(8,128)(2,1)S(1)} %bitcast.64), channel_id=1, source_target_pairs={{0,8},{8,16},{16,24},{24,0},{1,9},{9,17},{17,25},{25,1},{2,10},{10... | collective-permute-start | bytes 98312 | tf_op jit(solution)/shard_map/ppermute | solution.py:22
  26.5 13.2 %collective-permute-start.11 = (bf16[2,3,128,128]{3,2,1,0:T(8,128)(2,1)S(1)}, bf16[2,3,128,128]{3,2,1,0:T(8,128)(2,1)S(1)}, u32[]{:S(2)}, u32[]{:S(2)}) collective-permute-start(bf16[2,3,128,128]{3,2,1,0:T(8,128)(2,1)S(1)} %get-tuple-element.38), channel_id=1, source_target_pairs={{0,8},{8,16},{16,24},{24,0},{1,9},{9,17},{17,25},{25,1},{2,10},{10... | collective-permute-start | bytes 589832 | tf_op jit(solution)/shard_map/ppermute | solution.py:22
  26.6 13.1 %collective-permute-start.12 = (bf16[2,3,128,128]{3,2,1,0:T(8,128)(2,1)S(1)}, bf16[2,3,128,128]{3,2,1,0:T(8,128)(2,1)S(1)}, u32[]{:S(2)}, u32[]{:S(2)}) collective-permute-start(bf16[2,3,128,128]{3,2,1,0:T(8,128)(2,1)S(1)} %get-tuple-element.39), channel_id=1, source_target_pairs={{0,24},{8,0},{16,8},{24,16},{1,25},{9,1},{17,9},{25,17},{2,26},{10... | collective-permute-start | bytes 589832 | tf_op jit(solution)/shard_map/ppermute | solution.py:22
  32.7 3.2 %collective-permute-start.10 = (bf16[2,3,1,64,128]{4,3,2,1,0:T(8,128)(2,1)S(1)}, bf16[2,3,1,64,128]{4,3,2,1,0:T(8,128)(2,1)S(1)}, u32[]{:S(2)}, u32[]{:S(2)}) collective-permute-start(bf16[2,3,1,64,128]{4,3,2,1,0:T(8,128)(2,1)S(1)} %pad_maximum_fusion.7), channel_id=1, source_target_pairs={{0,6},{2,0},{4,2},{6,4},{1,7},{3,1},{5,3},{7,5},{8,14},{10,8},{12,... | collective-permute-start | bytes 294920 | tf_op jit(solution)/shard_map/ppermute | solution.py:22
  32.8 4.2 %collective-permute-start.9 = (bf16[2,3,1,64,128]{4,3,2,1,0:T(8,128)(2,1)S(1)}, bf16[2,3,1,64,128]{4,3,2,1,0:T(8,128)(2,1)S(1)}, u32[]{:S(2)}, u32[]{:S(2)}) collective-permute-start(bf16[2,3,1,64,128]{4,3,2,1,0:T(8,128)(2,1)S(1)} %pad_maximum_fusion.7), channel_id=1, source_target_pairs={{0,2},{2,4},{4,6},{6,0},{1,3},{3,5},{5,7},{7,1},{8,10},{10,12},{12... | collective-permute-start | bytes 294920 | tf_op jit(solution)/shard_map/ppermute | solution.py:22
  37.6 4.3 %collective-permute-start.16 = (bf16[2,1,1,64,128]{4,3,2,1,0:T(8,128)(2,1)S(1)}, bf16[2,1,1,64,128]{4,3,2,1,0:T(8,128)(2,1)S(1)}, u32[]{:S(2)}, u32[]{:S(2)}) collective-permute-start(bf16[2,1,1,64,128]{4,3,2,1,0:T(8,128)(2,1)S(1)} %bitcast.69), channel_id=1, source_target_pairs={{0,24},{8,0},{16,8},{24,16},{1,25},{9,1},{17,9},{25,17},{2,26},{10... | collective-permute-start | bytes 98312 | tf_op jit(solution)/shard_map/ppermute | solution.py:22
  37.7 5.9 %collective-permute-start.15 = (bf16[2,1,1,64,128]{4,3,2,1,0:T(8,128)(2,1)S(1)}, bf16[2,1,1,64,128]{4,3,2,1,0:T(8,128)(2,1)S(1)}, u32[]{:S(2)}, u32[]{:S(2)}) collective-permute-start(bf16[2,1,1,64,128]{4,3,2,1,0:T(8,128)(2,1)S(1)} %bitcast.70), channel_id=1, source_target_pairs={{0,8},{8,16},{16,24},{24,0},{1,9},{9,17},{17,25},{25,1},{2,10},{10... | collective-permute-start | bytes 98312 | tf_op jit(solution)/shard_map/ppermute | solution.py:22
  43.7 2.4 %collective-permute-start.18 = (bf16[2,3,1,64,128]{4,3,2,1,0:T(8,128)(2,1)S(1)}, bf16[2,3,1,64,128]{4,3,2,1,0:T(8,128)(2,1)S(1)}, u32[]{:S(2)}, u32[]{:S(2)}) collective-permute-start(bf16[2,3,1,64,128]{4,3,2,1,0:T(8,128)(2,1)S(1)} %pad_maximum_fusion.8), channel_id=1, source_target_pairs={{0,6},{2,0},{4,2},{6,4},{1,7},{3,1},{5,3},{7,5},{8,14},{10,8},{12,... | collective-permute-start | bytes 294920 | tf_op jit(solution)/shard_map/ppermute | solution.py:22
  43.7 5.1 %collective-permute-start.17 = (bf16[2,3,1,64,128]{4,3,2,1,0:T(8,128)(2,1)S(1)}, bf16[2,3,1,64,128]{4,3,2,1,0:T(8,128)(2,1)S(1)}, u32[]{:S(2)}, u32[]{:S(2)}) collective-permute-start(bf16[2,3,1,64,128]{4,3,2,1,0:T(8,128)(2,1)S(1)} %pad_maximum_fusion.8), channel_id=1, source_target_pairs={{0,2},{2,4},{4,6},{6,0},{1,3},{3,5},{5,7},{7,1},{8,10},{10,12},{12... | collective-permute-start | bytes 294920 | tf_op jit(solution)/shard_map/ppermute | solution.py:22
  44.3 8.5 %collective-permute-start.13 = (bf16[2,3,128,128]{3,2,1,0:T(8,128)(2,1)S(1)}, bf16[2,3,128,128]{3,2,1,0:T(8,128)(2,1)S(1)}, u32[]{:S(2)}, u32[]{:S(2)}) collective-permute-start(bf16[2,3,128,128]{3,2,1,0:T(8,128)(2,1)S(1)} %get-tuple-element.35), channel_id=1, source_target_pairs={{0,2},{2,4},{4,6},{6,0},{1,3},{3,5},{5,7},{7,1},{8,10},{10,12},{12... | collective-permute-start | bytes 589832 | tf_op jit(solution)/shard_map/ppermute | solution.py:22
  45.5 7.3 %collective-permute-start.14 = (bf16[2,3,128,128]{3,2,1,0:T(8,128)(2,1)S(1)}, bf16[2,3,128,128]{3,2,1,0:T(8,128)(2,1)S(1)}, u32[]{:S(2)}, u32[]{:S(2)}) collective-permute-start(bf16[2,3,128,128]{3,2,1,0:T(8,128)(2,1)S(1)} %get-tuple-element.36), channel_id=1, source_target_pairs={{0,6},{2,0},{4,2},{6,4},{1,7},{3,1},{5,3},{7,5},{8,14},{10,8},{12,... | collective-permute-start | bytes 589832 | tf_op jit(solution)/shard_map/ppermute | solution.py:22

commit v8 on v7

--- a/solution.py
+++ b/solution.py
@@ -28,15 +28,22 @@
     return jnp.concatenate([low, block, high], axis=dim)
 
 
-def ghosts_of(sheets, centre=None):
+def rows_of(sheets, centre):
     low, high = moved(sheets, "gx", 1), moved(sheets, "gx", -1)
-    centre = sheets if centre is None else centre
-    framed = with_halo(jnp.concatenate([low, centre, high], axis=1), "gy", 2)
-    return framed.reshape(-1, sheets.shape[-1])
-
-
-def across_rows(outgoing, crossed):
-    sheets = jnp.stack([outgoing[0], crossed])
+    return jnp.concatenate([low, centre, high], axis=1)
+
+
+def columns_of(rows, middle=None):
+    low, high = moved(rows, "gy", 1), moved(rows, "gy", -1)
+    table = jnp.concatenate([low, rows if middle is None else middle, high], axis=2)
+    return table.reshape(-1, rows.shape[-1])
+
+
+def ghosts_of(sheets, centre):
+    return columns_of(rows_of(sheets, centre))
+
+
+def across_rows(sheets):
     rows = [moved(sheets[:, i], "gx", i - 1) if i != 1 else sheets[:, i] for i in (2, 1, 0)]
     return jnp.stack(rows, axis=1)
 
@@ -442,9 +449,9 @@
         us=2.0,
     )
     outgoing = ordered.reshape(2, 3, 3, cap, channels)
-    crossed = swapped(outgoing[1], "layer")
-    shifted = across_rows(outgoing, crossed)
-    mirror = across_columns(shifted).reshape(owned, channels)
+    rowed = across_rows(outgoing)
+    columned = across_columns(rowed)
+    mirror = jnp.stack([columned[0], swapped(columned[1], "layer")]).reshape(owned, channels)
     hot_own, hot_mir, place = call(
         pairs_body,
         (array(owned, 128), array(owned, 128), array(fan, atoms, dtype=F32)),
@@ -473,7 +480,7 @@
     def edge(layer, own, after=(), hand_on=()):
         values = (ordered, hot_own) if own else (mirror, hot_mir)
         weights = (w_left, w_right) if own else (w_right, w_left)
-        outs = (state, array(2 * atoms, channels)) if hand_on else state
+        outs = (state,) + tuple(array(*v.shape) for v in hand_on) if hand_on else state
         return call(
             edge_body(layer, bool(hand_on)),
             outs,
@@ -493,14 +500,15 @@
         )
 
     ghosts_at = [ghosts_of(framed_sheets(sheets), framed_sheets(centre))]
-    sheets = node(0, (crossed,))
-    ghosts_at.append(ghosts_of(framed_sheets(sheets)))
-    ordered = edge(0, True)
-    sheets = node(1, (perm, ordered))
-    ordered, centre = edge(1, True, after=(shifted,), hand_on=(sheets,))
+    sheets = node(0, (hot_own,))
+    ordered, centre = edge(0, True, after=(rowed,), hand_on=(sheets,))
+    ghosts_at.append(ghosts_of(framed_sheets(sheets), framed_sheets(centre)))
+    sheets = node(1, (perm, columned))
+    ordered, centre = edge(1, True, hand_on=(sheets,))
     mirror = edge(0, False)
-    mirror = edge(1, False)
-    ghost = ghosts_of(framed_sheets(sheets), framed_sheets(centre))
+    rows = rows_of(framed_sheets(sheets), framed_sheets(centre))
+    mirror, middle = edge(1, False, hand_on=(rows.reshape(6 * atoms, channels),))
+    ghost = columns_of(rows, middle.reshape(rows.shape))
     return call(
         final_body(2),
         array(block, slots),

time: 61.6 us -> 60.6 us (0.984)
  waiting for transfers between devices: 15.9 us -> 14 us
  local copies, waits for them, and re-layouts: 0.94 us -> 1.89 us
    ppermute x16, waiting for transfers between devices: 15.9 us -> 14 us  [moved(): lax.ppermute(value, axis, [(i, (i + steps) % count) for i in range(count)])]
    unnamed x31 -> x33, local copies, waits for them, and re-layouts: 0.8 us -> 1.71 us
  transfers between devices with their start and end apart: 19 -> 19, of which waited for: 8 -> 6; matrix products, arithmetic and copies ran while one was open for 3% -> 3% of each run, Pallas kernels for 18% -> 24%
where the time goes in v8:
time: 60.6 us; the launch traced here: 60.3 us
  starting transfers between devices  22 us (36%)
  Pallas kernels  20.2 us (33%)
  waiting for transfers between devices  14 us (23%)
  local copies, waits for them, and re-layouts  1.89 us (3%)
  other arithmetic  1.82 us (3%)
    pallas_call x11, Pallas kernels, call(): pl.pallas_call(ordered_body if after else body, out_shape=outs, in_specs=...  20.2 us
    ppermute x16, starting transfers between devices, moved(): lax.ppermute(value, axis, [(i, (i + steps) % count) for i in range(count)])  17.4 us
    ppermute x16, waiting for transfers between devices, moved(): lax.ppermute(value, axis, [(i, (i + steps) % count) for i in range(count)])  14 us
    ppermute x3, starting transfers between devices, swapped(): return lax.ppermute(value, axis, [(0, 1), (1, 0)])  4.62 us
    unnamed x33, local copies, waits for them, and re-layouts  1.71 us
  transfers between devices with their start and end apart: 19, of which 6 were waited for; matrix products, arithmetic and copies ran while one was open for 3% of the time, Pallas kernels for 24%

profile of v8, /device:TPU:0, one launch (start us, length us, event | category | flops | bytes accessed | tf_op | source)
XLA Modules:
  0.0 60.3 jit_solution(12427293344112148650)
XLA Ops:
  0.0 3.0 %collective-permute-start = (bf16[64,128]{1,0:T(8,128)(2,1)}, bf16[64,128]{1,0:T(8,128)(2,1)S(1)}, u32[]{:S(2)}, u32[]{:S(2)}) collective-permute-start(bf16[64,128]{1,0:T(8,128)(2,1)} %h_ref.1), channel_id=1, source_target_pairs={{0,1},{1,0},{2,3},{3,2},{4,5},{5,4},{6,7},{7,6},{8,9},{9,8},{10,11... | collective-permute-start | bytes 49160 | tf_op jit(solution)/shard_map/ppermute | solution.py:17
  3.0 0.8 %or_convert_fusion = f32[36,128]{1,0:T(8,128)S(1)} fusion(s32[4608]{0:T(1024)} %param.23, s32[4608]{0:T(1024)} %param.20, s32[4608]{0:T(1024)} %param.19), kind=kLoop, calls=%fused_computation.16 | loop fusion | flops 27648 | bytes 73728 | tf_op jit(solution)/shard_map/convert_element_type | solution.py:435
  3.7 0.7 %pad_maximum_fusion.9.both_ref = f32[72,128]{1,0:T(8,128)S(1)} fusion(f32[36,128]{1,0:T(8,128)} %bitcast.94, f32[36,128]{1,0:T(8,128)S(1)} %or_convert_fusion), kind=kLoop, calls=%fused_computation.15 | loop fusion | flops 9216 | bytes 73728 | tf_op jit(solution)/shard_map/concatenate | solution.py:434
  4.5 0.7 %copy-done.12 = bf16[64,128]{1,0:T(8,128)(2,1)S(1)} copy-done((bf16[64,128]{1,0:T(8,128)(2,1)S(1)}, bf16[64,128]{1,0:T(8,128)(2,1)}, u32[]{:S(2)}) %copy-start.12) | copy-done | bytes 16408
  5.2 1.4 %shard_map.154 = (bf16[64,1152]{1,0:T(8,128)(2,1)S(1)}, s32[72,64]{1,0:T(8,128)S(1)}, bf16[64,128]{1,0:T(8,128)(2,1)S(1)}) custom-call(f32[72,128]{1,0:T(8,128)S(1)} %pad_maximum_fusion.9.both_ref, bf16[64,128]{1,0:T(8,128)(2,1)S(1)} %copy-done.12), custom_call_target="tpu_custom_call" | custom-call | flops 2200000000 | bytes 7200000 | tf_op jit(solution)/shard_map/pallas_call | solution.py:90
  6.6 0.1 collective-permute-start.5
  6.7 0.0 collective-permute-done
  6.7 4.1 %collective-permute-start.2 = (bf16[2,1,1,64,128]{4,3,2,1,0:T(8,128)(2,1)S(1)}, bf16[2,1,1,64,128]{4,3,2,1,0:T(8,128)(2,1)S(1)}, u32[]{:S(2)}, u32[]{:S(2)}) collective-permute-start(bf16[2,1,1,64,128]{4,3,2,1,0:T(8,128)(2,1)S(1)} %bitcast.79), channel_id=1, source_target_pairs={{0,24},{8,0},{16,8},{24,16},{1,25},{9,1},{17,9},{25,17},{2,26},{10... | collective-permute-start | bytes 98312 | tf_op jit(solution)/shard_map/ppermute | solution.py:22
  10.8 0.0 collective-permute-start.1
  10.8 1.9 %shard_map.155 = (bf16[2304,128]{1,0:T(8,128)(2,1)S(1)}, bf16[128,128]{1,0:T(8,128)(2,1)S(1)}) custom-call(s32[18,128]{1,0:T(8,128)S(1)} %bitcast.84, bf16[2304,128]{1,0:T(8,128)(2,1)S(1)} %copy-done.6, bf16[128,128]{1,0:T(8,128)(2,1)S(1)} %constant_dynamic-update-slice_fusion.h_ref), custom_call_target="tpu_custom_call" | custom-call | flops 2200000000 | bytes 7200000 | tf_op jit(solution)/shard_map/pallas_call | solution.py:90
  12.8 0.0 copy-start.2
  12.8 0.0 copy-start.3
  12.8 0.0 copy-start.4
  12.8 0.0 copy-start.14
  12.9 3.9 %collective-permute-start.7 = (bf16[2,3,128,128]{3,2,0,1:T(8,128)(2,1)S(1)}, bf16[2,3,128,128]{3,2,0,1:T(8,128)(2,1)S(1)}, u32[]{:S(2)}, u32[]{:S(2)}) collective-permute-start(bf16[2,3,128,128]{3,2,0,1:T(8,128)(2,1)S(1)} %bitcast.93), channel_id=1, source_target_pairs={{0,24},{8,0},{16,8},{24,16},{1,25},{9,1},{17,9},{25,17},{2,26},{10... | collective-permute-start | bytes 589832 | tf_op jit(solution)/shard_map/ppermute | solution.py:22
  16.8 0.0 collective-permute-start.6
  16.8 0.0 collective-permute-done.2
  16.8 0.0 collective-permute-done.1
  16.8 0.1 collective-permute-start.4
  16.9 0.5 collective-permute-start.3
  17.4 0.0 copy-start
  17.4 0.0 copy-start.1
  17.4 0.0 copy-start.5
  17.4 2.2 %shard_map.156 = (bf16[2304,128]{1,0:T(8,128)(2,1)S(1)}, bf16[2304,128]{1,0:T(8,128)(2,1)S(1)}, f32[72,64]{1,0:T(8,128)S(1)}) custom-call(s32[18,128]{1,0:T(8,128)S(1)} %bitcast.85, s32[18,128]{1,0:T(8,128)S(1)} %bitcast.86, s32[36,128]{1,0:T(8,128)S(1)} %bitcast.78, s32[36,128]{1,0:T(8,128)S(1)} %bitcast.77, s32[36,128]{1,0:T(8,128)S(1)} %bitcast.76, ...), custom_call_target="tpu_custom_call" | custom-call | flops 2750000128 | bytes 9000000 | tf_op jit(solution)/shard_map/pallas_call | solution.py:90
  19.6 0.0 collective-permute-done.4
  19.6 2.4 %collective-permute-done.3 = bf16[2,3,1,64,128]{4,3,2,1,0:T(8,128)(2,1)S(1)} collective-permute-done((bf16[2,3,1,64,128]{4,3,2,1,0:T(8,128)(2,1)S(1)}, bf16[2,3,1,64,128]{4,3,2,1,0:T(8,128)(2,1)S(1)}, u32[]{:S(2)}, u32[]{:S(2)}) %collective-permute-start.3) | collective-permute-done | bytes 98336 | tf_op jit(solution)/shard_map/ppermute | solution.py:22
  22.0 0.0 collective-permute-done.5.refs_1_
  22.1 0.6 %shard_map.157.refs_7_ = bf16[128,128]{1,0:T(8,128)(2,1)S(1)} custom-call(bf16[64,1152]{1,0:T(8,128)(2,1)S(1)} %get-tuple-element.29.refs_0_, bf16[64,1152]{1,0:T(8,128)(2,1)S(1)} %collective-permute-done.5.refs_1_, bf16[1152,128]{1,0:T(8,128)(2,1)S(1)} %bitcast.63, bf16[2,128,128]{2,1,0:T(8,128)(2,1)S(1)} %copy-done, bf16[2,128,128]{2,1,0:T(8,128)(2,1)S(1)} %copy-done.1, ...), custom_call_target="tpu_custom_call" | custom-call | flops 660000000 | bytes 2160000 | tf_op jit(solution)/shard_map/pallas_call | solution.py:90
  22.7 3.9 %collective-permute-start.9 = (bf16[2,1,1,64,128]{4,3,2,1,0:T(8,128)(2,1)S(1)}, bf16[2,1,1,64,128]{4,3,2,1,0:T(8,128)(2,1)S(1)}, u32[]{:S(2)}, u32[]{:S(2)}) collective-permute-start(bf16[2,1,1,64,128]{4,3,2,1,0:T(8,128)(2,1)S(1)} %bitcast.82), channel_id=1, source_target_pairs={{0,24},{8,0},{16,8},{24,16},{1,25},{9,1},{17,9},{25,17},{2,26},{10... | collective-permute-start | bytes 98312 | tf_op jit(solution)/shard_map/ppermute | solution.py:22
  26.6 0.0 copy-start.7
  26.6 0.0 copy-start.8
  26.6 0.0 copy-start.9
  26.7 0.0 copy-start.10
  26.8 0.7 %copy-done.7 = bf16[3,128,128]{2,1,0:T(8,128)(2,1)S(1)} copy-done((bf16[3,128,128]{2,1,0:T(8,128)(2,1)S(1)}, bf16[3,128,128]{2,1,0:T(8,128)(2,1)}, u32[]{:S(2)}) %copy-start.7) | copy-done | bytes 98328
  27.5 0.0 copy-done.8
  27.6 0.0 copy-done.9
  27.6 0.0 copy-done.10
  27.7 1.3 %shard_map.158 = (bf16[2304,128]{1,0:T(8,128)(2,1)S(1)}, bf16[128,128]{1,0:T(8,128)(2,1)S(1)}) custom-call(bf16[2304,128]{1,0:T(8,128)(2,1)S(1)} %get-tuple-element.25.refs_6_.refs_0_, bf16[2304,128]{1,0:T(8,128)(2,1)S(1)} %get-tuple-element.27.refs_6_.refs_1_.hot_ref.ho_ref, bf16[1152,128]{1,0:T(8,128)(2,1)S(1)} %bitcast.64, ...), custom_call_target="tpu_custom_call" | custom-call | flops 1540000000 | bytes 5040000 | tf_op jit(solution)/shard_map/pallas_call | solution.py:90
  29.0 0.0 collective-permute-done.9
  29.0 3.3 %collective-permute-done.8 = bf16[2,1,1,64,128]{4,3,2,1,0:T(8,128)(2,1)S(1)} collective-permute-done((bf16[2,1,1,64,128]{4,3,2,1,0:T(8,128)(2,1)S(1)}, bf16[2,1,1,64,128]{4,3,2,1,0:T(8,128)(2,1)S(1)}, u32[]{:S(2)}, u32[]{:S(2)}) %collective-permute-start.8) | collective-permute-done | bytes 32800 | tf_op jit(solution)/shard_map/ppermute | solution.py:22
  32.3 0.1 collective-permute-start.11
  32.4 0.5 collective-permute-start.10
  32.9 0.2 collective-permute-start.12
  33.1 1.5 %collective-permute-start.13 = (bf16[2,3,128,128]{3,2,1,0:T(8,128)(2,1)S(1)}, bf16[2,3,128,128]{3,2,1,0:T(8,128)(2,1)S(1)}, u32[]{:S(2)}, u32[]{:S(2)}) collective-permute-start(bf16[2,3,128,128]{3,2,1,0:T(8,128)(2,1)S(1)} %get-tuple-element.46), channel_id=1, source_target_pairs={{0,6},{2,0},{4,2},{6,4},{1,7},{3,1},{5,3},{7,5},{8,14},{10,8},{12,... | collective-permute-start | bytes 589832 | tf_op jit(solution)/shard_map/ppermute | solution.py:22
  34.6 2.4 %shard_map.159 = (bf16[2304,128]{1,0:T(8,128)(2,1)S(1)}, bf16[2304,128]{1,0:T(8,128)(2,1)S(1)}, bf16[4608,144]{1,0:T(8,128)(2,1)S(1)}, f32[72,64]{1,0:T(8,128)S(1)}, bf16[169,256]{1,0:T(8,128)(2,1)S(1)}) custom-call(s32[72,64]{1,0:T(8,128)S(1)} %get-tuple-element.26.refs_5_.pack_ref, f32[72,64]{1,0:T(8,128)S(1)} %get-tuple-element.32.place_ref, ...), custom_call_target="tpu_custom_call" | custom-call | flops 2750000128 | bytes 9000000 | tf_op jit(solution)/shard_map/pallas_call | solution.py:90
  37.0 0.0 collective-permute-done.11
  37.1 0.0 collective-permute-done.10
  37.1 3.4 %collective-permute-done.12 = bf16[2,3,128,128]{3,2,1,0:T(8,128)(2,1)S(1)} collective-permute-done((bf16[2,3,128,128]{3,2,1,0:T(8,128)(2,1)S(1)}, bf16[2,3,128,128]{3,2,1,0:T(8,128)(2,1)S(1)}, u32[]{:S(2)}, u32[]{:S(2)}) %collective-permute-start.12) | collective-permute-done | bytes 196640 | tf_op jit(solution)/shard_map/ppermute | solution.py:22
  40.6 0.0 collective-permute-done.13
  40.6 0.1 pad_maximum_fusion.1.refs_7_
  40.7 1.6 %collective-permute-start.14 = (bf16[3,3,128,128]{3,2,1,0:T(8,128)(2,1)S(1)}, bf16[3,3,128,128]{3,2,1,0:T(8,128)(2,1)S(1)}, u32[]{:S(2)}, u32[]{:S(2)}) collective-permute-start(bf16[3,3,128,128]{3,2,1,0:T(8,128)(2,1)S(1)} %get-tuple-element.44), channel_id=1, source_target_pairs={{0,1},{1,0},{2,3},{3,2},{4,5},{5,4},{6,7},{7,6},{8,9},{9,8},{10,11... | collective-permute-start | bytes 884744 | tf_op jit(solution)/shard_map/ppermute | solution.py:17
  42.3 0.6 %shard_map.160.refs_0_ = bf16[128,128]{1,0:T(8,128)(2,1)S(1)} custom-call(bf16[64,1152]{1,0:T(8,128)(2,1)S(1)} %get-tuple-element.29.refs_0_, bf16[64,1152]{1,0:T(8,128)(2,1)S(1)} %collective-permute-done.5.refs_1_, bf16[1152,128]{1,0:T(8,128)(2,1)S(1)} %bitcast.58, bf16[2,128,128]{2,1,0:T(8,128)(2,1)S(1)} %copy-done, bf16[2,128,128]{2,1,0:T(8,128)(2,1)S(1)} %copy-done.1, ...), custom_call_target="tpu_custom_call" | custom-call | flops 660000000 | bytes 2160000 | tf_op jit(solution)/shard_map/pallas_call | solution.py:90
  42.9 1.4 %collective-permute-start.16 = (bf16[2,1,1,64,128]{4,3,2,1,0:T(8,128)(2,1)S(1)}, bf16[2,1,1,64,128]{4,3,2,1,0:T(8,128)(2,1)S(1)}, u32[]{:S(2)}, u32[]{:S(2)}) collective-permute-start(bf16[2,1,1,64,128]{4,3,2,1,0:T(8,128)(2,1)S(1)} %bitcast.73), channel_id=1, source_target_pairs={{0,24},{8,0},{16,8},{24,16},{1,25},{9,1},{17,9},{25,17},{2,26},{10... | collective-permute-start | bytes 98312 | tf_op jit(solution)/shard_map/ppermute | solution.py:22
  44.3 0.7 %collective-permute-start.15 = (bf16[2,1,1,64,128]{4,3,2,1,0:T(8,128)(2,1)S(1)}, bf16[2,1,1,64,128]{4,3,2,1,0:T(8,128)(2,1)S(1)}, u32[]{:S(2)}, u32[]{:S(2)}) collective-permute-start(bf16[2,1,1,64,128]{4,3,2,1,0:T(8,128)(2,1)S(1)} %bitcast.74), channel_id=1, source_target_pairs={{0,8},{8,16},{16,24},{24,0},{1,9},{9,17},{17,25},{25,1},{2,10},{10... | collective-permute-start | bytes 98312 | tf_op jit(solution)/shard_map/ppermute | solution.py:22
  45.0 1.3 %shard_map.161 = (bf16[2304,128]{1,0:T(8,128)(2,1)S(1)}, bf16[128,128]{1,0:T(8,128)(2,1)S(1)}) custom-call(bf16[2304,128]{1,0:T(8,128)(2,1)S(1)} %get-tuple-element.30.e_ref, bf16[2304,128]{1,0:T(8,128)(2,1)S(1)} %get-tuple-element.27.refs_6_.refs_1_.hot_ref.ho_ref, bf16[1152,128]{1,0:T(8,128)(2,1)S(1)} %bitcast.59, bf16[3,128,128]{2,1,0:T(8,128)(2,1)S(1)} %copy-done.7, ...), custom_call_target="tpu_custom_call" | custom-call | flops 1540000000 | bytes 5040000 | tf_op jit(solution)/shard_map/pallas_call | solution.py:90
  46.3 0.6 collective-permute-done.16
  46.8 3.2 %collective-permute-done.15 = bf16[2,1,1,64,128]{4,3,2,1,0:T(8,128)(2,1)S(1)} collective-permute-done((bf16[2,1,1,64,128]{4,3,2,1,0:T(8,128)(2,1)S(1)}, bf16[2,1,1,64,128]{4,3,2,1,0:T(8,128)(2,1)S(1)}, u32[]{:S(2)}, u32[]{:S(2)}) %collective-permute-start.15) | collective-permute-done | bytes 32800 | tf_op jit(solution)/shard_map/ppermute | solution.py:22
  50.0 0.1 collective-permute-start.18
  50.1 0.5 collective-permute-start.17
  50.6 0.1 pad_maximum_fusion.2
  50.6 1.3 %shard_map.162.e_ref = bf16[2304,128]{1,0:T(8,128)(2,1)S(1)} custom-call(bf16[2304,128]{1,0:T(8,128)(2,1)S(1)} %bitcast.62, bf16[2304,128]{1,0:T(8,128)(2,1)S(1)} %get-tuple-element.35.hot_ref.hm_ref, bf16[1152,128]{1,0:T(8,128)(2,1)S(1)} %bitcast.65, bf16[3,128,128]{2,1,0:T(8,128)(2,1)S(1)} %copy-done.8, bf16[3,128,128]{2,1,0:T(8,128)(2,1)S(1)} %copy-done.7, ...), custom_call_target="tpu_custom_call" | custom-call | flops 1540000000 | bytes 5040000 | tf_op jit(solution)/shard_map/pallas_call | solution.py:90
  52.0 1.3 %shard_map.163 = (bf16[2304,128]{1,0:T(8,128)(2,1)S(1)}, bf16[384,128]{1,0:T(8,128)(2,1)S(1)}) custom-call(bf16[2304,128]{1,0:T(8,128)(2,1)S(1)} %shard_map.162.e_ref, bf16[2304,128]{1,0:T(8,128)(2,1)S(1)} %get-tuple-element.35.hot_ref.hm_ref, bf16[1152,128]{1,0:T(8,128)(2,1)S(1)} %bitcast.60, bf16[3,128,128]{2,1,0:T(8,128)(2,1)S(1)} %copy-done.8, ...), custom_call_target="tpu_custom_call" | custom-call | flops 1540000000 | bytes 5040000 | tf_op jit(solution)/shard_map/pallas_call | solution.py:90
  53.3 1.1 %collective-permute-done.17 = bf16[2,3,1,64,128]{4,3,2,1,0:T(8,128)(2,1)S(1)} collective-permute-done((bf16[2,3,1,64,128]{4,3,2,1,0:T(8,128)(2,1)S(1)}, bf16[2,3,1,64,128]{4,3,2,1,0:T(8,128)(2,1)S(1)}, u32[]{:S(2)}, u32[]{:S(2)}) %collective-permute-start.17) | collective-permute-done | bytes 98336 | tf_op jit(solution)/shard_map/ppermute | solution.py:22
  54.4 5.9 %shard_map.164 = bf16[169,4608]{1,0:T(8,128)(2,1)} custom-call(bf16[2304,128]{1,0:T(8,128)(2,1)S(1)} %get-tuple-element.34.own_ref, bf16[2304,128]{1,0:T(8,128)(2,1)S(1)} %get-tuple-element.37.mir_ref, bf16[2304,128]{1,0:T(8,128)(2,1)S(1)} %get-tuple-element.27.refs_6_.refs_1_.hot_ref.ho_ref, bf16[2304,128]{1,0:T(8,128)(2,1)S(1)} %get-tuple-element.35.hot_ref.hm_ref, ...), custom_call_target="tpu_custom_call" | custom-call | flops 7699999744 | bytes 25200000 | tf_op jit(solution)/shard_map/pallas_call | solution.py:90
  (34 shorter events, 0.4 us)
Async XLA Ops:
  0.0 6.7 %collective-permute-start = (bf16[64,128]{1,0:T(8,128)(2,1)}, bf16[64,128]{1,0:T(8,128)(2,1)S(1)}, u32[]{:S(2)}, u32[]{:S(2)}) collective-permute-start(bf16[64,128]{1,0:T(8,128)(2,1)} %h_ref.1), channel_id=1, source_target_pairs={{0,1},{1,0},{2,3},{3,2},{4,5},{5,4},{6,7},{7,6},{8,9},{9,8},{10,11... | collective-permute-start | bytes 49160 | tf_op jit(solution)/shard_map/ppermute | solution.py:17
  4.5 0.7 %copy-start.12 = (bf16[64,128]{1,0:T(8,128)(2,1)S(1)}, bf16[64,128]{1,0:T(8,128)(2,1)}, u32[]{:S(2)}) copy-start(bf16[64,128]{1,0:T(8,128)(2,1)} %h_ref.1) | copy-start | bytes 49156
  5.2 5.6 %copy-start.6 = (bf16[2304,128]{1,0:T(8,128)(2,1)S(1)}, bf16[2304,128]{1,0:T(8,128)(2,1)}, u32[]{:S(2)}) copy-start(bf16[2304,128]{1,0:T(8,128)(2,1)} %bond_ref.1) | copy-start | bytes 1769476
  5.2 5.6 %copy-start.13 = (s32[2304]{0:T(1024)S(1)}, s32[2304]{0:T(1024)}, u32[]{:S(2)}) copy-start(s32[2304]{0:T(1024)} %param.22) | copy-start | bytes 27652
  6.6 15.5 %collective-permute-start.5 = (bf16[64,1152]{1,0:T(8,128)(2,1)S(1)}, bf16[64,1152]{1,0:T(8,128)(2,1)S(1)}, u32[]{:S(2)}, u32[]{:S(2)}) collective-permute-start(bf16[64,1152]{1,0:T(8,128)(2,1)S(1)} %get-tuple-element.29.refs_0_), channel_id=1, source_target_pairs={{0,1},{1,0},{2,3},{3,2},{4,5},{5,4},{6,7},{7,6},{8,9},{9,8},{10,11... | collective-permute-start | bytes 442376 | tf_op jit(solution)/shard_map/ppermute | solution.py:17
  6.7 10.1 %collective-permute-start.2 = (bf16[2,1,1,64,128]{4,3,2,1,0:T(8,128)(2,1)S(1)}, bf16[2,1,1,64,128]{4,3,2,1,0:T(8,128)(2,1)S(1)}, u32[]{:S(2)}, u32[]{:S(2)}) collective-permute-start(bf16[2,1,1,64,128]{4,3,2,1,0:T(8,128)(2,1)S(1)} %bitcast.79), channel_id=1, source_target_pairs={{0,24},{8,0},{16,8},{24,16},{1,25},{9,1},{17,9},{25,17},{2,26},{10... | collective-permute-start | bytes 98312 | tf_op jit(solution)/shard_map/ppermute | solution.py:22
  10.8 6.0 %collective-permute-start.1 = (bf16[2,1,1,64,128]{4,3,2,1,0:T(8,128)(2,1)S(1)}, bf16[2,1,1,64,128]{4,3,2,1,0:T(8,128)(2,1)S(1)}, u32[]{:S(2)}, u32[]{:S(2)}) collective-permute-start(bf16[2,1,1,64,128]{4,3,2,1,0:T(8,128)(2,1)S(1)} %bitcast.80), channel_id=1, source_target_pairs={{0,8},{8,16},{16,24},{24,0},{1,9},{9,17},{17,25},{25,1},{2,10},{10... | collective-permute-start | bytes 98312 | tf_op jit(solution)/shard_map/ppermute | solution.py:22
  12.8 4.6 %copy-start.2 = (s32[4608]{0:T(1024)S(1)}, s32[4608]{0:T(1024)}, u32[]{:S(2)}) copy-start(s32[4608]{0:T(1024)} %param.23) | copy-start | bytes 55300
  12.8 4.6 %copy-start.3 = (s32[4608]{0:T(1024)S(1)}, s32[4608]{0:T(1024)}, u32[]{:S(2)}) copy-start(s32[4608]{0:T(1024)} %param.20) | copy-start | bytes 55300
  12.8 4.6 %copy-start.4 = (s32[4608]{0:T(1024)S(1)}, s32[4608]{0:T(1024)}, u32[]{:S(2)}) copy-start(s32[4608]{0:T(1024)} %param.19) | copy-start | bytes 55300
  12.8 4.6 %copy-start.14 = (s32[2304]{0:T(1024)S(1)}, s32[2304]{0:T(1024)}, u32[]{:S(2)}) copy-start(s32[2304]{0:T(1024)} %param.21) | copy-start | bytes 27652
  12.9 13.7 %collective-permute-start.7 = (bf16[2,3,128,128]{3,2,0,1:T(8,128)(2,1)S(1)}, bf16[2,3,128,128]{3,2,0,1:T(8,128)(2,1)S(1)}, u32[]{:S(2)}, u32[]{:S(2)}) collective-permute-start(bf16[2,3,128,128]{3,2,0,1:T(8,128)(2,1)S(1)} %bitcast.93), channel_id=1, source_target_pairs={{0,24},{8,0},{16,8},{24,16},{1,25},{9,1},{17,9},{25,17},{2,26},{10... | collective-permute-start | bytes 589832 | tf_op jit(solution)/shard_map/ppermute | solution.py:22
  16.8 9.8 %collective-permute-start.6 = (bf16[2,3,128,128]{3,2,0,1:T(8,128)(2,1)S(1)}, bf16[2,3,128,128]{3,2,0,1:T(8,128)(2,1)S(1)}, u32[]{:S(2)}, u32[]{:S(2)}) collective-permute-start(bf16[2,3,128,128]{3,2,0,1:T(8,128)(2,1)S(1)} %bitcast.92), channel_id=1, source_target_pairs={{0,8},{8,16},{16,24},{24,0},{1,9},{9,17},{17,25},{25,1},{2,10},{10... | collective-permute-start | bytes 589832 | tf_op jit(solution)/shard_map/ppermute | solution.py:22
  16.8 2.8 %collective-permute-start.4 = (bf16[2,3,1,64,128]{4,3,2,1,0:T(8,128)(2,1)S(1)}, bf16[2,3,1,64,128]{4,3,2,1,0:T(8,128)(2,1)S(1)}, u32[]{:S(2)}, u32[]{:S(2)}) collective-permute-start(bf16[2,3,1,64,128]{4,3,2,1,0:T(8,128)(2,1)S(1)} %pad_maximum_fusion.6), channel_id=1, source_target_pairs={{0,6},{2,0},{4,2},{6,4},{1,7},{3,1},{5,3},{7,5},{8,14},{10,8},{12,... | collective-permute-start | bytes 294920 | tf_op jit(solution)/shard_map/ppermute | solution.py:22
  16.9 5.1 %collective-permute-start.3 = (bf16[2,3,1,64,128]{4,3,2,1,0:T(8,128)(2,1)S(1)}, bf16[2,3,1,64,128]{4,3,2,1,0:T(8,128)(2,1)S(1)}, u32[]{:S(2)}, u32[]{:S(2)}) collective-permute-start(bf16[2,3,1,64,128]{4,3,2,1,0:T(8,128)(2,1)S(1)} %pad_maximum_fusion.6), channel_id=1, source_target_pairs={{0,2},{2,4},{4,6},{6,0},{1,3},{3,5},{5,7},{7,1},{8,10},{10,12},{12... | collective-permute-start | bytes 294920 | tf_op jit(solution)/shard_map/ppermute | solution.py:22
  17.4 4.7 %copy-start = (bf16[2,128,128]{2,1,0:T(8,128)(2,1)S(1)}, bf16[2,128,128]{2,1,0:T(8,128)(2,1)}, u32[]{:S(2)}) copy-start(bf16[2,128,128]{2,1,0:T(8,128)(2,1)} %refs_3_.5) | copy-start | bytes 196612
  17.4 4.7 %copy-start.1 = (bf16[2,128,128]{2,1,0:T(8,128)(2,1)S(1)}, bf16[2,128,128]{2,1,0:T(8,128)(2,1)}, u32[]{:S(2)}) copy-start(bf16[2,128,128]{2,1,0:T(8,128)(2,1)} %refs_4_.5) | copy-start | bytes 196612
  17.4 4.7 %copy-start.5 = (f32[2,128]{1,0:T(2,128)S(1)}, f32[2,128]{1,0:T(2,128)}, u32[]{:S(2)}) copy-start(f32[2,128]{1,0:T(2,128)} %refs_5_.5) | copy-start | bytes 3076
  22.7 6.3 %collective-permute-start.9 = (bf16[2,1,1,64,128]{4,3,2,1,0:T(8,128)(2,1)S(1)}, bf16[2,1,1,64,128]{4,3,2,1,0:T(8,128)(2,1)S(1)}, u32[]{:S(2)}, u32[]{:S(2)}) collective-permute-start(bf16[2,1,1,64,128]{4,3,2,1,0:T(8,128)(2,1)S(1)} %bitcast.82), channel_id=1, source_target_pairs={{0,24},{8,0},{16,8},{24,16},{1,25},{9,1},{17,9},{25,17},{2,26},{10... | collective-permute-start | bytes 98312 | tf_op jit(solution)/shard_map/ppermute | solution.py:22
  26.6 5.7 %collective-permute-start.8 = (bf16[2,1,1,64,128]{4,3,2,1,0:T(8,128)(2,1)S(1)}, bf16[2,1,1,64,128]{4,3,2,1,0:T(8,128)(2,1)S(1)}, u32[]{:S(2)}, u32[]{:S(2)}) collective-permute-start(bf16[2,1,1,64,128]{4,3,2,1,0:T(8,128)(2,1)S(1)} %bitcast.83), channel_id=1, source_target_pairs={{0,8},{8,16},{16,24},{24,0},{1,9},{9,17},{17,25},{25,1},{2,10},{10... | collective-permute-start | bytes 98312 | tf_op jit(solution)/shard_map/ppermute | solution.py:22
  26.6 0.9 %copy-start.7 = (bf16[3,128,128]{2,1,0:T(8,128)(2,1)S(1)}, bf16[3,128,128]{2,1,0:T(8,128)(2,1)}, u32[]{:S(2)}) copy-start(bf16[3,128,128]{2,1,0:T(8,128)(2,1)} %wl_ref.7) | copy-start | bytes 294916
  26.6 0.9 %copy-start.8 = (bf16[3,128,128]{2,1,0:T(8,128)(2,1)S(1)}, bf16[3,128,128]{2,1,0:T(8,128)(2,1)}, u32[]{:S(2)}) copy-start(bf16[3,128,128]{2,1,0:T(8,128)(2,1)} %wr_ref.1) | copy-start | bytes 294916
  26.6 1.0 %copy-start.9 = (bf16[3,128,128]{2,1,0:T(8,128)(2,1)S(1)}, bf16[3,128,128]{2,1,0:T(8,128)(2,1)}, u32[]{:S(2)}) copy-start(bf16[3,128,128]{2,1,0:T(8,128)(2,1)} %wi_ref.7) | copy-start | bytes 294916
  26.7 1.0 %copy-start.10 = (bf16[3,128,128]{2,1,0:T(8,128)(2,1)S(1)}, bf16[3,128,128]{2,1,0:T(8,128)(2,1)}, u32[]{:S(2)}) copy-start(bf16[3,128,128]{2,1,0:T(8,128)(2,1)} %wo_ref.7) | copy-start | bytes 294916
  27.7 6.9 %copy-start.11 = (bf16[128,169]{0,1:T(8,128)(2,1)S(1)}, bf16[128,169]{0,1:T(8,128)(2,1)}, u32[]{:S(2)}) copy-start(bf16[128,169]{0,1:T(8,128)(2,1)} %param.31) | copy-start | bytes 129796
  32.3 4.8 %collective-permute-start.11 = (bf16[2,3,1,64,128]{4,3,2,1,0:T(8,128)(2,1)S(1)}, bf16[2,3,1,64,128]{4,3,2,1,0:T(8,128)(2,1)S(1)}, u32[]{:S(2)}, u32[]{:S(2)}) collective-permute-start(bf16[2,3,1,64,128]{4,3,2,1,0:T(8,128)(2,1)S(1)} %pad_maximum_fusion.7), channel_id=1, source_target_pairs={{0,6},{2,0},{4,2},{6,4},{1,7},{3,1},{5,3},{7,5},{8,14},{10,8},{12,... | collective-permute-start | bytes 294920 | tf_op jit(solution)/shard_map/ppermute | solution.py:22
  32.4 4.7 %collective-permute-start.10 = (bf16[2,3,1,64,128]{4,3,2,1,0:T(8,128)(2,1)S(1)}, bf16[2,3,1,64,128]{4,3,2,1,0:T(8,128)(2,1)S(1)}, u32[]{:S(2)}, u32[]{:S(2)}) collective-permute-start(bf16[2,3,1,64,128]{4,3,2,1,0:T(8,128)(2,1)S(1)} %pad_maximum_fusion.7), channel_id=1, source_target_pairs={{0,2},{2,4},{4,6},{6,0},{1,3},{3,5},{5,7},{7,1},{8,10},{10,12},{12... | collective-permute-start | bytes 294920 | tf_op jit(solution)/shard_map/ppermute | solution.py:22
  32.9 7.7 %collective-permute-start.12 = (bf16[2,3,128,128]{3,2,1,0:T(8,128)(2,1)S(1)}, bf16[2,3,128,128]{3,2,1,0:T(8,128)(2,1)S(1)}, u32[]{:S(2)}, u32[]{:S(2)}) collective-permute-start(bf16[2,3,128,128]{3,2,1,0:T(8,128)(2,1)S(1)} %get-tuple-element.45), channel_id=1, source_target_pairs={{0,2},{2,4},{4,6},{6,0},{1,3},{3,5},{5,7},{7,1},{8,10},{10,12},{12... | collective-permute-start | bytes 589832 | tf_op jit(solution)/shard_map/ppermute | solution.py:22
  33.1 7.5 %collective-permute-start.13 = (bf16[2,3,128,128]{3,2,1,0:T(8,128)(2,1)S(1)}, bf16[2,3,128,128]{3,2,1,0:T(8,128)(2,1)S(1)}, u32[]{:S(2)}, u32[]{:S(2)}) collective-permute-start(bf16[2,3,128,128]{3,2,1,0:T(8,128)(2,1)S(1)} %get-tuple-element.46), channel_id=1, source_target_pairs={{0,6},{2,0},{4,2},{6,4},{1,7},{3,1},{5,3},{7,5},{8,14},{10,8},{12,... | collective-permute-start | bytes 589832 | tf_op jit(solution)/shard_map/ppermute | solution.py:22
  40.7 9.9 %collective-permute-start.14 = (bf16[3,3,128,128]{3,2,1,0:T(8,128)(2,1)S(1)}, bf16[3,3,128,128]{3,2,1,0:T(8,128)(2,1)S(1)}, u32[]{:S(2)}, u32[]{:S(2)}) collective-permute-start(bf16[3,3,128,128]{3,2,1,0:T(8,128)(2,1)S(1)} %get-tuple-element.44), channel_id=1, source_target_pairs={{0,1},{1,0},{2,3},{3,2},{4,5},{5,4},{6,7},{7,6},{8,9},{9,8},{10,11... | collective-permute-start | bytes 884744 | tf_op jit(solution)/shard_map/ppermute | solution.py:17
  42.9 4.0 %collective-permute-start.16 = (bf16[2,1,1,64,128]{4,3,2,1,0:T(8,128)(2,1)S(1)}, bf16[2,1,1,64,128]{4,3,2,1,0:T(8,128)(2,1)S(1)}, u32[]{:S(2)}, u32[]{:S(2)}) collective-permute-start(bf16[2,1,1,64,128]{4,3,2,1,0:T(8,128)(2,1)S(1)} %bitcast.73), channel_id=1, source_target_pairs={{0,24},{8,0},{16,8},{24,16},{1,25},{9,1},{17,9},{25,17},{2,26},{10... | collective-permute-start | bytes 98312 | tf_op jit(solution)/shard_map/ppermute | solution.py:22
  44.3 5.7 %collective-permute-start.15 = (bf16[2,1,1,64,128]{4,3,2,1,0:T(8,128)(2,1)S(1)}, bf16[2,1,1,64,128]{4,3,2,1,0:T(8,128)(2,1)S(1)}, u32[]{:S(2)}, u32[]{:S(2)}) collective-permute-start(bf16[2,1,1,64,128]{4,3,2,1,0:T(8,128)(2,1)S(1)} %bitcast.74), channel_id=1, source_target_pairs={{0,8},{8,16},{16,24},{24,0},{1,9},{9,17},{17,25},{25,1},{2,10},{10... | collective-permute-start | bytes 98312 | tf_op jit(solution)/shard_map/ppermute | solution.py:22
  50.0 3.2 %collective-permute-start.18 = (bf16[2,3,1,64,128]{4,3,2,1,0:T(8,128)(2,1)S(1)}, bf16[2,3,1,64,128]{4,3,2,1,0:T(8,128)(2,1)S(1)}, u32[]{:S(2)}, u32[]{:S(2)}) collective-permute-start(bf16[2,3,1,64,128]{4,3,2,1,0:T(8,128)(2,1)S(1)} %pad_maximum_fusion.8), channel_id=1, source_target_pairs={{0,6},{2,0},{4,2},{6,4},{1,7},{3,1},{5,3},{7,5},{8,14},{10,8},{12,... | collective-permute-start | bytes 294920 | tf_op jit(solution)/shard_map/ppermute | solution.py:22
  50.1 4.3 %collective-permute-start.17 = (bf16[2,3,1,64,128]{4,3,2,1,0:T(8,128)(2,1)S(1)}, bf16[2,3,1,64,128]{4,3,2,1,0:T(8,128)(2,1)S(1)}, u32[]{:S(2)}, u32[]{:S(2)}) collective-permute-start(bf16[2,3,1,64,128]{4,3,2,1,0:T(8,128)(2,1)S(1)} %pad_maximum_fusion.8), channel_id=1, source_target_pairs={{0,2},{2,4},{4,6},{6,0},{1,3},{3,5},{5,7},{7,1},{8,10},{10,12},{12... | collective-permute-start | bytes 294920 | tf_op jit(solution)/shard_map/ppermute | solution.py:22

commit v9 on v8

--- a/solution.py
+++ b/solution.py
@@ -43,7 +43,8 @@
     return columns_of(rows_of(sheets, centre))
 
 
-def across_rows(sheets):
+def across_rows(outgoing, crossed):
+    sheets = jnp.stack([outgoing[0], crossed])
     rows = [moved(sheets[:, i], "gx", i - 1) if i != 1 else sheets[:, i] for i in (2, 1, 0)]
     return jnp.stack(rows, axis=1)
 
@@ -449,9 +450,9 @@
         us=2.0,
     )
     outgoing = ordered.reshape(2, 3, 3, cap, channels)
-    rowed = across_rows(outgoing)
-    columned = across_columns(rowed)
-    mirror = jnp.stack([columned[0], swapped(columned[1], "layer")]).reshape(owned, channels)
+    crossed = swapped(outgoing[1], "layer")
+    shifted = across_rows(outgoing, crossed)
+    mirror = across_columns(shifted).reshape(owned, channels)
     hot_own, hot_mir, place = call(
         pairs_body,
         (array(owned, 128), array(owned, 128), array(fan, atoms, dtype=F32)),
@@ -500,10 +501,10 @@
         )
 
     ghosts_at = [ghosts_of(framed_sheets(sheets), framed_sheets(centre))]
-    sheets = node(0, (hot_own,))
-    ordered, centre = edge(0, True, after=(rowed,), hand_on=(sheets,))
-    ghosts_at.append(ghosts_of(framed_sheets(sheets), framed_sheets(centre)))
-    sheets = node(1, (perm, columned))
+    sheets = node(0, (crossed,))
+    ghosts_at.append(ghosts_of(framed_sheets(sheets), framed_sheets(sheets)))
+    ordered = edge(0, True)
+    sheets = node(1, (perm, ordered, shifted))
     ordered, centre = edge(1, True, hand_on=(sheets,))
     mirror = edge(0, False)
     rows = rows_of(framed_sheets(sheets), framed_sheets(centre))

time: 60.6 us -> 57.8 us (0.954)
  waiting for transfers between devices: 14 us -> 11.4 us
  local copies, waits for them, and re-layouts: 1.89 us -> 0.94 us
  starting transfers between devices: 22 us -> 22.8 us
    ppermute x16, waiting for transfers between devices: 14 us -> 11.4 us  [moved(): lax.ppermute(value, axis, [(i, (i + steps) % count) for i in range(count)])]
    unnamed x33 -> x31, local copies, waits for them, and re-layouts: 1.71 us -> 0.8 us
    ppermute x16, starting transfers between devices: 17.4 us -> 18.2 us  [moved(): lax.ppermute(value, axis, [(i, (i + steps) % count) for i in range(count)])]
  transfers between devices with their start and end apart: 19 -> 19, of which waited for: 6 -> 8; matrix products, arithmetic and copies ran while one was open for 3% -> 3% of each run, Pallas kernels for 24% -> 23%
where the time goes in v9:
time: 57.8 us; the launch traced here: 57.6 us
  starting transfers between devices  22.8 us (39%)
  Pallas kernels  20.2 us (35%)
  waiting for transfers between devices  11.4 us (20%)
  other arithmetic  1.84 us (3%)
  local copies, waits for them, and re-layouts  0.94 us (2%)
    pallas_call x11, Pallas kernels, call(): pl.pallas_call(ordered_body if after else body, out_shape=outs, in_specs=...  20.2 us
    ppermute x16, starting transfers between devices, moved(): lax.ppermute(value, axis, [(i, (i + steps) % count) for i in range(count)])  18.2 us
    ppermute x16, waiting for transfers between devices, moved(): lax.ppermute(value, axis, [(i, (i + steps) % count) for i in range(count)])  11.4 us
    ppermute x3, starting transfers between devices, swapped(): return lax.ppermute(value, axis, [(0, 1), (1, 0)])  4.62 us
  transfers between devices with their start and end apart: 19, of which 8 were waited for; matrix products, arithmetic and copies ran while one was open for 3% of the time, Pallas kernels for 23%

profile of v9, /device:TPU:0, one launch (start us, length us, event | category | flops | bytes accessed | tf_op | source)
XLA Modules:
  0.0 57.6 jit_solution(1412140087620203007)
XLA Ops:
  0.0 3.0 %collective-permute-start = (bf16[64,128]{1,0:T(8,128)(2,1)}, bf16[64,128]{1,0:T(8,128)(2,1)S(1)}, u32[]{:S(2)}, u32[]{:S(2)}) collective-permute-start(bf16[64,128]{1,0:T(8,128)(2,1)} %h_ref.1), channel_id=1, source_target_pairs={{0,1},{1,0},{2,3},{3,2},{4,5},{5,4},{6,7},{7,6},{8,9},{9,8},{10,11... | collective-permute-start | bytes 49160 | tf_op jit(solution)/shard_map/ppermute | solution.py:17
  3.0 0.8 %or_convert_fusion = f32[36,128]{1,0:T(8,128)S(1)} fusion(s32[4608]{0:T(1024)} %param.23, s32[4608]{0:T(1024)} %param.20, s32[4608]{0:T(1024)} %param.19), kind=kLoop, calls=%fused_computation.22 | loop fusion | flops 27648 | bytes 73728 | tf_op jit(solution)/shard_map/convert_element_type | solution.py:436
  3.7 0.7 %pad_maximum_fusion.9.both_ref = f32[72,128]{1,0:T(8,128)S(1)} fusion(f32[36,128]{1,0:T(8,128)} %bitcast.91, f32[36,128]{1,0:T(8,128)S(1)} %or_convert_fusion), kind=kLoop, calls=%fused_computation.21 | loop fusion | flops 9216 | bytes 73728 | tf_op jit(solution)/shard_map/concatenate | solution.py:435
  4.5 0.7 %copy-done.12 = bf16[64,128]{1,0:T(8,128)(2,1)S(1)} copy-done((bf16[64,128]{1,0:T(8,128)(2,1)S(1)}, bf16[64,128]{1,0:T(8,128)(2,1)}, u32[]{:S(2)}) %copy-start.12) | copy-done | bytes 16408
  5.2 1.4 %shard_map.154 = (bf16[64,1152]{1,0:T(8,128)(2,1)S(1)}, s32[72,64]{1,0:T(8,128)S(1)}, bf16[64,128]{1,0:T(8,128)(2,1)S(1)}) custom-call(f32[72,128]{1,0:T(8,128)S(1)} %pad_maximum_fusion.9.both_ref, bf16[64,128]{1,0:T(8,128)(2,1)S(1)} %copy-done.12), custom_call_target="tpu_custom_call" | custom-call | flops 2200000000 | bytes 7200000 | tf_op jit(solution)/shard_map/pallas_call | solution.py:91
  6.6 0.1 collective-permute-start.5
  6.7 0.0 collective-permute-done
  6.7 4.1 %collective-permute-start.2 = (bf16[2,1,1,64,128]{4,3,2,1,0:T(8,128)(2,1)S(1)}, bf16[2,1,1,64,128]{4,3,2,1,0:T(8,128)(2,1)S(1)}, u32[]{:S(2)}, u32[]{:S(2)}) collective-permute-start(bf16[2,1,1,64,128]{4,3,2,1,0:T(8,128)(2,1)S(1)} %bitcast.79), channel_id=1, source_target_pairs={{0,24},{8,0},{16,8},{24,16},{1,25},{9,1},{17,9},{25,17},{2,26},{10... | collective-permute-start | bytes 98312 | tf_op jit(solution)/shard_map/ppermute | solution.py:22
  10.8 0.0 collective-permute-start.1
  10.8 0.0 copy-start.2
  10.8 0.0 copy-start.3
  10.8 0.0 copy-start.4
  10.9 0.0 copy-start.14
  10.9 1.9 %shard_map.155 = (bf16[2304,128]{1,0:T(8,128)(2,1)S(1)}, bf16[128,128]{1,0:T(8,128)(2,1)S(1)}) custom-call(s32[18,128]{1,0:T(8,128)S(1)} %bitcast.82, bf16[2304,128]{1,0:T(8,128)(2,1)S(1)} %copy-done.6, bf16[128,128]{1,0:T(8,128)(2,1)S(1)} %constant_dynamic-update-slice_fusion.h_ref), custom_call_target="tpu_custom_call" | custom-call | flops 2200000000 | bytes 7200000 | tf_op jit(solution)/shard_map/pallas_call | solution.py:91
  12.8 1.6 %collective-permute-start.6 = (bf16[3,3,128,128]{3,2,1,0:T(8,128)(2,1)S(1)}, bf16[3,3,128,128]{3,2,1,0:T(8,128)(2,1)S(1)}, u32[]{:S(2)}, u32[]{:S(2)}) collective-permute-start(bf16[3,3,128,128]{3,2,1,0:T(8,128)(2,1)S(1)} %bitcast.86), channel_id=1, source_target_pairs={{0,1},{1,0},{2,3},{3,2},{4,5},{5,4},{6,7},{7,6},{8,9},{9,8},{10,11... | collective-permute-start | bytes 884744 | tf_op jit(solution)/shard_map/ppermute | solution.py:17
  14.4 0.0 copy-start.11
  14.5 2.2 %shard_map.156 = (bf16[2304,128]{1,0:T(8,128)(2,1)S(1)}, bf16[2304,128]{1,0:T(8,128)(2,1)S(1)}, f32[72,64]{1,0:T(8,128)S(1)}) custom-call(s32[18,128]{1,0:T(8,128)S(1)} %bitcast.83, s32[18,128]{1,0:T(8,128)S(1)} %bitcast.84, s32[36,128]{1,0:T(8,128)S(1)} %bitcast.78, s32[36,128]{1,0:T(8,128)S(1)} %bitcast.77, s32[36,128]{1,0:T(8,128)S(1)} %bitcast.76, ...), custom_call_target="tpu_custom_call" | custom-call | flops 2750000128 | bytes 9000000 | tf_op jit(solution)/shard_map/pallas_call | solution.py:91
  16.7 0.0 collective-permute-done.2
  16.7 0.0 collective-permute-done.1
  16.7 0.1 collective-permute-start.4
  16.8 0.5 collective-permute-start.3
  17.3 2.4 %shard_map.159 = (bf16[2304,128]{1,0:T(8,128)(2,1)S(1)}, bf16[2304,128]{1,0:T(8,128)(2,1)S(1)}, bf16[4608,144]{1,0:T(8,128)(2,1)S(1)}, f32[72,64]{1,0:T(8,128)S(1)}, bf16[169,256]{1,0:T(8,128)(2,1)S(1)}) custom-call(s32[72,64]{1,0:T(8,128)S(1)} %get-tuple-element.24.refs_5_.pack_ref, f32[72,64]{1,0:T(8,128)S(1)} %get-tuple-element.28.place_ref, ...), custom_call_target="tpu_custom_call" | custom-call | flops 2750000128 | bytes 9000000 | tf_op jit(solution)/shard_map/pallas_call | solution.py:91
  19.7 0.0 copy-start.7
  19.7 0.0 copy-start.8
  19.7 0.0 copy-start.9
  19.7 0.0 copy-start.10
  19.8 0.0 collective-permute-done.4
  19.8 2.1 %collective-permute-done.3 = bf16[2,3,1,64,128]{4,3,2,1,0:T(8,128)(2,1)S(1)} collective-permute-done((bf16[2,3,1,64,128]{4,3,2,1,0:T(8,128)(2,1)S(1)}, bf16[2,3,1,64,128]{4,3,2,1,0:T(8,128)(2,1)S(1)}, u32[]{:S(2)}, u32[]{:S(2)}) %collective-permute-start.3) | collective-permute-done | bytes 98336 | tf_op jit(solution)/shard_map/ppermute | solution.py:22
  21.9 0.0 collective-permute-done.5.refs_1_
  21.9 0.0 collective-permute-done.6.refs_6_
  22.0 0.6 %shard_map.158 = bf16[128,128]{1,0:T(8,128)(2,1)S(1)} custom-call(bf16[64,1152]{1,0:T(8,128)(2,1)S(1)} %get-tuple-element.27.refs_0_, bf16[64,1152]{1,0:T(8,128)(2,1)S(1)} %collective-permute-done.5.refs_1_, bf16[1152,128]{1,0:T(8,128)(2,1)S(1)} %bitcast.60, bf16[2,128,128]{2,1,0:T(8,128)(2,1)S(1)} %copy-done, bf16[2,128,128]{2,1,0:T(8,128)(2,1)S(1)} %copy-done.1, ...), custom_call_target="tpu_custom_call" | custom-call | flops 660000000 | bytes 2160000 | tf_op jit(solution)/shard_map/pallas_call | solution.py:91
  22.6 3.9 %collective-permute-start.8 = (bf16[2,1,1,64,128]{4,3,2,1,0:T(8,128)(2,1)S(1)}, bf16[2,1,1,64,128]{4,3,2,1,0:T(8,128)(2,1)S(1)}, u32[]{:S(2)}, u32[]{:S(2)}) collective-permute-start(bf16[2,1,1,64,128]{4,3,2,1,0:T(8,128)(2,1)S(1)} %bitcast.67), channel_id=1, source_target_pairs={{0,24},{8,0},{16,8},{24,16},{1,25},{9,1},{17,9},{25,17},{2,26},{10... | collective-permute-start | bytes 98312 | tf_op jit(solution)/shard_map/ppermute | solution.py:22
  26.4 0.0 collective-permute-start.7
  26.5 0.1 fusion.3
  26.5 0.1 collective-permute-start.11
  26.6 3.9 %collective-permute-start.12 = (bf16[2,3,128,128]{3,2,1,0:T(8,128)(2,1)S(1)}, bf16[2,3,128,128]{3,2,1,0:T(8,128)(2,1)S(1)}, u32[]{:S(2)}, u32[]{:S(2)}) collective-permute-start(bf16[2,3,128,128]{3,2,1,0:T(8,128)(2,1)S(1)} %get-tuple-element.43), channel_id=1, source_target_pairs={{0,24},{8,0},{16,8},{24,16},{1,25},{9,1},{17,9},{25,17},{2,26},{10... | collective-permute-start | bytes 589832 | tf_op jit(solution)/shard_map/ppermute | solution.py:22
  30.4 0.0 collective-permute-done.8
  30.5 2.2 %collective-permute-done.7 = bf16[2,1,1,64,128]{4,3,2,1,0:T(8,128)(2,1)S(1)} collective-permute-done((bf16[2,1,1,64,128]{4,3,2,1,0:T(8,128)(2,1)S(1)}, bf16[2,1,1,64,128]{4,3,2,1,0:T(8,128)(2,1)S(1)}, u32[]{:S(2)}, u32[]{:S(2)}) %collective-permute-start.7) | collective-permute-done | bytes 32800 | tf_op jit(solution)/shard_map/ppermute | solution.py:22
  32.7 0.1 collective-permute-start.10
  32.8 0.5 collective-permute-start.9
  33.3 1.3 %shard_map.157.refs_7_.e_ref = bf16[2304,128]{1,0:T(8,128)(2,1)S(1)} custom-call(bf16[2304,128]{1,0:T(8,128)(2,1)S(1)} %get-tuple-element.23.refs_6_.e_ref, bf16[2304,128]{1,0:T(8,128)(2,1)S(1)} %get-tuple-element.25.hot_ref.ho_ref, bf16[1152,128]{1,0:T(8,128)(2,1)S(1)} %bitcast.61, bf16[3,128,128]{2,1,0:T(8,128)(2,1)S(1)} %copy-done.7, ...), custom_call_target="tpu_custom_call" | custom-call | flops 1540000000 | bytes 5040000 | tf_op jit(solution)/shard_map/pallas_call | solution.py:91
  34.6 1.4 %collective-permute-done.10 = bf16[2,3,1,64,128]{4,3,2,1,0:T(8,128)(2,1)S(1)} collective-permute-done((bf16[2,3,1,64,128]{4,3,2,1,0:T(8,128)(2,1)S(1)}, bf16[2,3,1,64,128]{4,3,2,1,0:T(8,128)(2,1)S(1)}, u32[]{:S(2)}, u32[]{:S(2)}) %collective-permute-start.10) | collective-permute-done | bytes 98336 | tf_op jit(solution)/shard_map/ppermute | solution.py:22
  35.9 1.0 %collective-permute-done.9 = bf16[2,3,1,64,128]{4,3,2,1,0:T(8,128)(2,1)S(1)} collective-permute-done((bf16[2,3,1,64,128]{4,3,2,1,0:T(8,128)(2,1)S(1)}, bf16[2,3,1,64,128]{4,3,2,1,0:T(8,128)(2,1)S(1)}, u32[]{:S(2)}, u32[]{:S(2)}) %collective-permute-start.9) | collective-permute-done | bytes 98336 | tf_op jit(solution)/shard_map/ppermute | solution.py:22
  37.0 0.0 collective-permute-done.11
  37.0 1.2 %collective-permute-done.12 = bf16[2,3,128,128]{3,2,1,0:T(8,128)(2,1)S(1)} collective-permute-done((bf16[2,3,128,128]{3,2,1,0:T(8,128)(2,1)S(1)}, bf16[2,3,128,128]{3,2,1,0:T(8,128)(2,1)S(1)}, u32[]{:S(2)}, u32[]{:S(2)}) %collective-permute-start.12) | collective-permute-done | bytes 196640 | tf_op jit(solution)/shard_map/ppermute | solution.py:22
  38.2 0.1 pad_maximum_fusion.refs_8_
  38.3 0.6 %shard_map.160.refs_0_ = bf16[128,128]{1,0:T(8,128)(2,1)S(1)} custom-call(bf16[64,1152]{1,0:T(8,128)(2,1)S(1)} %get-tuple-element.27.refs_0_, bf16[64,1152]{1,0:T(8,128)(2,1)S(1)} %collective-permute-done.5.refs_1_, bf16[1152,128]{1,0:T(8,128)(2,1)S(1)} %bitcast.56, bf16[2,128,128]{2,1,0:T(8,128)(2,1)S(1)} %copy-done, bf16[2,128,128]{2,1,0:T(8,128)(2,1)S(1)} %copy-done.1, ...), custom_call_target="tpu_custom_call" | custom-call | flops 660000000 | bytes 2160000 | tf_op jit(solution)/shard_map/pallas_call | solution.py:91
  38.9 2.8 %collective-permute-start.16 = (bf16[2,1,1,64,128]{4,3,2,1,0:T(8,128)(2,1)S(1)}, bf16[2,1,1,64,128]{4,3,2,1,0:T(8,128)(2,1)S(1)}, u32[]{:S(2)}, u32[]{:S(2)}) collective-permute-start(bf16[2,1,1,64,128]{4,3,2,1,0:T(8,128)(2,1)S(1)} %bitcast.73), channel_id=1, source_target_pairs={{0,24},{8,0},{16,8},{24,16},{1,25},{9,1},{17,9},{25,17},{2,26},{10... | collective-permute-start | bytes 98312 | tf_op jit(solution)/shard_map/ppermute | solution.py:22
  41.7 0.0 collective-permute-start.15
  41.7 0.0 collective-permute-start.13
  41.7 1.7 %collective-permute-start.14 = (bf16[2,3,128,128]{3,2,1,0:T(8,128)(2,1)S(1)}, bf16[2,3,128,128]{3,2,1,0:T(8,128)(2,1)S(1)}, u32[]{:S(2)}, u32[]{:S(2)}) collective-permute-start(bf16[2,3,128,128]{3,2,1,0:T(8,128)(2,1)S(1)} %get-tuple-element.40), channel_id=1, source_target_pairs={{0,6},{2,0},{4,2},{6,4},{1,7},{3,1},{5,3},{7,5},{8,14},{10,8},{12,... | collective-permute-start | bytes 589832 | tf_op jit(solution)/shard_map/ppermute | solution.py:22
  43.5 1.3 %shard_map.161 = (bf16[2304,128]{1,0:T(8,128)(2,1)S(1)}, bf16[128,128]{1,0:T(8,128)(2,1)S(1)}) custom-call(bf16[2304,128]{1,0:T(8,128)(2,1)S(1)} %shard_map.157.refs_7_.e_ref, bf16[2304,128]{1,0:T(8,128)(2,1)S(1)} %get-tuple-element.25.hot_ref.ho_ref, bf16[1152,128]{1,0:T(8,128)(2,1)S(1)} %bitcast.57, bf16[3,128,128]{2,1,0:T(8,128)(2,1)S(1)} %copy-done.7, ...), custom_call_target="tpu_custom_call" | custom-call | flops 1540000000 | bytes 5040000 | tf_op jit(solution)/shard_map/pallas_call | solution.py:91
  44.8 0.0 collective-permute-done.16
  44.8 2.6 %collective-permute-done.15 = bf16[2,1,1,64,128]{4,3,2,1,0:T(8,128)(2,1)S(1)} collective-permute-done((bf16[2,1,1,64,128]{4,3,2,1,0:T(8,128)(2,1)S(1)}, bf16[2,1,1,64,128]{4,3,2,1,0:T(8,128)(2,1)S(1)}, u32[]{:S(2)}, u32[]{:S(2)}) %collective-permute-start.15) | collective-permute-done | bytes 32800 | tf_op jit(solution)/shard_map/ppermute | solution.py:22
  47.5 0.1 collective-permute-start.18
  47.5 0.5 collective-permute-start.17
  48.0 0.7 %collective-permute-done.13 = bf16[2,3,128,128]{3,2,1,0:T(8,128)(2,1)S(1)} collective-permute-done((bf16[2,3,128,128]{3,2,1,0:T(8,128)(2,1)S(1)}, bf16[2,3,128,128]{3,2,1,0:T(8,128)(2,1)S(1)}, u32[]{:S(2)}, u32[]{:S(2)}) %collective-permute-start.13) | collective-permute-done | bytes 196640 | tf_op jit(solution)/shard_map/ppermute | solution.py:22
  48.7 0.0 collective-permute-done.14
  48.7 0.1 pad_maximum_fusion.1
  48.9 1.3 %shard_map.162.e_ref = bf16[2304,128]{1,0:T(8,128)(2,1)S(1)} custom-call(bf16[2304,128]{1,0:T(8,128)(2,1)S(1)} %bitcast.59, bf16[2304,128]{1,0:T(8,128)(2,1)S(1)} %get-tuple-element.31.hot_ref.hm_ref, bf16[1152,128]{1,0:T(8,128)(2,1)S(1)} %bitcast.62, bf16[3,128,128]{2,1,0:T(8,128)(2,1)S(1)} %copy-done.8, bf16[3,128,128]{2,1,0:T(8,128)(2,1)S(1)} %copy-done.7, ...), custom_call_target="tpu_custom_call" | custom-call | flops 1540000000 | bytes 5040000 | tf_op jit(solution)/shard_map/pallas_call | solution.py:91
  50.2 1.3 %shard_map.163 = (bf16[2304,128]{1,0:T(8,128)(2,1)S(1)}, bf16[384,128]{1,0:T(8,128)(2,1)S(1)}) custom-call(bf16[2304,128]{1,0:T(8,128)(2,1)S(1)} %shard_map.162.e_ref, bf16[2304,128]{1,0:T(8,128)(2,1)S(1)} %get-tuple-element.31.hot_ref.hm_ref, bf16[1152,128]{1,0:T(8,128)(2,1)S(1)} %bitcast.58, bf16[3,128,128]{2,1,0:T(8,128)(2,1)S(1)} %copy-done.8, ...), custom_call_target="tpu_custom_call" | custom-call | flops 1540000000 | bytes 5040000 | tf_op jit(solution)/shard_map/pallas_call | solution.py:91
  51.5 0.0 collective-permute-done.18
  51.5 0.1 collective-permute-done.17
  51.7 5.9 %shard_map.164 = bf16[169,4608]{1,0:T(8,128)(2,1)} custom-call(bf16[2304,128]{1,0:T(8,128)(2,1)S(1)} %get-tuple-element.30.own_ref, bf16[2304,128]{1,0:T(8,128)(2,1)S(1)} %get-tuple-element.33.mir_ref, bf16[2304,128]{1,0:T(8,128)(2,1)S(1)} %get-tuple-element.25.hot_ref.ho_ref, bf16[2304,128]{1,0:T(8,128)(2,1)S(1)} %get-tuple-element.31.hot_ref.hm_ref, ...), custom_call_target="tpu_custom_call" | custom-call | flops 7699999744 | bytes 25200000 | tf_op jit(solution)/shard_map/pallas_call | solution.py:91
  (31 shorter events, 0.3 us)
Async XLA Ops:
  0.0 6.7 %collective-permute-start = (bf16[64,128]{1,0:T(8,128)(2,1)}, bf16[64,128]{1,0:T(8,128)(2,1)S(1)}, u32[]{:S(2)}, u32[]{:S(2)}) collective-permute-start(bf16[64,128]{1,0:T(8,128)(2,1)} %h_ref.1), channel_id=1, source_target_pairs={{0,1},{1,0},{2,3},{3,2},{4,5},{5,4},{6,7},{7,6},{8,9},{9,8},{10,11... | collective-permute-start | bytes 49160 | tf_op jit(solution)/shard_map/ppermute | solution.py:17
  4.5 0.7 %copy-start.12 = (bf16[64,128]{1,0:T(8,128)(2,1)S(1)}, bf16[64,128]{1,0:T(8,128)(2,1)}, u32[]{:S(2)}) copy-start(bf16[64,128]{1,0:T(8,128)(2,1)} %h_ref.1) | copy-start | bytes 49156
  5.2 5.6 %copy-start.6 = (bf16[2304,128]{1,0:T(8,128)(2,1)S(1)}, bf16[2304,128]{1,0:T(8,128)(2,1)}, u32[]{:S(2)}) copy-start(bf16[2304,128]{1,0:T(8,128)(2,1)} %bond_ref.1) | copy-start | bytes 1769476
  5.2 5.6 %copy-start.13 = (s32[2304]{0:T(1024)S(1)}, s32[2304]{0:T(1024)}, u32[]{:S(2)}) copy-start(s32[2304]{0:T(1024)} %param.22) | copy-start | bytes 27652
  6.6 15.4 %collective-permute-start.5 = (bf16[64,1152]{1,0:T(8,128)(2,1)S(1)}, bf16[64,1152]{1,0:T(8,128)(2,1)S(1)}, u32[]{:S(2)}, u32[]{:S(2)}) collective-permute-start(bf16[64,1152]{1,0:T(8,128)(2,1)S(1)} %get-tuple-element.27.refs_0_), channel_id=1, source_target_pairs={{0,1},{1,0},{2,3},{3,2},{4,5},{5,4},{6,7},{7,6},{8,9},{9,8},{10,11... | collective-permute-start | bytes 442376 | tf_op jit(solution)/shard_map/ppermute | solution.py:17
  6.7 10.0 %collective-permute-start.2 = (bf16[2,1,1,64,128]{4,3,2,1,0:T(8,128)(2,1)S(1)}, bf16[2,1,1,64,128]{4,3,2,1,0:T(8,128)(2,1)S(1)}, u32[]{:S(2)}, u32[]{:S(2)}) collective-permute-start(bf16[2,1,1,64,128]{4,3,2,1,0:T(8,128)(2,1)S(1)} %bitcast.79), channel_id=1, source_target_pairs={{0,24},{8,0},{16,8},{24,16},{1,25},{9,1},{17,9},{25,17},{2,26},{10... | collective-permute-start | bytes 98312 | tf_op jit(solution)/shard_map/ppermute | solution.py:22
  10.8 5.9 %collective-permute-start.1 = (bf16[2,1,1,64,128]{4,3,2,1,0:T(8,128)(2,1)S(1)}, bf16[2,1,1,64,128]{4,3,2,1,0:T(8,128)(2,1)S(1)}, u32[]{:S(2)}, u32[]{:S(2)}) collective-permute-start(bf16[2,1,1,64,128]{4,3,2,1,0:T(8,128)(2,1)S(1)} %bitcast.80), channel_id=1, source_target_pairs={{0,8},{8,16},{16,24},{24,0},{1,9},{9,17},{17,25},{25,1},{2,10},{10... | collective-permute-start | bytes 98312 | tf_op jit(solution)/shard_map/ppermute | solution.py:22
  10.8 3.6 %copy-start.2 = (s32[4608]{0:T(1024)S(1)}, s32[4608]{0:T(1024)}, u32[]{:S(2)}) copy-start(s32[4608]{0:T(1024)} %param.23) | copy-start | bytes 55300
  10.8 3.6 %copy-start.3 = (s32[4608]{0:T(1024)S(1)}, s32[4608]{0:T(1024)}, u32[]{:S(2)}) copy-start(s32[4608]{0:T(1024)} %param.20) | copy-start | bytes 55300
  10.8 3.6 %copy-start.4 = (s32[4608]{0:T(1024)S(1)}, s32[4608]{0:T(1024)}, u32[]{:S(2)}) copy-start(s32[4608]{0:T(1024)} %param.19) | copy-start | bytes 55300
  10.9 3.6 %copy-start.14 = (s32[2304]{0:T(1024)S(1)}, s32[2304]{0:T(1024)}, u32[]{:S(2)}) copy-start(s32[2304]{0:T(1024)} %param.21) | copy-start | bytes 27652
  12.8 9.1 %collective-permute-start.6 = (bf16[3,3,128,128]{3,2,1,0:T(8,128)(2,1)S(1)}, bf16[3,3,128,128]{3,2,1,0:T(8,128)(2,1)S(1)}, u32[]{:S(2)}, u32[]{:S(2)}) collective-permute-start(bf16[3,3,128,128]{3,2,1,0:T(8,128)(2,1)S(1)} %bitcast.86), channel_id=1, source_target_pairs={{0,1},{1,0},{2,3},{3,2},{4,5},{5,4},{6,7},{7,6},{8,9},{9,8},{10,11... | collective-permute-start | bytes 884744 | tf_op jit(solution)/shard_map/ppermute | solution.py:17
  14.4 2.8 %copy-start.11 = (bf16[128,169]{0,1:T(8,128)(2,1)S(1)}, bf16[128,169]{0,1:T(8,128)(2,1)}, u32[]{:S(2)}) copy-start(bf16[128,169]{0,1:T(8,128)(2,1)} %param.31) | copy-start | bytes 129796
  16.7 3.1 %collective-permute-start.4 = (bf16[2,3,1,64,128]{4,3,2,1,0:T(8,128)(2,1)S(1)}, bf16[2,3,1,64,128]{4,3,2,1,0:T(8,128)(2,1)S(1)}, u32[]{:S(2)}, u32[]{:S(2)}) collective-permute-start(bf16[2,3,1,64,128]{4,3,2,1,0:T(8,128)(2,1)S(1)} %pad_maximum_fusion.6), channel_id=1, source_target_pairs={{0,6},{2,0},{4,2},{6,4},{1,7},{3,1},{5,3},{7,5},{8,14},{10,8},{12,... | collective-permute-start | bytes 294920 | tf_op jit(solution)/shard_map/ppermute | solution.py:22
  16.8 5.1 %collective-permute-start.3 = (bf16[2,3,1,64,128]{4,3,2,1,0:T(8,128)(2,1)S(1)}, bf16[2,3,1,64,128]{4,3,2,1,0:T(8,128)(2,1)S(1)}, u32[]{:S(2)}, u32[]{:S(2)}) collective-permute-start(bf16[2,3,1,64,128]{4,3,2,1,0:T(8,128)(2,1)S(1)} %pad_maximum_fusion.6), channel_id=1, source_target_pairs={{0,2},{2,4},{4,6},{6,0},{1,3},{3,5},{5,7},{7,1},{8,10},{10,12},{12... | collective-permute-start | bytes 294920 | tf_op jit(solution)/shard_map/ppermute | solution.py:22
  17.3 4.7 %copy-start = (bf16[2,128,128]{2,1,0:T(8,128)(2,1)S(1)}, bf16[2,128,128]{2,1,0:T(8,128)(2,1)}, u32[]{:S(2)}) copy-start(bf16[2,128,128]{2,1,0:T(8,128)(2,1)} %refs_3_.3) | copy-start | bytes 196612
  17.3 4.7 %copy-start.1 = (bf16[2,128,128]{2,1,0:T(8,128)(2,1)S(1)}, bf16[2,128,128]{2,1,0:T(8,128)(2,1)}, u32[]{:S(2)}) copy-start(bf16[2,128,128]{2,1,0:T(8,128)(2,1)} %refs_4_.3) | copy-start | bytes 196612
  17.3 4.7 %copy-start.5 = (f32[2,128]{1,0:T(2,128)S(1)}, f32[2,128]{1,0:T(2,128)}, u32[]{:S(2)}) copy-start(f32[2,128]{1,0:T(2,128)} %refs_5_.3) | copy-start | bytes 3076
  19.7 13.6 %copy-start.7 = (bf16[3,128,128]{2,1,0:T(8,128)(2,1)S(1)}, bf16[3,128,128]{2,1,0:T(8,128)(2,1)}, u32[]{:S(2)}) copy-start(bf16[3,128,128]{2,1,0:T(8,128)(2,1)} %wl_ref.9) | copy-start | bytes 294916
  19.7 13.5 %copy-start.8 = (bf16[3,128,128]{2,1,0:T(8,128)(2,1)S(1)}, bf16[3,128,128]{2,1,0:T(8,128)(2,1)}, u32[]{:S(2)}) copy-start(bf16[3,128,128]{2,1,0:T(8,128)(2,1)} %wr_ref.1) | copy-start | bytes 294916
  19.7 13.5 %copy-start.9 = (bf16[3,128,128]{2,1,0:T(8,128)(2,1)S(1)}, bf16[3,128,128]{2,1,0:T(8,128)(2,1)}, u32[]{:S(2)}) copy-start(bf16[3,128,128]{2,1,0:T(8,128)(2,1)} %wi_ref.9) | copy-start | bytes 294916
  19.7 13.5 %copy-start.10 = (bf16[3,128,128]{2,1,0:T(8,128)(2,1)S(1)}, bf16[3,128,128]{2,1,0:T(8,128)(2,1)}, u32[]{:S(2)}) copy-start(bf16[3,128,128]{2,1,0:T(8,128)(2,1)} %wo_ref.9) | copy-start | bytes 294916
  22.6 7.9 %collective-permute-start.8 = (bf16[2,1,1,64,128]{4,3,2,1,0:T(8,128)(2,1)S(1)}, bf16[2,1,1,64,128]{4,3,2,1,0:T(8,128)(2,1)S(1)}, u32[]{:S(2)}, u32[]{:S(2)}) collective-permute-start(bf16[2,1,1,64,128]{4,3,2,1,0:T(8,128)(2,1)S(1)} %bitcast.67), channel_id=1, source_target_pairs={{0,24},{8,0},{16,8},{24,16},{1,25},{9,1},{17,9},{25,17},{2,26},{10... | collective-permute-start | bytes 98312 | tf_op jit(solution)/shard_map/ppermute | solution.py:22
  26.4 6.2 %collective-permute-start.7 = (bf16[2,1,1,64,128]{4,3,2,1,0:T(8,128)(2,1)S(1)}, bf16[2,1,1,64,128]{4,3,2,1,0:T(8,128)(2,1)S(1)}, u32[]{:S(2)}, u32[]{:S(2)}) collective-permute-start(bf16[2,1,1,64,128]{4,3,2,1,0:T(8,128)(2,1)S(1)} %bitcast.68), channel_id=1, source_target_pairs={{0,8},{8,16},{16,24},{24,0},{1,9},{9,17},{17,25},{25,1},{2,10},{10... | collective-permute-start | bytes 98312 | tf_op jit(solution)/shard_map/ppermute | solution.py:22
  26.5 10.4 %collective-permute-start.11 = (bf16[2,3,128,128]{3,2,1,0:T(8,128)(2,1)S(1)}, bf16[2,3,128,128]{3,2,1,0:T(8,128)(2,1)S(1)}, u32[]{:S(2)}, u32[]{:S(2)}) collective-permute-start(bf16[2,3,128,128]{3,2,1,0:T(8,128)(2,1)S(1)} %get-tuple-element.42), channel_id=1, source_target_pairs={{0,8},{8,16},{16,24},{24,0},{1,9},{9,17},{17,25},{25,1},{2,10},{10... | collective-permute-start | bytes 589832 | tf_op jit(solution)/shard_map/ppermute | solution.py:22
  26.6 11.6 %collective-permute-start.12 = (bf16[2,3,128,128]{3,2,1,0:T(8,128)(2,1)S(1)}, bf16[2,3,128,128]{3,2,1,0:T(8,128)(2,1)S(1)}, u32[]{:S(2)}, u32[]{:S(2)}) collective-permute-start(bf16[2,3,128,128]{3,2,1,0:T(8,128)(2,1)S(1)} %get-tuple-element.43), channel_id=1, source_target_pairs={{0,24},{8,0},{16,8},{24,16},{1,25},{9,1},{17,9},{25,17},{2,26},{10... | collective-permute-start | bytes 589832 | tf_op jit(solution)/shard_map/ppermute | solution.py:22
  32.7 3.2 %collective-permute-start.10 = (bf16[2,3,1,64,128]{4,3,2,1,0:T(8,128)(2,1)S(1)}, bf16[2,3,1,64,128]{4,3,2,1,0:T(8,128)(2,1)S(1)}, u32[]{:S(2)}, u32[]{:S(2)}) collective-permute-start(bf16[2,3,1,64,128]{4,3,2,1,0:T(8,128)(2,1)S(1)} %pad_maximum_fusion.7), channel_id=1, source_target_pairs={{0,6},{2,0},{4,2},{6,4},{1,7},{3,1},{5,3},{7,5},{8,14},{10,8},{12,... | collective-permute-start | bytes 294920 | tf_op jit(solution)/shard_map/ppermute | solution.py:22
  32.8 4.1 %collective-permute-start.9 = (bf16[2,3,1,64,128]{4,3,2,1,0:T(8,128)(2,1)S(1)}, bf16[2,3,1,64,128]{4,3,2,1,0:T(8,128)(2,1)S(1)}, u32[]{:S(2)}, u32[]{:S(2)}) collective-permute-start(bf16[2,3,1,64,128]{4,3,2,1,0:T(8,128)(2,1)S(1)} %pad_maximum_fusion.7), channel_id=1, source_target_pairs={{0,2},{2,4},{4,6},{6,0},{1,3},{3,5},{5,7},{7,1},{8,10},{10,12},{12... | collective-permute-start | bytes 294920 | tf_op jit(solution)/shard_map/ppermute | solution.py:22
  38.9 5.9 %collective-permute-start.16 = (bf16[2,1,1,64,128]{4,3,2,1,0:T(8,128)(2,1)S(1)}, bf16[2,1,1,64,128]{4,3,2,1,0:T(8,128)(2,1)S(1)}, u32[]{:S(2)}, u32[]{:S(2)}) collective-permute-start(bf16[2,1,1,64,128]{4,3,2,1,0:T(8,128)(2,1)S(1)} %bitcast.73), channel_id=1, source_target_pairs={{0,24},{8,0},{16,8},{24,16},{1,25},{9,1},{17,9},{25,17},{2,26},{10... | collective-permute-start | bytes 98312 | tf_op jit(solution)/shard_map/ppermute | solution.py:22
  41.7 5.7 %collective-permute-start.15 = (bf16[2,1,1,64,128]{4,3,2,1,0:T(8,128)(2,1)S(1)}, bf16[2,1,1,64,128]{4,3,2,1,0:T(8,128)(2,1)S(1)}, u32[]{:S(2)}, u32[]{:S(2)}) collective-permute-start(bf16[2,1,1,64,128]{4,3,2,1,0:T(8,128)(2,1)S(1)} %bitcast.74), channel_id=1, source_target_pairs={{0,8},{8,16},{16,24},{24,0},{1,9},{9,17},{17,25},{25,1},{2,10},{10... | collective-permute-start | bytes 98312 | tf_op jit(solution)/shard_map/ppermute | solution.py:22
  41.7 7.0 %collective-permute-start.13 = (bf16[2,3,128,128]{3,2,1,0:T(8,128)(2,1)S(1)}, bf16[2,3,128,128]{3,2,1,0:T(8,128)(2,1)S(1)}, u32[]{:S(2)}, u32[]{:S(2)}) collective-permute-start(bf16[2,3,128,128]{3,2,1,0:T(8,128)(2,1)S(1)} %get-tuple-element.39), channel_id=1, source_target_pairs={{0,2},{2,4},{4,6},{6,0},{1,3},{3,5},{5,7},{7,1},{8,10},{10,12},{12... | collective-permute-start | bytes 589832 | tf_op jit(solution)/shard_map/ppermute | solution.py:22
  41.7 7.0 %collective-permute-start.14 = (bf16[2,3,128,128]{3,2,1,0:T(8,128)(2,1)S(1)}, bf16[2,3,128,128]{3,2,1,0:T(8,128)(2,1)S(1)}, u32[]{:S(2)}, u32[]{:S(2)}) collective-permute-start(bf16[2,3,128,128]{3,2,1,0:T(8,128)(2,1)S(1)} %get-tuple-element.40), channel_id=1, source_target_pairs={{0,6},{2,0},{4,2},{6,4},{1,7},{3,1},{5,3},{7,5},{8,14},{10,8},{12,... | collective-permute-start | bytes 589832 | tf_op jit(solution)/shard_map/ppermute | solution.py:22
  47.5 4.0 %collective-permute-start.18 = (bf16[2,3,1,64,128]{4,3,2,1,0:T(8,128)(2,1)S(1)}, bf16[2,3,1,64,128]{4,3,2,1,0:T(8,128)(2,1)S(1)}, u32[]{:S(2)}, u32[]{:S(2)}) collective-permute-start(bf16[2,3,1,64,128]{4,3,2,1,0:T(8,128)(2,1)S(1)} %pad_maximum_fusion.8), channel_id=1, source_target_pairs={{0,6},{2,0},{4,2},{6,4},{1,7},{3,1},{5,3},{7,5},{8,14},{10,8},{12,... | collective-permute-start | bytes 294920 | tf_op jit(solution)/shard_map/ppermute | solution.py:22
  47.5 4.1 %collective-permute-start.17 = (bf16[2,3,1,64,128]{4,3,2,1,0:T(8,128)(2,1)S(1)}, bf16[2,3,1,64,128]{4,3,2,1,0:T(8,128)(2,1)S(1)}, u32[]{:S(2)}, u32[]{:S(2)}) collective-permute-start(bf16[2,3,1,64,128]{4,3,2,1,0:T(8,128)(2,1)S(1)} %pad_maximum_fusion.8), channel_id=1, source_target_pairs={{0,2},{2,4},{4,6},{6,0},{1,3},{3,5},{5,7},{7,1},{8,10},{10,12},{12... | collective-permute-start | bytes 294920 | tf_op jit(solution)/shard_map/ppermute | solution.py:22

commit v10 on v9

--- a/solution.py
+++ b/solution.py
@@ -43,10 +43,8 @@
     return columns_of(rows_of(sheets, centre))
 
 
-def across_rows(outgoing, crossed):
-    sheets = jnp.stack([outgoing[0], crossed])
-    rows = [moved(sheets[:, i], "gx", i - 1) if i != 1 else sheets[:, i] for i in (2, 1, 0)]
-    return jnp.stack(rows, axis=1)
+def across_rows(blocks):
+    return jnp.stack([moved(blocks[i], "gx", i - 1) if i != 1 else blocks[i] for i in (2, 1, 0)])
 
 
 def across_columns(shifted):
@@ -192,8 +190,10 @@
 
 
 def pairs_body(
-    send_ref, own_ref, nb_ref, kind_ref, recv_ref, pack_ref, hot_own_ref, hot_mir_ref, place_ref
+    send_ref, own_ref, nb_ref, kind_ref, recv_ref, pack_ref, e_ref,
+    hot_own_ref, hot_mir_ref, place_ref, near_ref,
 ):
+    near_ref[...] = e_ref[: near_ref.shape[0], :]
     fan, atoms = pack_ref.shape
     cap = hot_own_ref.shape[0] // OFFS
     send = as_row(send_ref[...])
@@ -451,14 +451,23 @@
     )
     outgoing = ordered.reshape(2, 3, 3, cap, channels)
     crossed = swapped(outgoing[1], "layer")
-    shifted = across_rows(outgoing, crossed)
+    hot_own, hot_mir, place, near = call(
+        pairs_body,
+        (
+            array(owned, 128),
+            array(owned, 128),
+            array(fan, atoms, dtype=F32),
+            array(owned // 2, channels),
+        ),
+        send, own, nb, kind, recv, pack, ordered,
+        after=(other,),
+        us=2.5,
+    )
+    near_rows = across_rows(near.reshape(3, 3, cap, channels))
+    shifted = jnp.stack([near_rows, across_rows(crossed)])
     mirror = across_columns(shifted).reshape(owned, channels)
-    hot_own, hot_mir, place = call(
-        pairs_body,
-        (array(owned, 128), array(owned, 128), array(fan, atoms, dtype=F32)),
-        send, own, nb, kind, recv, pack,
-        after=(ordered,),
-        us=2.5,
+    rows = rows_of(
+        sheets.reshape(2, 1, 1, atoms, channels), centre.reshape(2, 1, 1, atoms, channels)
     )
     pick_own, pick_mir, perm, mine, w_cat = call(
         places_body,
@@ -470,6 +479,7 @@
             array(block, 2 * channels),
         ),
         pack, place, w_block.T,
+        after=(rows,),
         us=2.5,
     )
     table = pltpu.VMEM((2 * ghosts, 2 * channels), BF16)
@@ -500,10 +510,10 @@
             us=0.6,
         )
 
-    ghosts_at = [ghosts_of(framed_sheets(sheets), framed_sheets(centre))]
-    sheets = node(0, (crossed,))
+    ghosts_at = [columns_of(rows)]
+    sheets = node(0, (crossed, near_rows))
     ghosts_at.append(ghosts_of(framed_sheets(sheets), framed_sheets(sheets)))
-    ordered = edge(0, True)
+    ordered = edge(0, True, after=(sheets,))
     sheets = node(1, (perm, ordered, shifted))
     ordered, centre = edge(1, True, hand_on=(sheets,))
     mirror = edge(0, False)

time: 57.8 us -> 65 us (1.12)
  waiting for transfers between devices: 11.4 us -> 18.5 us
    ppermute x16 -> x18, waiting for transfers between devices: 11.4 us -> 16.7 us  [moved(): lax.ppermute(value, axis, [(i, (i + steps) % count) for i in range(count)])]
    ppermute x3, waiting for transfers between devices: 0.01 us -> 1.87 us  [swapped(): return lax.ppermute(value, axis, [(0, 1), (1, 0)])]
    ppermute x16 -> x18, starting transfers between devices: 18.2 us -> 17.6 us  [moved(): lax.ppermute(value, axis, [(i, (i + steps) % count) for i in range(count)])]
  transfers between devices with their start and end apart: 19 -> 21, of which waited for: 8 -> 9; matrix products, arithmetic and copies ran while one was open for 3% -> 3% of each run, Pallas kernels for 23% -> 21%
where the time goes in v10:
time: 65 us; the launch traced here: 64.8 us
  starting transfers between devices  22.7 us (35%)
  Pallas kernels  20.3 us (31%)
  waiting for transfers between devices  18.5 us (28%)
  other arithmetic  1.91 us (3%)
  local copies, waits for them, and re-layouts  0.91 us (1%)
    pallas_call x11, Pallas kernels, call(): pl.pallas_call(ordered_body if after else body, out_shape=outs, in_specs=...  20.3 us
    ppermute x18, starting transfers between devices, moved(): lax.ppermute(value, axis, [(i, (i + steps) % count) for i in range(count)])  17.6 us
    ppermute x18, waiting for transfers between devices, moved(): lax.ppermute(value, axis, [(i, (i + steps) % count) for i in range(count)])  16.7 us
    ppermute x3, starting transfers between devices, swapped(): return lax.ppermute(value, axis, [(0, 1), (1, 0)])  5.06 us
    ppermute x3, waiting for transfers between devices, swapped(): return lax.ppermute(value, axis, [(0, 1), (1, 0)])  1.87 us
  transfers between devices with their start and end apart: 21, of which 9 were waited for; matrix products, arithmetic and copies ran while one was open for 3% of the time, Pallas kernels for 21%

profile of v10, /device:TPU:0, one launch (start us, length us, event | category | flops | bytes accessed | tf_op | source)
XLA Modules:
  0.0 64.8 jit_solution(8499873438467338345)
XLA Ops:
  0.0 3.0 %collective-permute-start = (bf16[64,128]{1,0:T(8,128)(2,1)}, bf16[64,128]{1,0:T(8,128)(2,1)S(1)}, u32[]{:S(2)}, u32[]{:S(2)}) collective-permute-start(bf16[64,128]{1,0:T(8,128)(2,1)} %h_ref.1), channel_id=1, source_target_pairs={{0,1},{1,0},{2,3},{3,2},{4,5},{5,4},{6,7},{7,6},{8,9},{9,8},{10,11... | collective-permute-start | bytes 49160 | tf_op jit(solution)/shard_map/ppermute | solution.py:17
  3.0 0.8 %or_convert_fusion = f32[36,128]{1,0:T(8,128)S(1)} fusion(s32[4608]{0:T(1024)} %param.23, s32[4608]{0:T(1024)} %param.20, s32[4608]{0:T(1024)} %param.19), kind=kLoop, calls=%fused_computation.25 | loop fusion | flops 27648 | bytes 73728 | tf_op jit(solution)/shard_map/convert_element_type | solution.py:436
  3.7 0.7 %pad_maximum_fusion.9.both_ref = f32[72,128]{1,0:T(8,128)S(1)} fusion(f32[36,128]{1,0:T(8,128)} %bitcast.93, f32[36,128]{1,0:T(8,128)S(1)} %or_convert_fusion), kind=kLoop, calls=%fused_computation.24 | loop fusion | flops 9216 | bytes 73728 | tf_op jit(solution)/shard_map/concatenate | solution.py:435
  4.5 0.7 %copy-done.12 = bf16[64,128]{1,0:T(8,128)(2,1)S(1)} copy-done((bf16[64,128]{1,0:T(8,128)(2,1)S(1)}, bf16[64,128]{1,0:T(8,128)(2,1)}, u32[]{:S(2)}) %copy-start.12) | copy-done | bytes 16408
  5.2 1.4 %shard_map.154 = (bf16[64,1152]{1,0:T(8,128)(2,1)S(1)}, s32[72,64]{1,0:T(8,128)S(1)}, bf16[64,128]{1,0:T(8,128)(2,1)S(1)}) custom-call(f32[72,128]{1,0:T(8,128)S(1)} %pad_maximum_fusion.9.both_ref, bf16[64,128]{1,0:T(8,128)(2,1)S(1)} %copy-done.12), custom_call_target="tpu_custom_call" | custom-call | flops 2200000000 | bytes 7200000 | tf_op jit(solution)/shard_map/pallas_call | solution.py:89
  6.6 0.0 collective-permute-done
  6.6 3.7 %collective-permute-start.3 = (bf16[2,1,1,64,128]{4,3,2,1,0:T(8,128)(2,1)S(1)}, bf16[2,1,1,64,128]{4,3,2,1,0:T(8,128)(2,1)S(1)}, u32[]{:S(2)}, u32[]{:S(2)}) collective-permute-start(bf16[2,1,1,64,128]{4,3,2,1,0:T(8,128)(2,1)S(1)} %bitcast.77), channel_id=1, source_target_pairs={{0,24},{8,0},{16,8},{24,16},{1,25},{9,1},{17,9},{25,17},{2,26},{10... | collective-permute-start | bytes 98312 | tf_op jit(solution)/shard_map/ppermute | solution.py:22
  10.3 0.0 collective-permute-start.2
  10.3 0.0 copy-start.2
  10.3 0.0 copy-start.3
  10.3 0.0 copy-start.4
  10.3 0.0 copy-start.14
  10.3 1.9 %shard_map.155 = (bf16[2304,128]{1,0:T(8,128)(2,1)S(1)}, bf16[128,128]{1,0:T(8,128)(2,1)S(1)}) custom-call(s32[18,128]{1,0:T(8,128)S(1)} %bitcast.80, bf16[2304,128]{1,0:T(8,128)(2,1)S(1)} %copy-done.6, bf16[128,128]{1,0:T(8,128)(2,1)S(1)} %constant_dynamic-update-slice_fusion.h_ref), custom_call_target="tpu_custom_call" | custom-call | flops 2200000000 | bytes 7200000 | tf_op jit(solution)/shard_map/pallas_call | solution.py:89
  12.2 0.0 collective-permute-done.3
  12.3 3.7 %collective-permute-done.2 = bf16[2,1,1,64,128]{4,3,2,1,0:T(8,128)(2,1)S(1)} collective-permute-done((bf16[2,1,1,64,128]{4,3,2,1,0:T(8,128)(2,1)S(1)}, bf16[2,1,1,64,128]{4,3,2,1,0:T(8,128)(2,1)S(1)}, u32[]{:S(2)}, u32[]{:S(2)}) %collective-permute-start.2) | collective-permute-done | bytes 32800 | tf_op jit(solution)/shard_map/ppermute | solution.py:22
  16.0 0.1 collective-permute-start.5
  16.1 0.5 collective-permute-start.4
  16.5 0.5 collective-permute-start.1
  17.1 1.6 %collective-permute-start.6 = (bf16[3,3,128,128]{3,2,1,0:T(8,128)(2,1)S(1)}, bf16[3,3,128,128]{3,2,1,0:T(8,128)(2,1)S(1)}, u32[]{:S(2)}, u32[]{:S(2)}) collective-permute-start(bf16[3,3,128,128]{3,2,1,0:T(8,128)(2,1)S(1)} %bitcast.84), channel_id=1, source_target_pairs={{0,1},{1,0},{2,3},{3,2},{4,5},{5,4},{6,7},{7,6},{8,9},{9,8},{10,11... | collective-permute-start | bytes 884744 | tf_op jit(solution)/shard_map/ppermute | solution.py:17
  18.7 0.0 collective-permute-done.5
  18.7 2.5 %collective-permute-done.4 = bf16[2,3,1,64,128]{4,3,2,1,0:T(8,128)(2,1)S(1)} collective-permute-done((bf16[2,3,1,64,128]{4,3,2,1,0:T(8,128)(2,1)S(1)}, bf16[2,3,1,64,128]{4,3,2,1,0:T(8,128)(2,1)S(1)}, u32[]{:S(2)}, u32[]{:S(2)}) %collective-permute-start.4) | collective-permute-done | bytes 98336 | tf_op jit(solution)/shard_map/ppermute | solution.py:22
  21.2 1.9 %collective-permute-done.1.refs_7_.refs_1_ = bf16[64,1152]{1,0:T(8,128)(2,1)S(1)} collective-permute-done((bf16[64,1152]{1,0:T(8,128)(2,1)S(1)}, bf16[64,1152]{1,0:T(8,128)(2,1)S(1)}, u32[]{:S(2)}, u32[]{:S(2)}) %collective-permute-start.1) | collective-permute-done | bytes 147488 | tf_op jit(solution)/shard_map/ppermute | solution.py:17
  23.1 0.0 copy-start.11
  23.1 2.2 %shard_map.156 = (bf16[2304,128]{1,0:T(8,128)(2,1)S(1)}, bf16[2304,128]{1,0:T(8,128)(2,1)S(1)}, f32[72,64]{1,0:T(8,128)S(1)}, bf16[1152,128]{1,0:T(8,128)(2,1)S(1)}) custom-call(s32[18,128]{1,0:T(8,128)S(1)} %bitcast.81, s32[18,128]{1,0:T(8,128)S(1)} %bitcast.82, s32[36,128]{1,0:T(8,128)S(1)} %bitcast.76, s32[36,128]{1,0:T(8,128)S(1)} %bitcast.75, ...), custom_call_target="tpu_custom_call" | custom-call | flops 2750000128 | bytes 9000000 | tf_op jit(solution)/shard_map/pallas_call | solution.py:89
  25.4 0.2 collective-permute-start.8
  25.5 1.9 %collective-permute-start.7 = (bf16[3,128,128]{2,1,0:T(8,128)(2,1)S(1)}, bf16[3,128,128]{2,1,0:T(8,128)(2,1)S(1)}, u32[]{:S(2)}, u32[]{:S(2)}) collective-permute-start(bf16[3,128,128]{2,1,0:T(8,128)(2,1)S(1)} %bitcast.90), channel_id=1, source_target_pairs={{0,8},{8,16},{16,24},{24,0},{1,9},{9,17},{17,25},{25,1},{2,10},{10... | collective-permute-start | bytes 294920 | tf_op jit(solution)/shard_map/ppermute | solution.py:22
  27.5 2.4 %shard_map.159 = (bf16[2304,128]{1,0:T(8,128)(2,1)S(1)}, bf16[2304,128]{1,0:T(8,128)(2,1)S(1)}, bf16[4608,144]{1,0:T(8,128)(2,1)S(1)}, f32[72,64]{1,0:T(8,128)S(1)}, bf16[169,256]{1,0:T(8,128)(2,1)S(1)}) custom-call(s32[72,64]{1,0:T(8,128)S(1)} %get-tuple-element.25.refs_5_.refs_0_, f32[72,64]{1,0:T(8,128)S(1)} %get-tuple-element.30.refs_1_, ...), custom_call_target="tpu_custom_call" | custom-call | flops 2750000128 | bytes 9000000 | tf_op jit(solution)/shard_map/pallas_call | solution.py:89
  29.9 0.0 copy-start.7
  29.9 0.0 copy-start.8
  29.9 0.0 copy-start.9
  29.9 0.0 copy-start.10
  29.9 2.8 %collective-permute-done.8 = bf16[3,128,128]{2,1,0:T(8,128)(2,1)S(1)} collective-permute-done((bf16[3,128,128]{2,1,0:T(8,128)(2,1)S(1)}, bf16[3,128,128]{2,1,0:T(8,128)(2,1)S(1)}, u32[]{:S(2)}, u32[]{:S(2)}) %collective-permute-start.8) | collective-permute-done | bytes 98336 | tf_op jit(solution)/shard_map/ppermute | solution.py:22
  32.7 0.0 collective-permute-done.7
  32.8 0.0 collective-permute-done.6.refs_6_
  32.8 0.6 shard_map.157.refs_7_
  33.4 0.3 collective-permute-start.10
  33.8 1.7 %collective-permute-start.9 = (bf16[2,1,1,64,128]{4,3,2,1,0:T(8,128)(2,1)S(1)}, bf16[2,1,1,64,128]{4,3,2,1,0:T(8,128)(2,1)S(1)}, u32[]{:S(2)}, u32[]{:S(2)}) collective-permute-start(bf16[2,1,1,64,128]{4,3,2,1,0:T(8,128)(2,1)S(1)} %bitcast.64), channel_id=1, source_target_pairs={{0,8},{8,16},{16,24},{24,0},{1,9},{9,17},{17,25},{25,1},{2,10},{10... | collective-permute-start | bytes 98312 | tf_op jit(solution)/shard_map/ppermute | solution.py:22
  35.5 0.3 collective-permute-start.13
  35.9 3.5 %collective-permute-start.14 = (bf16[3,128,128]{2,1,0:T(8,128)(2,1)S(1)}, bf16[3,128,128]{2,1,0:T(8,128)(2,1)S(1)}, u32[]{:S(2)}, u32[]{:S(2)}) collective-permute-start(bf16[3,128,128]{2,1,0:T(8,128)(2,1)S(1)} %get-tuple-element.47), channel_id=1, source_target_pairs={{0,24},{8,0},{16,8},{24,16},{1,25},{9,1},{17,9},{25,17},{2,26},{10... | collective-permute-start | bytes 294920 | tf_op jit(solution)/shard_map/ppermute | solution.py:22
  39.4 1.3 %shard_map.158.refs_7_.e_ref = bf16[2304,128]{1,0:T(8,128)(2,1)S(1)} custom-call(bf16[2304,128]{1,0:T(8,128)(2,1)S(1)} %get-tuple-element.24.refs_6_.refs_0_, bf16[2304,128]{1,0:T(8,128)(2,1)S(1)} %get-tuple-element.27.refs_1_.hot_ref.ho_ref, bf16[1152,128]{1,0:T(8,128)(2,1)S(1)} %bitcast.60, bf16[3,128,128]{2,1,0:T(8,128)(2,1)S(1)} %copy-done.7, ...), custom_call_target="tpu_custom_call" | custom-call | flops 1540000000 | bytes 5040000 | tf_op jit(solution)/shard_map/pallas_call | solution.py:89
  40.7 0.0 collective-permute-done.10
  40.8 0.1 collective-permute-start.12
  40.8 0.5 collective-permute-start.11
  41.3 1.1 %collective-permute-done.13 = bf16[3,128,128]{2,1,0:T(8,128)(2,1)S(1)} collective-permute-done((bf16[3,128,128]{2,1,0:T(8,128)(2,1)S(1)}, bf16[3,128,128]{2,1,0:T(8,128)(2,1)S(1)}, u32[]{:S(2)}, u32[]{:S(2)}) %collective-permute-start.13) | collective-permute-done | bytes 98336 | tf_op jit(solution)/shard_map/ppermute | solution.py:22
  42.5 0.1 fusion.1
  42.6 0.1 collective-permute-start.15
  42.7 1.7 %collective-permute-start.16 = (bf16[2,3,128,128]{3,2,1,0:T(8,128)(2,1)S(1)}, bf16[2,3,128,128]{3,2,1,0:T(8,128)(2,1)S(1)}, u32[]{:S(2)}, u32[]{:S(2)}) collective-permute-start(bf16[2,3,128,128]{3,2,1,0:T(8,128)(2,1)S(1)} %get-tuple-element.43), channel_id=1, source_target_pairs={{0,6},{2,0},{4,2},{6,4},{1,7},{3,1},{5,3},{7,5},{8,14},{10,8},{12,... | collective-permute-start | bytes 589832 | tf_op jit(solution)/shard_map/ppermute | solution.py:22
  44.4 0.1 pad_maximum_fusion.refs_8_
  44.5 0.9 %collective-permute-done.11 = bf16[2,3,1,64,128]{4,3,2,1,0:T(8,128)(2,1)S(1)} collective-permute-done((bf16[2,3,1,64,128]{4,3,2,1,0:T(8,128)(2,1)S(1)}, bf16[2,3,1,64,128]{4,3,2,1,0:T(8,128)(2,1)S(1)}, u32[]{:S(2)}, u32[]{:S(2)}) %collective-permute-start.11) | collective-permute-done | bytes 98336 | tf_op jit(solution)/shard_map/ppermute | solution.py:22
  45.4 0.6 shard_map.160.refs_0_
  46.0 2.5 %collective-permute-start.18 = (bf16[2,1,1,64,128]{4,3,2,1,0:T(8,128)(2,1)S(1)}, bf16[2,1,1,64,128]{4,3,2,1,0:T(8,128)(2,1)S(1)}, u32[]{:S(2)}, u32[]{:S(2)}) collective-permute-start(bf16[2,1,1,64,128]{4,3,2,1,0:T(8,128)(2,1)S(1)} %bitcast.71), channel_id=1, source_target_pairs={{0,24},{8,0},{16,8},{24,16},{1,25},{9,1},{17,9},{25,17},{2,26},{10... | collective-permute-start | bytes 98312 | tf_op jit(solution)/shard_map/ppermute | solution.py:22
  48.5 0.0 collective-permute-start.17
  48.5 1.3 %shard_map.161 = (bf16[2304,128]{1,0:T(8,128)(2,1)S(1)}, bf16[128,128]{1,0:T(8,128)(2,1)S(1)}) custom-call(bf16[2304,128]{1,0:T(8,128)(2,1)S(1)} %shard_map.158.refs_7_.e_ref, bf16[2304,128]{1,0:T(8,128)(2,1)S(1)} %get-tuple-element.27.refs_1_.hot_ref.ho_ref, bf16[1152,128]{1,0:T(8,128)(2,1)S(1)} %bitcast.56, bf16[3,128,128]{2,1,0:T(8,128)(2,1)S(1)} %copy-done.7, ...), custom_call_target="tpu_custom_call" | custom-call | flops 1540000000 | bytes 5040000 | tf_op jit(solution)/shard_map/pallas_call | solution.py:89
  49.8 0.3 collective-permute-done.18
  50.1 4.1 %collective-permute-done.17 = bf16[2,1,1,64,128]{4,3,2,1,0:T(8,128)(2,1)S(1)} collective-permute-done((bf16[2,1,1,64,128]{4,3,2,1,0:T(8,128)(2,1)S(1)}, bf16[2,1,1,64,128]{4,3,2,1,0:T(8,128)(2,1)S(1)}, u32[]{:S(2)}, u32[]{:S(2)}) %collective-permute-start.17) | collective-permute-done | bytes 32800 | tf_op jit(solution)/shard_map/ppermute | solution.py:22
  54.2 0.1 collective-permute-start.20
  54.3 0.5 collective-permute-start.19
  54.8 0.0 collective-permute-done.16
  54.8 0.1 pad_maximum_fusion.1
  54.9 1.3 %shard_map.162.e_ref = bf16[2304,128]{1,0:T(8,128)(2,1)S(1)} custom-call(bf16[2304,128]{1,0:T(8,128)(2,1)S(1)} %bitcast.58, bf16[2304,128]{1,0:T(8,128)(2,1)S(1)} %get-tuple-element.33.hot_ref.hm_ref, bf16[1152,128]{1,0:T(8,128)(2,1)S(1)} %bitcast.61, bf16[3,128,128]{2,1,0:T(8,128)(2,1)S(1)} %copy-done.8, bf16[3,128,128]{2,1,0:T(8,128)(2,1)S(1)} %copy-done.7, ...), custom_call_target="tpu_custom_call" | custom-call | flops 1540000000 | bytes 5040000 | tf_op jit(solution)/shard_map/pallas_call | solution.py:89
  56.3 1.3 %shard_map.163 = (bf16[2304,128]{1,0:T(8,128)(2,1)S(1)}, bf16[384,128]{1,0:T(8,128)(2,1)S(1)}) custom-call(bf16[2304,128]{1,0:T(8,128)(2,1)S(1)} %shard_map.162.e_ref, bf16[2304,128]{1,0:T(8,128)(2,1)S(1)} %get-tuple-element.33.hot_ref.hm_ref, bf16[1152,128]{1,0:T(8,128)(2,1)S(1)} %bitcast.57, bf16[3,128,128]{2,1,0:T(8,128)(2,1)S(1)} %copy-done.8, ...), custom_call_target="tpu_custom_call" | custom-call | flops 1540000000 | bytes 5040000 | tf_op jit(solution)/shard_map/pallas_call | solution.py:89
  57.6 0.0 collective-permute-done.20
  57.6 1.2 %collective-permute-done.19 = bf16[2,3,1,64,128]{4,3,2,1,0:T(8,128)(2,1)S(1)} collective-permute-done((bf16[2,3,1,64,128]{4,3,2,1,0:T(8,128)(2,1)S(1)}, bf16[2,3,1,64,128]{4,3,2,1,0:T(8,128)(2,1)S(1)}, u32[]{:S(2)}, u32[]{:S(2)}) %collective-permute-start.19) | collective-permute-done | bytes 98336 | tf_op jit(solution)/shard_map/ppermute | solution.py:22
  58.8 5.9 %shard_map.164 = bf16[169,4608]{1,0:T(8,128)(2,1)} custom-call(bf16[2304,128]{1,0:T(8,128)(2,1)S(1)} %get-tuple-element.32.own_ref, bf16[2304,128]{1,0:T(8,128)(2,1)S(1)} %get-tuple-element.35.mir_ref, bf16[2304,128]{1,0:T(8,128)(2,1)S(1)} %get-tuple-element.27.refs_1_.hot_ref.ho_ref, bf16[2304,128]{1,0:T(8,128)(2,1)S(1)} %get-tuple-element.33.hot_ref.hm_ref, ...), custom_call_target="tpu_custom_call" | custom-call | flops 7699999744 | bytes 25200000 | tf_op jit(solution)/shard_map/pallas_call | solution.py:89
  (38 shorter events, 0.4 us)
Async XLA Ops:
  0.0 6.6 %collective-permute-start = (bf16[64,128]{1,0:T(8,128)(2,1)}, bf16[64,128]{1,0:T(8,128)(2,1)S(1)}, u32[]{:S(2)}, u32[]{:S(2)}) collective-permute-start(bf16[64,128]{1,0:T(8,128)(2,1)} %h_ref.1), channel_id=1, source_target_pairs={{0,1},{1,0},{2,3},{3,2},{4,5},{5,4},{6,7},{7,6},{8,9},{9,8},{10,11... | collective-permute-start | bytes 49160 | tf_op jit(solution)/shard_map/ppermute | solution.py:17
  4.5 0.7 %copy-start.12 = (bf16[64,128]{1,0:T(8,128)(2,1)S(1)}, bf16[64,128]{1,0:T(8,128)(2,1)}, u32[]{:S(2)}) copy-start(bf16[64,128]{1,0:T(8,128)(2,1)} %h_ref.1) | copy-start | bytes 49156
  5.2 5.1 %copy-start.6 = (bf16[2304,128]{1,0:T(8,128)(2,1)S(1)}, bf16[2304,128]{1,0:T(8,128)(2,1)}, u32[]{:S(2)}) copy-start(bf16[2304,128]{1,0:T(8,128)(2,1)} %bond_ref.1) | copy-start | bytes 1769476
  5.2 5.1 %copy-start.13 = (s32[2304]{0:T(1024)S(1)}, s32[2304]{0:T(1024)}, u32[]{:S(2)}) copy-start(s32[2304]{0:T(1024)} %param.22) | copy-start | bytes 27652
  6.6 5.6 %collective-permute-start.3 = (bf16[2,1,1,64,128]{4,3,2,1,0:T(8,128)(2,1)S(1)}, bf16[2,1,1,64,128]{4,3,2,1,0:T(8,128)(2,1)S(1)}, u32[]{:S(2)}, u32[]{:S(2)}) collective-permute-start(bf16[2,1,1,64,128]{4,3,2,1,0:T(8,128)(2,1)S(1)} %bitcast.77), channel_id=1, source_target_pairs={{0,24},{8,0},{16,8},{24,16},{1,25},{9,1},{17,9},{25,17},{2,26},{10... | collective-permute-start | bytes 98312 | tf_op jit(solution)/shard_map/ppermute | solution.py:22
  10.3 5.7 %collective-permute-start.2 = (bf16[2,1,1,64,128]{4,3,2,1,0:T(8,128)(2,1)S(1)}, bf16[2,1,1,64,128]{4,3,2,1,0:T(8,128)(2,1)S(1)}, u32[]{:S(2)}, u32[]{:S(2)}) collective-permute-start(bf16[2,1,1,64,128]{4,3,2,1,0:T(8,128)(2,1)S(1)} %bitcast.78), channel_id=1, source_target_pairs={{0,8},{8,16},{16,24},{24,0},{1,9},{9,17},{17,25},{25,1},{2,10},{10... | collective-permute-start | bytes 98312 | tf_op jit(solution)/shard_map/ppermute | solution.py:22
  10.3 12.8 %copy-start.2 = (s32[4608]{0:T(1024)S(1)}, s32[4608]{0:T(1024)}, u32[]{:S(2)}) copy-start(s32[4608]{0:T(1024)} %param.23) | copy-start | bytes 55300
  10.3 12.8 %copy-start.3 = (s32[4608]{0:T(1024)S(1)}, s32[4608]{0:T(1024)}, u32[]{:S(2)}) copy-start(s32[4608]{0:T(1024)} %param.20) | copy-start | bytes 55300
  10.3 12.8 %copy-start.4 = (s32[4608]{0:T(1024)S(1)}, s32[4608]{0:T(1024)}, u32[]{:S(2)}) copy-start(s32[4608]{0:T(1024)} %param.19) | copy-start | bytes 55300
  10.3 12.8 %copy-start.14 = (s32[2304]{0:T(1024)S(1)}, s32[2304]{0:T(1024)}, u32[]{:S(2)}) copy-start(s32[2304]{0:T(1024)} %param.21) | copy-start | bytes 27652
  16.0 2.7 %collective-permute-start.5 = (bf16[2,3,1,64,128]{4,3,2,1,0:T(8,128)(2,1)S(1)}, bf16[2,3,1,64,128]{4,3,2,1,0:T(8,128)(2,1)S(1)}, u32[]{:S(2)}, u32[]{:S(2)}) collective-permute-start(bf16[2,3,1,64,128]{4,3,2,1,0:T(8,128)(2,1)S(1)} %pad_maximum_fusion.6.refs_3_), channel_id=1, source_target_pairs={{0,6},{2,0},{4,2},{6,4},{1,7},{3,1},{5,3},{7,5},{8,14},{10,8},{12,... | collective-permute-start | bytes 294920 | tf_op jit(solution)/shard_map/ppermute | solution.py:22
  16.1 5.1 %collective-permute-start.4 = (bf16[2,3,1,64,128]{4,3,2,1,0:T(8,128)(2,1)S(1)}, bf16[2,3,1,64,128]{4,3,2,1,0:T(8,128)(2,1)S(1)}, u32[]{:S(2)}, u32[]{:S(2)}) collective-permute-start(bf16[2,3,1,64,128]{4,3,2,1,0:T(8,128)(2,1)S(1)} %pad_maximum_fusion.6.refs_3_), channel_id=1, source_target_pairs={{0,2},{2,4},{4,6},{6,0},{1,3},{3,5},{5,7},{7,1},{8,10},{10,12},{12... | collective-permute-start | bytes 294920 | tf_op jit(solution)/shard_map/ppermute | solution.py:22
  16.5 6.5 %collective-permute-start.1 = (bf16[64,1152]{1,0:T(8,128)(2,1)S(1)}, bf16[64,1152]{1,0:T(8,128)(2,1)S(1)}, u32[]{:S(2)}, u32[]{:S(2)}) collective-permute-start(bf16[64,1152]{1,0:T(8,128)(2,1)S(1)} %get-tuple-element.26.refs_0_), channel_id=1, source_target_pairs={{0,1},{1,0},{2,3},{3,2},{4,5},{5,4},{6,7},{7,6},{8,9},{9,8},{10,11... | collective-permute-start | bytes 442376 | tf_op jit(solution)/shard_map/ppermute | solution.py:17
  17.1 15.7 %collective-permute-start.6 = (bf16[3,3,128,128]{3,2,1,0:T(8,128)(2,1)S(1)}, bf16[3,3,128,128]{3,2,1,0:T(8,128)(2,1)S(1)}, u32[]{:S(2)}, u32[]{:S(2)}) collective-permute-start(bf16[3,3,128,128]{3,2,1,0:T(8,128)(2,1)S(1)} %bitcast.84), channel_id=1, source_target_pairs={{0,1},{1,0},{2,3},{3,2},{4,5},{5,4},{6,7},{7,6},{8,9},{9,8},{10,11... | collective-permute-start | bytes 884744 | tf_op jit(solution)/shard_map/ppermute | solution.py:17
  23.1 4.3 %copy-start.11 = (bf16[128,169]{0,1:T(8,128)(2,1)S(1)}, bf16[128,169]{0,1:T(8,128)(2,1)}, u32[]{:S(2)}) copy-start(bf16[128,169]{0,1:T(8,128)(2,1)} %param.31) | copy-start | bytes 129796
  25.4 7.4 %collective-permute-start.8 = (bf16[3,128,128]{2,1,0:T(8,128)(2,1)S(1)}, bf16[3,128,128]{2,1,0:T(8,128)(2,1)S(1)}, u32[]{:S(2)}, u32[]{:S(2)}) collective-permute-start(bf16[3,128,128]{2,1,0:T(8,128)(2,1)S(1)} %bitcast.92), channel_id=1, source_target_pairs={{0,24},{8,0},{16,8},{24,16},{1,25},{9,1},{17,9},{25,17},{2,26},{10... | collective-permute-start | bytes 294920 | tf_op jit(solution)/shard_map/ppermute | solution.py:22
  25.5 7.2 %collective-permute-start.7 = (bf16[3,128,128]{2,1,0:T(8,128)(2,1)S(1)}, bf16[3,128,128]{2,1,0:T(8,128)(2,1)S(1)}, u32[]{:S(2)}, u32[]{:S(2)}) collective-permute-start(bf16[3,128,128]{2,1,0:T(8,128)(2,1)S(1)} %bitcast.90), channel_id=1, source_target_pairs={{0,8},{8,16},{16,24},{24,0},{1,9},{9,17},{17,25},{25,1},{2,10},{10... | collective-permute-start | bytes 294920 | tf_op jit(solution)/shard_map/ppermute | solution.py:22
  27.4 5.3 %copy-start = (bf16[2,128,128]{2,1,0:T(8,128)(2,1)S(1)}, bf16[2,128,128]{2,1,0:T(8,128)(2,1)}, u32[]{:S(2)}) copy-start(bf16[2,128,128]{2,1,0:T(8,128)(2,1)} %refs_3_.5) | copy-start | bytes 196612
  27.4 5.3 %copy-start.1 = (bf16[2,128,128]{2,1,0:T(8,128)(2,1)S(1)}, bf16[2,128,128]{2,1,0:T(8,128)(2,1)}, u32[]{:S(2)}) copy-start(bf16[2,128,128]{2,1,0:T(8,128)(2,1)} %refs_4_.5) | copy-start | bytes 196612
  27.4 5.4 %copy-start.5 = (f32[2,128]{1,0:T(2,128)S(1)}, f32[2,128]{1,0:T(2,128)}, u32[]{:S(2)}) copy-start(f32[2,128]{1,0:T(2,128)} %refs_5_.5) | copy-start | bytes 3076
  29.9 9.5 %copy-start.7 = (bf16[3,128,128]{2,1,0:T(8,128)(2,1)S(1)}, bf16[3,128,128]{2,1,0:T(8,128)(2,1)}, u32[]{:S(2)}) copy-start(bf16[3,128,128]{2,1,0:T(8,128)(2,1)} %wl_ref.7) | copy-start | bytes 294916
  29.9 9.5 %copy-start.8 = (bf16[3,128,128]{2,1,0:T(8,128)(2,1)S(1)}, bf16[3,128,128]{2,1,0:T(8,128)(2,1)}, u32[]{:S(2)}) copy-start(bf16[3,128,128]{2,1,0:T(8,128)(2,1)} %wr_ref.1) | copy-start | bytes 294916
  29.9 9.5 %copy-start.9 = (bf16[3,128,128]{2,1,0:T(8,128)(2,1)S(1)}, bf16[3,128,128]{2,1,0:T(8,128)(2,1)}, u32[]{:S(2)}) copy-start(bf16[3,128,128]{2,1,0:T(8,128)(2,1)} %wi_ref.7) | copy-start | bytes 294916
  29.9 9.5 %copy-start.10 = (bf16[3,128,128]{2,1,0:T(8,128)(2,1)S(1)}, bf16[3,128,128]{2,1,0:T(8,128)(2,1)}, u32[]{:S(2)}) copy-start(bf16[3,128,128]{2,1,0:T(8,128)(2,1)} %wo_ref.7) | copy-start | bytes 294916
  33.4 7.3 %collective-permute-start.10 = (bf16[2,1,1,64,128]{4,3,2,1,0:T(8,128)(2,1)S(1)}, bf16[2,1,1,64,128]{4,3,2,1,0:T(8,128)(2,1)S(1)}, u32[]{:S(2)}, u32[]{:S(2)}) collective-permute-start(bf16[2,1,1,64,128]{4,3,2,1,0:T(8,128)(2,1)S(1)} %bitcast.63), channel_id=1, source_target_pairs={{0,24},{8,0},{16,8},{24,16},{1,25},{9,1},{17,9},{25,17},{2,26},{10... | collective-permute-start | bytes 98312 | tf_op jit(solution)/shard_map/ppermute | solution.py:22
  33.8 7.0 %collective-permute-start.9 = (bf16[2,1,1,64,128]{4,3,2,1,0:T(8,128)(2,1)S(1)}, bf16[2,1,1,64,128]{4,3,2,1,0:T(8,128)(2,1)S(1)}, u32[]{:S(2)}, u32[]{:S(2)}) collective-permute-start(bf16[2,1,1,64,128]{4,3,2,1,0:T(8,128)(2,1)S(1)} %bitcast.64), channel_id=1, source_target_pairs={{0,8},{8,16},{16,24},{24,0},{1,9},{9,17},{17,25},{25,1},{2,10},{10... | collective-permute-start | bytes 98312 | tf_op jit(solution)/shard_map/ppermute | solution.py:22
  35.5 7.0 %collective-permute-start.13 = (bf16[3,128,128]{2,1,0:T(8,128)(2,1)S(1)}, bf16[3,128,128]{2,1,0:T(8,128)(2,1)S(1)}, u32[]{:S(2)}, u32[]{:S(2)}) collective-permute-start(bf16[3,128,128]{2,1,0:T(8,128)(2,1)S(1)} %get-tuple-element.46), channel_id=1, source_target_pairs={{0,8},{8,16},{16,24},{24,0},{1,9},{9,17},{17,25},{25,1},{2,10},{10... | collective-permute-start | bytes 294920 | tf_op jit(solution)/shard_map/ppermute | solution.py:22
  35.9 6.6 %collective-permute-start.14 = (bf16[3,128,128]{2,1,0:T(8,128)(2,1)S(1)}, bf16[3,128,128]{2,1,0:T(8,128)(2,1)S(1)}, u32[]{:S(2)}, u32[]{:S(2)}) collective-permute-start(bf16[3,128,128]{2,1,0:T(8,128)(2,1)S(1)} %get-tuple-element.47), channel_id=1, source_target_pairs={{0,24},{8,0},{16,8},{24,16},{1,25},{9,1},{17,9},{25,17},{2,26},{10... | collective-permute-start | bytes 294920 | tf_op jit(solution)/shard_map/ppermute | solution.py:22
  40.8 3.7 %collective-permute-start.12 = (bf16[2,3,1,64,128]{4,3,2,1,0:T(8,128)(2,1)S(1)}, bf16[2,3,1,64,128]{4,3,2,1,0:T(8,128)(2,1)S(1)}, u32[]{:S(2)}, u32[]{:S(2)}) collective-permute-start(bf16[2,3,1,64,128]{4,3,2,1,0:T(8,128)(2,1)S(1)} %pad_maximum_fusion.7), channel_id=1, source_target_pairs={{0,6},{2,0},{4,2},{6,4},{1,7},{3,1},{5,3},{7,5},{8,14},{10,8},{12,... | collective-permute-start | bytes 294920 | tf_op jit(solution)/shard_map/ppermute | solution.py:22
  40.8 4.5 %collective-permute-start.11 = (bf16[2,3,1,64,128]{4,3,2,1,0:T(8,128)(2,1)S(1)}, bf16[2,3,1,64,128]{4,3,2,1,0:T(8,128)(2,1)S(1)}, u32[]{:S(2)}, u32[]{:S(2)}) collective-permute-start(bf16[2,3,1,64,128]{4,3,2,1,0:T(8,128)(2,1)S(1)} %pad_maximum_fusion.7), channel_id=1, source_target_pairs={{0,2},{2,4},{4,6},{6,0},{1,3},{3,5},{5,7},{7,1},{8,10},{10,12},{12... | collective-permute-start | bytes 294920 | tf_op jit(solution)/shard_map/ppermute | solution.py:22
  42.6 12.2 %collective-permute-start.15 = (bf16[2,3,128,128]{3,2,1,0:T(8,128)(2,1)S(1)}, bf16[2,3,128,128]{3,2,1,0:T(8,128)(2,1)S(1)}, u32[]{:S(2)}, u32[]{:S(2)}) collective-permute-start(bf16[2,3,128,128]{3,2,1,0:T(8,128)(2,1)S(1)} %get-tuple-element.41), channel_id=1, source_target_pairs={{0,2},{2,4},{4,6},{6,0},{1,3},{3,5},{5,7},{7,1},{8,10},{10,12},{12... | collective-permute-start | bytes 589832 | tf_op jit(solution)/shard_map/ppermute | solution.py:22
  42.7 12.2 %collective-permute-start.16 = (bf16[2,3,128,128]{3,2,1,0:T(8,128)(2,1)S(1)}, bf16[2,3,128,128]{3,2,1,0:T(8,128)(2,1)S(1)}, u32[]{:S(2)}, u32[]{:S(2)}) collective-permute-start(bf16[2,3,128,128]{3,2,1,0:T(8,128)(2,1)S(1)} %get-tuple-element.43), channel_id=1, source_target_pairs={{0,6},{2,0},{4,2},{6,4},{1,7},{3,1},{5,3},{7,5},{8,14},{10,8},{12,... | collective-permute-start | bytes 589832 | tf_op jit(solution)/shard_map/ppermute | solution.py:22
  46.0 4.1 %collective-permute-start.18 = (bf16[2,1,1,64,128]{4,3,2,1,0:T(8,128)(2,1)S(1)}, bf16[2,1,1,64,128]{4,3,2,1,0:T(8,128)(2,1)S(1)}, u32[]{:S(2)}, u32[]{:S(2)}) collective-permute-start(bf16[2,1,1,64,128]{4,3,2,1,0:T(8,128)(2,1)S(1)} %bitcast.71), channel_id=1, source_target_pairs={{0,24},{8,0},{16,8},{24,16},{1,25},{9,1},{17,9},{25,17},{2,26},{10... | collective-permute-start | bytes 98312 | tf_op jit(solution)/shard_map/ppermute | solution.py:22
  48.5 5.7 %collective-permute-start.17 = (bf16[2,1,1,64,128]{4,3,2,1,0:T(8,128)(2,1)S(1)}, bf16[2,1,1,64,128]{4,3,2,1,0:T(8,128)(2,1)S(1)}, u32[]{:S(2)}, u32[]{:S(2)}) collective-permute-start(bf16[2,1,1,64,128]{4,3,2,1,0:T(8,128)(2,1)S(1)} %bitcast.72), channel_id=1, source_target_pairs={{0,8},{8,16},{16,24},{24,0},{1,9},{9,17},{17,25},{25,1},{2,10},{10... | collective-permute-start | bytes 98312 | tf_op jit(solution)/shard_map/ppermute | solution.py:22
  54.2 3.3 %collective-permute-start.20 = (bf16[2,3,1,64,128]{4,3,2,1,0:T(8,128)(2,1)S(1)}, bf16[2,3,1,64,128]{4,3,2,1,0:T(8,128)(2,1)S(1)}, u32[]{:S(2)}, u32[]{:S(2)}) collective-permute-start(bf16[2,3,1,64,128]{4,3,2,1,0:T(8,128)(2,1)S(1)} %pad_maximum_fusion.8), channel_id=1, source_target_pairs={{0,6},{2,0},{4,2},{6,4},{1,7},{3,1},{5,3},{7,5},{8,14},{10,8},{12,... | collective-permute-start | bytes 294920 | tf_op jit(solution)/shard_map/ppermute | solution.py:22
  54.3 4.5 %collective-permute-start.19 = (bf16[2,3,1,64,128]{4,3,2,1,0:T(8,128)(2,1)S(1)}, bf16[2,3,1,64,128]{4,3,2,1,0:T(8,128)(2,1)S(1)}, u32[]{:S(2)}, u32[]{:S(2)}) collective-permute-start(bf16[2,3,1,64,128]{4,3,2,1,0:T(8,128)(2,1)S(1)} %pad_maximum_fusion.8), channel_id=1, source_target_pairs={{0,2},{2,4},{4,6},{6,0},{1,3},{3,5},{5,7},{7,1},{8,10},{10,12},{12... | collective-permute-start | bytes 294920 | tf_op jit(solution)/shard_map/ppermute | solution.py:22

commit v11 on v9

--- a/solution.py
+++ b/solution.py
@@ -453,23 +453,14 @@
     crossed = swapped(outgoing[1], "layer")
     shifted = across_rows(outgoing, crossed)
     mirror = across_columns(shifted).reshape(owned, channels)
+    rows = rows_of(
+        sheets.reshape(2, 1, 1, atoms, channels), centre.reshape(2, 1, 1, atoms, channels)
+    )
     hot_own, hot_mir, place = call(
         pairs_body,
         (array(owned, 128), array(owned, 128), array(fan, atoms, dtype=F32)),
         send, own, nb, kind, recv, pack,
-        after=(ordered,),
-        us=2.5,
-    )
-    pick_own, pick_mir, perm, mine, w_cat = call(
-        places_body,
-        (
-            array(owned, cap),
-            array(owned, cap),
-            array(slots, 2 * fan),
-            array(fan, atoms, dtype=F32),
-            array(block, 2 * channels),
-        ),
-        pack, place, w_block.T,
+        after=(rows,),
         us=2.5,
     )
     table = pltpu.VMEM((2 * ghosts, 2 * channels), BF16)
@@ -500,8 +491,21 @@
             us=0.6,
         )
 
-    ghosts_at = [ghosts_of(framed_sheets(sheets), framed_sheets(centre))]
+    ghosts_at = [columns_of(rows)]
     sheets = node(0, (crossed,))
+    pick_own, pick_mir, perm, mine, w_cat = call(
+        places_body,
+        (
+            array(owned, cap),
+            array(owned, cap),
+            array(slots, 2 * fan),
+            array(fan, atoms, dtype=F32),
+            array(block, 2 * channels),
+        ),
+        pack, place, w_block.T,
+        after=(sheets,),
+        us=2.5,
+    )
     ghosts_at.append(ghosts_of(framed_sheets(sheets), framed_sheets(sheets)))
     ordered = edge(0, True)
     sheets = node(1, (perm, ordered, shifted))

time: 57.8 us -> 57 us (0.986)
  starting transfers between devices: 22.8 us -> 20.9 us
  waiting for transfers between devices: 11.4 us -> 12.4 us
    ppermute x16, starting transfers between devices: 18.2 us -> 16.3 us  [moved(): lax.ppermute(value, axis, [(i, (i + steps) % count) for i in range(count)])]
    ppermute x16, waiting for transfers between devices: 11.4 us -> 12.4 us  [moved(): lax.ppermute(value, axis, [(i, (i + steps) % count) for i in range(count)])]
where the time goes in v11:
time: 57 us; the launch traced here: 56.7 us
  starting transfers between devices  20.9 us (37%)
  Pallas kernels  20.2 us (35%)
  waiting for transfers between devices  12.4 us (22%)
  other arithmetic  1.83 us (3%)
  local copies, waits for them, and re-layouts  0.94 us (2%)
    pallas_call x11, Pallas kernels, call(): pl.pallas_call(ordered_body if after else body, out_shape=outs, in_specs=...  20.2 us
    ppermute x16, starting transfers between devices, moved(): lax.ppermute(value, axis, [(i, (i + steps) % count) for i in range(count)])  16.3 us
    ppermute x16, waiting for transfers between devices, moved(): lax.ppermute(value, axis, [(i, (i + steps) % count) for i in range(count)])  12.4 us
    ppermute x3, starting transfers between devices, swapped(): return lax.ppermute(value, axis, [(0, 1), (1, 0)])  4.62 us
  transfers between devices with their start and end apart: 19, of which 8 were waited for; matrix products, arithmetic and copies ran while one was open for 3% of the time, Pallas kernels for 23%

profile of v11, /device:TPU:0, one launch (start us, length us, event | category | flops | bytes accessed | tf_op | source)
XLA Modules:
  0.0 56.7 jit_solution(15440358777766035153)
XLA Ops:
  0.0 3.0 %collective-permute-start = (bf16[64,128]{1,0:T(8,128)(2,1)}, bf16[64,128]{1,0:T(8,128)(2,1)S(1)}, u32[]{:S(2)}, u32[]{:S(2)}) collective-permute-start(bf16[64,128]{1,0:T(8,128)(2,1)} %h_ref.1), channel_id=1, source_target_pairs={{0,1},{1,0},{2,3},{3,2},{4,5},{5,4},{6,7},{7,6},{8,9},{9,8},{10,11... | collective-permute-start | bytes 49160 | tf_op jit(solution)/shard_map/ppermute | solution.py:17
  3.0 0.8 %or_convert_fusion = f32[36,128]{1,0:T(8,128)S(1)} fusion(s32[4608]{0:T(1024)} %param.23, s32[4608]{0:T(1024)} %param.20, s32[4608]{0:T(1024)} %param.19), kind=kLoop, calls=%fused_computation.22 | loop fusion | flops 27648 | bytes 73728 | tf_op jit(solution)/shard_map/convert_element_type | solution.py:436
  3.7 0.7 %pad_maximum_fusion.9.both_ref = f32[72,128]{1,0:T(8,128)S(1)} fusion(f32[36,128]{1,0:T(8,128)} %bitcast.87, f32[36,128]{1,0:T(8,128)S(1)} %or_convert_fusion), kind=kLoop, calls=%fused_computation.21 | loop fusion | flops 9216 | bytes 73728 | tf_op jit(solution)/shard_map/concatenate | solution.py:435
  4.5 0.7 %copy-done.12 = bf16[64,128]{1,0:T(8,128)(2,1)S(1)} copy-done((bf16[64,128]{1,0:T(8,128)(2,1)S(1)}, bf16[64,128]{1,0:T(8,128)(2,1)}, u32[]{:S(2)}) %copy-start.12) | copy-done | bytes 16408
  5.2 1.4 %shard_map.154 = (bf16[64,1152]{1,0:T(8,128)(2,1)S(1)}, s32[72,64]{1,0:T(8,128)S(1)}, bf16[64,128]{1,0:T(8,128)(2,1)S(1)}) custom-call(f32[72,128]{1,0:T(8,128)S(1)} %pad_maximum_fusion.9.both_ref, bf16[64,128]{1,0:T(8,128)(2,1)S(1)} %copy-done.12), custom_call_target="tpu_custom_call" | custom-call | flops 2200000000 | bytes 7200000 | tf_op jit(solution)/shard_map/pallas_call | solution.py:91
  6.6 0.1 collective-permute-start.5
  6.7 0.0 collective-permute-done
  6.7 4.1 %collective-permute-start.2 = (bf16[2,1,1,64,128]{4,3,2,1,0:T(8,128)(2,1)S(1)}, bf16[2,1,1,64,128]{4,3,2,1,0:T(8,128)(2,1)S(1)}, u32[]{:S(2)}, u32[]{:S(2)}) collective-permute-start(bf16[2,1,1,64,128]{4,3,2,1,0:T(8,128)(2,1)S(1)} %bitcast.75), channel_id=1, source_target_pairs={{0,24},{8,0},{16,8},{24,16},{1,25},{9,1},{17,9},{25,17},{2,26},{10... | collective-permute-start | bytes 98312 | tf_op jit(solution)/shard_map/ppermute | solution.py:22
  10.8 0.0 collective-permute-start.1
  10.8 0.0 copy-start.2
  10.8 0.0 copy-start.3
  10.8 0.0 copy-start.4
  10.9 0.0 copy-start.14
  10.9 1.9 %shard_map.155 = (bf16[2304,128]{1,0:T(8,128)(2,1)S(1)}, bf16[128,128]{1,0:T(8,128)(2,1)S(1)}) custom-call(s32[18,128]{1,0:T(8,128)S(1)} %bitcast.78, bf16[2304,128]{1,0:T(8,128)(2,1)S(1)} %copy-done.6, bf16[128,128]{1,0:T(8,128)(2,1)S(1)} %constant_dynamic-update-slice_fusion.h_ref), custom_call_target="tpu_custom_call" | custom-call | flops 2200000000 | bytes 7200000 | tf_op jit(solution)/shard_map/pallas_call | solution.py:91
  12.8 1.6 %collective-permute-start.6 = (bf16[3,3,128,128]{3,2,1,0:T(8,128)(2,1)S(1)}, bf16[3,3,128,128]{3,2,1,0:T(8,128)(2,1)S(1)}, u32[]{:S(2)}, u32[]{:S(2)}) collective-permute-start(bf16[3,3,128,128]{3,2,1,0:T(8,128)(2,1)S(1)} %bitcast.82), channel_id=1, source_target_pairs={{0,1},{1,0},{2,3},{3,2},{4,5},{5,4},{6,7},{7,6},{8,9},{9,8},{10,11... | collective-permute-start | bytes 884744 | tf_op jit(solution)/shard_map/ppermute | solution.py:17
  14.4 0.0 collective-permute-done.2
  14.4 2.1 %collective-permute-done.1 = bf16[2,1,1,64,128]{4,3,2,1,0:T(8,128)(2,1)S(1)} collective-permute-done((bf16[2,1,1,64,128]{4,3,2,1,0:T(8,128)(2,1)S(1)}, bf16[2,1,1,64,128]{4,3,2,1,0:T(8,128)(2,1)S(1)}, u32[]{:S(2)}, u32[]{:S(2)}) %collective-permute-start.1) | collective-permute-done | bytes 32800 | tf_op jit(solution)/shard_map/ppermute | solution.py:22
  16.5 0.1 collective-permute-start.4
  16.6 0.5 collective-permute-start.3
  17.1 0.0 copy-start.7
  17.1 0.0 copy-start.8
  17.1 0.0 copy-start.9
  17.1 0.0 copy-start.10
  17.2 2.2 %shard_map.156 = (bf16[2304,128]{1,0:T(8,128)(2,1)S(1)}, bf16[2304,128]{1,0:T(8,128)(2,1)S(1)}, f32[72,64]{1,0:T(8,128)S(1)}) custom-call(s32[18,128]{1,0:T(8,128)S(1)} %bitcast.79, s32[18,128]{1,0:T(8,128)S(1)} %bitcast.80, s32[36,128]{1,0:T(8,128)S(1)} %bitcast.74, s32[36,128]{1,0:T(8,128)S(1)} %bitcast.73, s32[36,128]{1,0:T(8,128)S(1)} %bitcast.72, ...), custom_call_target="tpu_custom_call" | custom-call | flops 2750000128 | bytes 9000000 | tf_op jit(solution)/shard_map/pallas_call | solution.py:91
  19.3 0.0 collective-permute-done.4
  19.4 2.4 %collective-permute-done.3 = bf16[2,3,1,64,128]{4,3,2,1,0:T(8,128)(2,1)S(1)} collective-permute-done((bf16[2,3,1,64,128]{4,3,2,1,0:T(8,128)(2,1)S(1)}, bf16[2,3,1,64,128]{4,3,2,1,0:T(8,128)(2,1)S(1)}, u32[]{:S(2)}, u32[]{:S(2)}) %collective-permute-start.3) | collective-permute-done | bytes 98336 | tf_op jit(solution)/shard_map/ppermute | solution.py:22
  21.8 0.0 copy-start
  21.8 0.0 copy-start.1
  21.8 0.0 copy-start.5
  21.8 1.3 %shard_map.157.refs_7_.e_ref = bf16[2304,128]{1,0:T(8,128)(2,1)S(1)} custom-call(bf16[2304,128]{1,0:T(8,128)(2,1)S(1)} %get-tuple-element.23.e_ref, bf16[2304,128]{1,0:T(8,128)(2,1)S(1)} %get-tuple-element.26.hot_ref.ho_ref, bf16[1152,128]{1,0:T(8,128)(2,1)S(1)} %bitcast.56, bf16[3,128,128]{2,1,0:T(8,128)(2,1)S(1)} %copy-done.7, ...), custom_call_target="tpu_custom_call" | custom-call | flops 1540000000 | bytes 5040000 | tf_op jit(solution)/shard_map/pallas_call | solution.py:91
  23.2 0.0 copy-start.11
  23.2 0.0 collective-permute-done.5.refs_1_
  23.2 0.0 collective-permute-done.6.refs_6_
  23.2 0.6 %shard_map.158.refs_3_ = bf16[128,128]{1,0:T(8,128)(2,1)S(1)} custom-call(bf16[64,1152]{1,0:T(8,128)(2,1)S(1)} %get-tuple-element.27.refs_0_, bf16[64,1152]{1,0:T(8,128)(2,1)S(1)} %collective-permute-done.5.refs_1_, bf16[1152,128]{1,0:T(8,128)(2,1)S(1)} %bitcast.57, bf16[2,128,128]{2,1,0:T(8,128)(2,1)S(1)} %copy-done, bf16[2,128,128]{2,1,0:T(8,128)(2,1)S(1)} %copy-done.1, ...), custom_call_target="tpu_custom_call" | custom-call | flops 660000000 | bytes 2160000 | tf_op jit(solution)/shard_map/pallas_call | solution.py:91
  23.8 1.7 %collective-permute-start.8 = (bf16[2,1,1,64,128]{4,3,2,1,0:T(8,128)(2,1)S(1)}, bf16[2,1,1,64,128]{4,3,2,1,0:T(8,128)(2,1)S(1)}, u32[]{:S(2)}, u32[]{:S(2)}) collective-permute-start(bf16[2,1,1,64,128]{4,3,2,1,0:T(8,128)(2,1)S(1)} %bitcast.61), channel_id=1, source_target_pairs={{0,24},{8,0},{16,8},{24,16},{1,25},{9,1},{17,9},{25,17},{2,26},{10... | collective-permute-start | bytes 98312 | tf_op jit(solution)/shard_map/ppermute | solution.py:22
  25.6 0.3 collective-permute-start.7
  25.9 0.1 fusion.3
  26.0 0.1 collective-permute-start.11
  26.0 3.8 %collective-permute-start.12 = (bf16[2,3,128,128]{3,2,1,0:T(8,128)(2,1)S(1)}, bf16[2,3,128,128]{3,2,1,0:T(8,128)(2,1)S(1)}, u32[]{:S(2)}, u32[]{:S(2)}) collective-permute-start(bf16[2,3,128,128]{3,2,1,0:T(8,128)(2,1)S(1)} %get-tuple-element.43), channel_id=1, source_target_pairs={{0,24},{8,0},{16,8},{24,16},{1,25},{9,1},{17,9},{25,17},{2,26},{10... | collective-permute-start | bytes 589832 | tf_op jit(solution)/shard_map/ppermute | solution.py:22
  29.8 0.0 collective-permute-done.8
  29.8 2.0 %collective-permute-done.7 = bf16[2,1,1,64,128]{4,3,2,1,0:T(8,128)(2,1)S(1)} collective-permute-done((bf16[2,1,1,64,128]{4,3,2,1,0:T(8,128)(2,1)S(1)}, bf16[2,1,1,64,128]{4,3,2,1,0:T(8,128)(2,1)S(1)}, u32[]{:S(2)}, u32[]{:S(2)}) %collective-permute-start.7) | collective-permute-done | bytes 32800 | tf_op jit(solution)/shard_map/ppermute | solution.py:22
  31.8 0.1 collective-permute-start.10
  31.9 0.5 collective-permute-start.9
  32.4 2.4 %shard_map.159 = (bf16[2304,128]{1,0:T(8,128)(2,1)S(1)}, bf16[2304,128]{1,0:T(8,128)(2,1)S(1)}, bf16[4608,144]{1,0:T(8,128)(2,1)S(1)}, f32[72,64]{1,0:T(8,128)S(1)}, bf16[169,256]{1,0:T(8,128)(2,1)S(1)}) custom-call(s32[72,64]{1,0:T(8,128)S(1)} %get-tuple-element.24.refs_5_.refs_0_, f32[72,64]{1,0:T(8,128)S(1)} %get-tuple-element.28.refs_1_, ...), custom_call_target="tpu_custom_call" | custom-call | flops 2750000128 | bytes 9000000 | tf_op jit(solution)/shard_map/pallas_call | solution.py:91
  34.8 0.0 collective-permute-done.10
  34.8 1.5 %collective-permute-done.9 = bf16[2,3,1,64,128]{4,3,2,1,0:T(8,128)(2,1)S(1)} collective-permute-done((bf16[2,3,1,64,128]{4,3,2,1,0:T(8,128)(2,1)S(1)}, bf16[2,3,1,64,128]{4,3,2,1,0:T(8,128)(2,1)S(1)}, u32[]{:S(2)}, u32[]{:S(2)}) %collective-permute-start.9) | collective-permute-done | bytes 98336 | tf_op jit(solution)/shard_map/ppermute | solution.py:22
  36.4 0.0 collective-permute-done.11
  36.4 1.0 %collective-permute-done.12 = bf16[2,3,128,128]{3,2,1,0:T(8,128)(2,1)S(1)} collective-permute-done((bf16[2,3,128,128]{3,2,1,0:T(8,128)(2,1)S(1)}, bf16[2,3,128,128]{3,2,1,0:T(8,128)(2,1)S(1)}, u32[]{:S(2)}, u32[]{:S(2)}) %collective-permute-start.12) | collective-permute-done | bytes 196640 | tf_op jit(solution)/shard_map/ppermute | solution.py:22
  37.3 0.1 pad_maximum_fusion.refs_8_
  37.5 0.6 %shard_map.160.refs_0_ = bf16[128,128]{1,0:T(8,128)(2,1)S(1)} custom-call(bf16[64,1152]{1,0:T(8,128)(2,1)S(1)} %get-tuple-element.27.refs_0_, bf16[64,1152]{1,0:T(8,128)(2,1)S(1)} %collective-permute-done.5.refs_1_, bf16[1152,128]{1,0:T(8,128)(2,1)S(1)} %bitcast.52, bf16[2,128,128]{2,1,0:T(8,128)(2,1)S(1)} %copy-done, bf16[2,128,128]{2,1,0:T(8,128)(2,1)S(1)} %copy-done.1, ...), custom_call_target="tpu_custom_call" | custom-call | flops 660000000 | bytes 2160000 | tf_op jit(solution)/shard_map/pallas_call | solution.py:91
  38.1 2.8 %collective-permute-start.16 = (bf16[2,1,1,64,128]{4,3,2,1,0:T(8,128)(2,1)S(1)}, bf16[2,1,1,64,128]{4,3,2,1,0:T(8,128)(2,1)S(1)}, u32[]{:S(2)}, u32[]{:S(2)}) collective-permute-start(bf16[2,1,1,64,128]{4,3,2,1,0:T(8,128)(2,1)S(1)} %bitcast.69), channel_id=1, source_target_pairs={{0,24},{8,0},{16,8},{24,16},{1,25},{9,1},{17,9},{25,17},{2,26},{10... | collective-permute-start | bytes 98312 | tf_op jit(solution)/shard_map/ppermute | solution.py:22
  40.9 0.0 collective-permute-start.15
  40.9 0.0 collective-permute-start.13
  40.9 1.7 %collective-permute-start.14 = (bf16[2,3,128,128]{3,2,1,0:T(8,128)(2,1)S(1)}, bf16[2,3,128,128]{3,2,1,0:T(8,128)(2,1)S(1)}, u32[]{:S(2)}, u32[]{:S(2)}) collective-permute-start(bf16[2,3,128,128]{3,2,1,0:T(8,128)(2,1)S(1)} %get-tuple-element.40), channel_id=1, source_target_pairs={{0,6},{2,0},{4,2},{6,4},{1,7},{3,1},{5,3},{7,5},{8,14},{10,8},{12,... | collective-permute-start | bytes 589832 | tf_op jit(solution)/shard_map/ppermute | solution.py:22
  42.6 1.3 %shard_map.161 = (bf16[2304,128]{1,0:T(8,128)(2,1)S(1)}, bf16[128,128]{1,0:T(8,128)(2,1)S(1)}) custom-call(bf16[2304,128]{1,0:T(8,128)(2,1)S(1)} %shard_map.157.refs_7_.e_ref, bf16[2304,128]{1,0:T(8,128)(2,1)S(1)} %get-tuple-element.26.hot_ref.ho_ref, bf16[1152,128]{1,0:T(8,128)(2,1)S(1)} %bitcast.53, bf16[3,128,128]{2,1,0:T(8,128)(2,1)S(1)} %copy-done.7, ...), custom_call_target="tpu_custom_call" | custom-call | flops 1540000000 | bytes 5040000 | tf_op jit(solution)/shard_map/pallas_call | solution.py:91
  43.9 2.6 %collective-permute-done.15 = bf16[2,1,1,64,128]{4,3,2,1,0:T(8,128)(2,1)S(1)} collective-permute-done((bf16[2,1,1,64,128]{4,3,2,1,0:T(8,128)(2,1)S(1)}, bf16[2,1,1,64,128]{4,3,2,1,0:T(8,128)(2,1)S(1)}, u32[]{:S(2)}, u32[]{:S(2)}) %collective-permute-start.15) | collective-permute-done | bytes 32800 | tf_op jit(solution)/shard_map/ppermute | solution.py:22
  46.6 0.1 collective-permute-start.18
  46.6 0.5 collective-permute-start.17
  47.1 0.7 %collective-permute-done.13 = bf16[2,3,128,128]{3,2,1,0:T(8,128)(2,1)S(1)} collective-permute-done((bf16[2,3,128,128]{3,2,1,0:T(8,128)(2,1)S(1)}, bf16[2,3,128,128]{3,2,1,0:T(8,128)(2,1)S(1)}, u32[]{:S(2)}, u32[]{:S(2)}) %collective-permute-start.13) | collective-permute-done | bytes 196640 | tf_op jit(solution)/shard_map/ppermute | solution.py:22
  47.8 0.1 pad_maximum_fusion.1
  47.9 1.3 %shard_map.162.e_ref = bf16[2304,128]{1,0:T(8,128)(2,1)S(1)} custom-call(bf16[2304,128]{1,0:T(8,128)(2,1)S(1)} %bitcast.55, bf16[2304,128]{1,0:T(8,128)(2,1)S(1)} %get-tuple-element.31.hot_ref.hm_ref, bf16[1152,128]{1,0:T(8,128)(2,1)S(1)} %bitcast.58, bf16[3,128,128]{2,1,0:T(8,128)(2,1)S(1)} %copy-done.8, bf16[3,128,128]{2,1,0:T(8,128)(2,1)S(1)} %copy-done.7, ...), custom_call_target="tpu_custom_call" | custom-call | flops 1540000000 | bytes 5040000 | tf_op jit(solution)/shard_map/pallas_call | solution.py:91
  49.2 1.3 %shard_map.163 = (bf16[2304,128]{1,0:T(8,128)(2,1)S(1)}, bf16[384,128]{1,0:T(8,128)(2,1)S(1)}) custom-call(bf16[2304,128]{1,0:T(8,128)(2,1)S(1)} %shard_map.162.e_ref, bf16[2304,128]{1,0:T(8,128)(2,1)S(1)} %get-tuple-element.31.hot_ref.hm_ref, bf16[1152,128]{1,0:T(8,128)(2,1)S(1)} %bitcast.54, bf16[3,128,128]{2,1,0:T(8,128)(2,1)S(1)} %copy-done.8, ...), custom_call_target="tpu_custom_call" | custom-call | flops 1540000000 | bytes 5040000 | tf_op jit(solution)/shard_map/pallas_call | solution.py:91
  50.6 0.2 collective-permute-done.17
  50.8 5.9 %shard_map.164 = bf16[169,4608]{1,0:T(8,128)(2,1)} custom-call(bf16[2304,128]{1,0:T(8,128)(2,1)S(1)} %get-tuple-element.30.own_ref, bf16[2304,128]{1,0:T(8,128)(2,1)S(1)} %get-tuple-element.33.mir_ref, bf16[2304,128]{1,0:T(8,128)(2,1)S(1)} %get-tuple-element.26.hot_ref.ho_ref, bf16[2304,128]{1,0:T(8,128)(2,1)S(1)} %get-tuple-element.31.hot_ref.hm_ref, ...), custom_call_target="tpu_custom_call" | custom-call | flops 7699999744 | bytes 25200000 | tf_op jit(solution)/shard_map/pallas_call | solution.py:91
  (31 shorter events, 0.3 us)
Async XLA Ops:
  0.0 6.7 %collective-permute-start = (bf16[64,128]{1,0:T(8,128)(2,1)}, bf16[64,128]{1,0:T(8,128)(2,1)S(1)}, u32[]{:S(2)}, u32[]{:S(2)}) collective-permute-start(bf16[64,128]{1,0:T(8,128)(2,1)} %h_ref.1), channel_id=1, source_target_pairs={{0,1},{1,0},{2,3},{3,2},{4,5},{5,4},{6,7},{7,6},{8,9},{9,8},{10,11... | collective-permute-start | bytes 49160 | tf_op jit(solution)/shard_map/ppermute | solution.py:17
  4.5 0.7 %copy-start.12 = (bf16[64,128]{1,0:T(8,128)(2,1)S(1)}, bf16[64,128]{1,0:T(8,128)(2,1)}, u32[]{:S(2)}) copy-start(bf16[64,128]{1,0:T(8,128)(2,1)} %h_ref.1) | copy-start | bytes 49156
  5.2 5.6 %copy-start.6 = (bf16[2304,128]{1,0:T(8,128)(2,1)S(1)}, bf16[2304,128]{1,0:T(8,128)(2,1)}, u32[]{:S(2)}) copy-start(bf16[2304,128]{1,0:T(8,128)(2,1)} %bond_ref.1) | copy-start | bytes 1769476
  5.2 5.6 %copy-start.13 = (s32[2304]{0:T(1024)S(1)}, s32[2304]{0:T(1024)}, u32[]{:S(2)}) copy-start(s32[2304]{0:T(1024)} %param.22) | copy-start | bytes 27652
  6.6 16.6 %collective-permute-start.5 = (bf16[64,1152]{1,0:T(8,128)(2,1)S(1)}, bf16[64,1152]{1,0:T(8,128)(2,1)S(1)}, u32[]{:S(2)}, u32[]{:S(2)}) collective-permute-start(bf16[64,1152]{1,0:T(8,128)(2,1)S(1)} %get-tuple-element.27.refs_0_), channel_id=1, source_target_pairs={{0,1},{1,0},{2,3},{3,2},{4,5},{5,4},{6,7},{7,6},{8,9},{9,8},{10,11... | collective-permute-start | bytes 442376 | tf_op jit(solution)/shard_map/ppermute | solution.py:17
  6.7 7.7 %collective-permute-start.2 = (bf16[2,1,1,64,128]{4,3,2,1,0:T(8,128)(2,1)S(1)}, bf16[2,1,1,64,128]{4,3,2,1,0:T(8,128)(2,1)S(1)}, u32[]{:S(2)}, u32[]{:S(2)}) collective-permute-start(bf16[2,1,1,64,128]{4,3,2,1,0:T(8,128)(2,1)S(1)} %bitcast.75), channel_id=1, source_target_pairs={{0,24},{8,0},{16,8},{24,16},{1,25},{9,1},{17,9},{25,17},{2,26},{10... | collective-permute-start | bytes 98312 | tf_op jit(solution)/shard_map/ppermute | solution.py:22
  10.8 5.7 %collective-permute-start.1 = (bf16[2,1,1,64,128]{4,3,2,1,0:T(8,128)(2,1)S(1)}, bf16[2,1,1,64,128]{4,3,2,1,0:T(8,128)(2,1)S(1)}, u32[]{:S(2)}, u32[]{:S(2)}) collective-permute-start(bf16[2,1,1,64,128]{4,3,2,1,0:T(8,128)(2,1)S(1)} %bitcast.76), channel_id=1, source_target_pairs={{0,8},{8,16},{16,24},{24,0},{1,9},{9,17},{17,25},{25,1},{2,10},{10... | collective-permute-start | bytes 98312 | tf_op jit(solution)/shard_map/ppermute | solution.py:22
  10.8 6.3 %copy-start.2 = (s32[4608]{0:T(1024)S(1)}, s32[4608]{0:T(1024)}, u32[]{:S(2)}) copy-start(s32[4608]{0:T(1024)} %param.23) | copy-start | bytes 55300
  10.8 6.3 %copy-start.3 = (s32[4608]{0:T(1024)S(1)}, s32[4608]{0:T(1024)}, u32[]{:S(2)}) copy-start(s32[4608]{0:T(1024)} %param.20) | copy-start | bytes 55300
  10.8 6.3 %copy-start.4 = (s32[4608]{0:T(1024)S(1)}, s32[4608]{0:T(1024)}, u32[]{:S(2)}) copy-start(s32[4608]{0:T(1024)} %param.19) | copy-start | bytes 55300
  10.9 6.3 %copy-start.14 = (s32[2304]{0:T(1024)S(1)}, s32[2304]{0:T(1024)}, u32[]{:S(2)}) copy-start(s32[2304]{0:T(1024)} %param.21) | copy-start | bytes 27652
  12.8 10.4 %collective-permute-start.6 = (bf16[3,3,128,128]{3,2,1,0:T(8,128)(2,1)S(1)}, bf16[3,3,128,128]{3,2,1,0:T(8,128)(2,1)S(1)}, u32[]{:S(2)}, u32[]{:S(2)}) collective-permute-start(bf16[3,3,128,128]{3,2,1,0:T(8,128)(2,1)S(1)} %bitcast.82), channel_id=1, source_target_pairs={{0,1},{1,0},{2,3},{3,2},{4,5},{5,4},{6,7},{7,6},{8,9},{9,8},{10,11... | collective-permute-start | bytes 884744 | tf_op jit(solution)/shard_map/ppermute | solution.py:17
  16.5 2.8 %collective-permute-start.4 = (bf16[2,3,1,64,128]{4,3,2,1,0:T(8,128)(2,1)S(1)}, bf16[2,3,1,64,128]{4,3,2,1,0:T(8,128)(2,1)S(1)}, u32[]{:S(2)}, u32[]{:S(2)}) collective-permute-start(bf16[2,3,1,64,128]{4,3,2,1,0:T(8,128)(2,1)S(1)} %pad_maximum_fusion.6.refs_6_), channel_id=1, source_target_pairs={{0,6},{2,0},{4,2},{6,4},{1,7},{3,1},{5,3},{7,5},{8,14},{10,8},{12,... | collective-permute-start | bytes 294920 | tf_op jit(solution)/shard_map/ppermute | solution.py:22
  16.6 5.1 %collective-permute-start.3 = (bf16[2,3,1,64,128]{4,3,2,1,0:T(8,128)(2,1)S(1)}, bf16[2,3,1,64,128]{4,3,2,1,0:T(8,128)(2,1)S(1)}, u32[]{:S(2)}, u32[]{:S(2)}) collective-permute-start(bf16[2,3,1,64,128]{4,3,2,1,0:T(8,128)(2,1)S(1)} %pad_maximum_fusion.6.refs_6_), channel_id=1, source_target_pairs={{0,2},{2,4},{4,6},{6,0},{1,3},{3,5},{5,7},{7,1},{8,10},{10,12},{12... | collective-permute-start | bytes 294920 | tf_op jit(solution)/shard_map/ppermute | solution.py:22
  17.1 4.7 %copy-start.7 = (bf16[3,128,128]{2,1,0:T(8,128)(2,1)S(1)}, bf16[3,128,128]{2,1,0:T(8,128)(2,1)}, u32[]{:S(2)}) copy-start(bf16[3,128,128]{2,1,0:T(8,128)(2,1)} %wl_ref.9) | copy-start | bytes 294916
  17.1 4.7 %copy-start.8 = (bf16[3,128,128]{2,1,0:T(8,128)(2,1)S(1)}, bf16[3,128,128]{2,1,0:T(8,128)(2,1)}, u32[]{:S(2)}) copy-start(bf16[3,128,128]{2,1,0:T(8,128)(2,1)} %wr_ref.1) | copy-start | bytes 294916
  17.1 4.7 %copy-start.9 = (bf16[3,128,128]{2,1,0:T(8,128)(2,1)S(1)}, bf16[3,128,128]{2,1,0:T(8,128)(2,1)}, u32[]{:S(2)}) copy-start(bf16[3,128,128]{2,1,0:T(8,128)(2,1)} %wi_ref.9) | copy-start | bytes 294916
  17.1 4.7 %copy-start.10 = (bf16[3,128,128]{2,1,0:T(8,128)(2,1)S(1)}, bf16[3,128,128]{2,1,0:T(8,128)(2,1)}, u32[]{:S(2)}) copy-start(bf16[3,128,128]{2,1,0:T(8,128)(2,1)} %wo_ref.9) | copy-start | bytes 294916
  21.8 1.4 %copy-start = (bf16[2,128,128]{2,1,0:T(8,128)(2,1)S(1)}, bf16[2,128,128]{2,1,0:T(8,128)(2,1)}, u32[]{:S(2)}) copy-start(bf16[2,128,128]{2,1,0:T(8,128)(2,1)} %refs_3_.3) | copy-start | bytes 196612
  21.8 1.4 %copy-start.1 = (bf16[2,128,128]{2,1,0:T(8,128)(2,1)S(1)}, bf16[2,128,128]{2,1,0:T(8,128)(2,1)}, u32[]{:S(2)}) copy-start(bf16[2,128,128]{2,1,0:T(8,128)(2,1)} %refs_4_.3) | copy-start | bytes 196612
  21.8 1.4 %copy-start.5 = (f32[2,128]{1,0:T(2,128)S(1)}, f32[2,128]{1,0:T(2,128)}, u32[]{:S(2)}) copy-start(f32[2,128]{1,0:T(2,128)} %refs_5_.3) | copy-start | bytes 3076
  23.2 9.2 %copy-start.11 = (bf16[128,169]{0,1:T(8,128)(2,1)S(1)}, bf16[128,169]{0,1:T(8,128)(2,1)}, u32[]{:S(2)}) copy-start(bf16[128,169]{0,1:T(8,128)(2,1)} %param.31) | copy-start | bytes 129796
  23.8 6.0 %collective-permute-start.8 = (bf16[2,1,1,64,128]{4,3,2,1,0:T(8,128)(2,1)S(1)}, bf16[2,1,1,64,128]{4,3,2,1,0:T(8,128)(2,1)S(1)}, u32[]{:S(2)}, u32[]{:S(2)}) collective-permute-start(bf16[2,1,1,64,128]{4,3,2,1,0:T(8,128)(2,1)S(1)} %bitcast.61), channel_id=1, source_target_pairs={{0,24},{8,0},{16,8},{24,16},{1,25},{9,1},{17,9},{25,17},{2,26},{10... | collective-permute-start | bytes 98312 | tf_op jit(solution)/shard_map/ppermute | solution.py:22
  25.6 6.2 %collective-permute-start.7 = (bf16[2,1,1,64,128]{4,3,2,1,0:T(8,128)(2,1)S(1)}, bf16[2,1,1,64,128]{4,3,2,1,0:T(8,128)(2,1)S(1)}, u32[]{:S(2)}, u32[]{:S(2)}) collective-permute-start(bf16[2,1,1,64,128]{4,3,2,1,0:T(8,128)(2,1)S(1)} %bitcast.62), channel_id=1, source_target_pairs={{0,8},{8,16},{16,24},{24,0},{1,9},{9,17},{17,25},{25,1},{2,10},{10... | collective-permute-start | bytes 98312 | tf_op jit(solution)/shard_map/ppermute | solution.py:22
  26.0 10.4 %collective-permute-start.11 = (bf16[2,3,128,128]{3,2,1,0:T(8,128)(2,1)S(1)}, bf16[2,3,128,128]{3,2,1,0:T(8,128)(2,1)S(1)}, u32[]{:S(2)}, u32[]{:S(2)}) collective-permute-start(bf16[2,3,128,128]{3,2,1,0:T(8,128)(2,1)S(1)} %get-tuple-element.42), channel_id=1, source_target_pairs={{0,8},{8,16},{16,24},{24,0},{1,9},{9,17},{17,25},{25,1},{2,10},{10... | collective-permute-start | bytes 589832 | tf_op jit(solution)/shard_map/ppermute | solution.py:22
  26.0 11.3 %collective-permute-start.12 = (bf16[2,3,128,128]{3,2,1,0:T(8,128)(2,1)S(1)}, bf16[2,3,128,128]{3,2,1,0:T(8,128)(2,1)S(1)}, u32[]{:S(2)}, u32[]{:S(2)}) collective-permute-start(bf16[2,3,128,128]{3,2,1,0:T(8,128)(2,1)S(1)} %get-tuple-element.43), channel_id=1, source_target_pairs={{0,24},{8,0},{16,8},{24,16},{1,25},{9,1},{17,9},{25,17},{2,26},{10... | collective-permute-start | bytes 589832 | tf_op jit(solution)/shard_map/ppermute | solution.py:22
  31.8 3.0 %collective-permute-start.10 = (bf16[2,3,1,64,128]{4,3,2,1,0:T(8,128)(2,1)S(1)}, bf16[2,3,1,64,128]{4,3,2,1,0:T(8,128)(2,1)S(1)}, u32[]{:S(2)}, u32[]{:S(2)}) collective-permute-start(bf16[2,3,1,64,128]{4,3,2,1,0:T(8,128)(2,1)S(1)} %pad_maximum_fusion.7), channel_id=1, source_target_pairs={{0,6},{2,0},{4,2},{6,4},{1,7},{3,1},{5,3},{7,5},{8,14},{10,8},{12,... | collective-permute-start | bytes 294920 | tf_op jit(solution)/shard_map/ppermute | solution.py:22
  31.9 4.4 %collective-permute-start.9 = (bf16[2,3,1,64,128]{4,3,2,1,0:T(8,128)(2,1)S(1)}, bf16[2,3,1,64,128]{4,3,2,1,0:T(8,128)(2,1)S(1)}, u32[]{:S(2)}, u32[]{:S(2)}) collective-permute-start(bf16[2,3,1,64,128]{4,3,2,1,0:T(8,128)(2,1)S(1)} %pad_maximum_fusion.7), channel_id=1, source_target_pairs={{0,2},{2,4},{4,6},{6,0},{1,3},{3,5},{5,7},{7,1},{8,10},{10,12},{12... | collective-permute-start | bytes 294920 | tf_op jit(solution)/shard_map/ppermute | solution.py:22
  38.1 5.8 %collective-permute-start.16 = (bf16[2,1,1,64,128]{4,3,2,1,0:T(8,128)(2,1)S(1)}, bf16[2,1,1,64,128]{4,3,2,1,0:T(8,128)(2,1)S(1)}, u32[]{:S(2)}, u32[]{:S(2)}) collective-permute-start(bf16[2,1,1,64,128]{4,3,2,1,0:T(8,128)(2,1)S(1)} %bitcast.69), channel_id=1, source_target_pairs={{0,24},{8,0},{16,8},{24,16},{1,25},{9,1},{17,9},{25,17},{2,26},{10... | collective-permute-start | bytes 98312 | tf_op jit(solution)/shard_map/ppermute | solution.py:22
  40.9 5.7 %collective-permute-start.15 = (bf16[2,1,1,64,128]{4,3,2,1,0:T(8,128)(2,1)S(1)}, bf16[2,1,1,64,128]{4,3,2,1,0:T(8,128)(2,1)S(1)}, u32[]{:S(2)}, u32[]{:S(2)}) collective-permute-start(bf16[2,1,1,64,128]{4,3,2,1,0:T(8,128)(2,1)S(1)} %bitcast.70), channel_id=1, source_target_pairs={{0,8},{8,16},{16,24},{24,0},{1,9},{9,17},{17,25},{25,1},{2,10},{10... | collective-permute-start | bytes 98312 | tf_op jit(solution)/shard_map/ppermute | solution.py:22
  40.9 7.0 %collective-permute-start.13 = (bf16[2,3,128,128]{3,2,1,0:T(8,128)(2,1)S(1)}, bf16[2,3,128,128]{3,2,1,0:T(8,128)(2,1)S(1)}, u32[]{:S(2)}, u32[]{:S(2)}) collective-permute-start(bf16[2,3,128,128]{3,2,1,0:T(8,128)(2,1)S(1)} %get-tuple-element.39), channel_id=1, source_target_pairs={{0,2},{2,4},{4,6},{6,0},{1,3},{3,5},{5,7},{7,1},{8,10},{10,12},{12... | collective-permute-start | bytes 589832 | tf_op jit(solution)/shard_map/ppermute | solution.py:22
  40.9 7.0 %collective-permute-start.14 = (bf16[2,3,128,128]{3,2,1,0:T(8,128)(2,1)S(1)}, bf16[2,3,128,128]{3,2,1,0:T(8,128)(2,1)S(1)}, u32[]{:S(2)}, u32[]{:S(2)}) collective-permute-start(bf16[2,3,128,128]{3,2,1,0:T(8,128)(2,1)S(1)} %get-tuple-element.40), channel_id=1, source_target_pairs={{0,6},{2,0},{4,2},{6,4},{1,7},{3,1},{5,3},{7,5},{8,14},{10,8},{12,... | collective-permute-start | bytes 589832 | tf_op jit(solution)/shard_map/ppermute | solution.py:22
  46.6 4.0 %collective-permute-start.18 = (bf16[2,3,1,64,128]{4,3,2,1,0:T(8,128)(2,1)S(1)}, bf16[2,3,1,64,128]{4,3,2,1,0:T(8,128)(2,1)S(1)}, u32[]{:S(2)}, u32[]{:S(2)}) collective-permute-start(bf16[2,3,1,64,128]{4,3,2,1,0:T(8,128)(2,1)S(1)} %pad_maximum_fusion.8), channel_id=1, source_target_pairs={{0,6},{2,0},{4,2},{6,4},{1,7},{3,1},{5,3},{7,5},{8,14},{10,8},{12,... | collective-permute-start | bytes 294920 | tf_op jit(solution)/shard_map/ppermute | solution.py:22
  46.6 4.1 %collective-permute-start.17 = (bf16[2,3,1,64,128]{4,3,2,1,0:T(8,128)(2,1)S(1)}, bf16[2,3,1,64,128]{4,3,2,1,0:T(8,128)(2,1)S(1)}, u32[]{:S(2)}, u32[]{:S(2)}) collective-permute-start(bf16[2,3,1,64,128]{4,3,2,1,0:T(8,128)(2,1)S(1)} %pad_maximum_fusion.8), channel_id=1, source_target_pairs={{0,2},{2,4},{4,6},{6,0},{1,3},{3,5},{5,7},{7,1},{8,10},{10,12},{12... | collective-permute-start | bytes 294920 | tf_op jit(solution)/shard_map/ppermute | solution.py:22
